TPU v7x, 512 devices: a whole 4x4x16 slice. The times are simulated.
512 devices in a mesh: section: 16 (over x, z_hi), mp: 8 (over y, core), dp: 4 (over z_lo).
Axes of the slice: x: 4, y: 4, z: 16 (z_hi: 4, z_lo: 4; z = z_hi * 4 + z_lo), core: 2. Of those that a mesh axis runs over, the one named last changes fastest.
Arguments:
- section_inputs: bfloat16 [16, 8, 64, 5120], P('section', None, 'dp'), may hold values from -480 to 480
- out_grads: bfloat16 [8, 64, 5120], P(None, 'dp'), may hold values from -6 to 6
- proj_weight: bfloat16 [16, 5120, 5120], P('section', 'mp', 'dp'), may hold values from -0.13975425 to 0.13975425
- norm_gain: float32 [16, 5120], P('section', 'mp'), may hold values from 0.1 to 1.9
- adapter_down: bfloat16 [16, 8, 5120, 16], P('section', None, 'mp'), may hold values from -0.078125 to 0.078125
- adapter_up: bfloat16 [16, 8, 16, 5120], P('section'), may hold values from -0.25 to 0.25
- tenant_ids: int32 [8], replicated, may hold values from 0 to 7, each once
- slot_table: int32 [16, 8], P('section'), may hold values from 0 to 7, each once within a row
Outputs:
- input_grads: bfloat16 [16, 8, 64, 5120], P('section', None, 'dp', 'mp')
- down_grads: float32 [16, 8, 5120, 16], P('section', None, 'mp')
- up_grads: float32 [16, 8, 16, 5120], P('section', None, None, 'mp')
Inputs may be any that keep to these rules, and one draw needn't show every extreme that they name: `tenant_ids`: each micro-batch belongs to another tenant. `slot_table`: each row is a permutation.
All inputs are finite; a program needn't handle non-finite values.
Results may differ from a plain program's by a relative error of at most 0.015.
Values may be sent and summed in bfloat16 or wider, within the bound.
No kernel may reach another device: no remote copies, remote signals or barrier semaphores. Data moves between devices by JAX's collectives and lax.ppermute only.
A program may use at most 64 MiB of HBM per device.

v0:
```python
import jax
import jax.numpy as jnp
from jax import lax
from jax.sharding import PartitionSpec as P

norm_eps = 1e-05
low_rank_scale = 2.0


def shifted(value, axis, steps):
    count = lax.axis_size(axis)
    initial, last = (max(0, -steps), min(count, count - steps))
    return lax.ppermute(value, axis, [(source, source + steps) for source in range(initial, last)])


def local(
    section_inputs,
    out_grads,
    proj_weight,
    norm_gain,
    adapter_down,
    adapter_up,
    tenant_ids,
    slot_table,
):
    section_count = lax.axis_size("section")
    section_pos = lax.axis_index("section")
    width_pos = lax.axis_index("mp")
    micro_count = section_inputs.shape[1]
    row_count = section_inputs.shape[2]
    width_all = section_inputs.shape[3]
    width_local = proj_weight.shape[1]
    rank_size = adapter_down.shape[3]
    gathered_tokens = row_count * lax.axis_size("dp")
    multiplier = low_rank_scale / gathered_tokens
    contract_last = (((1,), (1,)), ((), ()))
    contract_first = (((0,), (0,)), ((), ()))
    weight_full = lax.all_gather(proj_weight[0], "dp", axis=1, tiled=True)
    inputs = section_inputs[0].astype(jnp.float32)
    inv_rms = lax.rsqrt(jnp.mean(inputs * inputs, axis=-1, keepdims=True) + norm_eps)
    normed = inputs * inv_rms
    normed_local = lax.dynamic_slice_in_dim(normed, width_pos * width_local, width_local, 2)
    shard_norm_gain = norm_gain[0]
    hidden_local = (normed_local * shard_norm_gain).astype(jnp.bfloat16)
    micro_iota = jnp.arange(micro_count, dtype=jnp.int32)
    tenant_hot = tenant_ids[:, None] == micro_iota[None, :]
    slot_ids = jnp.sum(jnp.where(tenant_hot, slot_table[0][None, :], 0), axis=1)
    selected_down_weight = adapter_down[0][slot_ids]
    up_sel = adapter_up[0][slot_ids]
    partial_in = jnp.einsum(
        "mtd,mdr->mtr", hidden_local, selected_down_weight, preferred_element_type=jnp.float32
    )
    low_in = lax.psum(partial_in, "mp").astype(jnp.bfloat16)

    def project_grads(grad_rows, micro_idx):
        up_one = lax.dynamic_index_in_dim(up_sel, micro_idx, 0, keepdims=False)
        down_one = lax.dynamic_index_in_dim(selected_down_weight, micro_idx, 0, keepdims=False)
        low_rank_output = lax.dot_general(
            grad_rows, up_one, contract_last, preferred_element_type=jnp.float32
        ).astype(jnp.bfloat16)
        frozen_path_gradient = lax.dot_general(
            grad_rows, weight_full, contract_last, preferred_element_type=jnp.float32
        )
        low_rank_contribution = lax.dot_general(
            low_rank_output, down_one, contract_last, preferred_element_type=jnp.float32
        )
        normalized_gradient = (
            (frozen_path_gradient + low_rank_scale * low_rank_contribution) * shard_norm_gain
        ).astype(jnp.bfloat16)
        return (normalized_gradient, low_rank_output)

    def empty_grads(grad_rows, micro_idx):
        return (
            jnp.zeros((row_count, width_local), jnp.bfloat16),
            jnp.zeros((row_count, rank_size), jnp.bfloat16),
        )

    def one_tick(tick_step, state_tuple):
        incoming, kept_grads, down_acc, up_acc = state_tuple
        micro_step = tick_step - (section_count - 1 - section_pos)
        in_range = (micro_step >= 0) & (micro_step < micro_count)
        clipped = jnp.clip(micro_step, 0, micro_count - 1)
        last_grads = lax.dynamic_index_in_dim(out_grads, clipped, 0, keepdims=False)
        inv_one = lax.dynamic_index_in_dim(inv_rms, clipped, 0, keepdims=False)
        grad_rows = jnp.where(section_pos == section_count - 1, last_grads, incoming)
        normalized_gradient, low_rank_output = lax.cond(
            in_range, project_grads, empty_grads, grad_rows, clipped
        )
        full_grad = lax.all_gather(normalized_gradient, "mp", axis=1, tiled=True)
        normed_one = lax.dynamic_index_in_dim(normed, clipped, 0, keepdims=False)
        norm_rows = full_grad.astype(jnp.float32)
        row_stat = jnp.mean(norm_rows * normed_one, axis=-1, keepdims=True)
        new_grads = (
            grad_rows.astype(jnp.float32) + inv_one * (norm_rows - normed_one * row_stat)
        ).astype(jnp.bfloat16)
        passed_grads = shifted(new_grads, "section", -1)
        local_new = lax.dynamic_slice_in_dim(new_grads, width_pos * width_local, width_local, 1)
        grads_local = lax.dynamic_slice_in_dim(grad_rows, width_pos * width_local, width_local, 1)
        micro_hot = micro_iota == micro_step
        kept_grads = jnp.where(micro_hot[:, None, None], local_new[None], kept_grads)
        hidden_one = lax.dynamic_index_in_dim(hidden_local, clipped, 0, keepdims=False)
        low_in_one = lax.dynamic_index_in_dim(low_in, clipped, 0, keepdims=False)
        down_term = multiplier * lax.dot_general(
            hidden_one, low_rank_output, contract_first, preferred_element_type=jnp.float32
        )
        up_term = multiplier * lax.dot_general(
            low_in_one, grads_local, contract_first, preferred_element_type=jnp.float32
        )
        down_acc = down_acc + jnp.where(micro_hot[:, None, None], down_term[None], 0.0)
        up_acc = up_acc + jnp.where(micro_hot[:, None, None], up_term[None], 0.0)
        return (passed_grads, kept_grads, down_acc, up_acc)

    start_state = (
        jnp.zeros((row_count, width_all), jnp.bfloat16),
        jnp.zeros((micro_count, row_count, width_local), jnp.bfloat16),
        jnp.zeros((micro_count, width_local, rank_size), jnp.float32),
        jnp.zeros((micro_count, rank_size, width_local), jnp.float32),
    )
    final_state = lax.fori_loop(0, section_count + micro_count - 1, one_tick, start_state)
    kept_grads = final_state[1]
    down_acc = final_state[2]
    up_acc = final_state[3]
    down_acc, up_acc = lax.psum((down_acc, up_acc), "dp")
    slot_hot = slot_ids[None, :] == micro_iota[:, None]
    down_out = jnp.sum(jnp.where(slot_hot[:, :, None, None], down_acc[None], 0.0), axis=1)
    up_out = jnp.sum(jnp.where(slot_hot[:, :, None, None], up_acc[None], 0.0), axis=1)
    return (kept_grads[None], down_out[None], up_out[None])


def solution(mesh):
    placed = (
        P("section", None, "dp", None),
        P(None, "dp", None),
        P("section", "mp", "dp"),
        P("section", "mp"),
        P("section", None, "mp", None),
        P("section", None, None, None),
        P(),
        P("section", None),
    )
    return jax.shard_map(
        local,
        mesh=mesh,
        in_specs=placed,
        out_specs=(
            P("section", None, "dp", "mp"),
            P("section", None, "mp", None),
            P("section", None, None, "mp"),
        ),
        check_vma=False,
    )
```

profile of v0, /device:TPU:1, one launch (start us, length us, event | category | flops | bytes accessed | tf_op | source)
XLA Modules:
  0.0 1072.0 jit_solution(14016219959135633366)
XLA Ops:
  14.7 28.1 %psum.21 = bf16[8,16,16]{2,1,0:T(8,128)(2,1)S(1)} all-reduce(f32[8,16,16]{2,1,0:T(8,128)S(1)} %fusion.26), channel_id=1, replica_groups=mesh['section'=16,'mp'=8,'dp'=4] {'mp'}, use_global_device_ids=true, to_apply=%region_2.3 | all-reduce | flops 2048 | bytes 12288 | tf_op jit(solution)/shard_map/psum | solution.py:53
  42.8 100.7 %all-gather.3.cloned.1.call-done = bf16[1,640,5120]{2,1,0:T(8,128)(2,1)} async-done(((bf16[1,640,1280]{2,1,0:T(8,128)(2,1)}), bf16[1,640,5120]{2,1,0:T(8,128)(2,1)}) %all-gather.3.cloned.1.call-update) | async-done | bytes 6553616 | tf_op jit(solution)/shard_map/all_gather | solution.py:38
  143.4 842.6 %while.22 = (s32[]{:T(128)}, bf16[16,5120]{1,0:T(8,128)(2,1)S(1)}, bf16[8,16,640]{2,1,0:T(8,128)(2,1)}, f32[8,640,16]{1,2,0:T(8,128)S(1)}, f32[8,16,640]{2,1,0:T...) while((s32[]{:T(128)}, bf16[16,5120]{1,0:T(8,128)(2,1)S(1)}, ...), condition=%wide.region_7.8_spmd.clone, body=%wide.region_3.7_spmd.clone.sunk | while | flops 110080272 | bytes 13041114 | solution.py:119
  145.0 13.8 %all_gather.15 = bf16[16,5120]{1,0:T(8,128)(2,1)S(1)} all-gather(bf16[16,640]{1,0:T(8,128)(2,1)S(1)} %get-tuple-element.668), channel_id=1, replica_groups=mesh['section'=16,'mp'=8,'dp'=4] {'mp'}, dimensions={1}, use_global_device_ids=true | all-gather | bytes 184320 | tf_op jit(solution)/shard_map/while/body/eval_jaxpr/all_gather | solution.py:89
  163.7 19.5 %collective-permute-done = bf16[16,5120]{1,0:T(8,128)(2,1)S(1)} collective-permute-done((bf16[16,5120]{1,0:T(8,128)(2,1)S(1)}, bf16[16,5120]{1,0:T(8,128)(2,1)S(1)}, u32[]{:S(2)}, u32[]{:S(2)}) %collective-permute-start) | collective-permute-done | bytes 163872 | tf_op jit(solution)/shard_map/while/body/eval_jaxpr/ppermute | solution.py:13
  184.8 13.6 %all_gather.15 = bf16[16,5120]{1,0:T(8,128)(2,1)S(1)} all-gather(bf16[16,640]{1,0:T(8,128)(2,1)S(1)} %get-tuple-element.668), channel_id=1, replica_groups=mesh['section'=16,'mp'=8,'dp'=4] {'mp'}, dimensions={1}, use_global_device_ids=true | all-gather | bytes 184320 | tf_op jit(solution)/shard_map/while/body/eval_jaxpr/all_gather | solution.py:89
  203.4 14.0 %collective-permute-done = bf16[16,5120]{1,0:T(8,128)(2,1)S(1)} collective-permute-done((bf16[16,5120]{1,0:T(8,128)(2,1)S(1)}, bf16[16,5120]{1,0:T(8,128)(2,1)S(1)}, u32[]{:S(2)}, u32[]{:S(2)}) %collective-permute-start) | collective-permute-done | bytes 163872 | tf_op jit(solution)/shard_map/while/body/eval_jaxpr/ppermute | solution.py:13
  218.9 13.2 %all_gather.15 = bf16[16,5120]{1,0:T(8,128)(2,1)S(1)} all-gather(bf16[16,640]{1,0:T(8,128)(2,1)S(1)} %get-tuple-element.668), channel_id=1, replica_groups=mesh['section'=16,'mp'=8,'dp'=4] {'mp'}, dimensions={1}, use_global_device_ids=true | all-gather | bytes 184320 | tf_op jit(solution)/shard_map/while/body/eval_jaxpr/all_gather | solution.py:89
  237.0 13.0 %collective-permute-done = bf16[16,5120]{1,0:T(8,128)(2,1)S(1)} collective-permute-done((bf16[16,5120]{1,0:T(8,128)(2,1)S(1)}, bf16[16,5120]{1,0:T(8,128)(2,1)S(1)}, u32[]{:S(2)}, u32[]{:S(2)}) %collective-permute-start) | collective-permute-done | bytes 163872 | tf_op jit(solution)/shard_map/while/body/eval_jaxpr/ppermute | solution.py:13
  251.6 13.2 %all_gather.15 = bf16[16,5120]{1,0:T(8,128)(2,1)S(1)} all-gather(bf16[16,640]{1,0:T(8,128)(2,1)S(1)} %get-tuple-element.668), channel_id=1, replica_groups=mesh['section'=16,'mp'=8,'dp'=4] {'mp'}, dimensions={1}, use_global_device_ids=true | all-gather | bytes 184320 | tf_op jit(solution)/shard_map/while/body/eval_jaxpr/all_gather | solution.py:89
  269.7 12.9 %collective-permute-done = bf16[16,5120]{1,0:T(8,128)(2,1)S(1)} collective-permute-done((bf16[16,5120]{1,0:T(8,128)(2,1)S(1)}, bf16[16,5120]{1,0:T(8,128)(2,1)S(1)}, u32[]{:S(2)}, u32[]{:S(2)}) %collective-permute-start) | collective-permute-done | bytes 163872 | tf_op jit(solution)/shard_map/while/body/eval_jaxpr/ppermute | solution.py:13
  284.2 13.2 %all_gather.15 = bf16[16,5120]{1,0:T(8,128)(2,1)S(1)} all-gather(bf16[16,640]{1,0:T(8,128)(2,1)S(1)} %get-tuple-element.668), channel_id=1, replica_groups=mesh['section'=16,'mp'=8,'dp'=4] {'mp'}, dimensions={1}, use_global_device_ids=true | all-gather | bytes 184320 | tf_op jit(solution)/shard_map/while/body/eval_jaxpr/all_gather | solution.py:89
  302.4 12.2 %collective-permute-done = bf16[16,5120]{1,0:T(8,128)(2,1)S(1)} collective-permute-done((bf16[16,5120]{1,0:T(8,128)(2,1)S(1)}, bf16[16,5120]{1,0:T(8,128)(2,1)S(1)}, u32[]{:S(2)}, u32[]{:S(2)}) %collective-permute-start) | collective-permute-done | bytes 163872 | tf_op jit(solution)/shard_map/while/body/eval_jaxpr/ppermute | solution.py:13
  316.2 13.7 %all_gather.15 = bf16[16,5120]{1,0:T(8,128)(2,1)S(1)} all-gather(bf16[16,640]{1,0:T(8,128)(2,1)S(1)} %get-tuple-element.668), channel_id=1, replica_groups=mesh['section'=16,'mp'=8,'dp'=4] {'mp'}, dimensions={1}, use_global_device_ids=true | all-gather | bytes 184320 | tf_op jit(solution)/shard_map/while/body/eval_jaxpr/all_gather | solution.py:89
  334.8 10.8 %collective-permute-done = bf16[16,5120]{1,0:T(8,128)(2,1)S(1)} collective-permute-done((bf16[16,5120]{1,0:T(8,128)(2,1)S(1)}, bf16[16,5120]{1,0:T(8,128)(2,1)S(1)}, u32[]{:S(2)}, u32[]{:S(2)}) %collective-permute-start) | collective-permute-done | bytes 163872 | tf_op jit(solution)/shard_map/while/body/eval_jaxpr/ppermute | solution.py:13
  347.2 13.2 %all_gather.15 = bf16[16,5120]{1,0:T(8,128)(2,1)S(1)} all-gather(bf16[16,640]{1,0:T(8,128)(2,1)S(1)} %get-tuple-element.668), channel_id=1, replica_groups=mesh['section'=16,'mp'=8,'dp'=4] {'mp'}, dimensions={1}, use_global_device_ids=true | all-gather | bytes 184320 | tf_op jit(solution)/shard_map/while/body/eval_jaxpr/all_gather | solution.py:89
  365.3 9.0 collective-permute-done
  375.9 13.6 %all_gather.15 = bf16[16,5120]{1,0:T(8,128)(2,1)S(1)} all-gather(bf16[16,640]{1,0:T(8,128)(2,1)S(1)} %get-tuple-element.668), channel_id=1, replica_groups=mesh['section'=16,'mp'=8,'dp'=4] {'mp'}, dimensions={1}, use_global_device_ids=true | all-gather | bytes 184320 | tf_op jit(solution)/shard_map/while/body/eval_jaxpr/all_gather | solution.py:89
  394.4 8.8 collective-permute-done
  404.8 13.7 %all_gather.15 = bf16[16,5120]{1,0:T(8,128)(2,1)S(1)} all-gather(bf16[16,640]{1,0:T(8,128)(2,1)S(1)} %get-tuple-element.668), channel_id=1, replica_groups=mesh['section'=16,'mp'=8,'dp'=4] {'mp'}, dimensions={1}, use_global_device_ids=true | all-gather | bytes 184320 | tf_op jit(solution)/shard_map/while/body/eval_jaxpr/all_gather | solution.py:89
  423.4 8.8 collective-permute-done
  433.8 13.7 %all_gather.15 = bf16[16,5120]{1,0:T(8,128)(2,1)S(1)} all-gather(bf16[16,640]{1,0:T(8,128)(2,1)S(1)} %get-tuple-element.668), channel_id=1, replica_groups=mesh['section'=16,'mp'=8,'dp'=4] {'mp'}, dimensions={1}, use_global_device_ids=true | all-gather | bytes 184320 | tf_op jit(solution)/shard_map/while/body/eval_jaxpr/all_gather | solution.py:89
  452.4 8.8 collective-permute-done
  462.8 13.7 %all_gather.15 = bf16[16,5120]{1,0:T(8,128)(2,1)S(1)} all-gather(bf16[16,640]{1,0:T(8,128)(2,1)S(1)} %get-tuple-element.668), channel_id=1, replica_groups=mesh['section'=16,'mp'=8,'dp'=4] {'mp'}, dimensions={1}, use_global_device_ids=true | all-gather | bytes 184320 | tf_op jit(solution)/shard_map/while/body/eval_jaxpr/all_gather | solution.py:89
  481.4 8.9 collective-permute-done
  491.9 13.7 %all_gather.15 = bf16[16,5120]{1,0:T(8,128)(2,1)S(1)} all-gather(bf16[16,640]{1,0:T(8,128)(2,1)S(1)} %get-tuple-element.668), channel_id=1, replica_groups=mesh['section'=16,'mp'=8,'dp'=4] {'mp'}, dimensions={1}, use_global_device_ids=true | all-gather | bytes 184320 | tf_op jit(solution)/shard_map/while/body/eval_jaxpr/all_gather | solution.py:89
  510.5 10.0 collective-permute-done
  522.1 13.5 %all_gather.15 = bf16[16,5120]{1,0:T(8,128)(2,1)S(1)} all-gather(bf16[16,640]{1,0:T(8,128)(2,1)S(1)} %get-tuple-element.668), channel_id=1, replica_groups=mesh['section'=16,'mp'=8,'dp'=4] {'mp'}, dimensions={1}, use_global_device_ids=true | all-gather | bytes 184320 | tf_op jit(solution)/shard_map/while/body/eval_jaxpr/all_gather | solution.py:89
  540.5 10.0 collective-permute-done
  552.1 13.5 %all_gather.15 = bf16[16,5120]{1,0:T(8,128)(2,1)S(1)} all-gather(bf16[16,640]{1,0:T(8,128)(2,1)S(1)} %get-tuple-element.668), channel_id=1, replica_groups=mesh['section'=16,'mp'=8,'dp'=4] {'mp'}, dimensions={1}, use_global_device_ids=true | all-gather | bytes 184320 | tf_op jit(solution)/shard_map/while/body/eval_jaxpr/all_gather | solution.py:89
  570.5 9.9 collective-permute-done
  582.0 13.5 %all_gather.15 = bf16[16,5120]{1,0:T(8,128)(2,1)S(1)} all-gather(bf16[16,640]{1,0:T(8,128)(2,1)S(1)} %get-tuple-element.668), channel_id=1, replica_groups=mesh['section'=16,'mp'=8,'dp'=4] {'mp'}, dimensions={1}, use_global_device_ids=true | all-gather | bytes 184320 | tf_op jit(solution)/shard_map/while/body/eval_jaxpr/all_gather | solution.py:89
  600.4 63.9 %collective-permute-done = bf16[16,5120]{1,0:T(8,128)(2,1)S(1)} collective-permute-done((bf16[16,5120]{1,0:T(8,128)(2,1)S(1)}, bf16[16,5120]{1,0:T(8,128)(2,1)S(1)}, u32[]{:S(2)}, u32[]{:S(2)}) %collective-permute-start) | collective-permute-done | bytes 163872 | tf_op jit(solution)/shard_map/while/body/eval_jaxpr/ppermute | solution.py:13
  665.2 7.3 conditional.3
  666.9 4.6 fusion.25
  672.5 13.4 %all_gather.15 = bf16[16,5120]{1,0:T(8,128)(2,1)S(1)} all-gather(bf16[16,640]{1,0:T(8,128)(2,1)S(1)} %get-tuple-element.668), channel_id=1, replica_groups=mesh['section'=16,'mp'=8,'dp'=4] {'mp'}, dimensions={1}, use_global_device_ids=true | all-gather | bytes 184320 | tf_op jit(solution)/shard_map/while/body/eval_jaxpr/all_gather | solution.py:89
  690.8 23.9 %collective-permute-done = bf16[16,5120]{1,0:T(8,128)(2,1)S(1)} collective-permute-done((bf16[16,5120]{1,0:T(8,128)(2,1)S(1)}, bf16[16,5120]{1,0:T(8,128)(2,1)S(1)}, u32[]{:S(2)}, u32[]{:S(2)}) %collective-permute-start) | collective-permute-done | bytes 163872 | tf_op jit(solution)/shard_map/while/body/eval_jaxpr/ppermute | solution.py:13
  715.7 7.3 conditional.3
  717.5 4.6 fusion.25
  723.0 13.4 %all_gather.15 = bf16[16,5120]{1,0:T(8,128)(2,1)S(1)} all-gather(bf16[16,640]{1,0:T(8,128)(2,1)S(1)} %get-tuple-element.668), channel_id=1, replica_groups=mesh['section'=16,'mp'=8,'dp'=4] {'mp'}, dimensions={1}, use_global_device_ids=true | all-gather | bytes 184320 | tf_op jit(solution)/shard_map/while/body/eval_jaxpr/all_gather | solution.py:89
  741.4 10.1 collective-permute-done
  752.4 7.3 conditional.3
  754.1 4.6 fusion.25
  759.7 13.4 %all_gather.15 = bf16[16,5120]{1,0:T(8,128)(2,1)S(1)} all-gather(bf16[16,640]{1,0:T(8,128)(2,1)S(1)} %get-tuple-element.668), channel_id=1, replica_groups=mesh['section'=16,'mp'=8,'dp'=4] {'mp'}, dimensions={1}, use_global_device_ids=true | all-gather | bytes 184320 | tf_op jit(solution)/shard_map/while/body/eval_jaxpr/all_gather | solution.py:89
  778.1 10.1 collective-permute-done
  789.1 7.3 conditional.3
  790.8 4.6 fusion.25
  796.4 13.4 %all_gather.15 = bf16[16,5120]{1,0:T(8,128)(2,1)S(1)} all-gather(bf16[16,640]{1,0:T(8,128)(2,1)S(1)} %get-tuple-element.668), channel_id=1, replica_groups=mesh['section'=16,'mp'=8,'dp'=4] {'mp'}, dimensions={1}, use_global_device_ids=true | all-gather | bytes 184320 | tf_op jit(solution)/shard_map/while/body/eval_jaxpr/all_gather | solution.py:89
  814.7 15.8 %collective-permute-done = bf16[16,5120]{1,0:T(8,128)(2,1)S(1)} collective-permute-done((bf16[16,5120]{1,0:T(8,128)(2,1)S(1)}, bf16[16,5120]{1,0:T(8,128)(2,1)S(1)}, u32[]{:S(2)}, u32[]{:S(2)}) %collective-permute-start) | collective-permute-done | bytes 163872 | tf_op jit(solution)/shard_map/while/body/eval_jaxpr/ppermute | solution.py:13
  831.4 7.3 conditional.3
  833.2 4.6 fusion.25
  838.7 13.4 %all_gather.15 = bf16[16,5120]{1,0:T(8,128)(2,1)S(1)} all-gather(bf16[16,640]{1,0:T(8,128)(2,1)S(1)} %get-tuple-element.668), channel_id=1, replica_groups=mesh['section'=16,'mp'=8,'dp'=4] {'mp'}, dimensions={1}, use_global_device_ids=true | all-gather | bytes 184320 | tf_op jit(solution)/shard_map/while/body/eval_jaxpr/all_gather | solution.py:89
  857.1 10.1 collective-permute-done
  868.1 7.3 conditional.3
  869.8 4.6 fusion.25
  875.4 13.4 %all_gather.15 = bf16[16,5120]{1,0:T(8,128)(2,1)S(1)} all-gather(bf16[16,640]{1,0:T(8,128)(2,1)S(1)} %get-tuple-element.668), channel_id=1, replica_groups=mesh['section'=16,'mp'=8,'dp'=4] {'mp'}, dimensions={1}, use_global_device_ids=true | all-gather | bytes 184320 | tf_op jit(solution)/shard_map/while/body/eval_jaxpr/all_gather | solution.py:89
  893.8 10.3 collective-permute-done
  905.0 7.3 conditional.3
  912.3 13.4 %all_gather.15 = bf16[16,5120]{1,0:T(8,128)(2,1)S(1)} all-gather(bf16[16,640]{1,0:T(8,128)(2,1)S(1)} %get-tuple-element.668), channel_id=1, replica_groups=mesh['section'=16,'mp'=8,'dp'=4] {'mp'}, dimensions={1}, use_global_device_ids=true | all-gather | bytes 184320 | tf_op jit(solution)/shard_map/while/body/eval_jaxpr/all_gather | solution.py:89
  930.6 15.6 %collective-permute-done = bf16[16,5120]{1,0:T(8,128)(2,1)S(1)} collective-permute-done((bf16[16,5120]{1,0:T(8,128)(2,1)S(1)}, bf16[16,5120]{1,0:T(8,128)(2,1)S(1)}, u32[]{:S(2)}, u32[]{:S(2)}) %collective-permute-start) | collective-permute-done | bytes 163872 | tf_op jit(solution)/shard_map/while/body/eval_jaxpr/ppermute | solution.py:13
  947.2 7.3 conditional.3
  954.5 13.4 %all_gather.15 = bf16[16,5120]{1,0:T(8,128)(2,1)S(1)} all-gather(bf16[16,640]{1,0:T(8,128)(2,1)S(1)} %get-tuple-element.668), channel_id=1, replica_groups=mesh['section'=16,'mp'=8,'dp'=4] {'mp'}, dimensions={1}, use_global_device_ids=true | all-gather | bytes 184320 | tf_op jit(solution)/shard_map/while/body/eval_jaxpr/all_gather | solution.py:89
  972.9 13.2 %collective-permute-done = bf16[16,5120]{1,0:T(8,128)(2,1)S(1)} collective-permute-done((bf16[16,5120]{1,0:T(8,128)(2,1)S(1)}, bf16[16,5120]{1,0:T(8,128)(2,1)S(1)}, u32[]{:S(2)}, u32[]{:S(2)}) %collective-permute-start) | collective-permute-done | bytes 163872 | tf_op jit(solution)/shard_map/while/body/eval_jaxpr/ppermute | solution.py:13
  986.9 74.1 %all-reduce.3.cloned.1.call-done = (f32[8,640,16]{1,2,0:T(8,128)}, f32[8,16,640]{2,1,0:T(8,128)}) async-done(((f32[8,640,16]{1,2,0:T(8,128)}, f32[8,16,640]{2,1,0:T(8,128)}), (f32[8,640,16]{1,2,0:T(8,128)}, f32[8,16,640]{2,1,0:T(8,128)})) %all-reduce.3.cloned.1.call-update) | async-done | bytes 655376 | tf_op jit(solution)/shard_map/psum | solution.py:123
  (496 shorter events, 194.7 us)
Async XLA Ops:
  7.2 136.2 %all-gather.3.cloned.1.call-start = ((), (), s32[]{:S(2)}) async-start(), calls=%async_computation | async-start | bytes 8192000 | tf_op jit(solution)/shard_map/all_gather | solution.py:38
  7.9 1053.1 %all-reduce.3.cloned.1.call-start = ((), (), s32[]{:S(2)}) async-start(), calls=%async_computation.1 | async-start | bytes 1310720 | tf_op jit(solution)/shard_map/psum | solution.py:123
  145.0 18.6 %copy-start.5 = (bf16[8,16,640]{2,1,0:T(8,128)(2,1)S(1)}, bf16[8,16,640]{2,1,0:T(8,128)(2,1)}, u32[]{:S(2)}) copy-start(bf16[8,16,640]{2,1,0:T(8,128)(2,1)} %get-tuple-element.697) | copy-start | bytes 491524 | tf_op jit(solution)/shard_map/while
  161.1 22.2 %collective-permute-start = (bf16[16,5120]{1,0:T(8,128)(2,1)S(1)}, bf16[16,5120]{1,0:T(8,128)(2,1)S(1)}, u32[]{:S(2)}, u32[]{:S(2)}) collective-permute-start(bf16[16,5120]{1,0:T(8,128)(2,1)S(1)} %fusion.47), channel_id=1, source_target_pairs={{32,0},{64,32},{96,64},{128,96},{160,128},{192,160},{224,192},{256... | collective-permute-start | bytes 491528 | tf_op jit(solution)/shard_map/while/body/eval_jaxpr/ppermute | solution.py:13
  163.7 19.5 %copy-start.6 = (bf16[8,16,640]{2,1,0:T(8,128)(2,1)}, bf16[8,16,640]{2,1,0:T(8,128)(2,1)S(1)}, u32[]{:S(2)}) copy-start(bf16[8,16,640]{2,1,0:T(8,128)(2,1)S(1)} %select_select_fusion.2) | copy-start | bytes 491524 | tf_op jit(solution)/shard_map/while
  184.8 18.4 %copy-start.5 = (bf16[8,16,640]{2,1,0:T(8,128)(2,1)S(1)}, bf16[8,16,640]{2,1,0:T(8,128)(2,1)}, u32[]{:S(2)}) copy-start(bf16[8,16,640]{2,1,0:T(8,128)(2,1)} %get-tuple-element.697) | copy-start | bytes 491524 | tf_op jit(solution)/shard_map/while
  200.7 16.6 %collective-permute-start = (bf16[16,5120]{1,0:T(8,128)(2,1)S(1)}, bf16[16,5120]{1,0:T(8,128)(2,1)S(1)}, u32[]{:S(2)}, u32[]{:S(2)}) collective-permute-start(bf16[16,5120]{1,0:T(8,128)(2,1)S(1)} %fusion.47), channel_id=1, source_target_pairs={{32,0},{64,32},{96,64},{128,96},{160,128},{192,160},{224,192},{256... | collective-permute-start | bytes 491528 | tf_op jit(solution)/shard_map/while/body/eval_jaxpr/ppermute | solution.py:13
  203.3 14.0 %copy-start.6 = (bf16[8,16,640]{2,1,0:T(8,128)(2,1)}, bf16[8,16,640]{2,1,0:T(8,128)(2,1)S(1)}, u32[]{:S(2)}) copy-start(bf16[8,16,640]{2,1,0:T(8,128)(2,1)S(1)} %select_select_fusion.2) | copy-start | bytes 491524 | tf_op jit(solution)/shard_map/while
  218.9 18.0 %copy-start.5 = (bf16[8,16,640]{2,1,0:T(8,128)(2,1)S(1)}, bf16[8,16,640]{2,1,0:T(8,128)(2,1)}, u32[]{:S(2)}) copy-start(bf16[8,16,640]{2,1,0:T(8,128)(2,1)} %get-tuple-element.697) | copy-start | bytes 491524 | tf_op jit(solution)/shard_map/while
  234.4 15.7 %collective-permute-start = (bf16[16,5120]{1,0:T(8,128)(2,1)S(1)}, bf16[16,5120]{1,0:T(8,128)(2,1)S(1)}, u32[]{:S(2)}, u32[]{:S(2)}) collective-permute-start(bf16[16,5120]{1,0:T(8,128)(2,1)S(1)} %fusion.47), channel_id=1, source_target_pairs={{32,0},{64,32},{96,64},{128,96},{160,128},{192,160},{224,192},{256... | collective-permute-start | bytes 491528 | tf_op jit(solution)/shard_map/while/body/eval_jaxpr/ppermute | solution.py:13
  237.0 13.0 %copy-start.6 = (bf16[8,16,640]{2,1,0:T(8,128)(2,1)}, bf16[8,16,640]{2,1,0:T(8,128)(2,1)S(1)}, u32[]{:S(2)}) copy-start(bf16[8,16,640]{2,1,0:T(8,128)(2,1)S(1)} %select_select_fusion.2) | copy-start | bytes 491524 | tf_op jit(solution)/shard_map/while
  251.6 18.0 %copy-start.5 = (bf16[8,16,640]{2,1,0:T(8,128)(2,1)S(1)}, bf16[8,16,640]{2,1,0:T(8,128)(2,1)}, u32[]{:S(2)}) copy-start(bf16[8,16,640]{2,1,0:T(8,128)(2,1)} %get-tuple-element.697) | copy-start | bytes 491524 | tf_op jit(solution)/shard_map/while
  267.1 15.6 %collective-permute-start = (bf16[16,5120]{1,0:T(8,128)(2,1)S(1)}, bf16[16,5120]{1,0:T(8,128)(2,1)S(1)}, u32[]{:S(2)}, u32[]{:S(2)}) collective-permute-start(bf16[16,5120]{1,0:T(8,128)(2,1)S(1)} %fusion.47), channel_id=1, source_target_pairs={{32,0},{64,32},{96,64},{128,96},{160,128},{192,160},{224,192},{256... | collective-permute-start | bytes 491528 | tf_op jit(solution)/shard_map/while/body/eval_jaxpr/ppermute | solution.py:13
  269.7 12.9 %copy-start.6 = (bf16[8,16,640]{2,1,0:T(8,128)(2,1)}, bf16[8,16,640]{2,1,0:T(8,128)(2,1)S(1)}, u32[]{:S(2)}) copy-start(bf16[8,16,640]{2,1,0:T(8,128)(2,1)S(1)} %select_select_fusion.2) | copy-start | bytes 491524 | tf_op jit(solution)/shard_map/while
  284.2 18.0 %copy-start.5 = (bf16[8,16,640]{2,1,0:T(8,128)(2,1)S(1)}, bf16[8,16,640]{2,1,0:T(8,128)(2,1)}, u32[]{:S(2)}) copy-start(bf16[8,16,640]{2,1,0:T(8,128)(2,1)} %get-tuple-element.697) | copy-start | bytes 491524 | tf_op jit(solution)/shard_map/while
  299.7 14.9 %collective-permute-start = (bf16[16,5120]{1,0:T(8,128)(2,1)S(1)}, bf16[16,5120]{1,0:T(8,128)(2,1)S(1)}, u32[]{:S(2)}, u32[]{:S(2)}) collective-permute-start(bf16[16,5120]{1,0:T(8,128)(2,1)S(1)} %fusion.47), channel_id=1, source_target_pairs={{32,0},{64,32},{96,64},{128,96},{160,128},{192,160},{224,192},{256... | collective-permute-start | bytes 491528 | tf_op jit(solution)/shard_map/while/body/eval_jaxpr/ppermute | solution.py:13
  302.4 12.3 %copy-start.6 = (bf16[8,16,640]{2,1,0:T(8,128)(2,1)}, bf16[8,16,640]{2,1,0:T(8,128)(2,1)S(1)}, u32[]{:S(2)}) copy-start(bf16[8,16,640]{2,1,0:T(8,128)(2,1)S(1)} %select_select_fusion.2) | copy-start | bytes 491524 | tf_op jit(solution)/shard_map/while
  316.2 18.5 %copy-start.5 = (bf16[8,16,640]{2,1,0:T(8,128)(2,1)S(1)}, bf16[8,16,640]{2,1,0:T(8,128)(2,1)}, u32[]{:S(2)}) copy-start(bf16[8,16,640]{2,1,0:T(8,128)(2,1)} %get-tuple-element.697) | copy-start | bytes 491524 | tf_op jit(solution)/shard_map/while
  332.1 13.5 %collective-permute-start = (bf16[16,5120]{1,0:T(8,128)(2,1)S(1)}, bf16[16,5120]{1,0:T(8,128)(2,1)S(1)}, u32[]{:S(2)}, u32[]{:S(2)}) collective-permute-start(bf16[16,5120]{1,0:T(8,128)(2,1)S(1)} %fusion.47), channel_id=1, source_target_pairs={{32,0},{64,32},{96,64},{128,96},{160,128},{192,160},{224,192},{256... | collective-permute-start | bytes 491528 | tf_op jit(solution)/shard_map/while/body/eval_jaxpr/ppermute | solution.py:13
  334.8 10.8 %copy-start.6 = (bf16[8,16,640]{2,1,0:T(8,128)(2,1)}, bf16[8,16,640]{2,1,0:T(8,128)(2,1)S(1)}, u32[]{:S(2)}) copy-start(bf16[8,16,640]{2,1,0:T(8,128)(2,1)S(1)} %select_select_fusion.2) | copy-start | bytes 491524 | tf_op jit(solution)/shard_map/while
  347.2 18.0 %copy-start.5 = (bf16[8,16,640]{2,1,0:T(8,128)(2,1)S(1)}, bf16[8,16,640]{2,1,0:T(8,128)(2,1)}, u32[]{:S(2)}) copy-start(bf16[8,16,640]{2,1,0:T(8,128)(2,1)} %get-tuple-element.697) | copy-start | bytes 491524 | tf_op jit(solution)/shard_map/while
  362.7 11.6 %collective-permute-start = (bf16[16,5120]{1,0:T(8,128)(2,1)S(1)}, bf16[16,5120]{1,0:T(8,128)(2,1)S(1)}, u32[]{:S(2)}, u32[]{:S(2)}) collective-permute-start(bf16[16,5120]{1,0:T(8,128)(2,1)S(1)} %fusion.47), channel_id=1, source_target_pairs={{32,0},{64,32},{96,64},{128,96},{160,128},{192,160},{224,192},{256... | collective-permute-start | bytes 491528 | tf_op jit(solution)/shard_map/while/body/eval_jaxpr/ppermute | solution.py:13
  375.9 18.4 %copy-start.5 = (bf16[8,16,640]{2,1,0:T(8,128)(2,1)S(1)}, bf16[8,16,640]{2,1,0:T(8,128)(2,1)}, u32[]{:S(2)}) copy-start(bf16[8,16,640]{2,1,0:T(8,128)(2,1)} %get-tuple-element.697) | copy-start | bytes 491524 | tf_op jit(solution)/shard_map/while
  391.8 11.5 %collective-permute-start = (bf16[16,5120]{1,0:T(8,128)(2,1)S(1)}, bf16[16,5120]{1,0:T(8,128)(2,1)S(1)}, u32[]{:S(2)}, u32[]{:S(2)}) collective-permute-start(bf16[16,5120]{1,0:T(8,128)(2,1)S(1)} %fusion.47), channel_id=1, source_target_pairs={{32,0},{64,32},{96,64},{128,96},{160,128},{192,160},{224,192},{256... | collective-permute-start | bytes 491528 | tf_op jit(solution)/shard_map/while/body/eval_jaxpr/ppermute | solution.py:13
  404.8 18.5 %copy-start.5 = (bf16[8,16,640]{2,1,0:T(8,128)(2,1)S(1)}, bf16[8,16,640]{2,1,0:T(8,128)(2,1)}, u32[]{:S(2)}) copy-start(bf16[8,16,640]{2,1,0:T(8,128)(2,1)} %get-tuple-element.697) | copy-start | bytes 491524 | tf_op jit(solution)/shard_map/while
  420.8 11.4 %collective-permute-start = (bf16[16,5120]{1,0:T(8,128)(2,1)S(1)}, bf16[16,5120]{1,0:T(8,128)(2,1)S(1)}, u32[]{:S(2)}, u32[]{:S(2)}) collective-permute-start(bf16[16,5120]{1,0:T(8,128)(2,1)S(1)} %fusion.47), channel_id=1, source_target_pairs={{32,0},{64,32},{96,64},{128,96},{160,128},{192,160},{224,192},{256... | collective-permute-start | bytes 491528 | tf_op jit(solution)/shard_map/while/body/eval_jaxpr/ppermute | solution.py:13
  433.8 18.5 %copy-start.5 = (bf16[8,16,640]{2,1,0:T(8,128)(2,1)S(1)}, bf16[8,16,640]{2,1,0:T(8,128)(2,1)}, u32[]{:S(2)}) copy-start(bf16[8,16,640]{2,1,0:T(8,128)(2,1)} %get-tuple-element.697) | copy-start | bytes 491524 | tf_op jit(solution)/shard_map/while
  449.8 11.4 %collective-permute-start = (bf16[16,5120]{1,0:T(8,128)(2,1)S(1)}, bf16[16,5120]{1,0:T(8,128)(2,1)S(1)}, u32[]{:S(2)}, u32[]{:S(2)}) collective-permute-start(bf16[16,5120]{1,0:T(8,128)(2,1)S(1)} %fusion.47), channel_id=1, source_target_pairs={{32,0},{64,32},{96,64},{128,96},{160,128},{192,160},{224,192},{256... | collective-permute-start | bytes 491528 | tf_op jit(solution)/shard_map/while/body/eval_jaxpr/ppermute | solution.py:13
  462.8 18.5 %copy-start.5 = (bf16[8,16,640]{2,1,0:T(8,128)(2,1)S(1)}, bf16[8,16,640]{2,1,0:T(8,128)(2,1)}, u32[]{:S(2)}) copy-start(bf16[8,16,640]{2,1,0:T(8,128)(2,1)} %get-tuple-element.697) | copy-start | bytes 491524 | tf_op jit(solution)/shard_map/while
  478.8 11.6 %collective-permute-start = (bf16[16,5120]{1,0:T(8,128)(2,1)S(1)}, bf16[16,5120]{1,0:T(8,128)(2,1)S(1)}, u32[]{:S(2)}, u32[]{:S(2)}) collective-permute-start(bf16[16,5120]{1,0:T(8,128)(2,1)S(1)} %fusion.47), channel_id=1, source_target_pairs={{32,0},{64,32},{96,64},{128,96},{160,128},{192,160},{224,192},{256... | collective-permute-start | bytes 491528 | tf_op jit(solution)/shard_map/while/body/eval_jaxpr/ppermute | solution.py:13
  491.9 18.5 %copy-start.5 = (bf16[8,16,640]{2,1,0:T(8,128)(2,1)S(1)}, bf16[8,16,640]{2,1,0:T(8,128)(2,1)}, u32[]{:S(2)}) copy-start(bf16[8,16,640]{2,1,0:T(8,128)(2,1)} %get-tuple-element.697) | copy-start | bytes 491524 | tf_op jit(solution)/shard_map/while
  507.8 12.7 %collective-permute-start = (bf16[16,5120]{1,0:T(8,128)(2,1)S(1)}, bf16[16,5120]{1,0:T(8,128)(2,1)S(1)}, u32[]{:S(2)}, u32[]{:S(2)}) collective-permute-start(bf16[16,5120]{1,0:T(8,128)(2,1)S(1)} %fusion.47), channel_id=1, source_target_pairs={{32,0},{64,32},{96,64},{128,96},{160,128},{192,160},{224,192},{256... | collective-permute-start | bytes 491528 | tf_op jit(solution)/shard_map/while/body/eval_jaxpr/ppermute | solution.py:13
  522.1 18.3 %copy-start.5 = (bf16[8,16,640]{2,1,0:T(8,128)(2,1)S(1)}, bf16[8,16,640]{2,1,0:T(8,128)(2,1)}, u32[]{:S(2)}) copy-start(bf16[8,16,640]{2,1,0:T(8,128)(2,1)} %get-tuple-element.697) | copy-start | bytes 491524 | tf_op jit(solution)/shard_map/while
  537.8 12.7 %collective-permute-start = (bf16[16,5120]{1,0:T(8,128)(2,1)S(1)}, bf16[16,5120]{1,0:T(8,128)(2,1)S(1)}, u32[]{:S(2)}, u32[]{:S(2)}) collective-permute-start(bf16[16,5120]{1,0:T(8,128)(2,1)S(1)} %fusion.47), channel_id=1, source_target_pairs={{32,0},{64,32},{96,64},{128,96},{160,128},{192,160},{224,192},{256... | collective-permute-start | bytes 491528 | tf_op jit(solution)/shard_map/while/body/eval_jaxpr/ppermute | solution.py:13
  540.5 10.0 copy-start.6
  552.1 18.3 %copy-start.5 = (bf16[8,16,640]{2,1,0:T(8,128)(2,1)S(1)}, bf16[8,16,640]{2,1,0:T(8,128)(2,1)}, u32[]{:S(2)}) copy-start(bf16[8,16,640]{2,1,0:T(8,128)(2,1)} %get-tuple-element.697) | copy-start | bytes 491524 | tf_op jit(solution)/shard_map/while
  567.8 12.6 %collective-permute-start = (bf16[16,5120]{1,0:T(8,128)(2,1)S(1)}, bf16[16,5120]{1,0:T(8,128)(2,1)S(1)}, u32[]{:S(2)}, u32[]{:S(2)}) collective-permute-start(bf16[16,5120]{1,0:T(8,128)(2,1)S(1)} %fusion.47), channel_id=1, source_target_pairs={{32,0},{64,32},{96,64},{128,96},{160,128},{192,160},{224,192},{256... | collective-permute-start | bytes 491528 | tf_op jit(solution)/shard_map/while/body/eval_jaxpr/ppermute | solution.py:13
  582.0 18.3 %copy-start.5 = (bf16[8,16,640]{2,1,0:T(8,128)(2,1)S(1)}, bf16[8,16,640]{2,1,0:T(8,128)(2,1)}, u32[]{:S(2)}) copy-start(bf16[8,16,640]{2,1,0:T(8,128)(2,1)} %get-tuple-element.697) | copy-start | bytes 491524 | tf_op jit(solution)/shard_map/while
  597.7 66.5 %collective-permute-start = (bf16[16,5120]{1,0:T(8,128)(2,1)S(1)}, bf16[16,5120]{1,0:T(8,128)(2,1)S(1)}, u32[]{:S(2)}, u32[]{:S(2)}) collective-permute-start(bf16[16,5120]{1,0:T(8,128)(2,1)S(1)} %fusion.47), channel_id=1, source_target_pairs={{32,0},{64,32},{96,64},{128,96},{160,128},{192,160},{224,192},{256... | collective-permute-start | bytes 491528 | tf_op jit(solution)/shard_map/while/body/eval_jaxpr/ppermute | solution.py:13
  600.4 63.9 %copy-start.6 = (bf16[8,16,640]{2,1,0:T(8,128)(2,1)}, bf16[8,16,640]{2,1,0:T(8,128)(2,1)S(1)}, u32[]{:S(2)}) copy-start(bf16[8,16,640]{2,1,0:T(8,128)(2,1)S(1)} %select_select_fusion.2) | copy-start | bytes 491524 | tf_op jit(solution)/shard_map/while
  672.5 18.2 %copy-start.5 = (bf16[8,16,640]{2,1,0:T(8,128)(2,1)S(1)}, bf16[8,16,640]{2,1,0:T(8,128)(2,1)}, u32[]{:S(2)}) copy-start(bf16[8,16,640]{2,1,0:T(8,128)(2,1)} %get-tuple-element.697) | copy-start | bytes 491524 | tf_op jit(solution)/shard_map/while
  688.2 26.6 %collective-permute-start = (bf16[16,5120]{1,0:T(8,128)(2,1)S(1)}, bf16[16,5120]{1,0:T(8,128)(2,1)S(1)}, u32[]{:S(2)}, u32[]{:S(2)}) collective-permute-start(bf16[16,5120]{1,0:T(8,128)(2,1)S(1)} %fusion.47), channel_id=1, source_target_pairs={{32,0},{64,32},{96,64},{128,96},{160,128},{192,160},{224,192},{256... | collective-permute-start | bytes 491528 | tf_op jit(solution)/shard_map/while/body/eval_jaxpr/ppermute | solution.py:13
  690.8 24.0 %copy-start.6 = (bf16[8,16,640]{2,1,0:T(8,128)(2,1)}, bf16[8,16,640]{2,1,0:T(8,128)(2,1)S(1)}, u32[]{:S(2)}) copy-start(bf16[8,16,640]{2,1,0:T(8,128)(2,1)S(1)} %select_select_fusion.2) | copy-start | bytes 491524 | tf_op jit(solution)/shard_map/while
  723.0 18.2 %copy-start.5 = (bf16[8,16,640]{2,1,0:T(8,128)(2,1)S(1)}, bf16[8,16,640]{2,1,0:T(8,128)(2,1)}, u32[]{:S(2)}) copy-start(bf16[8,16,640]{2,1,0:T(8,128)(2,1)} %get-tuple-element.697) | copy-start | bytes 491524 | tf_op jit(solution)/shard_map/while
  738.7 12.8 %collective-permute-start = (bf16[16,5120]{1,0:T(8,128)(2,1)S(1)}, bf16[16,5120]{1,0:T(8,128)(2,1)S(1)}, u32[]{:S(2)}, u32[]{:S(2)}) collective-permute-start(bf16[16,5120]{1,0:T(8,128)(2,1)S(1)} %fusion.47), channel_id=1, source_target_pairs={{32,0},{64,32},{96,64},{128,96},{160,128},{192,160},{224,192},{256... | collective-permute-start | bytes 491528 | tf_op jit(solution)/shard_map/while/body/eval_jaxpr/ppermute | solution.py:13
  741.4 10.1 copy-start.6
  759.7 18.2 %copy-start.5 = (bf16[8,16,640]{2,1,0:T(8,128)(2,1)S(1)}, bf16[8,16,640]{2,1,0:T(8,128)(2,1)}, u32[]{:S(2)}) copy-start(bf16[8,16,640]{2,1,0:T(8,128)(2,1)} %get-tuple-element.697) | copy-start | bytes 491524 | tf_op jit(solution)/shard_map/while
  775.4 12.8 %collective-permute-start = (bf16[16,5120]{1,0:T(8,128)(2,1)S(1)}, bf16[16,5120]{1,0:T(8,128)(2,1)S(1)}, u32[]{:S(2)}, u32[]{:S(2)}) collective-permute-start(bf16[16,5120]{1,0:T(8,128)(2,1)S(1)} %fusion.47), channel_id=1, source_target_pairs={{32,0},{64,32},{96,64},{128,96},{160,128},{192,160},{224,192},{256... | collective-permute-start | bytes 491528 | tf_op jit(solution)/shard_map/while/body/eval_jaxpr/ppermute | solution.py:13
  778.0 10.1 copy-start.6
  796.4 18.2 %copy-start.5 = (bf16[8,16,640]{2,1,0:T(8,128)(2,1)S(1)}, bf16[8,16,640]{2,1,0:T(8,128)(2,1)}, u32[]{:S(2)}) copy-start(bf16[8,16,640]{2,1,0:T(8,128)(2,1)} %get-tuple-element.697) | copy-start | bytes 491524 | tf_op jit(solution)/shard_map/while
  812.1 18.4 %collective-permute-start = (bf16[16,5120]{1,0:T(8,128)(2,1)S(1)}, bf16[16,5120]{1,0:T(8,128)(2,1)S(1)}, u32[]{:S(2)}, u32[]{:S(2)}) collective-permute-start(bf16[16,5120]{1,0:T(8,128)(2,1)S(1)} %fusion.47), channel_id=1, source_target_pairs={{32,0},{64,32},{96,64},{128,96},{160,128},{192,160},{224,192},{256... | collective-permute-start | bytes 491528 | tf_op jit(solution)/shard_map/while/body/eval_jaxpr/ppermute | solution.py:13
  814.7 15.8 %copy-start.6 = (bf16[8,16,640]{2,1,0:T(8,128)(2,1)}, bf16[8,16,640]{2,1,0:T(8,128)(2,1)S(1)}, u32[]{:S(2)}) copy-start(bf16[8,16,640]{2,1,0:T(8,128)(2,1)S(1)} %select_select_fusion.2) | copy-start | bytes 491524 | tf_op jit(solution)/shard_map/while
  838.7 18.2 %copy-start.5 = (bf16[8,16,640]{2,1,0:T(8,128)(2,1)S(1)}, bf16[8,16,640]{2,1,0:T(8,128)(2,1)}, u32[]{:S(2)}) copy-start(bf16[8,16,640]{2,1,0:T(8,128)(2,1)} %get-tuple-element.697) | copy-start | bytes 491524 | tf_op jit(solution)/shard_map/while
  854.4 12.8 %collective-permute-start = (bf16[16,5120]{1,0:T(8,128)(2,1)S(1)}, bf16[16,5120]{1,0:T(8,128)(2,1)S(1)}, u32[]{:S(2)}, u32[]{:S(2)}) collective-permute-start(bf16[16,5120]{1,0:T(8,128)(2,1)S(1)} %fusion.47), channel_id=1, source_target_pairs={{32,0},{64,32},{96,64},{128,96},{160,128},{192,160},{224,192},{256... | collective-permute-start | bytes 491528 | tf_op jit(solution)/shard_map/while/body/eval_jaxpr/ppermute | solution.py:13
  857.1 10.1 copy-start.6
  875.4 18.2 %copy-start.5 = (bf16[8,16,640]{2,1,0:T(8,128)(2,1)S(1)}, bf16[8,16,640]{2,1,0:T(8,128)(2,1)}, u32[]{:S(2)}) copy-start(bf16[8,16,640]{2,1,0:T(8,128)(2,1)} %get-tuple-element.697) | copy-start | bytes 491524 | tf_op jit(solution)/shard_map/while
  891.1 12.9 %collective-permute-start = (bf16[16,5120]{1,0:T(8,128)(2,1)S(1)}, bf16[16,5120]{1,0:T(8,128)(2,1)S(1)}, u32[]{:S(2)}, u32[]{:S(2)}) collective-permute-start(bf16[16,5120]{1,0:T(8,128)(2,1)S(1)} %fusion.47), channel_id=1, source_target_pairs={{32,0},{64,32},{96,64},{128,96},{160,128},{192,160},{224,192},{256... | collective-permute-start | bytes 491528 | tf_op jit(solution)/shard_map/while/body/eval_jaxpr/ppermute | solution.py:13
  893.8 10.3 copy-start.6
  912.3 18.2 %copy-start.5 = (bf16[8,16,640]{2,1,0:T(8,128)(2,1)S(1)}, bf16[8,16,640]{2,1,0:T(8,128)(2,1)}, u32[]{:S(2)}) copy-start(bf16[8,16,640]{2,1,0:T(8,128)(2,1)} %get-tuple-element.697) | copy-start | bytes 491524 | tf_op jit(solution)/shard_map/while
  928.0 18.3 %collective-permute-start = (bf16[16,5120]{1,0:T(8,128)(2,1)S(1)}, bf16[16,5120]{1,0:T(8,128)(2,1)S(1)}, u32[]{:S(2)}, u32[]{:S(2)}) collective-permute-start(bf16[16,5120]{1,0:T(8,128)(2,1)S(1)} %fusion.47), channel_id=1, source_target_pairs={{32,0},{64,32},{96,64},{128,96},{160,128},{192,160},{224,192},{256... | collective-permute-start | bytes 491528 | tf_op jit(solution)/shard_map/while/body/eval_jaxpr/ppermute | solution.py:13
  930.6 15.7 %copy-start.6 = (bf16[8,16,640]{2,1,0:T(8,128)(2,1)}, bf16[8,16,640]{2,1,0:T(8,128)(2,1)S(1)}, u32[]{:S(2)}) copy-start(bf16[8,16,640]{2,1,0:T(8,128)(2,1)S(1)} %select_select_fusion.2) | copy-start | bytes 491524 | tf_op jit(solution)/shard_map/while
  954.5 18.2 %copy-start.5 = (bf16[8,16,640]{2,1,0:T(8,128)(2,1)S(1)}, bf16[8,16,640]{2,1,0:T(8,128)(2,1)}, u32[]{:S(2)}) copy-start(bf16[8,16,640]{2,1,0:T(8,128)(2,1)} %get-tuple-element.697) | copy-start | bytes 491524 | tf_op jit(solution)/shard_map/while
  970.2 15.9 %collective-permute-start = (bf16[16,5120]{1,0:T(8,128)(2,1)S(1)}, bf16[16,5120]{1,0:T(8,128)(2,1)S(1)}, u32[]{:S(2)}, u32[]{:S(2)}) collective-permute-start(bf16[16,5120]{1,0:T(8,128)(2,1)S(1)} %fusion.47), channel_id=1, source_target_pairs={{32,0},{64,32},{96,64},{128,96},{160,128},{192,160},{224,192},{256... | collective-permute-start | bytes 491528 | tf_op jit(solution)/shard_map/while/body/eval_jaxpr/ppermute | solution.py:13
  972.9 13.2 %copy-start.6 = (bf16[8,16,640]{2,1,0:T(8,128)(2,1)}, bf16[8,16,640]{2,1,0:T(8,128)(2,1)S(1)}, u32[]{:S(2)}) copy-start(bf16[8,16,640]{2,1,0:T(8,128)(2,1)S(1)} %select_select_fusion.2) | copy-start | bytes 491524 | tf_op jit(solution)/shard_map/while
  (13 other events, 77.3 us)
Sparse Core Ops, SparseCore 0:
  10.1 133.2 all-gather.2
  987.0 73.9 all-reduce.2
where the time goes:
time: 1080 us; the launch traced here: 1070 us
  waiting for transfers between devices  505 us (47%)
  blocking collectives  338 us (31%)
  other arithmetic  86.5 us (8%)
  matrix products  80.7 us (7%)
  starting transfers between devices  29.8 us (3%)
  local copies, waits for them, and re-layouts  15.4 us (1%)
  between operations  14.2 us (1%)
    ppermute x23, waiting for transfers between devices, shifted(): lax.ppermute(value, axis, [(source, source + steps) for source in range(i...  329 us
    all_gather x23, blocking collectives, one_tick(): full_grad = lax.all_gather(normalized_gradient, 'mp', axis=1, tiled=True)  310 us
    all_gather x1, waiting for transfers between devices, local(): weight_full = lax.all_gather(proj_weight[0], 'dp', axis=1, tiled=True)  101 us
    psum x1, waiting for transfers between devices, local(): down_acc, up_acc = lax.psum((down_acc, up_acc), 'dp')  74.1 us
    dot_general x8, matrix products, project_grads(): lax.dot_general(grad_rows, weight_full, contract_last, preferred_element_...  37.1 us
    ppermute x23, starting transfers between devices, shifted(): lax.ppermute(value, axis, [(source, source + steps) for source in range(i...  29.7 us
    psum x1, blocking collectives, local(): low_in = lax.psum(partial_in, 'mp').astype(jnp.bfloat16)  28.1 us
    reduce_sum x23, other arithmetic, one_tick(): row_stat = jnp.mean(norm_rows * normed_one, axis=-1, keepdims=True)  25.9 us
  transfers between devices with their start and end apart: 25, of which 25 were waited for; matrix products, arithmetic and copies ran while one was open for 3% of the time, Pallas kernels for 0%

commit v1 on v0

v1 whole, which is shorter than its diff:
```python
import jax
import jax.numpy as jnp
from jax import lax
from jax.sharding import Mesh, PartitionSpec as P

norm_eps = 1e-05
low_rank_scale = 2.0
CHUNKS = 2
TAIL = 128
SWAP = [(0, 1), (1, 0)]
ODD = [(s, s - 1) for s in range(15, 0, -2)]
EVEN = [(s, s - 1) for s in range(14, 0, -2)]
EVERY = [(s, s - 1) for s in range(15, 0, -1)]
f32 = jnp.float32
bf16 = jnp.bfloat16
contract_last = (((1,), (1,)), ((), ()))


def both_cores(value, axis):
    core = lax.axis_index("c")
    other = lax.ppermute(value, "c", SWAP)
    low = jnp.where(core == 0, value, other)
    high = jnp.where(core == 0, other, value)
    return jnp.concatenate([low, high], axis)


def half_sum(value, axis):
    core = lax.axis_index("c")
    width = value.shape[axis] // 2
    low = lax.slice_in_dim(value, 0, width, axis=axis)
    high = lax.slice_in_dim(value, width, 2 * width, axis=axis)
    mine = jnp.where(core == 0, low, high)
    theirs = jnp.where(core == 0, high, low)
    return mine + lax.ppermute(theirs, "c", SWAP)


def spread(value):
    sent = jnp.broadcast_to(value[None], (4,) + value.shape)
    return lax.all_to_all(sent, "y", 0, 0)


def local(
    section_inputs,
    out_grads,
    proj_weight,
    norm_gain,
    adapter_down,
    adapter_up,
    tenant_ids,
    slot_table,
):
    sec = lax.axis_index("s")
    ypos = lax.axis_index("y")
    core = lax.axis_index("c")
    micro = section_inputs.shape[1]
    width_all = section_inputs.shape[3]
    half = proj_weight.shape[1]
    width = 2 * half
    toks = section_inputs.shape[2] // 2
    rank = adapter_down.shape[3]
    rows_all = micro * toks
    group = micro // CHUNKS
    rows = group * toks
    multiplier = low_rank_scale / (toks * 2 * lax.axis_size("z"))

    w_own = lax.all_gather(proj_weight[0], "z", axis=1, tiled=True)
    w_other = lax.ppermute(w_own, "c", SWAP)

    x_full = section_inputs[0]
    x_mine = lax.dynamic_slice_in_dim(x_full, core * toks, toks, 1).reshape(rows_all, width_all)
    x_f = x_mine.astype(f32)
    inv_rms = lax.rsqrt(jnp.mean(x_f * x_f, axis=-1, keepdims=True) + norm_eps)
    x_y = lax.dynamic_slice_in_dim(x_mine, ypos * width, width, 1)
    normed_y = x_y.astype(f32) * inv_rms
    x_before = spread(lax.ppermute(x_y, "s", EVERY))
    gain_y = both_cores(norm_gain, 1)
    down_y = both_cores(adapter_down[0], 1)
    h_y = (normed_y * gain_y).astype(bf16)

    iota = jnp.arange(micro, dtype=jnp.int32)
    tenant_hot = tenant_ids[:, None] == iota[None, :]
    slot_ids = jnp.sum(jnp.where(tenant_hot, slot_table[0][None, :], 0), axis=1)
    down_sel = down_y[slot_ids]
    up_sel = adapter_up[0][slot_ids]
    low_in = jnp.einsum(
        "mtd,mdr->mtr", h_y.reshape(micro, toks, width), down_sel, preferred_element_type=f32
    )
    low_in = lax.psum(low_in, "y").astype(bf16)
    low_in_all = lax.all_gather(low_in, "z")
    h_all = lax.all_gather(h_y, "z")

    grads_top = lax.dynamic_slice_in_dim(out_grads, core * toks, toks, 1)
    grads_top = grads_top.reshape(CHUNKS, rows, width_all)
    x_before = x_before.reshape(4, CHUNKS, rows, width).transpose(1, 0, 2, 3)
    x_chunk = x_y.reshape(CHUNKS, rows, width)
    inv_chunk = inv_rms.reshape(CHUNKS, rows, 1)
    down_chunk = down_sel.reshape(CHUNKS, group, width, rank)
    up_chunk = up_sel.reshape(CHUNKS, group, rank, width_all)

    def pick(array, m):
        return lax.dynamic_index_in_dim(array, m, 0, keepdims=False)

    def gathered(box, m):
        parts = spread(box)
        tail = parts[:, :, width:].astype(f32)
        coef = jnp.sum(tail[:, :, 0:1] + tail[:, :, 1:2], axis=0)
        rows_u = parts[:, :, :width].astype(f32) - coef[None] * pick(x_before, m).astype(f32)
        return rows_u.astype(bf16).transpose(1, 0, 2).reshape(rows, width_all)

    def stage(m, box):
        grad = lax.cond(
            sec == 15, lambda box: pick(grads_top, m), lambda box: gathered(box, m), box
        )
        low = jnp.einsum(
            "mtd,mrd->mtr",
            grad.reshape(group, toks, width_all),
            pick(up_chunk, m),
            preferred_element_type=f32,
        ).astype(bf16)
        part_own = lax.dot_general(grad, w_own, contract_last, preferred_element_type=f32)
        part_other = lax.dot_general(grad, w_other, contract_last, preferred_element_type=f32)
        frozen = jnp.concatenate(
            [
                jnp.where(core == 0, part_own, part_other),
                jnp.where(core == 0, part_other, part_own),
            ],
            1,
        )
        adapt = jnp.einsum(
            "mtr,mdr->mtd", low, pick(down_chunk, m), preferred_element_type=f32
        ).reshape(rows, width)
        normed_grad = ((frozen + low_rank_scale * adapt) * gain_y).astype(bf16).astype(f32)
        inv = pick(inv_chunk, m)
        x_m = pick(x_chunk, m).astype(f32)
        grad_y = lax.dynamic_slice_in_dim(grad, ypos * width, width, 1)
        sent = (grad_y.astype(f32) + inv * normed_grad).astype(bf16)
        coef = jnp.sum(normed_grad * x_m, axis=1, keepdims=True) * (inv * inv * inv / width_all)
        high = lax.reduce_precision(coef, 8, 7)
        rest = coef - high
        lane = lax.broadcasted_iota(jnp.int32, (rows, TAIL), 1)
        tail = jnp.where(lane == 0, high, jnp.where(lane == 1, rest, 0.0)).astype(bf16)
        return jnp.concatenate([sent, tail], 1), low.reshape(rows, rank), grad_y, coef

    def put(array, value, m):
        return lax.dynamic_update_index_in_dim(array, value, m, 0)

    def step(u, state):
        box, sent_all, low_all, grad_all, coef_all = state
        t, m = u // CHUNKS, u % CHUNKS
        turn = 15 - t + m

        def work(args):
            sent_all, low_all, grad_all, coef_all = args
            sent, low, grad_y, coef = stage(m, box)
            return (
                put(sent_all, sent, m),
                put(low_all, low, m),
                put(grad_all, grad_y, m),
                put(coef_all, coef, m),
            )

        sent_all, low_all, grad_all, coef_all = lax.cond(
            sec == turn, work, lambda args: args, (sent_all, low_all, grad_all, coef_all)
        )
        part = ((sec == turn) | (sec == turn - 1)) & (turn >= 1) & (turn <= 15)
        kind = jnp.where(part, jnp.where(turn % 2 == 1, 1, 2), 0)
        outgoing = pick(sent_all, m)
        box = lax.switch(
            kind,
            [
                lambda box, out: box,
                lambda box, out: lax.ppermute(out, "s", ODD),
                lambda box, out: lax.ppermute(out, "s", EVEN),
            ],
            box,
            outgoing,
        )
        return box, sent_all, low_all, grad_all, coef_all

    start = (
        jnp.zeros((rows, width + TAIL), bf16),
        jnp.zeros((CHUNKS, rows, width + TAIL), bf16),
        jnp.zeros((CHUNKS, rows, rank), bf16),
        jnp.zeros((CHUNKS, rows, width), bf16),
        jnp.zeros((CHUNKS, rows, 1), f32),
    )
    _, sent_all, low_all, grad_all, coef_all = lax.fori_loop(0, 15 * CHUNKS + 2 * CHUNKS, step, start)

    coef_sum = lax.psum(coef_all, "y")
    new_grads = sent_all[:, :, :width].astype(f32) - coef_sum * x_chunk.astype(f32)
    new_grads = new_grads.astype(bf16).reshape(micro, toks, width)
    keep = jnp.where(core == 0, new_grads[:, :, :half], new_grads[:, :, half:])
    give = jnp.where(core == 0, new_grads[:, :, half:], new_grads[:, :, :half])
    got = lax.ppermute(give, "c", SWAP)
    kept = jnp.concatenate(
        [jnp.where(core == 0, keep, got), jnp.where(core == 0, got, keep)], 1
    )

    both = jnp.concatenate(
        [
            grad_all.reshape(rows_all, width),
            jnp.pad(low_all.reshape(rows_all, rank), ((0, 0), (0, TAIL - rank))),
        ],
        1,
    )
    both = lax.all_gather(both, "z").reshape(4, micro, toks, width + TAIL)
    grads_z = both[..., :width]
    low_z = both[..., width : width + rank]
    hidden_z = h_all.reshape(4, micro, toks, width)
    down_part = multiplier * jnp.einsum(
        "zmtd,zmtr->mdr", hidden_z, low_z, preferred_element_type=f32
    )
    up_part = multiplier * jnp.einsum(
        "zmtr,zmtd->mrd", low_in_all, grads_z, preferred_element_type=f32
    )
    down_acc = half_sum(down_part, 1)
    up_acc = half_sum(up_part, 2)
    slot_hot = slot_ids[None, :] == iota[:, None]
    down_out = jnp.sum(jnp.where(slot_hot[:, :, None, None], down_acc[None], 0.0), axis=1)
    up_out = jnp.sum(jnp.where(slot_hot[:, :, None, None], up_acc[None], 0.0), axis=1)
    return (kept[None], down_out[None], up_out[None])


def solution(mesh):
    fine = Mesh(mesh.devices.reshape(16, 4, 2, 4), ("s", "y", "c", "z"))
    mp = ("y", "c")
    placed = (
        P("s", None, "z", None),
        P(None, "z", None),
        P("s", mp, "z"),
        P("s", mp),
        P("s", None, mp, None),
        P("s", None, None, None),
        P(),
        P("s", None),
    )
    return jax.shard_map(
        local,
        mesh=fine,
        in_specs=placed,
        out_specs=(
            P("s", None, "z", mp),
            P("s", None, mp, None),
            P("s", None, None, mp),
        ),
        check_vma=False,
    )
```

time: 1080 us -> 809 us (0.75)
  blocking collectives: 338 us -> 62.1 us
  waiting for transfers between devices: 505 us -> 612 us
  other arithmetic: 86.5 us -> 7.67 us
  matrix products: 80.7 us -> 23.7 us
  starting transfers between devices: 29.8 us -> 74.3 us
    all_gather x23 -> x3, blocking collectives: 310 us -> 50.2 us  [the longest x1 24.9 us: local(): h_all = lax.all_gather(h_y, 'z')]
    ppermute x23 -> x9, waiting for transfers between devices: 329 us -> 457 us  [the longest x2 457 us: step(): lax.ppermute(out, 's', ODD)]
    psum x1 -> x0, waiting for transfers between devices: 74.1 us -> none  [local(): down_acc, up_acc = lax.psum((down_acc, up_acc), 'dp')]
    dot_general x71 -> x11, matrix products: 80.7 us -> 23.7 us  [the longest x2 9.79 us: stage(): lax.dot_general(grad, w_own, contract_last, preferred_element_type=f32)]
    all_gather x1, waiting for transfers between devices: 101 us -> 136 us  [local(): w_own = lax.all_gather(proj_weight[0], 'z', axis=1, tiled=True)]
    ppermute x23 -> x9, starting transfers between devices: 29.7 us -> 63.4 us  [the longest x2 50.7 us: half_sum(): return mine + lax.ppermute(theirs, 'c', SWAP)]
    convert_element_type x24 -> x8, other arithmetic: 25.8 us -> 0.58 us  [the longest x2 0.18 us: stage(): sent = (grad_y.astype(f32) + inv * normed_grad).astype(bf16)]
    reduce_sum x24 -> x3, other arithmetic: 26.2 us -> 1.69 us  [the longest x1 1.31 us: local(): inv_rms = lax.rsqrt(jnp.mean(x_f * x_f, axis=-1, keepdims=True) + norm_eps)]
  transfers between devices with their start and end apart: 25 -> 13, of which waited for: 25 -> 6; matrix products, arithmetic and copies ran while one was open for 3% -> 1% of each run, Pallas kernels for 0% -> 0%
where the time goes in v1:
time: 809 us; the launch traced here: 808 us
  waiting for transfers between devices  612 us (76%)
  starting transfers between devices  74.3 us (9%)
  blocking collectives  62.1 us (8%)
  matrix products  23.7 us (3%)
  between operations  14.3 us (2%)
  local copies, waits for them, and re-layouts  9.84 us (1%)
    ppermute x2, waiting for transfers between devices, step(): lax.ppermute(out, 's', ODD)  457 us
    all_gather x1, waiting for transfers between devices, local(): w_own = lax.all_gather(proj_weight[0], 'z', axis=1, tiled=True)  136 us
    ppermute x2, starting transfers between devices, half_sum(): return mine + lax.ppermute(theirs, 'c', SWAP)  50.7 us
    all_gather x1, blocking collectives, local(): h_all = lax.all_gather(h_y, 'z')  24.9 us
    all_to_all x3, waiting for transfers between devices, spread(): return lax.all_to_all(sent, 'y', 0, 0)  19 us
  transfers between devices with their start and end apart: 13, of which 6 were waited for; matrix products, arithmetic and copies ran while one was open for 1% of the time, Pallas kernels for 0%

profile of v1, /device:TPU:1, one launch (start us, length us, event | category | flops | bytes accessed | tf_op | source)
XLA Modules:
  0.0 808.0 jit_solution(3170273248016541835)
XLA Ops:
  7.2 0.7 all-gather.6.cloned.1.call-update
  7.9 135.5 %all-gather.6.cloned.1.call-done = bf16[1,640,5120]{2,1,0:T(8,128)(2,1)} async-done(((bf16[1,640,1280]{2,1,0:T(8,128)(2,1)}), bf16[1,640,5120]{2,1,0:T(8,128)(2,1)}) %all-gather.6.cloned.1.call-update) | async-done | bytes 6553616 | tf_op jit(solution)/shard_map/all_gather | solution.py:66
  143.4 2.6 collective-permute-start.3
  146.0 1.9 collective-permute-start.5
  147.9 2.4 collective-permute-start.4
  150.4 1.3 multiply_reduce_fusion
  151.7 0.9 select_reduce_fusion.2
  152.6 2.0 constant_dynamic-slice_fusion.1
  154.8 1.7 gather_fusion
  156.5 0.1 multiply_convert_fusion
  156.6 1.3 collective-permute-start.2
  157.9 24.9 %all-gather.1 = bf16[256,1280]{1,0:T(8,128)(2,1)} all-gather(bf16[64,1280]{1,0:T(8,128)(2,1)S(1)} %get-tuple-element.745), channel_id=3, replica_groups=mesh['s'=16,'y'=4,'c'=2,'z'=4] {'z'}, dimensions={0}, use_global_device_ids=true | all-gather | bytes 819200 | tf_op jit(solution)/shard_map/all_gather | solution.py:90
  182.9 0.9 broadcast_in_dim.142
  183.8 4.0 all-to-all-start.1
  187.8 1.0 broadcast_select_fusion.3
  188.8 0.6 gather_fusion.1
  189.3 0.2 fusion.27
  189.5 7.0 all-to-all-done.1
  196.6 0.6 broadcast_in_dim.137
  197.3 510.2 %while.27 = (s32[]{:T(128)}, bf16[32,1408]{1,0:T(8,128)(2,1)}, bf16[2,32,1408]{2,1,0:T(8,128)(2,1)S(1)}, bf16[2,32,16]{2,1,0:T(8,128)(2,1)S(1)}, bf16[2,32,1280]...) while((s32[]{:T(128)}, bf16[32,1408]{1,0:T(8,128)(2,1)}, ...), condition=%wide.region_12.13_spmd, body=%wide.region_2.12_spmd.sunk | while | flops 427787616 | bytes 20356076 | solution.py:187
  200.7 446.1 %conditional.6 = (bf16[32,1408]{1,0:T(8,128)(2,1)}) conditional(s32[]{:T(128)} %clamp.15, bf16[32,1408]{1,0:T(8,128)(2,1)} %get-tuple-element.912, (s32[]{:T(128)}, bf16[2,32,1408]{2,1,0:T(8,128)(2,1)S(1)}) %tuple.103, (s32[]{:T(128)}, bf16[2,32,1408]{2,1,0:T(8,128)(2,1)S(1)}) %tuple.103), branch_computations={%region_9.9_spmd, %region_10.10_spmd, %region_11.11_spmd} | conditional | flops 3 | bytes 540758 | solution.py:168
  200.8 1.3 collective-permute-start
  202.1 444.8 %collective-permute-done = bf16[32,1408]{1,0:T(8,128)(2,1)} collective-permute-done((bf16[32,1408]{1,0:T(8,128)(2,1)S(1)}, bf16[32,1408]{1,0:T(8,128)(2,1)}, u32[]{:S(2)}, u32[]{:S(2)}) %collective-permute-start) | collective-permute-done | bytes 90144 | tf_op jit(solution)/shard_map/while/body/eval_jaxpr/cond/branch_1_fun/ppermute | solution.py:172
  646.8 23.5 %conditional.5 = ((bf16[2,32,1408]{2,1,0:T(8,128)(2,1)S(1)}, bf16[2,32,16]{2,1,0:T(8,128)(2,1)S(1)}, bf16[2,32,1280]{2,1,0:T(8,128)(2,1)S(1)}, f32[2,32,1]{1,2,0:T(1,128)S(1)})) conditional(s32[]{:T(128)} %convert_element_type.119, (bf16[2,32,1408]{2,1,0:T(8,128)(2,1)S(1)}, bf16[2,32,16]{2,1,0:T(8,128)(2,1)S(1)}, bf16[2,32,1280]{2,1,0:T(8,128)(2,1)S(1)}, ...), branch_computations={%region_3.3_spmd, %region_4.8_spmd} | conditional | flops 427787584 | bytes 19814560 | solution.py:162
  646.8 11.6 %conditional = (bf16[32,5120]{1,0:T(8,128)(2,1)S(1)}) conditional(s32[]{:T(128)} %convert_element_type.65, (bf16[32,1408]{1,0:T(8,128)(2,1)}, s32[]{:T(128)}, bf16[2,4,32,1280]{3,2,1,0:T(8,128)(2,1)S(1)}) %tuple.62, (s32[]{:T(128)}, bf16[2,32,5120]{2,1,0:T(8,128)(2,1)}) %tuple.63), branch_computations={%region_5.5_spmd, %region_7.6_spmd} | conditional | flops 835811 | bytes 3269966 | solution.py:111
  646.8 1.7 broadcast_in_dim.82
  648.5 3.5 all-to-all-start
  652.0 6.0 all-to-all-done
  658.0 0.2 fusion.3
  658.2 0.2 fusion.2
  658.4 1.4 bitcast_dynamic-update-slice_fusion.1
  659.8 4.9 fusion.35
  664.7 4.9 broadcast_select_fusion.1
  669.7 0.2 fusion.11
  669.9 0.1 reduce_sum.48
  670.0 0.1 add_convert_fusion
  670.5 13.5 %conditional.6 = (bf16[32,1408]{1,0:T(8,128)(2,1)}) conditional(s32[]{:T(128)} %clamp.15, bf16[32,1408]{1,0:T(8,128)(2,1)} %get-tuple-element.912, (s32[]{:T(128)}, bf16[2,32,1408]{2,1,0:T(8,128)(2,1)S(1)}) %tuple.103, (s32[]{:T(128)}, bf16[2,32,1408]{2,1,0:T(8,128)(2,1)S(1)}) %tuple.103), branch_computations={%region_9.9_spmd, %region_10.10_spmd, %region_11.11_spmd} | conditional | flops 3 | bytes 540758 | solution.py:168
  670.5 1.3 collective-permute-start
  671.8 12.1 %collective-permute-done = bf16[32,1408]{1,0:T(8,128)(2,1)} collective-permute-done((bf16[32,1408]{1,0:T(8,128)(2,1)S(1)}, bf16[32,1408]{1,0:T(8,128)(2,1)}, u32[]{:S(2)}, u32[]{:S(2)}) %collective-permute-start) | collective-permute-done | bytes 90144 | tf_op jit(solution)/shard_map/while/body/eval_jaxpr/cond/branch_1_fun/ppermute | solution.py:172
  684.0 23.5 %conditional.5 = ((bf16[2,32,1408]{2,1,0:T(8,128)(2,1)S(1)}, bf16[2,32,16]{2,1,0:T(8,128)(2,1)S(1)}, bf16[2,32,1280]{2,1,0:T(8,128)(2,1)S(1)}, f32[2,32,1]{1,2,0:T(1,128)S(1)})) conditional(s32[]{:T(128)} %convert_element_type.119, (bf16[2,32,1408]{2,1,0:T(8,128)(2,1)S(1)}, bf16[2,32,16]{2,1,0:T(8,128)(2,1)S(1)}, bf16[2,32,1280]{2,1,0:T(8,128)(2,1)S(1)}, ...), branch_computations={%region_3.3_spmd, %region_4.8_spmd} | conditional | flops 427787584 | bytes 19814560 | solution.py:162
  684.0 11.6 %conditional = (bf16[32,5120]{1,0:T(8,128)(2,1)S(1)}) conditional(s32[]{:T(128)} %convert_element_type.65, (bf16[32,1408]{1,0:T(8,128)(2,1)}, s32[]{:T(128)}, bf16[2,4,32,1280]{3,2,1,0:T(8,128)(2,1)S(1)}) %tuple.62, (s32[]{:T(128)}, bf16[2,32,5120]{2,1,0:T(8,128)(2,1)}) %tuple.63), branch_computations={%region_5.5_spmd, %region_7.6_spmd} | conditional | flops 835811 | bytes 3269966 | solution.py:111
  684.0 1.7 broadcast_in_dim.82
  685.6 3.5 all-to-all-start
  689.1 6.0 all-to-all-done
  695.1 0.2 fusion.3
  695.3 0.2 fusion.2
  695.5 1.4 bitcast_dynamic-update-slice_fusion.1
  697.0 4.9 fusion.35
  701.8 4.9 broadcast_select_fusion.1
  706.8 0.2 fusion.11
  707.0 0.1 reduce_sum.48
  707.1 0.1 add_convert_fusion
  707.6 14.9 %all-gather.2 = bf16[256,1408]{1,0:T(8,128)(2,1)S(1)} all-gather(bf16[64,1408]{1,0:T(8,128)(2,1)S(1)} %fusion.26), channel_id=4, replica_groups=mesh['s'=16,'y'=4,'c'=2,'z'=4] {'z'}, dimensions={0}, use_global_device_ids=true | all-gather | bytes 901120 | tf_op jit(solution)/shard_map/all_gather | solution.py:206
  722.4 11.9 %all-reduce.1 = (f32[2,32]{1,0:T(2,128)S(1)}, bf16[8,8,16]{2,1,0:T(8,128)(2,1)S(1)}) all-reduce(f32[2,32]{1,0:T(2,128)S(1)} %bitcast.119, f32[8,8,16]{2,1,0:T(8,128)S(1)} %fusion.27), channel_id=1, replica_groups=mesh['s'=16,'y'=4,'c'=2,'z'=4] {'y'}, use_global_device_ids=true, to_apply=%region_13.14 | all-reduce | flops 1088 | bytes 6656 | tf_op jit(solution)/shard_map/psum | solution.py:189
  734.3 10.4 %all-gather.3 = bf16[32,8,16]{2,1,0:T(8,128)(2,1)S(1)} all-gather(bf16[8,8,16]{2,1,0:T(8,128)(2,1)S(1)} %get-tuple-element.741), channel_id=5, replica_groups=mesh['s'=16,'y'=4,'c'=2,'z'=4] {'z'}, dimensions={0}, use_global_device_ids=true | all-gather | bytes 10240 | tf_op jit(solution)/shard_map/all_gather | solution.py:89
  744.7 0.3 fusion.22
  745.1 48.3 %collective-permute-start.8 = (f32[8,16,640]{2,1,0:T(8,128)S(1)}, f32[8,16,640]{2,1,0:T(8,128)S(1)}, u32[]{:S(2)}, u32[]{:S(2)}) collective-permute-start(f32[8,16,640]{2,1,0:T(8,128)S(1)} %slice_select_fusion), channel_id=1, source_target_pairs={{0,4},{4,0},{1,5},{5,1},{2,6},{6,2},{3,7},{7,3},{8,12},{12,8},{9,1... | collective-permute-start | bytes 983048 | tf_op jit(solution)/shard_map/ppermute | solution.py:34
  793.4 0.3 fusion.23
  793.7 0.1 subtract_convert_fusion
  793.8 1.9 collective-permute-start.6
  795.8 2.4 collective-permute-start.7
  798.2 0.7 maximum_bitcast_fusion.1
  799.0 1.0 select_reduce_fusion
  800.1 1.0 select_reduce_fusion.1
  (128 shorter events, 2.0 us)
Async XLA Ops:
  7.2 147.6 %copy-start = (bf16[1,8,16,5120]{3,2,1,0:T(8,128)(2,1)S(1)}, bf16[1,8,16,5120]{3,2,1,0:T(8,128)(2,1)}, u32[]{:S(2)}) copy-start(bf16[1,8,16,5120]{3,2,1,0:T(8,128)(2,1)} %param.22) | copy-start | bytes 3932164
  7.2 145.4 %copy-start.2 = (bf16[1,8,16,5120]{3,2,1,0:T(8,128)(2,1)S(1)}, bf16[1,8,16,5120]{3,2,1,0:T(8,128)(2,1)}, u32[]{:S(2)}) copy-start(bf16[1,8,16,5120]{3,2,1,0:T(8,128)(2,1)} %param.17) | copy-start | bytes 3932164
  7.2 136.2 %all-gather.6.cloned.1.call-start = ((), (), s32[]{:S(2)}) async-start(), calls=%async_computation.2 | async-start | bytes 8192000 | tf_op jit(solution)/shard_map/all_gather | solution.py:66
  143.4 53.1 %collective-permute-start.3 = (bf16[640,5120]{1,0:T(8,128)(2,1)}, bf16[640,5120]{1,0:T(8,128)(2,1)}, u32[]{:S(2)}, u32[]{:S(2)}) collective-permute-start(bf16[640,5120]{1,0:T(8,128)(2,1)} %bitcast.100), channel_id=1, source_target_pairs={{0,4},{4,0},{1,5},{5,1},{2,6},{6,2},{3,7},{7,3},{8,12},{12,8},{9,1... | collective-permute-start | bytes 19660808 | tf_op jit(solution)/shard_map/ppermute | solution.py:67
  146.0 10.5 %collective-permute-start.5 = (f32[1,640]{1,0:T(1,128)}, f32[1,640]{1,0:T(1,128)S(1)}, u32[]{:S(2)}, u32[]{:S(2)}) collective-permute-start(f32[1,640]{1,0:T(1,128)} %param.20), channel_id=1, source_target_pairs={{0,4},{4,0},{1,5},{5,1},{2,6},{6,2},{3,7},{7,3},{8,12},{12,8},{9,1... | collective-permute-start | bytes 7688 | tf_op jit(solution)/shard_map/ppermute | solution.py:21
  147.9 39.8 %collective-permute-start.4 = (bf16[8,640,16]{1,2,0:T(8,128)(2,1)}, bf16[8,640,16]{1,2,0:T(8,128)(2,1)}, u32[]{:S(2)}, u32[]{:S(2)}) collective-permute-start(bf16[8,640,16]{1,2,0:T(8,128)(2,1)} %bitcast.116), channel_id=1, source_target_pairs={{0,4},{4,0},{1,5},{5,1},{2,6},{6,2},{3,7},{7,3},{8,12},{12,8},{9,1... | collective-permute-start | bytes 491528 | tf_op jit(solution)/shard_map/ppermute | solution.py:21
  152.6 3.9 copy-start.4
  154.8 33.0 %copy-start.3 = (bf16[1,8,640,16]{2,3,1,0:T(8,128)(2,1)S(1)}, bf16[1,8,640,16]{2,3,1,0:T(8,128)(2,1)}, u32[]{:S(2)}) copy-start(bf16[1,8,640,16]{2,3,1,0:T(8,128)(2,1)} %param.21) | copy-start | bytes 491524
  156.6 26.2 %collective-permute-start.2 = (bf16[64,1280]{1,0:T(8,128)(2,1)S(1)}, bf16[64,1280]{1,0:T(8,128)(2,1)S(1)}, u32[]{:S(2)}, u32[]{:S(2)}) collective-permute-start(bf16[64,1280]{1,0:T(8,128)(2,1)S(1)} %get-tuple-element.746), channel_id=1, source_target_pairs={{480,448},{448,416},{416,384},{384,352},{352,320},{320,288},{288,2... | collective-permute-start | bytes 491528 | tf_op jit(solution)/shard_map/ppermute | solution.py:75
  183.8 12.8 %all-to-all-start.1 = ((bf16[4,64,1280]{2,1,0:T(8,128)(2,1)}), bf16[4,64,1280]{2,1,0:T(8,128)(2,1)S(1)}, u32[]{:S(2)}, u32[]{:S(2)}) async-start(bf16[4,64,1280]{2,1,0:T(8,128)(2,1)} %broadcast_in_dim.142), calls=%async_computation.1 | async-start | bytes 1310720 | tf_op jit(solution)/shard_map/all_to_all | solution.py:39
  200.8 446.1 %collective-permute-start = (bf16[32,1408]{1,0:T(8,128)(2,1)S(1)}, bf16[32,1408]{1,0:T(8,128)(2,1)}, u32[]{:S(2)}, u32[]{:S(2)}) collective-permute-start(bf16[32,1408]{1,0:T(8,128)(2,1)S(1)} %dynamic-slice_bitcast_fusion.1), channel_id=1, source_target_pairs={{480,448},{416,384},{352,320},{288,256},{224,192},{160,128},{96,64... | collective-permute-start | bytes 270344 | tf_op jit(solution)/shard_map/while/body/eval_jaxpr/cond/branch_1_fun/ppermute | solution.py:172
  648.5 9.5 %all-to-all-start = ((bf16[4,32,1408]{2,1,0:T(8,128)(2,1)}), bf16[4,32,1408]{2,1,0:T(8,128)(2,1)S(1)}, u32[]{:S(2)}, u32[]{:S(2)}) async-start(bf16[4,32,1408]{2,1,0:T(8,128)(2,1)} %broadcast_in_dim.82), calls=%async_computation | async-start | bytes 720896 | tf_op jit(solution)/shard_map/while/body/eval_jaxpr/cond/branch_1_fun/cond/branch_0_fun/all_to_all | solution.py:39
  670.5 13.4 %collective-permute-start = (bf16[32,1408]{1,0:T(8,128)(2,1)S(1)}, bf16[32,1408]{1,0:T(8,128)(2,1)}, u32[]{:S(2)}, u32[]{:S(2)}) collective-permute-start(bf16[32,1408]{1,0:T(8,128)(2,1)S(1)} %dynamic-slice_bitcast_fusion.1), channel_id=1, source_target_pairs={{480,448},{416,384},{352,320},{288,256},{224,192},{160,128},{96,64... | collective-permute-start | bytes 270344 | tf_op jit(solution)/shard_map/while/body/eval_jaxpr/cond/branch_1_fun/ppermute | solution.py:172
  685.6 9.5 %all-to-all-start = ((bf16[4,32,1408]{2,1,0:T(8,128)(2,1)}), bf16[4,32,1408]{2,1,0:T(8,128)(2,1)S(1)}, u32[]{:S(2)}, u32[]{:S(2)}) async-start(bf16[4,32,1408]{2,1,0:T(8,128)(2,1)} %broadcast_in_dim.82), calls=%async_computation | async-start | bytes 720896 | tf_op jit(solution)/shard_map/while/body/eval_jaxpr/cond/branch_1_fun/cond/branch_0_fun/all_to_all | solution.py:39
  734.3 59.0 %copy-start.1 = (bf16[256,1280]{1,0:T(8,128)(2,1)S(1)}, bf16[256,1280]{1,0:T(8,128)(2,1)}, u32[]{:S(2)}) copy-start(bf16[256,1280]{1,0:T(8,128)(2,1)} %all-gather.1) | copy-start | bytes 1966084
  745.1 53.9 %collective-permute-start.8 = (f32[8,16,640]{2,1,0:T(8,128)S(1)}, f32[8,16,640]{2,1,0:T(8,128)S(1)}, u32[]{:S(2)}, u32[]{:S(2)}) collective-permute-start(f32[8,16,640]{2,1,0:T(8,128)S(1)} %slice_select_fusion), channel_id=1, source_target_pairs={{0,4},{4,0},{1,5},{5,1},{2,6},{6,2},{3,7},{7,3},{8,12},{12,8},{9,1... | collective-permute-start | bytes 983048 | tf_op jit(solution)/shard_map/ppermute | solution.py:34
  793.8 4.4 collective-permute-start.6
  795.8 4.2 collective-permute-start.7
Sparse Core Ops, SparseCore 0:
  10.1 133.2 all-gather.5

commit v2 on v1

v2 whole, which is shorter than its diff:
```python
import functools

import jax
import jax.numpy as jnp
from jax import lax
from jax.experimental import pallas as pl
from jax.experimental.pallas import tpu as pltpu
from jax.sharding import Mesh, PartitionSpec as P

norm_eps = 1e-05
low_rank_scale = 2.0
CHUNKS = 2
TAIL = 128
SWAP = [(0, 1), (1, 0)]
ODD = [(s, s - 1) for s in range(15, 0, -2)]
EVEN = [(s, s - 1) for s in range(14, 0, -2)]
EVERY = [(s, s - 1) for s in range(15, 0, -1)]
f32 = jnp.float32
bf16 = jnp.bfloat16
contract_last = (((1,), (1,)), ((), ()))


def both_cores(value, axis):
    core = lax.axis_index("c")
    other = lax.ppermute(value, "c", SWAP)
    low = jnp.where(core == 0, value, other)
    high = jnp.where(core == 0, other, value)
    return jnp.concatenate([low, high], axis)


def half_sum(value, axis):
    core = lax.axis_index("c")
    width = value.shape[axis] // 2
    low = lax.slice_in_dim(value, 0, width, axis=axis)
    high = lax.slice_in_dim(value, width, 2 * width, axis=axis)
    mine = jnp.where(core == 0, low, high)
    theirs = jnp.where(core == 0, high, low)
    return mine + lax.ppermute(theirs, "c", SWAP)


def spread(value):
    sent = jnp.broadcast_to(value[None], (4,) + value.shape)
    return lax.all_to_all(sent, "y", 0, 0)


def stage_kernel(
    place_ref,
    parts_ref,
    before_ref,
    up_ref,
    down_ref,
    gain_ref,
    inv_ref,
    x_ref,
    own_ref,
    other_ref,
    sent_in,
    low_in,
    grad_in,
    coef_in,
    box_ref,
    sent_ref,
    low_ref,
    grad_ref,
    coef_ref,
    full,
    frozen,
    low_sc,
    *,
    group,
):
    del sent_in, low_in, grad_in, coef_in
    step = pl.program_id(0)
    ypos, core = place_ref[1], place_ref[2]
    rows, width = x_ref.shape[1], x_ref.shape[2]
    width_all = full.shape[1]
    half = width // 2
    block = own_ref.shape[0]
    toks = rows // group
    rank = up_ref.shape[1] // group

    @pl.when(step == 0)
    def _():
        tail = parts_ref[:, :, width:].astype(f32)
        coef = jnp.sum(jnp.sum(tail, axis=0), axis=1, keepdims=True)
        for part in range(4):
            fixed = parts_ref[part, :, :width].astype(f32) - coef * before_ref[0, part].astype(f32)
            full[:, part * width : (part + 1) * width] = fixed.astype(bf16)
        low = lax.dot_general(full[...], up_ref[0], contract_last, preferred_element_type=f32)
        row_group = lax.broadcasted_iota(jnp.int32, low.shape, 0) // toks
        col_group = lax.broadcasted_iota(jnp.int32, low.shape, 1) // rank
        low_sc[...] = jnp.where(row_group == col_group, low, 0.0).astype(bf16)

    grad = full[...]
    offset = step * block
    for ref, base in ((own_ref, core * half), (other_ref, (1 - core) * half)):
        frozen[:, pl.ds(pl.multiple_of(base + offset, 128), block)] = lax.dot_general(
            grad, ref[...], contract_last, preferred_element_type=f32
        )

    @pl.when(step == pl.num_programs(0) - 1)
    def _():
        low = low_sc[...]
        adapt = lax.dot_general(
            low, down_ref[0], (((1,), (0,)), ((), ())), preferred_element_type=f32
        )
        normed_grad = ((frozen[...] + low_rank_scale * adapt) * gain_ref[...]).astype(bf16)
        normed_grad = normed_grad.astype(f32)
        inv = inv_ref[0]
        grad_y = full[:, pl.ds(pl.multiple_of(ypos * width, 128), width)]
        sent = (grad_y.astype(f32) + inv * normed_grad).astype(bf16)
        coef = jnp.sum(normed_grad * x_ref[0].astype(f32), axis=1, keepdims=True)
        coef = coef * (inv * inv * inv / width_all)
        high = coef.astype(bf16).astype(f32)
        lane = lax.broadcasted_iota(jnp.int32, (rows, TAIL), 1)
        tail = jnp.where(lane == 0, high, jnp.where(lane == 1, coef - high, 0.0)).astype(bf16)
        box_ref[:, :width] = sent
        box_ref[:, width:] = tail
        sent_ref[0] = sent
        low_ref[0] = low
        grad_ref[0] = grad_y
        coef_ref[0] = jnp.where(lane == 0, coef, 0.0)


def run_stage(place, parts, before, up, down, gain, inv, x, own, other, kept):
    sent_all, low_all, grad_all, coef_all = kept
    _, rows, width = x.shape
    half, width_all = own.shape
    group = up.shape[1] // 16
    block = 128

    def whole(shape):
        return pl.BlockSpec(shape, lambda i, place: (0,) * len(shape))

    def chunk(array):
        shape = array.shape[1:]
        return pl.BlockSpec((1,) + shape, lambda i, place: (place[0],) + (0,) * len(shape))

    weight = pl.BlockSpec((block, width_all), lambda i, place: (i, 0))
    any_space = pl.BlockSpec(memory_space=pl.ANY)
    keeps = [sent_all, low_all, grad_all, coef_all]
    return pl.pallas_call(
        functools.partial(stage_kernel, group=group),
        grid_spec=pltpu.PrefetchScalarGridSpec(
            num_scalar_prefetch=1,
            grid=(half // block,),
            in_specs=[
                whole(parts.shape),
                chunk(before),
                chunk(up),
                chunk(down),
                whole(gain.shape),
                chunk(inv),
                chunk(x),
                weight,
                weight,
            ]
            + [any_space] * 4,
            out_specs=[whole((rows, width + TAIL))] + [chunk(k) for k in keeps],
            scratch_shapes=[
                pltpu.VMEM((rows, width_all), bf16),
                pltpu.VMEM((rows, width), f32),
                pltpu.VMEM((rows, up.shape[1]), bf16),
            ],
        ),
        out_shape=[jax.ShapeDtypeStruct((rows, width + TAIL), bf16)]
        + [jax.ShapeDtypeStruct(k.shape, k.dtype) for k in keeps],
        input_output_aliases={10: 1, 11: 2, 12: 3, 13: 4},
        compiler_params=pltpu.CompilerParams(
            dimension_semantics=("arbitrary",), vmem_limit_bytes=32 * 1024 * 1024
        ),
        cost_estimate=pl.CostEstimate(
            flops=2 * rows * width * width_all, bytes_accessed=2 * width * width_all, transcendentals=0
        ),
        name="stage",
    )(place, parts, before, up, down, gain, inv, x, own, other, *keeps)


def local(
    section_inputs,
    out_grads,
    proj_weight,
    norm_gain,
    adapter_down,
    adapter_up,
    tenant_ids,
    slot_table,
):
    sec = lax.axis_index("s")
    ypos = lax.axis_index("y")
    core = lax.axis_index("c")
    micro = section_inputs.shape[1]
    width_all = section_inputs.shape[3]
    half = proj_weight.shape[1]
    width = 2 * half
    toks = section_inputs.shape[2] // 2
    rank = adapter_down.shape[3]
    rows_all = micro * toks
    group = micro // CHUNKS
    rows = group * toks
    multiplier = low_rank_scale / (toks * 2 * lax.axis_size("z"))

    w_own = lax.all_gather(proj_weight[0], "z", axis=1, tiled=True)

    x_full = section_inputs[0]
    x_mine = lax.dynamic_slice_in_dim(x_full, core * toks, toks, 1).reshape(rows_all, width_all)
    x_f = x_mine.astype(f32)
    inv_rms = lax.rsqrt(jnp.mean(x_f * x_f, axis=-1, keepdims=True) + norm_eps)
    x_y = lax.dynamic_slice_in_dim(x_mine, ypos * width, width, 1)
    normed_y = x_y.astype(f32) * inv_rms
    x_before = spread(lax.ppermute(x_y, "s", EVERY))
    gain_y = both_cores(norm_gain, 1)
    down_y = both_cores(adapter_down[0], 1)
    h_y = (normed_y * gain_y).astype(bf16)

    iota = jnp.arange(micro, dtype=jnp.int32)
    tenant_hot = tenant_ids[:, None] == iota[None, :]
    slot_ids = jnp.sum(jnp.where(tenant_hot, slot_table[0][None, :], 0), axis=1)
    down_sel = down_y[slot_ids]
    up_sel = adapter_up[0][slot_ids]
    low_in = jnp.einsum(
        "mtd,mdr->mtr", h_y.reshape(micro, toks, width), down_sel, preferred_element_type=f32
    )
    low_in = lax.psum(low_in, "y").astype(bf16)
    low_in_all = lax.all_gather(low_in, "z")
    h_all = lax.all_gather(h_y, "z")

    grads_top = lax.dynamic_slice_in_dim(out_grads, core * toks, toks, 1)
    grads_top = grads_top.reshape(CHUNKS, rows, 4, width).transpose(0, 2, 1, 3)
    grads_top = jnp.pad(grads_top, ((0, 0), (0, 0), (0, 0), (0, TAIL)))
    x_before = x_before.reshape(4, CHUNKS, rows, width).transpose(1, 0, 2, 3)
    x_chunk = x_y.reshape(CHUNKS, rows, width)
    inv_chunk = inv_rms.reshape(CHUNKS, rows, 1)
    down_chunk = down_sel.transpose(0, 2, 1).reshape(CHUNKS, group * rank, width)
    up_chunk = up_sel.reshape(CHUNKS, group * rank, width_all)

    ready = (x_before, low_in_all, h_all, grads_top, down_chunk, up_chunk, inv_chunk, gain_y)
    w_own, ready = lax.optimization_barrier((w_own, ready))
    x_before, low_in_all, h_all, grads_top, down_chunk, up_chunk, inv_chunk, gain_y = ready
    w_other = lax.ppermute(w_own, "c", SWAP)

    def pick(array, m):
        return lax.dynamic_index_in_dim(array, m, 0, keepdims=False)

    def step(u, state):
        t, m = u // CHUNKS, u % CHUNKS
        turn = 15 - t + m

        def work(state):
            box, kept = state
            parts = lax.cond(sec == 15, lambda box: pick(grads_top, m), spread, box)
            place = jnp.stack([m, ypos, core]).astype(jnp.int32)
            box, *kept = run_stage(
                place,
                parts,
                x_before,
                up_chunk,
                down_chunk,
                gain_y,
                inv_chunk,
                x_chunk,
                w_own,
                w_other,
                kept,
            )
            return box, tuple(kept)

        box, kept = lax.cond(sec == turn, work, lambda state: state, state)
        part = ((sec == turn) | (sec == turn - 1)) & (turn >= 1) & (turn <= 15)
        kind = jnp.where(part, jnp.where(turn % 2 == 1, 1, 2), 0)
        box = lax.switch(
            kind,
            [
                lambda box: box,
                lambda box: lax.ppermute(box, "s", ODD),
                lambda box: lax.ppermute(box, "s", EVEN),
            ],
            box,
        )
        return box, kept

    start = (
        jnp.zeros((rows, width + TAIL), bf16),
        (
            jnp.zeros((CHUNKS, rows, width), bf16),
            jnp.zeros((CHUNKS, rows, group * rank), bf16),
            jnp.zeros((CHUNKS, rows, width), bf16),
            jnp.zeros((CHUNKS, rows, TAIL), f32),
        ),
    )
    _, kept = lax.fori_loop(0, 15 * CHUNKS + 2 * CHUNKS, step, start)
    sent_all, low_all, grad_all, coef_all = kept

    coef_sum = jnp.sum(spread(coef_all), axis=(0, -1))[..., None]
    new_grads = sent_all.astype(f32) - coef_sum * x_chunk.astype(f32)
    new_grads = new_grads.astype(bf16).reshape(micro, toks, width)
    keep = jnp.where(core == 0, new_grads[:, :, :half], new_grads[:, :, half:])
    give = jnp.where(core == 0, new_grads[:, :, half:], new_grads[:, :, :half])
    got = lax.ppermute(give, "c", SWAP)
    kept = jnp.concatenate(
        [jnp.where(core == 0, keep, got), jnp.where(core == 0, got, keep)], 1
    )

    both = jnp.concatenate(
        [
            grad_all.reshape(rows_all, width),
            jnp.pad(low_all.reshape(rows_all, group * rank), ((0, 0), (0, TAIL - group * rank))),
        ],
        1,
    )
    both = lax.all_gather(both, "z").reshape(4, micro, toks, width + TAIL)
    grads_z = both[..., :width]
    low_z = both[..., width : width + group * rank].reshape(4, micro, toks, group, rank)
    low_z = jnp.sum(low_z.astype(f32), axis=3).astype(bf16)
    hidden_z = h_all.reshape(4, micro, toks, width)
    down_part = multiplier * jnp.einsum(
        "zmtd,zmtr->mdr", hidden_z, low_z, preferred_element_type=f32
    )
    up_part = multiplier * jnp.einsum(
        "zmtr,zmtd->mrd", low_in_all, grads_z, preferred_element_type=f32
    )
    down_acc = half_sum(down_part, 1)
    up_acc = half_sum(up_part, 2)
    slot_hot = slot_ids[None, :] == iota[:, None]
    down_out = jnp.sum(jnp.where(slot_hot[:, :, None, None], down_acc[None], 0.0), axis=1)
    up_out = jnp.sum(jnp.where(slot_hot[:, :, None, None], up_acc[None], 0.0), axis=1)
    return (kept[None], down_out[None], up_out[None])


def solution(mesh):
    fine = Mesh(mesh.devices.reshape(16, 4, 2, 4), ("s", "y", "c", "z"))
    mp = ("y", "c")
    placed = (
        P("s", None, "z", None),
        P(None, "z", None),
        P("s", mp, "z"),
        P("s", mp),
        P("s", None, mp, None),
        P("s", None, None, None),
        P(),
        P("s", None),
    )
    return jax.shard_map(
        local,
        mesh=fine,
        in_specs=placed,
        out_specs=(
            P("s", None, "z", mp),
            P("s", None, mp, None),
            P("s", None, None, mp),
        ),
        check_vma=False,
    )
```

time: 809 us -> 711 us (0.88)
  waiting for transfers between devices: 612 us -> 490 us
  blocking collectives: 62.1 us -> 91.8 us
  matrix products: 23.7 us -> 1.85 us
  Pallas kernels: 0 us -> 20.4 us
  starting transfers between devices: 74.3 us -> 64.5 us
    all_gather x1, waiting for transfers between devices: 136 us -> 60.5 us  [local(): w_own = lax.all_gather(proj_weight[0], 'z', axis=1, tiled=True)]
    ppermute x2, waiting for transfers between devices: 457 us -> 423 us  [step(): lax.ppermute(box, 's', ODD)]
    dot_general x8 -> x0, matrix products: 22.9 us -> none  [the longest x2 9.79 us: stage(): lax.dot_general(grad, w_own, contract_last, preferred_element_type=f32)]
    pallas_call x0 -> x2, Pallas kernels: none -> 20.4 us  [run_stage(): pl.pallas_call(functools.partial(stage_kernel, group=group), grid_spec=pl...]
    all_to_all x3 -> x2, waiting for transfers between devices: 19 us -> 0.01 us  [spread(): return lax.all_to_all(sent, 'y', 0, 0)]
    all_to_all x0 -> x2, blocking collectives: none -> 16.9 us  [spread(): return lax.all_to_all(sent, 'y', 0, 0)]
    ppermute x2, starting transfers between devices: 50.7 us -> 37.9 us  [half_sum(): return mine + lax.ppermute(theirs, 'c', SWAP)]
  transfers between devices with their start and end apart: 13 -> 12, of which waited for: 6 -> 4; matrix products, arithmetic and copies ran while one was open for 1% -> 2% of each run, Pallas kernels for 0% -> 0%
where the time goes in v2:
time: 711 us; the launch traced here: 710 us
  waiting for transfers between devices  490 us (69%)
  blocking collectives  91.8 us (13%)
  starting transfers between devices  64.5 us (9%)
  Pallas kernels  20.4 us (3%)
  local copies, waits for them, and re-layouts  15.5 us (2%)
  between operations  14.5 us (2%)
  other arithmetic  7.89 us (1%)
    ppermute x2, waiting for transfers between devices, step(): lax.ppermute(box, 's', ODD)  423 us
    all_gather x1, waiting for transfers between devices, local(): w_own = lax.all_gather(proj_weight[0], 'z', axis=1, tiled=True)  60.5 us
    ppermute x2, starting transfers between devices, half_sum(): return mine + lax.ppermute(theirs, 'c', SWAP)  37.9 us
    all_gather x1, blocking collectives, local(): h_all = lax.all_gather(h_y, 'z')  32 us
    pallas_call x2, Pallas kernels, run_stage(): pl.pallas_call(functools.partial(stage_kernel, group=group), grid_spec=pl...  20.4 us
    all_to_all x2, blocking collectives, spread(): return lax.all_to_all(sent, 'y', 0, 0)  16.9 us
    psum x1, blocking collectives, local(): low_in = lax.psum(low_in, 'y').astype(bf16)  16.1 us
  transfers between devices with their start and end apart: 12, of which 4 were waited for; matrix products, arithmetic and copies ran while one was open for 2% of the time, Pallas kernels for 0%

profile of v2, /device:TPU:1, one launch (start us, length us, event | category | flops | bytes accessed | tf_op | source)
XLA Modules:
  0.0 710.2 jit_solution(2422539964122148905)
XLA Ops:
  7.3 0.7 all-gather.6.cloned.1.call-update
  8.0 8.9 %collective-permute-start.3 = (f32[1,640]{1,0:T(1,128)S(1)}, f32[1,640]{1,0:T(1,128)S(1)}, u32[]{:S(2)}, u32[]{:S(2)}) collective-permute-start(f32[1,640]{1,0:T(1,128)S(1)} %copy-done.11), channel_id=1, source_target_pairs={{0,4},{4,0},{1,5},{5,1},{2,6},{6,2},{3,7},{7,3},{8,12},{12,8},{9,1... | collective-permute-start | bytes 7688 | tf_op jit(solution)/shard_map/ppermute | solution.py:25
  16.9 1.9 collective-permute-start.4
  18.9 0.2 multiply_reduce_fusion
  19.1 0.2 select_reduce_fusion.2
  19.3 0.9 dynamic-slice_bitcast_fusion.1
  20.4 0.5 reshape.128
  20.9 1.1 pad.8
  22.0 0.6 gather_fusion.1
  22.7 1.0 multiply_convert_fusion
  23.8 1.3 collective-permute-start.2
  25.1 32.0 %all-gather.2 = bf16[256,1280]{1,0:T(8,128)(2,1)} all-gather(bf16[64,1280]{1,0:T(8,128)(2,1)S(1)} %get-tuple-element.742), channel_id=4, replica_groups=mesh['s'=16,'y'=4,'c'=2,'z'=4] {'z'}, dimensions={0}, use_global_device_ids=true | all-gather | bytes 819200 | tf_op jit(solution)/shard_map/all_gather | solution.py:226
  57.0 0.9 broadcast_in_dim.105
  57.9 4.2 all-to-all-start.1
  62.2 0.6 gather_fusion
  62.8 0.3 copy-done.6
  63.1 0.2 fusion.6
  63.3 16.1 %psum.7 = bf16[8,8,16]{2,1,0:T(8,128)(2,1)S(1)} all-reduce(f32[8,8,16]{2,1,0:T(8,128)S(1)} %fusion.6), channel_id=1, replica_groups=mesh['s'=16,'y'=4,'c'=2,'z'=4] {'y'}, use_global_device_ids=true, to_apply=%region_2.3 | all-reduce | flops 1024 | bytes 6144 | tf_op jit(solution)/shard_map/psum | solution.py:224
  79.4 13.7 %all-gather.1 = bf16[32,8,16]{2,1,0:T(8,128)(2,1)} all-gather(bf16[8,8,16]{2,1,0:T(8,128)(2,1)S(1)} %psum.7), channel_id=3, replica_groups=mesh['s'=16,'y'=4,'c'=2,'z'=4] {'z'}, dimensions={0}, use_global_device_ids=true | all-gather | bytes 10240 | tf_op jit(solution)/shard_map/all_gather | solution.py:225
  93.1 60.5 %all-gather.6.cloned.1.call-done = bf16[1,640,5120]{2,1,0:T(8,128)(2,1)} async-done(((bf16[1,640,1280]{2,1,0:T(8,128)(2,1)}), bf16[1,640,5120]{2,1,0:T(8,128)(2,1)}) %all-gather.6.cloned.1.call-update) | async-done | bytes 6553616 | tf_op jit(solution)/shard_map/all_gather | solution.py:203
  153.6 2.4 collective-permute-start.5
  156.0 2.0 copy.29
  158.0 2.0 copy.30
  160.1 6.4 collective-permute-done.5
  166.5 0.6 broadcast_in_dim.102
  167.1 0.7 broadcast.80
  167.8 0.6 broadcast_in_dim.103
  168.4 469.4 %while.27 = (s32[]{:T(128)}, bf16[32,1408]{1,0:T(8,128)(2,1)}, bf16[2,32,1280]{2,1,0:T(8,128)(2,1)}, bf16[2,32,64]{2,1,0:T(8,128)(2,1)}, bf16[2,32,1280]{2,1,0:T...) while((s32[]{:T(128)}, bf16[32,1408]{1,0:T(8,128)(2,1)}, ...), condition=%wide.region_11.12_spmd, body=%wide.region_3.11_spmd.sunk | while | flops 419430432 | bytes 14820244 | solution.py:291
  171.8 411.8 %conditional.6 = (bf16[32,1408]{1,0:T(8,128)(2,1)}) conditional(s32[]{:T(128)} %clamp.15, bf16[32,1408]{1,0:T(8,128)(2,1)} %get-tuple-element.866, bf16[32,1408]{1,0:T(8,128)(2,1)} %get-tuple-element.866, bf16[32,1408]{1,0:T(8,128)(2,1)} %get-tuple-element.866), branch_computations={%region_8.8_spmd, %region_9.9_spmd, %region_10.10_spmd} | conditional | bytes 540720 | solution.py:271
  171.8 1.3 collective-permute-start
  173.1 409.8 %collective-permute-done = bf16[32,1408]{1,0:T(8,128)(2,1)S(1)} collective-permute-done((bf16[32,1408]{1,0:T(8,128)(2,1)}, bf16[32,1408]{1,0:T(8,128)(2,1)S(1)}, u32[]{:S(2)}, u32[]{:S(2)}) %collective-permute-start) | collective-permute-done | bytes 90144 | tf_op jit(solution)/shard_map/while/body/eval_jaxpr/cond/branch_1_fun/ppermute | solution.py:275
  582.9 0.6 copy.49
  583.6 19.7 %conditional.5 = ((bf16[2,32,1280]{2,1,0:T(8,128)(2,1)}, bf16[2,32,64]{2,1,0:T(8,128)(2,1)}, bf16[2,32,1280]{2,1,0:T(8,128)(2,1)S(1)}, f32[2,32,128]{2,1,0:T(8,128)S(1)}, bf16[32,1408]{1,0:T(8,128)(2,1)})) conditional(s32[]{:T(128)} %convert_element_type.56, (bf16[2,32,1280]{2,1,0:T(8,128)(2,1)}, bf16[2,32,64]{2,1,0:T(8,128)(2,1)}, ...), branch_computations={%region_4.4_spmd, %region_5.7_spmd} | conditional | flops 419430400 | bytes 14278766 | solution.py:268
  583.6 9.4 %conditional = (bf16[4,32,1408]{2,1,0:T(8,128)(2,1)S(1)}) conditional(s32[]{:T(128)} %convert_element_type.33, bf16[32,1408]{1,0:T(8,128)(2,1)} %get-tuple-element.562, (s32[]{:T(128)}, bf16[2,4,32,1408]{3,2,1,0:T(8,128)(2,1)}) %tuple.56), branch_computations={%region_6.5_spmd, %region_7.6_spmd} | conditional | flops 3 | bytes 1171464 | solution.py:251
  583.6 0.9 broadcast_in_dim.51
  584.6 8.4 %all_to_all.14 = bf16[4,32,1408]{2,1,0:T(8,128)(2,1)S(1)} all-to-all(bf16[4,32,1408]{2,1,0:T(8,128)(2,1)S(1)} %broadcast_in_dim.51), channel_id=1, replica_groups=mesh['s'=16,'y'=4,'c'=2,'z'=4] {'y'}, dimensions={0} | all-to-all | bytes 720896 | tf_op jit(solution)/shard_map/while/body/eval_jaxpr/cond/branch_1_fun/cond/branch_0_fun/all_to_all | solution.py:43
  593.0 10.2 %stage.1 = (bf16[32,1408]{1,0:T(8,128)(2,1)}, bf16[2,32,1280]{2,1,0:T(8,128)(2,1)}, bf16[2,32,64]{2,1,0:T(8,128)(2,1)}, bf16[2,32,1280]{2,1,0:T(8,128)(2,1)S(1)}, f32[2,32,128]{2,1,0:T(8,128)S(1)}) custom-call(s32[3]{0:T(128)S(1)} %pad_add_fusion.place_ref, ...), custom_call_target="tpu_custom_call", output_to_operand_aliasing={{1}: (10, {}), {2}: (11, {}), {3}: (12, {}), {4}: (13, {})} | custom-call | flops 419430400 | bytes 13107200 | tf_op jit(solution)/shard_map/while/body/eval_jaxpr/cond/branch_1_fun/stage/pallas_call | solution.py:142
  603.2 14.9 %conditional.6 = (bf16[32,1408]{1,0:T(8,128)(2,1)}) conditional(s32[]{:T(128)} %clamp.15, bf16[32,1408]{1,0:T(8,128)(2,1)} %get-tuple-element.866, bf16[32,1408]{1,0:T(8,128)(2,1)} %get-tuple-element.866, bf16[32,1408]{1,0:T(8,128)(2,1)} %get-tuple-element.866), branch_computations={%region_8.8_spmd, %region_9.9_spmd, %region_10.10_spmd} | conditional | bytes 540720 | solution.py:271
  603.2 1.3 collective-permute-start
  604.5 13.0 %collective-permute-done = bf16[32,1408]{1,0:T(8,128)(2,1)S(1)} collective-permute-done((bf16[32,1408]{1,0:T(8,128)(2,1)}, bf16[32,1408]{1,0:T(8,128)(2,1)S(1)}, u32[]{:S(2)}, u32[]{:S(2)}) %collective-permute-start) | collective-permute-done | bytes 90144 | tf_op jit(solution)/shard_map/while/body/eval_jaxpr/cond/branch_1_fun/ppermute | solution.py:275
  617.5 0.6 copy.49
  618.1 19.7 %conditional.5 = ((bf16[2,32,1280]{2,1,0:T(8,128)(2,1)}, bf16[2,32,64]{2,1,0:T(8,128)(2,1)}, bf16[2,32,1280]{2,1,0:T(8,128)(2,1)S(1)}, f32[2,32,128]{2,1,0:T(8,128)S(1)}, bf16[32,1408]{1,0:T(8,128)(2,1)})) conditional(s32[]{:T(128)} %convert_element_type.56, (bf16[2,32,1280]{2,1,0:T(8,128)(2,1)}, bf16[2,32,64]{2,1,0:T(8,128)(2,1)}, ...), branch_computations={%region_4.4_spmd, %region_5.7_spmd} | conditional | flops 419430400 | bytes 14278766 | solution.py:268
  618.2 9.4 %conditional = (bf16[4,32,1408]{2,1,0:T(8,128)(2,1)S(1)}) conditional(s32[]{:T(128)} %convert_element_type.33, bf16[32,1408]{1,0:T(8,128)(2,1)} %get-tuple-element.562, (s32[]{:T(128)}, bf16[2,4,32,1408]{3,2,1,0:T(8,128)(2,1)}) %tuple.56), branch_computations={%region_6.5_spmd, %region_7.6_spmd} | conditional | flops 3 | bytes 1171464 | solution.py:251
  618.2 0.9 broadcast_in_dim.51
  619.1 8.4 %all_to_all.14 = bf16[4,32,1408]{2,1,0:T(8,128)(2,1)S(1)} all-to-all(bf16[4,32,1408]{2,1,0:T(8,128)(2,1)S(1)} %broadcast_in_dim.51), channel_id=1, replica_groups=mesh['s'=16,'y'=4,'c'=2,'z'=4] {'y'}, dimensions={0} | all-to-all | bytes 720896 | tf_op jit(solution)/shard_map/while/body/eval_jaxpr/cond/branch_1_fun/cond/branch_0_fun/all_to_all | solution.py:43
  627.6 10.2 %stage.1 = (bf16[32,1408]{1,0:T(8,128)(2,1)}, bf16[2,32,1280]{2,1,0:T(8,128)(2,1)}, bf16[2,32,64]{2,1,0:T(8,128)(2,1)}, bf16[2,32,1280]{2,1,0:T(8,128)(2,1)S(1)}, f32[2,32,128]{2,1,0:T(8,128)S(1)}) custom-call(s32[3]{0:T(128)S(1)} %pad_add_fusion.place_ref, ...), custom_call_target="tpu_custom_call", output_to_operand_aliasing={{1}: (10, {}), {2}: (11, {}), {3}: (12, {}), {4}: (13, {})} | custom-call | flops 419430400 | bytes 13107200 | tf_op jit(solution)/shard_map/while/body/eval_jaxpr/cond/branch_1_fun/stage/pallas_call | solution.py:142
  637.8 0.7 broadcast_in_dim.109
  638.5 3.3 all-to-all-start.2
  641.8 0.7 fusion.5
  642.5 13.1 %all-gather.3 = bf16[256,1408]{1,0:T(8,128)(2,1)S(1)} all-gather(bf16[64,1408]{1,0:T(8,128)(2,1)S(1)} %fusion.5), channel_id=5, replica_groups=mesh['s'=16,'y'=4,'c'=2,'z'=4] {'z'}, dimensions={0}, use_global_device_ids=true | all-gather | bytes 901120 | tf_op jit(solution)/shard_map/all_gather | solution.py:311
  655.7 0.2 reshape.137
  655.9 0.4 reduce_sum.63
  656.2 0.3 copy-done.3
  656.6 1.4 fusion.1
  658.0 35.5 %collective-permute-start.7 = (f32[8,640,16]{1,2,0:T(8,128)S(1)}, f32[8,640,16]{1,2,0:T(8,128)}, u32[]{:S(2)}, u32[]{:S(2)}) collective-permute-start(f32[8,640,16]{1,2,0:T(8,128)S(1)} %slice_select_fusion.1), channel_id=1, source_target_pairs={{0,4},{4,0},{1,5},{5,1},{2,6},{6,2},{3,7},{7,3},{8,12},{12,8},{9,1... | collective-permute-start | bytes 983048 | tf_op jit(solution)/shard_map/ppermute | solution.py:38
  693.6 0.3 fusion
  693.9 0.1 reduce_sum.62
  694.0 1.0 subtract_convert_fusion
  695.1 1.9 collective-permute-start.6
  697.0 2.4 collective-permute-start.8
  699.5 0.7 maximum_bitcast_fusion
  700.2 1.0 select_add_fusion.1
  701.2 1.0 select_reduce_fusion.1
  702.3 1.0 select_reduce_fusion
  (121 shorter events, 1.8 us)
Async XLA Ops:
  7.2 14.8 %copy-start = (bf16[1,8,16,5120]{3,2,1,0:T(8,128)(2,1)S(1)}, bf16[1,8,16,5120]{3,2,1,0:T(8,128)(2,1)}, u32[]{:S(2)}) copy-start(bf16[1,8,16,5120]{3,2,1,0:T(8,128)(2,1)} %param.22) | copy-start | bytes 3932164
  7.2 0.8 copy-start.11
  7.2 9.7 %copy-start.10 = (bf16[1,8,640,16]{2,3,1,0:T(8,128)(2,1)S(1)}, bf16[1,8,640,16]{2,3,1,0:T(8,128)(2,1)}, u32[]{:S(2)}) copy-start(bf16[1,8,640,16]{2,3,1,0:T(8,128)(2,1)} %param.21) | copy-start | bytes 491524
  7.2 11.6 %copy-start.7 = (bf16[1,8,16,5120]{3,2,1,0:T(8,128)(2,1)S(1)}, bf16[1,8,16,5120]{3,2,1,0:T(8,128)(2,1)}, u32[]{:S(2)}) copy-start(bf16[1,8,16,5120]{3,2,1,0:T(8,128)(2,1)} %param.17) | copy-start | bytes 3932164
  7.2 11.9 %copy-start.12 = (s32[1,8]{1,0:T(1,128)S(1)}, s32[1,8]{1,0:T(1,128)}, u32[]{:S(2)}) copy-start(s32[1,8]{1,0:T(1,128)} %param.24) | copy-start | bytes 100
  7.2 11.9 %copy-start.13 = (s32[8]{0:T(128)S(1)}, s32[8]{0:T(128)}, u32[]{:S(2)}) copy-start(s32[8]{0:T(128)} %param.23) | copy-start | bytes 100
  7.2 146.3 %all-gather.6.cloned.1.call-start = ((), (), s32[]{:S(2)}) async-start(), calls=%async_computation.3 | async-start | bytes 8192000 | tf_op jit(solution)/shard_map/all_gather | solution.py:203
  8.0 14.7 %collective-permute-start.3 = (f32[1,640]{1,0:T(1,128)S(1)}, f32[1,640]{1,0:T(1,128)S(1)}, u32[]{:S(2)}, u32[]{:S(2)}) collective-permute-start(f32[1,640]{1,0:T(1,128)S(1)} %copy-done.11), channel_id=1, source_target_pairs={{0,4},{4,0},{1,5},{5,1},{2,6},{6,2},{3,7},{7,3},{8,12},{12,8},{9,1... | collective-permute-start | bytes 7688 | tf_op jit(solution)/shard_map/ppermute | solution.py:25
  16.9 45.2 %collective-permute-start.4 = (bf16[8,640,16]{1,2,0:T(8,128)(2,1)S(1)}, bf16[8,640,16]{1,2,0:T(8,128)(2,1)S(1)}, u32[]{:S(2)}, u32[]{:S(2)}) collective-permute-start(bf16[8,640,16]{1,2,0:T(8,128)(2,1)S(1)} %bitcast.71), channel_id=1, source_target_pairs={{0,4},{4,0},{1,5},{5,1},{2,6},{6,2},{3,7},{7,3},{8,12},{12,8},{9,1... | collective-permute-start | bytes 491528 | tf_op jit(solution)/shard_map/ppermute | solution.py:25
  18.9 1.3 copy-start.8
  23.7 34.2 %copy-start.1 = (bf16[64,1280]{1,0:T(8,128)(2,1)}, bf16[64,1280]{1,0:T(8,128)(2,1)S(1)}, u32[]{:S(2)}) copy-start(bf16[64,1280]{1,0:T(8,128)(2,1)S(1)} %get-tuple-element.743) | copy-start | bytes 491524
  23.8 34.2 %copy-start.5 = (bf16[64,1280]{1,0:T(8,128)(2,1)}, bf16[64,1280]{1,0:T(8,128)(2,1)S(1)}, u32[]{:S(2)}) copy-start(bf16[64,1280]{1,0:T(8,128)(2,1)S(1)} %get-tuple-element.742) | copy-start | bytes 491524
  23.8 33.3 %collective-permute-start.2 = (bf16[64,1280]{1,0:T(8,128)(2,1)S(1)}, bf16[64,1280]{1,0:T(8,128)(2,1)S(1)}, u32[]{:S(2)}, u32[]{:S(2)}) collective-permute-start(bf16[64,1280]{1,0:T(8,128)(2,1)S(1)} %get-tuple-element.743), channel_id=1, source_target_pairs={{480,448},{448,416},{416,384},{384,352},{352,320},{320,288},{288,2... | collective-permute-start | bytes 491528 | tf_op jit(solution)/shard_map/ppermute | solution.py:211
  57.9 35.2 %all-to-all-start.1 = ((bf16[4,64,1280]{2,1,0:T(8,128)(2,1)}), bf16[4,64,1280]{2,1,0:T(8,128)(2,1)}, u32[]{:S(2)}, u32[]{:S(2)}) async-start(bf16[4,64,1280]{2,1,0:T(8,128)(2,1)} %broadcast_in_dim.105), calls=%async_computation.1 | async-start | bytes 1310720 | tf_op jit(solution)/shard_map/all_to_all | solution.py:43
  62.2 0.9 copy-start.6
  153.6 12.9 %collective-permute-start.5 = (bf16[640,5120]{1,0:T(8,128)(2,1)}, bf16[640,5120]{1,0:T(8,128)(2,1)}, u32[]{:S(2)}, u32[]{:S(2)}) collective-permute-start(bf16[640,5120]{1,0:T(8,128)(2,1)} %bitcast.56), channel_id=1, source_target_pairs={{0,4},{4,0},{1,5},{5,1},{2,6},{6,2},{3,7},{7,3},{8,12},{12,8},{9,1... | collective-permute-start | bytes 19660808 | tf_op jit(solution)/shard_map/ppermute | solution.py:240
  171.8 411.1 %collective-permute-start = (bf16[32,1408]{1,0:T(8,128)(2,1)}, bf16[32,1408]{1,0:T(8,128)(2,1)S(1)}, u32[]{:S(2)}, u32[]{:S(2)}) collective-permute-start(bf16[32,1408]{1,0:T(8,128)(2,1)} %param.5), channel_id=1, source_target_pairs={{480,448},{416,384},{352,320},{288,256},{224,192},{160,128},{96,64... | collective-permute-start | bytes 270344 | tf_op jit(solution)/shard_map/while/body/eval_jaxpr/cond/branch_1_fun/ppermute | solution.py:275
  603.2 14.3 %collective-permute-start = (bf16[32,1408]{1,0:T(8,128)(2,1)}, bf16[32,1408]{1,0:T(8,128)(2,1)S(1)}, u32[]{:S(2)}, u32[]{:S(2)}) collective-permute-start(bf16[32,1408]{1,0:T(8,128)(2,1)} %param.5), channel_id=1, source_target_pairs={{480,448},{416,384},{352,320},{288,256},{224,192},{160,128},{96,64... | collective-permute-start | bytes 270344 | tf_op jit(solution)/shard_map/while/body/eval_jaxpr/cond/branch_1_fun/ppermute | solution.py:275
  638.5 55.4 %all-to-all-start.2 = ((f32[4,2,32,128]{3,2,1,0:T(8,128)}), f32[4,2,32,128]{3,2,1,0:T(8,128)S(1)}, u32[]{:S(2)}, u32[]{:S(2)}) async-start(f32[4,2,32,128]{3,2,1,0:T(8,128)} %broadcast_in_dim.109), calls=%async_computation.2 | async-start | bytes 262144 | tf_op jit(solution)/shard_map/all_to_all | solution.py:43
  655.7 0.9 copy-start.3
  655.9 37.7 %copy-start.9 = (bf16[32,8,16]{2,1,0:T(8,128)(2,1)S(1)}, bf16[32,8,16]{2,1,0:T(8,128)(2,1)}, u32[]{:S(2)}) copy-start(bf16[32,8,16]{2,1,0:T(8,128)(2,1)} %all-gather.1) | copy-start | bytes 24580
  657.9 35.6 %copy-start.4 = (bf16[256,1408]{1,0:T(8,128)(2,1)S(1)}, bf16[256,1408]{1,0:T(8,128)(2,1)}, u32[]{:S(2)}) copy-start(bf16[256,1408]{1,0:T(8,128)(2,1)} %copy-done.3) | copy-start | bytes 2162692
  658.0 36.0 %copy-start.2 = (bf16[2,32,1280]{2,1,0:T(8,128)(2,1)S(1)}, bf16[2,32,1280]{2,1,0:T(8,128)(2,1)}, u32[]{:S(2)}) copy-start(bf16[2,32,1280]{2,1,0:T(8,128)(2,1)} %get-tuple-element.958) | copy-start | bytes 491524
  658.0 42.2 %collective-permute-start.7 = (f32[8,640,16]{1,2,0:T(8,128)S(1)}, f32[8,640,16]{1,2,0:T(8,128)}, u32[]{:S(2)}, u32[]{:S(2)}) collective-permute-start(f32[8,640,16]{1,2,0:T(8,128)S(1)} %slice_select_fusion.1), channel_id=1, source_target_pairs={{0,4},{4,0},{1,5},{5,1},{2,6},{6,2},{3,7},{7,3},{8,12},{12,8},{9,1... | collective-permute-start | bytes 983048 | tf_op jit(solution)/shard_map/ppermute | solution.py:38
  695.1 4.4 collective-permute-start.6
  697.0 5.2 collective-permute-start.8
Sparse Core Ops, SparseCore 0:
  10.2 143.3 all-gather.5

commit v3 on v2

--- a/solution.py
+++ b/solution.py
@@ -64,70 +64,74 @@
     grad_ref,
     coef_ref,
     full,
-    frozen,
-    low_sc,
+    weight,
+    sems,
     *,
     group,
 ):
     del sent_in, low_in, grad_in, coef_in
-    step = pl.program_id(0)
     ypos, core = place_ref[1], place_ref[2]
     rows, width = x_ref.shape[1], x_ref.shape[2]
     width_all = full.shape[1]
     half = width // 2
-    block = own_ref.shape[0]
     toks = rows // group
     rank = up_ref.shape[1] // group
-
-    @pl.when(step == 0)
-    def _():
-        tail = parts_ref[:, :, width:].astype(f32)
-        coef = jnp.sum(jnp.sum(tail, axis=0), axis=1, keepdims=True)
-        for part in range(4):
-            fixed = parts_ref[part, :, :width].astype(f32) - coef * before_ref[0, part].astype(f32)
-            full[:, part * width : (part + 1) * width] = fixed.astype(bf16)
-        low = lax.dot_general(full[...], up_ref[0], contract_last, preferred_element_type=f32)
-        row_group = lax.broadcasted_iota(jnp.int32, low.shape, 0) // toks
-        col_group = lax.broadcasted_iota(jnp.int32, low.shape, 1) // rank
-        low_sc[...] = jnp.where(row_group == col_group, low, 0.0).astype(bf16)
-
-    grad = full[...]
-    offset = step * block
-    for ref, base in ((own_ref, core * half), (other_ref, (1 - core) * half)):
-        frozen[:, pl.ds(pl.multiple_of(base + offset, 128), block)] = lax.dot_general(
-            grad, ref[...], contract_last, preferred_element_type=f32
+    pieces = sems.shape[0]
+    depth = width_all // pieces
+    copies = []
+    for piece in range(pieces):
+        span = pl.ds(piece * depth, depth)
+        pair = []
+        for side, (ref, base) in enumerate(((own_ref, core * half), (other_ref, (1 - core) * half))):
+            lanes = pl.ds(pl.multiple_of(base, 128), half)
+            copy = pltpu.make_async_copy(
+                ref.at[span], weight.at[span, lanes], sems.at[piece, side]
+            )
+            copy.start()
+            pair.append(copy)
+        copies.append(pair)
+
+    tail = parts_ref[:, :, width:].astype(f32)
+    coef = jnp.sum(jnp.sum(tail, axis=0), axis=1, keepdims=True)
+    for part in range(4):
+        fixed = parts_ref[part, :, :width].astype(f32) - coef * before_ref[0, part].astype(f32)
+        full[:, part * width : (part + 1) * width] = fixed.astype(bf16)
+    low = lax.dot_general(full[...], up_ref[0], contract_last, preferred_element_type=f32)
+    row_group = lax.broadcasted_iota(jnp.int32, low.shape, 0) // toks
+    col_group = lax.broadcasted_iota(jnp.int32, low.shape, 1) // rank
+    low = jnp.where(row_group == col_group, low, 0.0).astype(bf16)
+    total = low_rank_scale * lax.dot_general(
+        low, down_ref[0], (((1,), (0,)), ((), ())), preferred_element_type=f32
+    )
+    for piece in range(pieces):
+        for copy in copies[piece]:
+            copy.wait()
+        span = slice(piece * depth, (piece + 1) * depth)
+        total = total + lax.dot_general(
+            full[:, span], weight[span], (((1,), (0,)), ((), ())), preferred_element_type=f32
         )
-
-    @pl.when(step == pl.num_programs(0) - 1)
-    def _():
-        low = low_sc[...]
-        adapt = lax.dot_general(
-            low, down_ref[0], (((1,), (0,)), ((), ())), preferred_element_type=f32
-        )
-        normed_grad = ((frozen[...] + low_rank_scale * adapt) * gain_ref[...]).astype(bf16)
-        normed_grad = normed_grad.astype(f32)
-        inv = inv_ref[0]
-        grad_y = full[:, pl.ds(pl.multiple_of(ypos * width, 128), width)]
-        sent = (grad_y.astype(f32) + inv * normed_grad).astype(bf16)
-        coef = jnp.sum(normed_grad * x_ref[0].astype(f32), axis=1, keepdims=True)
-        coef = coef * (inv * inv * inv / width_all)
-        high = coef.astype(bf16).astype(f32)
-        lane = lax.broadcasted_iota(jnp.int32, (rows, TAIL), 1)
-        tail = jnp.where(lane == 0, high, jnp.where(lane == 1, coef - high, 0.0)).astype(bf16)
-        box_ref[:, :width] = sent
-        box_ref[:, width:] = tail
-        sent_ref[0] = sent
-        low_ref[0] = low
-        grad_ref[0] = grad_y
-        coef_ref[0] = jnp.where(lane == 0, coef, 0.0)
+    normed_grad = (total * gain_ref[...]).astype(bf16).astype(f32)
+    inv = inv_ref[0]
+    grad_y = full[:, pl.ds(pl.multiple_of(ypos * width, 128), width)]
+    sent = (grad_y.astype(f32) + inv * normed_grad).astype(bf16)
+    coef = jnp.sum(normed_grad * x_ref[0].astype(f32), axis=1, keepdims=True)
+    coef = coef * (inv * inv * inv / width_all)
+    lane = lax.broadcasted_iota(jnp.int32, (rows, TAIL), 1)
+    high = coef.astype(bf16).astype(f32)
+    tail = jnp.where(lane == 0, high, jnp.where(lane == 1, coef - high, 0.0)).astype(bf16)
+    box_ref[:, :width] = sent
+    box_ref[:, width:] = tail
+    sent_ref[0] = sent
+    low_ref[0] = low
+    grad_ref[0] = grad_y
+    coef_ref[0] = jnp.where(lane == 0, coef, 0.0)
 
 
 def run_stage(place, parts, before, up, down, gain, inv, x, own, other, kept):
-    sent_all, low_all, grad_all, coef_all = kept
     _, rows, width = x.shape
-    half, width_all = own.shape
+    width_all = own.shape[0]
     group = up.shape[1] // 16
-    block = 128
+    pieces = 5
 
     def whole(shape):
         return pl.BlockSpec(shape, lambda i, place: (0,) * len(shape))
@@ -136,14 +140,13 @@
         shape = array.shape[1:]
         return pl.BlockSpec((1,) + shape, lambda i, place: (place[0],) + (0,) * len(shape))
 
-    weight = pl.BlockSpec((block, width_all), lambda i, place: (i, 0))
     any_space = pl.BlockSpec(memory_space=pl.ANY)
-    keeps = [sent_all, low_all, grad_all, coef_all]
+    keeps = list(kept)
     return pl.pallas_call(
         functools.partial(stage_kernel, group=group),
         grid_spec=pltpu.PrefetchScalarGridSpec(
             num_scalar_prefetch=1,
-            grid=(half // block,),
+            grid=(1,),
             in_specs=[
                 whole(parts.shape),
                 chunk(before),
@@ -152,22 +155,20 @@
                 whole(gain.shape),
                 chunk(inv),
                 chunk(x),
-                weight,
-                weight,
             ]
-            + [any_space] * 4,
+            + [any_space] * 6,
             out_specs=[whole((rows, width + TAIL))] + [chunk(k) for k in keeps],
             scratch_shapes=[
                 pltpu.VMEM((rows, width_all), bf16),
-                pltpu.VMEM((rows, width), f32),
-                pltpu.VMEM((rows, up.shape[1]), bf16),
+                pltpu.VMEM((width_all, width), bf16),
+                pltpu.SemaphoreType.DMA((pieces, 2)),
             ],
         ),
         out_shape=[jax.ShapeDtypeStruct((rows, width + TAIL), bf16)]
         + [jax.ShapeDtypeStruct(k.shape, k.dtype) for k in keeps],
         input_output_aliases={10: 1, 11: 2, 12: 3, 13: 4},
         compiler_params=pltpu.CompilerParams(
-            dimension_semantics=("arbitrary",), vmem_limit_bytes=32 * 1024 * 1024
+            dimension_semantics=("arbitrary",), vmem_limit_bytes=40 * 1024 * 1024
         ),
         cost_estimate=pl.CostEstimate(
             flops=2 * rows * width * width_all, bytes_accessed=2 * width * width_all, transcendentals=0
@@ -200,7 +201,7 @@
     rows = group * toks
     multiplier = low_rank_scale / (toks * 2 * lax.axis_size("z"))
 
-    w_own = lax.all_gather(proj_weight[0], "z", axis=1, tiled=True)
+    w_own = lax.all_gather(proj_weight[0].T, "z", axis=0, tiled=True)
 
     x_full = section_inputs[0]
     x_mine = lax.dynamic_slice_in_dim(x_full, core * toks, toks, 1).reshape(rows_all, width_all)

time: 711 us -> 685 us (0.963)
  waiting for transfers between devices: 490 us -> 462 us
    ppermute x2, waiting for transfers between devices: 423 us -> 395 us  [step(): lax.ppermute(box, 's', ODD)]
  transfers between devices with their start and end apart: 12 -> 12, of which waited for: 4 -> 4; matrix products, arithmetic and copies ran while one was open for 2% -> 3% of each run, Pallas kernels for 0% -> 0%
where the time goes in v3:
time: 685 us; the launch traced here: 684 us
  waiting for transfers between devices  462 us (67%)
  blocking collectives  93.2 us (14%)
  starting transfers between devices  64.6 us (9%)
  local copies, waits for them, and re-layouts  19.8 us (3%)
  Pallas kernels  16.7 us (2%)
  between operations  14.5 us (2%)
  other arithmetic  7.89 us (1%)
    ppermute x2, waiting for transfers between devices, step(): lax.ppermute(box, 's', ODD)  395 us
    all_gather x1, waiting for transfers between devices, local(): w_own = lax.all_gather(proj_weight[0].T, 'z', axis=0, tiled=True)  60.3 us
    ppermute x2, starting transfers between devices, half_sum(): return mine + lax.ppermute(theirs, 'c', SWAP)  38.2 us
    all_gather x1, blocking collectives, local(): h_all = lax.all_gather(h_y, 'z')  32.5 us
    all_to_all x2, blocking collectives, spread(): return lax.all_to_all(sent, 'y', 0, 0)  16.9 us
    pallas_call x2, Pallas kernels, run_stage(): pl.pallas_call(functools.partial(stage_kernel, group=group), grid_spec=pl...  16.7 us
    psum x1, blocking collectives, local(): low_in = lax.psum(low_in, 'y').astype(bf16)  16.1 us
    all_gather x1, blocking collectives, local(): both = lax.all_gather(both, 'z').reshape(4, micro, toks, width + TAIL)  14.4 us
  transfers between devices with their start and end apart: 12, of which 4 were waited for; matrix products, arithmetic and copies ran while one was open for 3% of the time, Pallas kernels for 0%

profile of v3, /device:TPU:1, one launch (start us, length us, event | category | flops | bytes accessed | tf_op | source)
XLA Modules:
  0.0 684.0 jit_solution(5696633987075697036)
XLA Ops:
  7.2 3.7 copy.32
  10.9 0.6 copy-done.11
  11.6 8.8 %collective-permute-start.3 = (f32[1,640]{1,0:T(1,128)S(1)}, f32[1,640]{1,0:T(1,128)S(1)}, u32[]{:S(2)}, u32[]{:S(2)}) collective-permute-start(f32[1,640]{1,0:T(1,128)S(1)} %copy-done.11), channel_id=1, source_target_pairs={{0,4},{4,0},{1,5},{5,1},{2,6},{6,2},{3,7},{7,3},{8,12},{12,8},{9,1... | collective-permute-start | bytes 7688 | tf_op jit(solution)/shard_map/ppermute | solution.py:25
  20.4 1.9 collective-permute-start.4
  22.3 0.2 multiply_reduce_fusion
  22.6 0.2 select_reduce_fusion.2
  22.7 0.9 dynamic-slice_bitcast_fusion.1
  23.9 0.5 reshape.128
  24.4 1.1 pad.8
  25.5 0.6 gather_fusion.1
  26.2 1.0 multiply_convert_fusion
  27.3 1.3 collective-permute-start.2
  28.6 32.5 %all-gather.1 = bf16[256,1280]{1,0:T(8,128)(2,1)} all-gather(bf16[64,1280]{1,0:T(8,128)(2,1)S(1)} %get-tuple-element.742), channel_id=3, replica_groups=mesh['s'=16,'y'=4,'c'=2,'z'=4] {'z'}, dimensions={0}, use_global_device_ids=true | all-gather | bytes 819200 | tf_op jit(solution)/shard_map/all_gather | solution.py:227
  61.1 0.9 broadcast_in_dim.105
  62.0 4.2 all-to-all-start.1
  66.3 0.6 gather_fusion
  66.9 0.3 copy-done.6
  67.2 0.2 fusion.6
  67.4 16.1 %psum.7 = bf16[8,8,16]{2,1,0:T(8,128)(2,1)S(1)} all-reduce(f32[8,8,16]{2,1,0:T(8,128)S(1)} %fusion.6), channel_id=1, replica_groups=mesh['s'=16,'y'=4,'c'=2,'z'=4] {'y'}, use_global_device_ids=true, to_apply=%region_2.3 | all-reduce | flops 1024 | bytes 6144 | tf_op jit(solution)/shard_map/psum | solution.py:225
  83.5 13.3 %all-gather = bf16[32,8,16]{2,1,0:T(8,128)(2,1)} all-gather(bf16[8,8,16]{2,1,0:T(8,128)(2,1)S(1)} %psum.7), channel_id=2, replica_groups=mesh['s'=16,'y'=4,'c'=2,'z'=4] {'z'}, dimensions={0}, use_global_device_ids=true | all-gather | bytes 10240 | tf_op jit(solution)/shard_map/all_gather | solution.py:226
  96.8 60.3 %all-gather.5.cloned.1.call-done = bf16[5120,640]{1,0:T(8,128)(2,1)} async-done(((bf16[1280,640]{1,0:T(8,128)(2,1)}), bf16[5120,640]{1,0:T(8,128)(2,1)}) %all-gather.5.cloned.1.call-update) | async-done | bytes 6553616 | tf_op jit(solution)/shard_map/all_gather | solution.py:204
  157.1 2.4 collective-permute-start.5
  159.5 2.0 copy.33
  161.6 2.0 copy.34
  163.6 6.4 collective-permute-done.5
  170.0 0.6 broadcast_in_dim.102
  170.6 0.7 broadcast.80
  171.3 0.6 broadcast_in_dim.103
  171.9 438.2 %while.27 = (s32[]{:T(128)}, bf16[32,1408]{1,0:T(8,128)(2,1)}, bf16[2,32,1280]{2,1,0:T(8,128)(2,1)}, bf16[2,32,64]{2,1,0:T(8,128)(2,1)}, bf16[2,32,1280]{2,1,0:T...) while((s32[]{:T(128)}, bf16[32,1408]{1,0:T(8,128)(2,1)}, ...), condition=%wide.region_11.12_spmd, body=%wide.region_3.11_spmd.sunk | while | flops 419430432 | bytes 14820244 | solution.py:292
  175.3 384.3 %conditional.6 = (bf16[32,1408]{1,0:T(8,128)(2,1)}) conditional(s32[]{:T(128)} %clamp.15, bf16[32,1408]{1,0:T(8,128)(2,1)} %get-tuple-element.866, bf16[32,1408]{1,0:T(8,128)(2,1)} %get-tuple-element.866, bf16[32,1408]{1,0:T(8,128)(2,1)} %get-tuple-element.866), branch_computations={%region_8.8_spmd, %region_9.9_spmd, %region_10.10_spmd} | conditional | bytes 540720 | solution.py:272
  175.3 1.3 collective-permute-start
  176.6 382.3 %collective-permute-done = bf16[32,1408]{1,0:T(8,128)(2,1)S(1)} collective-permute-done((bf16[32,1408]{1,0:T(8,128)(2,1)}, bf16[32,1408]{1,0:T(8,128)(2,1)S(1)}, u32[]{:S(2)}, u32[]{:S(2)}) %collective-permute-start) | collective-permute-done | bytes 90144 | tf_op jit(solution)/shard_map/while/body/eval_jaxpr/cond/branch_1_fun/ppermute | solution.py:276
  558.9 0.6 copy.53
  559.6 17.8 %conditional.5 = ((bf16[2,32,1280]{2,1,0:T(8,128)(2,1)}, bf16[2,32,64]{2,1,0:T(8,128)(2,1)}, bf16[2,32,1280]{2,1,0:T(8,128)(2,1)S(1)}, f32[2,32,128]{2,1,0:T(8,128)S(1)}, bf16[32,1408]{1,0:T(8,128)(2,1)})) conditional(s32[]{:T(128)} %convert_element_type.56, (bf16[2,32,1280]{2,1,0:T(8,128)(2,1)}, bf16[2,32,64]{2,1,0:T(8,128)(2,1)}, ...), branch_computations={%region_4.4_spmd, %region_5.7_spmd} | conditional | flops 419430400 | bytes 14278766 | solution.py:269
  559.6 9.4 %conditional = (bf16[4,32,1408]{2,1,0:T(8,128)(2,1)S(1)}) conditional(s32[]{:T(128)} %convert_element_type.33, bf16[32,1408]{1,0:T(8,128)(2,1)} %get-tuple-element.562, (s32[]{:T(128)}, bf16[2,4,32,1408]{3,2,1,0:T(8,128)(2,1)}) %tuple.56), branch_computations={%region_6.5_spmd, %region_7.6_spmd} | conditional | flops 3 | bytes 1171464 | solution.py:252
  559.6 0.9 broadcast_in_dim.51
  560.6 8.4 %all_to_all.14 = bf16[4,32,1408]{2,1,0:T(8,128)(2,1)S(1)} all-to-all(bf16[4,32,1408]{2,1,0:T(8,128)(2,1)S(1)} %broadcast_in_dim.51), channel_id=1, replica_groups=mesh['s'=16,'y'=4,'c'=2,'z'=4] {'y'}, dimensions={0} | all-to-all | bytes 720896 | tf_op jit(solution)/shard_map/while/body/eval_jaxpr/cond/branch_1_fun/cond/branch_0_fun/all_to_all | solution.py:43
  569.0 8.3 %stage.1 = (bf16[32,1408]{1,0:T(8,128)(2,1)}, bf16[2,32,1280]{2,1,0:T(8,128)(2,1)}, bf16[2,32,64]{2,1,0:T(8,128)(2,1)}, bf16[2,32,1280]{2,1,0:T(8,128)(2,1)S(1)}, f32[2,32,128]{2,1,0:T(8,128)S(1)}) custom-call(s32[3]{0:T(128)S(1)} %pad_add_fusion.place_ref, ...), custom_call_target="tpu_custom_call", output_to_operand_aliasing={{1}: (10, {}), {2}: (11, {}), {3}: (12, {}), {4}: (13, {})} | custom-call | flops 419430400 | bytes 13107200 | tf_op jit(solution)/shard_map/while/body/eval_jaxpr/cond/branch_1_fun/stage/pallas_call | solution.py:145
  577.5 14.8 %conditional.6 = (bf16[32,1408]{1,0:T(8,128)(2,1)}) conditional(s32[]{:T(128)} %clamp.15, bf16[32,1408]{1,0:T(8,128)(2,1)} %get-tuple-element.866, bf16[32,1408]{1,0:T(8,128)(2,1)} %get-tuple-element.866, bf16[32,1408]{1,0:T(8,128)(2,1)} %get-tuple-element.866), branch_computations={%region_8.8_spmd, %region_9.9_spmd, %region_10.10_spmd} | conditional | bytes 540720 | solution.py:272
  577.5 1.3 collective-permute-start
  578.8 12.9 %collective-permute-done = bf16[32,1408]{1,0:T(8,128)(2,1)S(1)} collective-permute-done((bf16[32,1408]{1,0:T(8,128)(2,1)}, bf16[32,1408]{1,0:T(8,128)(2,1)S(1)}, u32[]{:S(2)}, u32[]{:S(2)}) %collective-permute-start) | collective-permute-done | bytes 90144 | tf_op jit(solution)/shard_map/while/body/eval_jaxpr/cond/branch_1_fun/ppermute | solution.py:276
  591.7 0.6 copy.53
  592.3 17.8 %conditional.5 = ((bf16[2,32,1280]{2,1,0:T(8,128)(2,1)}, bf16[2,32,64]{2,1,0:T(8,128)(2,1)}, bf16[2,32,1280]{2,1,0:T(8,128)(2,1)S(1)}, f32[2,32,128]{2,1,0:T(8,128)S(1)}, bf16[32,1408]{1,0:T(8,128)(2,1)})) conditional(s32[]{:T(128)} %convert_element_type.56, (bf16[2,32,1280]{2,1,0:T(8,128)(2,1)}, bf16[2,32,64]{2,1,0:T(8,128)(2,1)}, ...), branch_computations={%region_4.4_spmd, %region_5.7_spmd} | conditional | flops 419430400 | bytes 14278766 | solution.py:269
  592.4 9.4 %conditional = (bf16[4,32,1408]{2,1,0:T(8,128)(2,1)S(1)}) conditional(s32[]{:T(128)} %convert_element_type.33, bf16[32,1408]{1,0:T(8,128)(2,1)} %get-tuple-element.562, (s32[]{:T(128)}, bf16[2,4,32,1408]{3,2,1,0:T(8,128)(2,1)}) %tuple.56), branch_computations={%region_6.5_spmd, %region_7.6_spmd} | conditional | flops 3 | bytes 1171464 | solution.py:252
  592.4 0.9 broadcast_in_dim.51
  593.3 8.4 %all_to_all.14 = bf16[4,32,1408]{2,1,0:T(8,128)(2,1)S(1)} all-to-all(bf16[4,32,1408]{2,1,0:T(8,128)(2,1)S(1)} %broadcast_in_dim.51), channel_id=1, replica_groups=mesh['s'=16,'y'=4,'c'=2,'z'=4] {'y'}, dimensions={0} | all-to-all | bytes 720896 | tf_op jit(solution)/shard_map/while/body/eval_jaxpr/cond/branch_1_fun/cond/branch_0_fun/all_to_all | solution.py:43
  601.7 8.3 %stage.1 = (bf16[32,1408]{1,0:T(8,128)(2,1)}, bf16[2,32,1280]{2,1,0:T(8,128)(2,1)}, bf16[2,32,64]{2,1,0:T(8,128)(2,1)}, bf16[2,32,1280]{2,1,0:T(8,128)(2,1)S(1)}, f32[2,32,128]{2,1,0:T(8,128)S(1)}) custom-call(s32[3]{0:T(128)S(1)} %pad_add_fusion.place_ref, ...), custom_call_target="tpu_custom_call", output_to_operand_aliasing={{1}: (10, {}), {2}: (11, {}), {3}: (12, {}), {4}: (13, {})} | custom-call | flops 419430400 | bytes 13107200 | tf_op jit(solution)/shard_map/while/body/eval_jaxpr/cond/branch_1_fun/stage/pallas_call | solution.py:145
  610.1 0.7 broadcast_in_dim.109
  610.8 3.3 all-to-all-start.2
  614.1 0.7 fusion.5
  614.8 14.4 %all-gather.2 = bf16[256,1408]{1,0:T(8,128)(2,1)S(1)} all-gather(bf16[64,1408]{1,0:T(8,128)(2,1)S(1)} %fusion.5), channel_id=4, replica_groups=mesh['s'=16,'y'=4,'c'=2,'z'=4] {'z'}, dimensions={0}, use_global_device_ids=true | all-gather | bytes 901120 | tf_op jit(solution)/shard_map/all_gather | solution.py:312
  629.3 0.2 reshape.137
  629.5 0.4 reduce_sum.63
  629.8 0.3 copy-done.3
  630.2 1.4 fusion.1
  631.6 35.8 %collective-permute-start.7 = (f32[8,640,16]{1,2,0:T(8,128)S(1)}, f32[8,640,16]{1,2,0:T(8,128)}, u32[]{:S(2)}, u32[]{:S(2)}) collective-permute-start(f32[8,640,16]{1,2,0:T(8,128)S(1)} %slice_select_fusion.1), channel_id=1, source_target_pairs={{0,4},{4,0},{1,5},{5,1},{2,6},{6,2},{3,7},{7,3},{8,12},{12,8},{9,1... | collective-permute-start | bytes 983048 | tf_op jit(solution)/shard_map/ppermute | solution.py:38
  667.4 0.3 fusion
  667.8 1.0 subtract_convert_fusion
  668.9 1.9 collective-permute-start.6
  670.9 2.4 collective-permute-start.8
  673.3 0.7 maximum_bitcast_fusion
  674.0 1.0 select_add_fusion.1
  675.0 1.0 select_reduce_fusion.1
  676.1 1.0 select_reduce_fusion
  (122 shorter events, 1.9 us)
Async XLA Ops:
  7.2 18.3 %copy-start = (bf16[1,8,16,5120]{3,2,1,0:T(8,128)(2,1)S(1)}, bf16[1,8,16,5120]{3,2,1,0:T(8,128)(2,1)}, u32[]{:S(2)}) copy-start(bf16[1,8,16,5120]{3,2,1,0:T(8,128)(2,1)} %param.22) | copy-start | bytes 3932164
  7.2 149.9 %all-gather.5.cloned.1.call-start = ((), (), s32[]{:S(2)}) async-start(), calls=%async_computation.3 | async-start | bytes 8192000 | tf_op jit(solution)/shard_map/all_gather | solution.py:204
  10.9 0.7 copy-start.11
  10.9 9.5 %copy-start.10 = (bf16[1,8,640,16]{2,3,1,0:T(8,128)(2,1)S(1)}, bf16[1,8,640,16]{2,3,1,0:T(8,128)(2,1)}, u32[]{:S(2)}) copy-start(bf16[1,8,640,16]{2,3,1,0:T(8,128)(2,1)} %param.21) | copy-start | bytes 491524
  10.9 11.4 %copy-start.7 = (bf16[1,8,16,5120]{3,2,1,0:T(8,128)(2,1)S(1)}, bf16[1,8,16,5120]{3,2,1,0:T(8,128)(2,1)}, u32[]{:S(2)}) copy-start(bf16[1,8,16,5120]{3,2,1,0:T(8,128)(2,1)} %param.17) | copy-start | bytes 3932164
  10.9 11.7 %copy-start.12 = (s32[1,8]{1,0:T(1,128)S(1)}, s32[1,8]{1,0:T(1,128)}, u32[]{:S(2)}) copy-start(s32[1,8]{1,0:T(1,128)} %param.24) | copy-start | bytes 100
  10.9 11.7 %copy-start.13 = (s32[8]{0:T(128)S(1)}, s32[8]{0:T(128)}, u32[]{:S(2)}) copy-start(s32[8]{0:T(128)} %param.23) | copy-start | bytes 100
  11.6 14.6 %collective-permute-start.3 = (f32[1,640]{1,0:T(1,128)S(1)}, f32[1,640]{1,0:T(1,128)S(1)}, u32[]{:S(2)}, u32[]{:S(2)}) collective-permute-start(f32[1,640]{1,0:T(1,128)S(1)} %copy-done.11), channel_id=1, source_target_pairs={{0,4},{4,0},{1,5},{5,1},{2,6},{6,2},{3,7},{7,3},{8,12},{12,8},{9,1... | collective-permute-start | bytes 7688 | tf_op jit(solution)/shard_map/ppermute | solution.py:25
  20.4 45.8 %collective-permute-start.4 = (bf16[8,640,16]{1,2,0:T(8,128)(2,1)S(1)}, bf16[8,640,16]{1,2,0:T(8,128)(2,1)S(1)}, u32[]{:S(2)}, u32[]{:S(2)}) collective-permute-start(bf16[8,640,16]{1,2,0:T(8,128)(2,1)S(1)} %bitcast.72), channel_id=1, source_target_pairs={{0,4},{4,0},{1,5},{5,1},{2,6},{6,2},{3,7},{7,3},{8,12},{12,8},{9,1... | collective-permute-start | bytes 491528 | tf_op jit(solution)/shard_map/ppermute | solution.py:25
  22.3 1.4 copy-start.8
  27.2 34.8 %copy-start.1 = (bf16[64,1280]{1,0:T(8,128)(2,1)}, bf16[64,1280]{1,0:T(8,128)(2,1)S(1)}, u32[]{:S(2)}) copy-start(bf16[64,1280]{1,0:T(8,128)(2,1)S(1)} %get-tuple-element.743) | copy-start | bytes 491524
  27.2 34.8 %copy-start.5 = (bf16[64,1280]{1,0:T(8,128)(2,1)}, bf16[64,1280]{1,0:T(8,128)(2,1)S(1)}, u32[]{:S(2)}) copy-start(bf16[64,1280]{1,0:T(8,128)(2,1)S(1)} %get-tuple-element.742) | copy-start | bytes 491524
  27.3 33.8 %collective-permute-start.2 = (bf16[64,1280]{1,0:T(8,128)(2,1)S(1)}, bf16[64,1280]{1,0:T(8,128)(2,1)S(1)}, u32[]{:S(2)}, u32[]{:S(2)}) collective-permute-start(bf16[64,1280]{1,0:T(8,128)(2,1)S(1)} %get-tuple-element.743), channel_id=1, source_target_pairs={{480,448},{448,416},{416,384},{384,352},{352,320},{320,288},{288,2... | collective-permute-start | bytes 491528 | tf_op jit(solution)/shard_map/ppermute | solution.py:212
  62.0 34.7 %all-to-all-start.1 = ((bf16[4,64,1280]{2,1,0:T(8,128)(2,1)}), bf16[4,64,1280]{2,1,0:T(8,128)(2,1)}, u32[]{:S(2)}, u32[]{:S(2)}) async-start(bf16[4,64,1280]{2,1,0:T(8,128)(2,1)} %broadcast_in_dim.105), calls=%async_computation.1 | async-start | bytes 1310720 | tf_op jit(solution)/shard_map/all_to_all | solution.py:43
  66.3 0.9 copy-start.6
  157.1 12.9 %collective-permute-start.5 = (bf16[5120,640]{1,0:T(8,128)(2,1)}, bf16[5120,640]{1,0:T(8,128)(2,1)}, u32[]{:S(2)}, u32[]{:S(2)}) collective-permute-start(bf16[5120,640]{1,0:T(8,128)(2,1)} %all-gather.5.cloned.1.call-done), channel_id=1, source_target_pairs={{0,4},{4,0},{1,5},{5,1},{2,6},{6,2},{3,7},{7,3},{8,12},{12,8},{9,1... | collective-permute-start | bytes 19660808 | tf_op jit(solution)/shard_map/ppermute | solution.py:241
  175.3 383.6 %collective-permute-start = (bf16[32,1408]{1,0:T(8,128)(2,1)}, bf16[32,1408]{1,0:T(8,128)(2,1)S(1)}, u32[]{:S(2)}, u32[]{:S(2)}) collective-permute-start(bf16[32,1408]{1,0:T(8,128)(2,1)} %param.5), channel_id=1, source_target_pairs={{480,448},{416,384},{352,320},{288,256},{224,192},{160,128},{96,64... | collective-permute-start | bytes 270344 | tf_op jit(solution)/shard_map/while/body/eval_jaxpr/cond/branch_1_fun/ppermute | solution.py:276
  577.5 14.2 %collective-permute-start = (bf16[32,1408]{1,0:T(8,128)(2,1)}, bf16[32,1408]{1,0:T(8,128)(2,1)S(1)}, u32[]{:S(2)}, u32[]{:S(2)}) collective-permute-start(bf16[32,1408]{1,0:T(8,128)(2,1)} %param.5), channel_id=1, source_target_pairs={{480,448},{416,384},{352,320},{288,256},{224,192},{160,128},{96,64... | collective-permute-start | bytes 270344 | tf_op jit(solution)/shard_map/while/body/eval_jaxpr/cond/branch_1_fun/ppermute | solution.py:276
  610.8 56.9 %all-to-all-start.2 = ((f32[4,2,32,128]{3,2,1,0:T(8,128)}), f32[4,2,32,128]{3,2,1,0:T(8,128)S(1)}, u32[]{:S(2)}, u32[]{:S(2)}) async-start(f32[4,2,32,128]{3,2,1,0:T(8,128)} %broadcast_in_dim.109), calls=%async_computation.2 | async-start | bytes 262144 | tf_op jit(solution)/shard_map/all_to_all | solution.py:43
  629.3 0.9 copy-start.3
  629.5 37.9 %copy-start.9 = (bf16[32,8,16]{2,1,0:T(8,128)(2,1)S(1)}, bf16[32,8,16]{2,1,0:T(8,128)(2,1)}, u32[]{:S(2)}) copy-start(bf16[32,8,16]{2,1,0:T(8,128)(2,1)} %all-gather) | copy-start | bytes 24580
  631.5 35.9 %copy-start.4 = (bf16[256,1408]{1,0:T(8,128)(2,1)S(1)}, bf16[256,1408]{1,0:T(8,128)(2,1)}, u32[]{:S(2)}) copy-start(bf16[256,1408]{1,0:T(8,128)(2,1)} %copy-done.3) | copy-start | bytes 2162692
  631.6 36.3 %copy-start.2 = (bf16[2,32,1280]{2,1,0:T(8,128)(2,1)S(1)}, bf16[2,32,1280]{2,1,0:T(8,128)(2,1)}, u32[]{:S(2)}) copy-start(bf16[2,32,1280]{2,1,0:T(8,128)(2,1)} %get-tuple-element.958) | copy-start | bytes 491524
  631.6 42.4 %collective-permute-start.7 = (f32[8,640,16]{1,2,0:T(8,128)S(1)}, f32[8,640,16]{1,2,0:T(8,128)}, u32[]{:S(2)}, u32[]{:S(2)}) collective-permute-start(f32[8,640,16]{1,2,0:T(8,128)S(1)} %slice_select_fusion.1), channel_id=1, source_target_pairs={{0,4},{4,0},{1,5},{5,1},{2,6},{6,2},{3,7},{7,3},{8,12},{12,8},{9,1... | collective-permute-start | bytes 983048 | tf_op jit(solution)/shard_map/ppermute | solution.py:38
  668.9 4.4 collective-permute-start.6
  670.9 5.2 collective-permute-start.8
Sparse Core Ops, SparseCore 0:
  11.1 145.9 all-gather.4

commit v4 on v1

v4 whole, which is shorter than its diff:
```python
import functools

import jax
import jax.numpy as jnp
from jax import lax
from jax.experimental import pallas as pl
from jax.experimental.pallas import tpu as pltpu
from jax.sharding import Mesh, PartitionSpec as P

norm_eps = 1e-05
low_rank_scale = 2.0
CHUNKS = 2
TAIL = 128
SWAP = [(0, 1), (1, 0)]
ODD = [(s, s - 1) for s in range(15, 0, -2)]
EVEN = [(s, s - 1) for s in range(14, 0, -2)]
EVERY = [(s, s - 1) for s in range(15, 0, -1)]
f32 = jnp.float32
bf16 = jnp.bfloat16
contract_last = (((1,), (1,)), ((), ()))
contract_inner = (((1,), (0,)), ((), ()))
LATE = 13
RIGHT = [(4 * s + z, 4 * s + (z + 1) % 4) for s in range(LATE) for z in range(4)]
LEFT = [(4 * s + z, 4 * s + (z + 3) % 4) for s in range(LATE) for z in range(4)]
LATE_SWAP = [(2 * s + c, 2 * s + 1 - c) for s in range(LATE) for c in range(2)]


def both_cores(value, axis):
    core = lax.axis_index("c")
    other = lax.ppermute(value, "c", SWAP)
    low = jnp.where(core == 0, value, other)
    high = jnp.where(core == 0, other, value)
    return jnp.concatenate([low, high], axis)


def half_sum(value, axis):
    core = lax.axis_index("c")
    width = value.shape[axis] // 2
    low = lax.slice_in_dim(value, 0, width, axis=axis)
    high = lax.slice_in_dim(value, width, 2 * width, axis=axis)
    mine = jnp.where(core == 0, low, high)
    theirs = jnp.where(core == 0, high, low)
    return mine + lax.ppermute(theirs, "c", SWAP)


def spread(value):
    sent = jnp.broadcast_to(value[None], (4,) + value.shape)
    return lax.all_to_all(sent, "y", 0, 0)


def corrected(parts_ref, before_ref, part, coef):
    width = before_ref.shape[3]
    fixed = parts_ref[part, :, :width].astype(f32)
    return (fixed - coef * before_ref[part, 0].astype(f32)).astype(bf16)


def stat_total(parts_ref, width):
    tail = parts_ref[:, :, width:].astype(f32)
    return jnp.sum(jnp.sum(tail, axis=0), axis=1, keepdims=True)


def own_group(low, group):
    rows, cols = low.shape
    row_group = lax.broadcasted_iota(jnp.int32, low.shape, 0) // (rows // group)
    col_group = lax.broadcasted_iota(jnp.int32, low.shape, 1) // (cols // group)
    return jnp.where(row_group == col_group, low, 0.0).astype(bf16)


def adapted(low, down_ref):
    return low_rank_scale * lax.dot_general(
        low, down_ref[0], contract_inner, preferred_element_type=f32
    )


def finish(total, grad_y, gain_ref, inv_ref, x_ref, box_ref, sent_ref, coef_ref, width_all):
    rows, width = total.shape
    normed_grad = (total * gain_ref[...]).astype(bf16).astype(f32)
    inv = inv_ref[0]
    sent = (grad_y.astype(f32) + inv * normed_grad).astype(bf16)
    coef = jnp.sum(normed_grad * x_ref[0].astype(f32), axis=1, keepdims=True)
    coef = coef * (inv * inv * inv / width_all)
    lane = lax.broadcasted_iota(jnp.int32, (rows, TAIL), 1)
    high = coef.astype(bf16).astype(f32)
    tail = jnp.where(lane == 0, high, jnp.where(lane == 1, coef - high, 0.0)).astype(bf16)
    box_ref[:, :width] = sent
    box_ref[:, width:] = tail
    sent_ref[0] = sent
    coef_ref[0] = jnp.where(lane == 0, coef, 0.0)


def stage_kernel(place_ref, parts_ref, before_ref, up_ref, down_ref, gain_ref, inv_ref, x_ref, *refs, group):
    weights, refs = refs[:14], refs[14 + 4 :]
    box_ref, sent_ref, low_ref, grad_ref, coef_ref, full, weight, sems = refs
    ypos, core, zpos = place_ref[1], place_ref[2], place_ref[3]
    width = x_ref.shape[2]
    width_all = full.shape[1]
    half = width // 2
    copies = []
    for piece in range(7):
        pair = []
        for side, base in enumerate((core * half, (1 - core) * half)):
            ref = weights[side * 7 + piece]
            start = 0 if piece == 0 else width + (piece - 1) * half
            lanes = pl.ds(pl.multiple_of(base, 128), half)
            target = weight.at[pl.ds(start, ref.shape[0]), lanes]
            copy = pltpu.make_async_copy(ref, target, sems.at[piece, side])
            copy.start()
            pair.append(copy)
        copies.append(pair)

    coef = stat_total(parts_ref, width)
    low = None
    for part in range(4):
        fixed = corrected(parts_ref, before_ref, part, coef)
        first = 2 * lax.rem(zpos - part + 4, 4) * half
        second = (2 * lax.rem(part - zpos + 4, 4) + 1) * half
        full[:, pl.ds(pl.multiple_of(first, 128), half)] = fixed[:, :half]
        full[:, pl.ds(pl.multiple_of(second, 128), half)] = fixed[:, half:]

        @pl.when(part == ypos)
        def _(fixed=fixed):
            grad_ref[0] = fixed

        term = lax.dot_general(
            fixed,
            up_ref[0, :, part * width : (part + 1) * width],
            contract_last,
            preferred_element_type=f32,
        )
        low = term if low is None else low + term
    low = own_group(low, group)
    low_ref[0] = low
    total = adapted(low, down_ref)
    for part in range(4):
        for copy in copies[0] if part == 0 else copies[2 * part - 1] + copies[2 * part]:
            copy.wait()
        span = slice(part * width, (part + 1) * width)
        total = total + lax.dot_general(
            full[:, span], weight[span], contract_inner, preferred_element_type=f32
        )
    finish(
        total, grad_ref[0], gain_ref, inv_ref, x_ref, box_ref, sent_ref, coef_ref, width_all
    )


def correct_kernel(place_ref, parts_ref, before_ref, up_ref, low_in, grad_in, blocks_ref, low_ref, grad_ref, *, group):
    del low_in, grad_in
    width = before_ref.shape[3]
    coef = stat_total(parts_ref, width)
    low = None
    for part in range(4):
        fixed = corrected(parts_ref, before_ref, part, coef)
        blocks_ref[part] = fixed

        @pl.when(part == place_ref[1])
        def _(fixed=fixed):
            grad_ref[0] = fixed

        term = lax.dot_general(
            fixed,
            up_ref[0, :, part * width : (part + 1) * width],
            contract_last,
            preferred_element_type=f32,
        )
        low = term if low is None else low + term
    low_ref[0] = own_group(low, group)


def product_kernel(place_ref, rows_ref, own_ref, other_ref, out_ref):
    core = place_ref[2]
    half = own_ref.shape[1]
    for ref, base in ((own_ref, core * half), (other_ref, (1 - core) * half)):
        out = lax.dot_general(rows_ref[...], ref[...], contract_inner, preferred_element_type=f32)
        out_ref[:, pl.ds(pl.multiple_of(base, 128), half)] = out.astype(bf16)


def finish_kernel(
    place_ref,
    terms_ref,
    low_ref,
    grad_ref,
    down_ref,
    gain_ref,
    inv_ref,
    x_ref,
    sent_in,
    coef_in,
    box_ref,
    sent_ref,
    coef_ref,
):
    del place_ref, sent_in, coef_in
    total = adapted(low_ref[0], down_ref)
    for part in range(4):
        total = total + terms_ref[part].astype(f32)
    width_all = 4 * total.shape[1]
    finish(
        total, grad_ref[0], gain_ref, inv_ref, x_ref, box_ref, sent_ref, coef_ref, width_all
    )


def whole(array):
    shape = array.shape
    return pl.BlockSpec(shape, lambda i, place: (0,) * len(shape))


def chunk(array):
    shape = array.shape[1:]
    return pl.BlockSpec((1,) + shape, lambda i, place: (place[0],) + (0,) * len(shape))


def second_chunk(array):
    shape = array.shape
    block = (shape[0], 1) + shape[2:]
    return pl.BlockSpec(block, lambda i, place: (0, place[0]) + (0,) * (len(shape) - 2))


any_space = pl.BlockSpec(memory_space=pl.ANY)


def call(kernel, place, inputs, keeps, outs, scratch, limit, flops, name):
    arrays = [a for a, _ in inputs]
    return pl.pallas_call(
        kernel,
        grid_spec=pltpu.PrefetchScalarGridSpec(
            num_scalar_prefetch=1,
            grid=(1,),
            in_specs=[spec for _, spec in inputs] + [any_space] * len(keeps),
            out_specs=[whole(o) for o in outs] + [chunk(k) for k in keeps],
            scratch_shapes=scratch,
        ),
        out_shape=list(outs) + [jax.ShapeDtypeStruct(k.shape, k.dtype) for k in keeps],
        input_output_aliases={1 + len(arrays) + i: len(outs) + i for i in range(len(keeps))},
        compiler_params=pltpu.CompilerParams(
            dimension_semantics=("arbitrary",), vmem_limit_bytes=limit * 1024 * 1024
        ),
        cost_estimate=pl.CostEstimate(
            flops=flops, bytes_accessed=sum(a.size * a.dtype.itemsize for a in arrays), transcendentals=0
        ),
        name=name,
    )(place, *arrays, *keeps)


def local(
    section_inputs,
    out_grads,
    proj_weight,
    norm_gain,
    adapter_down,
    adapter_up,
    tenant_ids,
    slot_table,
):
    sec = lax.axis_index("s")
    ypos = lax.axis_index("y")
    core = lax.axis_index("c")
    micro = section_inputs.shape[1]
    width_all = section_inputs.shape[3]
    half = proj_weight.shape[1]
    width = 2 * half
    toks = section_inputs.shape[2] // 2
    rank = adapter_down.shape[3]
    rows_all = micro * toks
    group = micro // CHUNKS
    rows = group * toks
    multiplier = low_rank_scale / (toks * 2 * lax.axis_size("z"))

    zpos = lax.axis_index("z")
    shard = proj_weight[0].T
    first, second = shard[:half], shard[half:]
    right_1 = lax.ppermute(first, ("s", "z"), RIGHT)
    left_1 = lax.ppermute(second, ("s", "z"), LEFT)
    shard_x = lax.ppermute(shard, "c", SWAP)

    x_full = section_inputs[0]
    x_mine = lax.dynamic_slice_in_dim(x_full, core * toks, toks, 1).reshape(rows_all, width_all)
    x_f = x_mine.astype(f32)
    inv_rms = lax.rsqrt(jnp.mean(x_f * x_f, axis=-1, keepdims=True) + norm_eps)
    x_y = lax.dynamic_slice_in_dim(x_mine, ypos * width, width, 1)
    normed_y = x_y.astype(f32) * inv_rms
    x_before = lax.cond(
        sec == 15,
        lambda x: jnp.zeros((4,) + x.shape, x.dtype),
        spread,
        lax.ppermute(x_y, "s", EVERY),
    )
    gain_y = both_cores(norm_gain, 1)
    down_y = both_cores(adapter_down[0], 1)
    h_y = (normed_y * gain_y).astype(bf16)

    iota = jnp.arange(micro, dtype=jnp.int32)
    tenant_hot = tenant_ids[:, None] == iota[None, :]
    slot_ids = jnp.sum(jnp.where(tenant_hot, slot_table[0][None, :], 0), axis=1)
    down_sel = down_y[slot_ids]
    up_sel = adapter_up[0][slot_ids]
    low_part = jnp.einsum(
        "mtd,mdr->mtr", h_y.reshape(micro, toks, width), down_sel, preferred_element_type=f32
    )

    def low_in_of(part):
        return lax.all_gather(lax.psum(part, "y").astype(bf16), "z")

    x_before = x_before.reshape(4, CHUNKS, rows, width)
    x_chunk = x_y.reshape(CHUNKS, rows, width)
    inv_chunk = inv_rms.reshape(CHUNKS, rows, 1)
    down_chunk = down_sel.transpose(0, 2, 1).reshape(CHUNKS, group * rank, width)
    up_chunk = up_sel.reshape(CHUNKS, group * rank, width_all)
    grads_top = lax.dynamic_slice_in_dim(out_grads, core * toks, toks, 1)
    grads_top = grads_top.reshape(CHUNKS, rows, width_all)

    ready = (shard_x, x_before, x_chunk, inv_chunk, down_chunk, up_chunk, gain_y, grads_top)
    right_1, left_1, ready = lax.optimization_barrier((right_1, left_1, ready))
    shard_x, x_before, x_chunk, inv_chunk, down_chunk, up_chunk, gain_y, grads_top = ready

    def around(args):
        right_1, left_1, h_y, low_part = args

        def swapped(value):
            return lax.ppermute(value, ("s", "c"), LATE_SWAP)

        right_2 = lax.ppermute(right_1, ("s", "z"), RIGHT)
        left_2 = lax.ppermute(left_1, ("s", "z"), LEFT)
        other_1 = (swapped(right_1), swapped(left_1))
        h_all = lax.all_gather(h_y, "z")
        right_2, left_2, other_1, h_all = lax.optimization_barrier(
            (right_2, left_2, other_1, h_all)
        )
        right_3 = lax.ppermute(right_2, ("s", "z"), RIGHT)
        left_3 = lax.ppermute(left_2, ("s", "z"), LEFT)
        other_2 = (swapped(right_2), swapped(left_2))
        low_in_all = low_in_of(low_part)
        right_3, left_3, other_2, low_in_all = lax.optimization_barrier(
            (right_3, left_3, other_2, low_in_all)
        )
        other_3 = (swapped(right_3), swapped(left_3))
        return (right_2, left_2, right_3, left_3) + other_1 + other_2 + other_3, (h_all, low_in_all)

    def alone(args):
        shapes = jax.eval_shape(around, args)
        return jax.tree.map(lambda a: jnp.zeros(a.shape, a.dtype), shapes)

    moved, extras = lax.cond(sec < LATE, around, alone, (right_1, left_1, h_y, low_part))
    mine = [shard, right_1, left_1, *moved[:4]]
    theirs = [shard_x, *moved[4:]]

    def pick(array, m):
        return lax.dynamic_index_in_dim(array, m, 0, keepdims=False)

    def step(u, state):
        t, m = u // CHUNKS, u % CHUNKS
        turn = 15 - t + m

        place = jnp.stack([m, ypos, core, zpos]).astype(jnp.int32)
        box_shape = jax.ShapeDtypeStruct((rows, width + TAIL), bf16)

        def top(box):
            grad = pick(grads_top, m).reshape(rows, 4, width).transpose(1, 0, 2)
            return jnp.pad(grad, ((0, 0), (0, 0), (0, TAIL)))

        def with_all(args):
            parts, kept = args
            inputs = [
                (parts, whole(parts)),
                (x_before, second_chunk(x_before)),
                (up_chunk, chunk(up_chunk)),
                (down_chunk, chunk(down_chunk)),
                (gain_y, whole(gain_y)),
                (inv_chunk, chunk(inv_chunk)),
                (x_chunk, chunk(x_chunk)),
            ] + [(w, any_space) for w in mine + theirs]
            scratch = [
                pltpu.VMEM((rows, width_all), bf16),
                pltpu.VMEM((width_all, width), bf16),
                pltpu.SemaphoreType.DMA((7, 2)),
            ]
            box, *kept = call(
                functools.partial(stage_kernel, group=group),
                place,
                inputs,
                list(kept),
                [box_shape],
                scratch,
                40,
                2 * rows * width * width_all,
                "stage",
            )
            return box, tuple(kept)

        def with_shard(args):
            parts, (sent_all, low_all, grad_all, coef_all) = args
            inputs = [
                (parts, whole(parts)),
                (x_before, second_chunk(x_before)),
                (up_chunk, chunk(up_chunk)),
            ]
            blocks, low_all, grad_all = call(
                functools.partial(correct_kernel, group=group),
                place,
                inputs,
                [low_all, grad_all],
                [jax.ShapeDtypeStruct((4, rows, width), bf16)],
                [],
                16,
                2 * rows * width_all * rank * group,
                "correct",
            )
            blocks = lax.all_to_all(blocks, "z", 0, 0).reshape(4 * rows, width)
            inputs = [(blocks, whole(blocks)), (shard, whole(shard)), (shard_x, whole(shard_x))]
            (terms,) = call(
                product_kernel,
                place,
                inputs,
                [],
                [jax.ShapeDtypeStruct((4 * rows, width), bf16)],
                [],
                24,
                8 * rows * width * width,
                "product",
            )
            terms = lax.all_to_all(terms.reshape(4, rows, width), "z", 0, 0)
            inputs = [
                (terms, whole(terms)),
                (low_all, chunk(low_all)),
                (grad_all, chunk(grad_all)),
                (down_chunk, chunk(down_chunk)),
                (gain_y, whole(gain_y)),
                (inv_chunk, chunk(inv_chunk)),
                (x_chunk, chunk(x_chunk)),
            ]
            box, sent_all, coef_all = call(
                finish_kernel,
                place,
                inputs,
                [sent_all, coef_all],
                [box_shape],
                [],
                16,
                2 * rows * width * rank * group,
                "finish",
            )
            return box, (sent_all, low_all, grad_all, coef_all)

        def work(state):
            box, kept = state
            parts = lax.cond(sec == 15, top, spread, box)
            return lax.cond(sec < LATE, with_all, with_shard, (parts, kept))

        box, kept = lax.cond(sec == turn, work, lambda state: state, state)
        part = ((sec == turn) | (sec == turn - 1)) & (turn >= 1) & (turn <= 15)
        kind = jnp.where(part, jnp.where(turn % 2 == 1, 1, 2), 0)
        box = lax.switch(
            kind,
            [
                lambda box: box,
                lambda box: lax.ppermute(box, "s", ODD),
                lambda box: lax.ppermute(box, "s", EVEN),
            ],
            box,
        )
        return box, kept

    start = (
        jnp.zeros((rows, width + TAIL), bf16),
        (
            jnp.zeros((CHUNKS, rows, width), bf16),
            jnp.zeros((CHUNKS, rows, group * rank), bf16),
            jnp.zeros((CHUNKS, rows, width), bf16),
            jnp.zeros((CHUNKS, rows, TAIL), f32),
        ),
    )
    _, kept = lax.fori_loop(0, 15 * CHUNKS + 2 * CHUNKS, step, start)
    sent_all, low_all, grad_all, coef_all = kept

    h_all, low_in_all = lax.cond(
        sec < LATE,
        lambda args: args[0],
        lambda args: (lax.all_gather(args[1], "z"), low_in_of(args[2])),
        (extras, h_y, low_part),
    )
    coef_sum = jnp.sum(spread(coef_all), axis=(0, -1))[..., None]
    new_grads = sent_all.astype(f32) - coef_sum * x_chunk.astype(f32)
    new_grads = new_grads.astype(bf16).reshape(micro, toks, width)
    keep = jnp.where(core == 0, new_grads[:, :, :half], new_grads[:, :, half:])
    give = jnp.where(core == 0, new_grads[:, :, half:], new_grads[:, :, :half])
    got = lax.ppermute(give, "c", SWAP)
    kept = jnp.concatenate(
        [jnp.where(core == 0, keep, got), jnp.where(core == 0, got, keep)], 1
    )

    both = jnp.concatenate(
        [
            grad_all.reshape(rows_all, width),
            jnp.pad(low_all.reshape(rows_all, group * rank), ((0, 0), (0, TAIL - group * rank))),
        ],
        1,
    )
    both = lax.all_gather(both, "z").reshape(4, micro, toks, width + TAIL)
    grads_z = both[..., :width]
    low_z = both[..., width : width + group * rank].reshape(4, micro, toks, group, rank)
    low_z = jnp.sum(low_z.astype(f32), axis=3).astype(bf16)
    hidden_z = h_all.reshape(4, micro, toks, width)
    down_part = multiplier * jnp.einsum(
        "zmtd,zmtr->mdr", hidden_z, low_z, preferred_element_type=f32
    )
    up_part = multiplier * jnp.einsum(
        "zmtr,zmtd->mrd", low_in_all, grads_z, preferred_element_type=f32
    )
    down_acc = half_sum(down_part, 1)
    up_acc = half_sum(up_part, 2)
    slot_hot = slot_ids[None, :] == iota[:, None]
    down_out = jnp.sum(jnp.where(slot_hot[:, :, None, None], down_acc[None], 0.0), axis=1)
    up_out = jnp.sum(jnp.where(slot_hot[:, :, None, None], up_acc[None], 0.0), axis=1)
    return (kept[None], down_out[None], up_out[None])


def solution(mesh):
    fine = Mesh(mesh.devices.reshape(16, 4, 2, 4), ("s", "y", "c", "z"))
    mp = ("y", "c")
    placed = (
        P("s", None, "z", None),
        P(None, "z", None),
        P("s", mp, "z"),
        P("s", mp),
        P("s", None, mp, None),
        P("s", None, None, None),
        P(),
        P("s", None),
    )
    return jax.shard_map(
        local,
        mesh=fine,
        in_specs=placed,
        out_specs=(
            P("s", None, "z", mp),
            P("s", None, mp, None),
            P("s", None, None, mp),
        ),
        check_vma=False,
    )
```

time: 809 us -> 700 us (0.87)
  waiting for transfers between devices: 612 us -> 409 us
  blocking collectives: 62.1 us -> 110 us
  starting transfers between devices: 74.3 us -> 121 us
  matrix products: 23.7 us -> 3.9 us
  Pallas kernels: 0 us -> 15.6 us
  between operations: 14.3 us -> 1 us
  local copies, waits for them, and re-layouts: 9.84 us -> 22.3 us
    all_gather x1 -> x0, waiting for transfers between devices: 136 us -> none  [local(): w_own = lax.all_gather(proj_weight[0], 'z', axis=1, tiled=True)]
    ppermute x4 -> x16, starting transfers between devices: 6.45 us -> 74.8 us  [the longest x1 30 us: around(): right_2 = lax.ppermute(right_1, ('s', 'z'), RIGHT)]
    ppermute x4 -> x16, waiting for transfers between devices: 457 us -> 406 us  [the longest x2 391 us: step(): lax.ppermute(box, 's', ODD)]
    all_to_all x0 -> x3, blocking collectives: none -> 29.3 us  [spread(): return lax.all_to_all(sent, 'y', 0, 0)]
    dot_general x8 -> x0, matrix products: 22.9 us -> none  [the longest x2 9.79 us: stage(): lax.dot_general(grad, w_own, contract_last, preferred_element_type=f32)]
    ppermute x2, starting transfers between devices: 50.7 us -> 29.5 us  [half_sum(): return mine + lax.ppermute(theirs, 'c', SWAP)]
    all_gather x2, blocking collectives: 35.3 us -> 54.5 us  [the longest x1 37.8 us: around(): h_all = lax.all_gather(h_y, 'z')]
    all_to_all x3 -> x1, waiting for transfers between devices: 19 us -> 3.34 us  [spread(): return lax.all_to_all(sent, 'y', 0, 0)]
  transfers between devices with their start and end apart: 13 -> 22, of which waited for: 6 -> 7; matrix products, arithmetic and copies ran while one was open for 1% -> 3% of each run, Pallas kernels for 0% -> 0%
where the time goes in v4:
time: 700 us; the launch traced here: 698 us
  waiting for transfers between devices  409 us (58%)
  starting transfers between devices  121 us (17%)
  blocking collectives  110 us (16%)
  local copies, waits for them, and re-layouts  22.3 us (3%)
  Pallas kernels  15.6 us (2%)
  other arithmetic  12.1 us (2%)
    ppermute x2, waiting for transfers between devices, step(): lax.ppermute(box, 's', ODD)  391 us
    all_gather x1, blocking collectives, around(): h_all = lax.all_gather(h_y, 'z')  37.8 us
    ppermute x1, starting transfers between devices, around(): right_2 = lax.ppermute(right_1, ('s', 'z'), RIGHT)  30 us
    ppermute x2, starting transfers between devices, half_sum(): return mine + lax.ppermute(theirs, 'c', SWAP)  29.5 us
    all_to_all x3, blocking collectives, spread(): return lax.all_to_all(sent, 'y', 0, 0)  29.3 us
    ppermute x6, starting transfers between devices, swapped(): return lax.ppermute(value, ('s', 'c'), LATE_SWAP)  22.4 us
    all_gather x1, blocking collectives, low_in_of(): return lax.all_gather(lax.psum(part, 'y').astype(bf16), 'z')  16.7 us
    pallas_call x2, Pallas kernels, call(): pl.pallas_call(kernel, grid_spec=pltpu.PrefetchScalarGridSpec(num_scalar_...  15.6 us
  transfers between devices with their start and end apart: 22, of which 7 were waited for; matrix products, arithmetic and copies ran while one was open for 3% of the time, Pallas kernels for 0%

profile of v4, /device:TPU:1, one launch (start us, length us, event | category | flops | bytes accessed | tf_op | source)
XLA Modules:
  0.0 698.2 jit_solution(534815742262812274)
XLA Ops:
  0.6 8.9 %collective-permute-start.17 = (f32[1,640]{1,0:T(1,128)}, f32[1,640]{1,0:T(1,128)S(1)}, u32[]{:S(2)}, u32[]{:S(2)}) collective-permute-start(f32[1,640]{1,0:T(1,128)} %param.28), channel_id=1, source_target_pairs={{0,4},{4,0},{1,5},{5,1},{2,6},{6,2},{3,7},{7,3},{8,12},{12,8},{9,1... | collective-permute-start | bytes 7688 | tf_op jit(solution)/shard_map/ppermute | solution.py:30
  9.6 1.9 collective-permute-start.16
  11.5 2.9 copy.43
  14.4 2.4 collective-permute-start.14
  16.8 1.4 fusion.9
  18.2 1.9 collective-permute-start.12
  20.1 5.2 collective-permute-start.13
  25.3 1.4 multiply_reduce_fusion
  26.7 2.0 dynamic-slice_bitcast_fusion
  30.0 1.7 gather_fusion.1
  31.7 1.7 multiply_convert_fusion
  33.4 1.3 collective-permute-start.15
  35.5 1.5 gather_fusion
  37.1 1.1 fusion.5
  38.2 6.4 collective-permute-done.15
  44.5 13.4 %conditional.7 = (bf16[4,2,32,1280]{3,2,1,0:T(8,128)(2,1)}) conditional(s32[]{:T(128)} %convert_element_type.55, bf16[64,1280]{1,0:T(8,128)(2,1)} %collective-permute-done.15, () %tuple.100), branch_computations={%region_0.0_spmd, %region_1.0_spmd} | conditional | bytes 2129928 | solution.py:281
  44.5 1.0 broadcast_in_dim.55
  45.5 12.4 %all_to_all.21 = bf16[4,64,1280]{2,1,0:T(8,128)(2,1)} all-to-all(bf16[4,64,1280]{2,1,0:T(8,128)(2,1)S(1)} %broadcast_in_dim.55), channel_id=1, replica_groups=mesh['s'=16,'y'=4,'c'=2,'z'=4] {'y'}, dimensions={0} | all-to-all | bytes 1310720 | tf_op jit(solution)/shard_map/cond/branch_0_fun/all_to_all | solution.py:48
  58.0 5.6 collective-permute-done.13
  63.7 132.0 %conditional.8 = (bf16[640,640]{1,0:T(8,128)(2,1)}, bf16[640,640]{1,0:T(8,128)(2,1)}, bf16[640,640]{1,0:T(8,128)(2,1)}, bf16[640,640]{1,0:T(8,128)(2,1)}, bf16[6...) conditional(s32[]{:T(128)} %convert_element_type.57, () %tuple.102, ...), branch_computations={%region_4.5_spmd, %region_5.7_spmd} | conditional | flops 1024 | bytes 33604080 | solution.py:342
  63.7 30.0 %collective-permute-start = (bf16[640,640]{1,0:T(8,128)(2,1)}, bf16[640,640]{1,0:T(8,128)(2,1)}, u32[]{:S(2)}, u32[]{:S(2)}) collective-permute-start(bf16[640,640]{1,0:T(8,128)(2,1)} %get-tuple-element.981), channel_id=1, source_target_pairs={{0,1},{1,2},{2,3},{3,0},{32,33},{33,34},{34,35},{35,32},{64,65},{6... | collective-permute-start | bytes 2457608 | tf_op jit(solution)/shard_map/cond/branch_1_fun/ppermute | solution.py:321
  93.7 1.9 collective-permute-start.1
  95.6 4.1 collective-permute-start.2
  99.7 1.9 collective-permute-start.3
  101.6 37.8 %all-gather = bf16[256,1280]{1,0:T(8,128)(2,1)} all-gather(bf16[64,1280]{1,0:T(8,128)(2,1)S(1)} %get-tuple-element.983), channel_id=2, replica_groups=mesh['s'=16,'y'=4,'c'=2,'z'=4] {'z'}, dimensions={0}, use_global_device_ids=true | all-gather | bytes 819200 | tf_op jit(solution)/shard_map/cond/branch_1_fun/all_gather | solution.py:324
  139.5 2.2 collective-permute-start.4
  141.7 4.9 collective-permute-start.5
  146.6 8.2 %collective-permute-start.6 = (bf16[640,640]{1,0:T(8,128)(2,1)}, bf16[640,640]{1,0:T(8,128)(2,1)}, u32[]{:S(2)}, u32[]{:S(2)}) collective-permute-start(bf16[640,640]{1,0:T(8,128)(2,1)} %collective-permute-done), channel_id=1, source_target_pairs={{0,4},{4,0},{32,36},{36,32},{64,68},{68,64},{96,100},{100,96},{128... | collective-permute-start | bytes 2457608 | tf_op jit(solution)/shard_map/cond/branch_1_fun/ppermute | solution.py:319
  154.8 1.9 collective-permute-start.7
  156.8 13.3 %psum.12 = bf16[8,8,16]{2,1,0:T(8,128)(2,1)S(1)} all-reduce(f32[8,8,16]{2,1,0:T(8,128)S(1)} %get-tuple-element.986), channel_id=1, replica_groups=mesh['s'=16,'y'=4,'c'=2,'z'=4] {'y'}, use_global_device_ids=true, to_apply=%region_6.6 | all-reduce | flops 1024 | bytes 6144 | tf_op jit(solution)/shard_map/cond/branch_1_fun/psum | solution.py:301
  170.1 16.7 %all-gather.1 = bf16[32,8,16]{2,1,0:T(8,128)(2,1)S(1)} all-gather(bf16[8,8,16]{2,1,0:T(8,128)(2,1)S(1)} %psum.12), channel_id=3, replica_groups=mesh['s'=16,'y'=4,'c'=2,'z'=4] {'z'}, dimensions={0}, use_global_device_ids=true | all-gather | bytes 10240 | tf_op jit(solution)/shard_map/cond/branch_1_fun/all_gather | solution.py:301
  186.8 4.3 collective-permute-start.8
  191.1 1.9 collective-permute-start.9
  193.4 2.3 collective-permute-done.9
  197.7 438.7 %while.27 = (s32[]{:T(128)}, bf16[32,1408]{1,0:T(8,128)(2,1)}, bf16[2,32,1280]{2,1,0:T(8,128)(2,1)}, bf16[2,32,64]{2,1,0:T(8,128)(2,1)S(1)}, bf16[2,32,1280]{2,1...) while((s32[]{:T(128)}, bf16[32,1408]{1,0:T(8,128)(2,1)}, ...), condition=%wide.region_17.18_spmd, body=%wide.region_7.17_spmd.sunk | while | flops 445644864 | bytes 19192528 | solution.py:471
  202.1 364.5 %conditional.13 = (bf16[32,1408]{1,0:T(8,128)(2,1)}) conditional(s32[]{:T(128)} %clamp.15, bf16[32,1408]{1,0:T(8,128)(2,1)} %get-tuple-element.1727, bf16[32,1408]{1,0:T(8,128)(2,1)} %get-tuple-element.1727, bf16[32,1408]{1,0:T(8,128)(2,1)} %get-tuple-element.1727), branch_computations={%region_14.14_spmd, %region_15.15_spmd, %region_16.16_spmd} | conditional | bytes 540720 | solution.py:451
  202.1 1.3 collective-permute-start.10
  203.4 362.5 %collective-permute-done.10 = bf16[32,1408]{1,0:T(8,128)(2,1)S(1)} collective-permute-done((bf16[32,1408]{1,0:T(8,128)(2,1)}, bf16[32,1408]{1,0:T(8,128)(2,1)S(1)}, u32[]{:S(2)}, u32[]{:S(2)}) %collective-permute-start.10) | collective-permute-done | bytes 90144 | tf_op jit(solution)/shard_map/while/body/eval_jaxpr/cond/branch_1_fun/ppermute | solution.py:455
  566.7 19.1 %conditional.12 = ((bf16[2,32,1280]{2,1,0:T(8,128)(2,1)}, bf16[2,32,64]{2,1,0:T(8,128)(2,1)S(1)}, bf16[2,32,1280]{2,1,0:T(8,128)(2,1)S(1)}, f32[2,32,128]{2,1,0:T(8,128)S(1)}, bf16[32,1408]{1,0:T(8,128)(2,1)})) conditional(s32[]{:T(128)} %convert_element_type.70, (bf16[2,32,1280]{2,1,0:T(8,128)(2,1)}, bf16[2,32,64]{2,1,0:T(8,128)(2,1)S(1)}, ...), branch_computations={%region_8.8_spmd, %region_9.13_spmd} | conditional | flops 445644800 | bytes 18650836 | solution.py:448
  566.7 10.3 %conditional = (bf16[4,32,1408]{2,0,1:T(4,128)(2,1)}) conditional(s32[]{:T(128)} %convert_element_type.44, bf16[32,1408]{1,0:T(8,128)(2,1)} %get-tuple-element.1045, (s32[]{:T(128)}, bf16[2,32,5120]{2,1,0:T(8,128)(2,1)}) %tuple.82), branch_computations={%region_10.9_spmd, %region_11.10_spmd} | conditional | flops 3 | bytes 1998896 | solution.py:445
  567.7 8.4 %all_to_all.22 = bf16[4,32,1408]{2,1,0:T(8,128)(2,1)S(1)} all-to-all(bf16[4,32,1408]{2,1,0:T(8,128)(2,1)S(1)} %broadcast_in_dim.56), channel_id=1, replica_groups=mesh['s'=16,'y'=4,'c'=2,'z'=4] {'y'}, dimensions={0} | all-to-all | bytes 720896 | tf_op jit(solution)/shard_map/while/body/eval_jaxpr/cond/branch_1_fun/cond/branch_0_fun/all_to_all | solution.py:48
  577.0 8.8 %conditional.1 = ((bf16[32,1408]{1,0:T(8,128)(2,1)}, bf16[2,32,1280]{2,1,0:T(8,128)(2,1)}, bf16[2,32,64]{2,1,0:T(8,128)(2,1)S(1)}, bf16[2,32,1280]{2,1,0:T(8,128)(2,1)S(1)}, f32[2,32,128]{2,1,0:T(8,128)S(1)})) conditional(s32[]{:T(128)} %convert_element_type.43, (s32[4]{0:T(128)S(1)}, bf16[4,32,1408]{2,0,1:T(4,128)(2,1)}, ...), branch_computations={%region_12.11_spmd, %region_13.12_spmd} | conditional | flops 445644800 | bytes 16651528 | solution.py:446
  577.0 1.0 copy.42.parts_ref
  578.1 7.8 %stage.1 = (bf16[32,1408]{1,0:T(8,128)(2,1)}, bf16[2,32,1280]{2,1,0:T(8,128)(2,1)}, bf16[2,32,64]{2,1,0:T(8,128)(2,1)S(1)}, bf16[2,32,1280]{2,1,0:T(8,128)(2,1)S(1)}, f32[2,32,128]{2,1,0:T(8,128)S(1)}) custom-call(s32[4]{0:T(128)S(1)} %get-tuple-element.1017.place_ref, ...), custom_call_target="tpu_custom_call", output_to_operand_aliasing={{1}: (22, {}), {2}: (23, {}), {3}: (24, {}), {4}: (25, {})} | custom-call | flops 419430400 | bytes 15930624 | tf_op jit(solution)/shard_map/while/body/eval_jaxpr/cond/branch_1_fun/cond/branch_1_fun/stage/pallas_call | solution.py:223
  586.1 30.9 %conditional.13 = (bf16[32,1408]{1,0:T(8,128)(2,1)}) conditional(s32[]{:T(128)} %clamp.15, bf16[32,1408]{1,0:T(8,128)(2,1)} %get-tuple-element.1727, bf16[32,1408]{1,0:T(8,128)(2,1)} %get-tuple-element.1727, bf16[32,1408]{1,0:T(8,128)(2,1)} %get-tuple-element.1727), branch_computations={%region_14.14_spmd, %region_15.15_spmd, %region_16.16_spmd} | conditional | bytes 540720 | solution.py:451
  586.1 1.3 collective-permute-start.10
  587.4 28.9 %collective-permute-done.10 = bf16[32,1408]{1,0:T(8,128)(2,1)S(1)} collective-permute-done((bf16[32,1408]{1,0:T(8,128)(2,1)}, bf16[32,1408]{1,0:T(8,128)(2,1)S(1)}, u32[]{:S(2)}, u32[]{:S(2)}) %collective-permute-start.10) | collective-permute-done | bytes 90144 | tf_op jit(solution)/shard_map/while/body/eval_jaxpr/cond/branch_1_fun/ppermute | solution.py:455
  617.2 19.1 %conditional.12 = ((bf16[2,32,1280]{2,1,0:T(8,128)(2,1)}, bf16[2,32,64]{2,1,0:T(8,128)(2,1)S(1)}, bf16[2,32,1280]{2,1,0:T(8,128)(2,1)S(1)}, f32[2,32,128]{2,1,0:T(8,128)S(1)}, bf16[32,1408]{1,0:T(8,128)(2,1)})) conditional(s32[]{:T(128)} %convert_element_type.70, (bf16[2,32,1280]{2,1,0:T(8,128)(2,1)}, bf16[2,32,64]{2,1,0:T(8,128)(2,1)S(1)}, ...), branch_computations={%region_8.8_spmd, %region_9.13_spmd} | conditional | flops 445644800 | bytes 18650836 | solution.py:448
  617.2 10.3 %conditional = (bf16[4,32,1408]{2,0,1:T(4,128)(2,1)}) conditional(s32[]{:T(128)} %convert_element_type.44, bf16[32,1408]{1,0:T(8,128)(2,1)} %get-tuple-element.1045, (s32[]{:T(128)}, bf16[2,32,5120]{2,1,0:T(8,128)(2,1)}) %tuple.82), branch_computations={%region_10.9_spmd, %region_11.10_spmd} | conditional | flops 3 | bytes 1998896 | solution.py:445
  618.1 8.4 %all_to_all.22 = bf16[4,32,1408]{2,1,0:T(8,128)(2,1)S(1)} all-to-all(bf16[4,32,1408]{2,1,0:T(8,128)(2,1)S(1)} %broadcast_in_dim.56), channel_id=1, replica_groups=mesh['s'=16,'y'=4,'c'=2,'z'=4] {'y'}, dimensions={0} | all-to-all | bytes 720896 | tf_op jit(solution)/shard_map/while/body/eval_jaxpr/cond/branch_1_fun/cond/branch_0_fun/all_to_all | solution.py:48
  627.4 8.8 %conditional.1 = ((bf16[32,1408]{1,0:T(8,128)(2,1)}, bf16[2,32,1280]{2,1,0:T(8,128)(2,1)}, bf16[2,32,64]{2,1,0:T(8,128)(2,1)S(1)}, bf16[2,32,1280]{2,1,0:T(8,128)(2,1)S(1)}, f32[2,32,128]{2,1,0:T(8,128)S(1)})) conditional(s32[]{:T(128)} %convert_element_type.43, (s32[4]{0:T(128)S(1)}, bf16[4,32,1408]{2,0,1:T(4,128)(2,1)}, ...), branch_computations={%region_12.11_spmd, %region_13.12_spmd} | conditional | flops 445644800 | bytes 16651528 | solution.py:446
  627.4 1.0 copy.42.parts_ref
  628.5 7.8 %stage.1 = (bf16[32,1408]{1,0:T(8,128)(2,1)}, bf16[2,32,1280]{2,1,0:T(8,128)(2,1)}, bf16[2,32,64]{2,1,0:T(8,128)(2,1)S(1)}, bf16[2,32,1280]{2,1,0:T(8,128)(2,1)S(1)}, f32[2,32,128]{2,1,0:T(8,128)S(1)}) custom-call(s32[4]{0:T(128)S(1)} %get-tuple-element.1017.place_ref, ...), custom_call_target="tpu_custom_call", output_to_operand_aliasing={{1}: (22, {}), {2}: (23, {}), {3}: (24, {}), {4}: (25, {})} | custom-call | flops 419430400 | bytes 15930624 | tf_op jit(solution)/shard_map/while/body/eval_jaxpr/cond/branch_1_fun/cond/branch_1_fun/stage/pallas_call | solution.py:223
  636.4 12.8 %all-gather.4 = bf16[256,1408]{1,0:T(8,128)(2,1)S(1)} all-gather(bf16[64,1408]{1,0:T(8,128)(2,1)S(1)} %fusion.4), channel_id=6, replica_groups=mesh['s'=16,'y'=4,'c'=2,'z'=4] {'z'}, dimensions={0}, use_global_device_ids=true | all-gather | bytes 901120 | tf_op jit(solution)/shard_map/all_gather | solution.py:497
  650.0 1.4 fusion
  652.2 27.6 %collective-permute-start.20 = (f32[8,16,640]{2,1,0:T(8,128)}, f32[8,16,640]{2,1,0:T(8,128)}, u32[]{:S(2)}, u32[]{:S(2)}) collective-permute-start(f32[8,16,640]{2,1,0:T(8,128)} %slice_select_fusion), channel_id=1, source_target_pairs={{0,4},{4,0},{1,5},{5,1},{2,6},{6,2},{3,7},{7,3},{8,12},{12,8},{9,1... | collective-permute-start | bytes 983048 | tf_op jit(solution)/shard_map/ppermute | solution.py:43
  680.6 3.3 all-to-all-start.4
  684.3 1.4 fusion.1
  685.7 3.3 all-to-all-done.4
  689.3 3.0 collective-permute-start.18
  692.3 1.9 collective-permute-start.19
  695.0 1.0 select_add_fusion
  696.0 1.0 select_reduce_fusion
  697.1 1.0 select_reduce_fusion.1
  (182 shorter events, 16.5 us)
Async XLA Ops:
  0.6 29.3 %copy-start = (bf16[1,8,16,5120]{3,2,1,0:T(8,128)(2,1)S(1)}, bf16[1,8,16,5120]{3,2,1,0:T(8,128)(2,1)}, u32[]{:S(2)}) copy-start(bf16[1,8,16,5120]{3,2,1,0:T(8,128)(2,1)} %param.30) | copy-start | bytes 3932164
  0.6 31.0 %collective-permute-start.17 = (f32[1,640]{1,0:T(1,128)}, f32[1,640]{1,0:T(1,128)S(1)}, u32[]{:S(2)}, u32[]{:S(2)}) collective-permute-start(f32[1,640]{1,0:T(1,128)} %param.28), channel_id=1, source_target_pairs={{0,4},{4,0},{1,5},{5,1},{2,6},{6,2},{3,7},{7,3},{8,12},{12,8},{9,1... | collective-permute-start | bytes 7688 | tf_op jit(solution)/shard_map/ppermute | solution.py:30
  9.6 25.1 %collective-permute-start.16 = (bf16[8,640,16]{1,2,0:T(8,128)(2,1)}, bf16[8,640,16]{1,2,0:T(8,128)(2,1)S(1)}, u32[]{:S(2)}, u32[]{:S(2)}) collective-permute-start(bf16[8,640,16]{1,2,0:T(8,128)(2,1)} %bitcast.88), channel_id=1, source_target_pairs={{0,4},{4,0},{1,5},{5,1},{2,6},{6,2},{3,7},{7,3},{8,12},{12,8},{9,1... | collective-permute-start | bytes 491528 | tf_op jit(solution)/shard_map/ppermute | solution.py:30
  14.4 49.2 %collective-permute-start.14 = (bf16[1280,640]{1,0:T(8,128)(2,1)S(1)}, bf16[1280,640]{1,0:T(8,128)(2,1)}, u32[]{:S(2)}, u32[]{:S(2)}) collective-permute-start(bf16[1280,640]{1,0:T(8,128)(2,1)S(1)} %bitcast.69), channel_id=1, source_target_pairs={{0,4},{4,0},{1,5},{5,1},{2,6},{6,2},{3,7},{7,3},{8,12},{12,8},{9,1... | collective-permute-start | bytes 4915208 | tf_op jit(solution)/shard_map/ppermute | solution.py:273
  18.2 39.8 %collective-permute-start.12 = (bf16[640,640]{1,0:T(8,128)(2,1)}, bf16[640,640]{1,0:T(8,128)(2,1)}, u32[]{:S(2)}, u32[]{:S(2)}) collective-permute-start(bf16[640,640]{1,0:T(8,128)(2,1)} %get-tuple-element.1528), channel_id=1, source_target_pairs={{0,1},{1,2},{2,3},{3,0},{32,33},{33,34},{34,35},{35,32},{64,65},{6... | collective-permute-start | bytes 2457608 | tf_op jit(solution)/shard_map/ppermute | solution.py:271
  20.1 43.5 %collective-permute-start.13 = (bf16[640,640]{1,0:T(8,128)(2,1)}, bf16[640,640]{1,0:T(8,128)(2,1)}, u32[]{:S(2)}, u32[]{:S(2)}) collective-permute-start(bf16[640,640]{1,0:T(8,128)(2,1)} %get-tuple-element.1527), channel_id=1, source_target_pairs={{0,3},{1,0},{2,1},{3,2},{32,35},{33,32},{34,33},{35,34},{64,67},{6... | collective-permute-start | bytes 2457608 | tf_op jit(solution)/shard_map/ppermute | solution.py:272
  25.2 3.4 copy-start.10
  26.7 2.9 copy-start.16
  26.7 2.9 copy-start.17
  30.0 1.7 copy-start.15
  30.0 4.7 copy-start.14
  33.4 3.7 copy-start.1
  33.4 11.1 %collective-permute-start.15 = (bf16[64,1280]{1,0:T(8,128)(2,1)S(1)}, bf16[64,1280]{1,0:T(8,128)(2,1)}, u32[]{:S(2)}, u32[]{:S(2)}) collective-permute-start(bf16[64,1280]{1,0:T(8,128)(2,1)S(1)} %get-tuple-element.1524), channel_id=1, source_target_pairs={{480,448},{448,416},{416,384},{384,352},{352,320},{320,288},{288,2... | collective-permute-start | bytes 491528 | tf_op jit(solution)/shard_map/ppermute | solution.py:285
  38.2 25.5 %copy-start.11 = (f32[8,8,16]{2,1,0:T(8,128)}, f32[8,8,16]{2,1,0:T(8,128)S(1)}, u32[]{:S(2)}) copy-start(f32[8,8,16]{2,1,0:T(8,128)S(1)} %fusion.5) | copy-start | bytes 12292
  44.5 19.1 %copy-start.8 = (bf16[64,1280]{1,0:T(8,128)(2,1)S(1)}, bf16[64,1280]{1,0:T(8,128)(2,1)}, u32[]{:S(2)}) copy-start(bf16[64,1280]{1,0:T(8,128)(2,1)} %get-tuple-element.1523) | copy-start | bytes 491524
  63.7 75.8 %collective-permute-start = (bf16[640,640]{1,0:T(8,128)(2,1)}, bf16[640,640]{1,0:T(8,128)(2,1)}, u32[]{:S(2)}, u32[]{:S(2)}) collective-permute-start(bf16[640,640]{1,0:T(8,128)(2,1)} %get-tuple-element.981), channel_id=1, source_target_pairs={{0,1},{1,2},{2,3},{3,0},{32,33},{33,34},{34,35},{35,32},{64,65},{6... | collective-permute-start | bytes 2457608 | tf_op jit(solution)/shard_map/cond/branch_1_fun/ppermute | solution.py:321
  93.7 45.8 %collective-permute-start.1 = (bf16[640,640]{1,0:T(8,128)(2,1)}, bf16[640,640]{1,0:T(8,128)(2,1)}, u32[]{:S(2)}, u32[]{:S(2)}) collective-permute-start(bf16[640,640]{1,0:T(8,128)(2,1)} %get-tuple-element.982), channel_id=1, source_target_pairs={{0,3},{1,0},{2,1},{3,2},{32,35},{33,32},{34,33},{35,34},{64,67},{6... | collective-permute-start | bytes 2457608 | tf_op jit(solution)/shard_map/cond/branch_1_fun/ppermute | solution.py:322
  95.6 43.9 %collective-permute-start.2 = (bf16[640,640]{1,0:T(8,128)(2,1)}, bf16[640,640]{1,0:T(8,128)(2,1)}, u32[]{:S(2)}, u32[]{:S(2)}) collective-permute-start(bf16[640,640]{1,0:T(8,128)(2,1)} %get-tuple-element.981), channel_id=1, source_target_pairs={{0,4},{4,0},{32,36},{36,32},{64,68},{68,64},{96,100},{100,96},{128... | collective-permute-start | bytes 2457608 | tf_op jit(solution)/shard_map/cond/branch_1_fun/ppermute | solution.py:319
  99.7 39.8 %collective-permute-start.3 = (bf16[640,640]{1,0:T(8,128)(2,1)}, bf16[640,640]{1,0:T(8,128)(2,1)}, u32[]{:S(2)}, u32[]{:S(2)}) collective-permute-start(bf16[640,640]{1,0:T(8,128)(2,1)} %get-tuple-element.982), channel_id=1, source_target_pairs={{0,4},{4,0},{32,36},{36,32},{64,68},{68,64},{96,100},{100,96},{128... | collective-permute-start | bytes 2457608 | tf_op jit(solution)/shard_map/cond/branch_1_fun/ppermute | solution.py:319
  139.5 47.3 %collective-permute-start.4 = (bf16[640,640]{1,0:T(8,128)(2,1)}, bf16[640,640]{1,0:T(8,128)(2,1)}, u32[]{:S(2)}, u32[]{:S(2)}) collective-permute-start(bf16[640,640]{1,0:T(8,128)(2,1)} %collective-permute-done), channel_id=1, source_target_pairs={{0,1},{1,2},{2,3},{3,0},{32,33},{33,34},{34,35},{35,32},{64,65},{6... | collective-permute-start | bytes 2457608 | tf_op jit(solution)/shard_map/cond/branch_1_fun/ppermute | solution.py:328
  141.7 45.0 %collective-permute-start.5 = (bf16[640,640]{1,0:T(8,128)(2,1)}, bf16[640,640]{1,0:T(8,128)(2,1)}, u32[]{:S(2)}, u32[]{:S(2)}) collective-permute-start(bf16[640,640]{1,0:T(8,128)(2,1)} %collective-permute-done.1), channel_id=1, source_target_pairs={{0,3},{1,0},{2,1},{3,2},{32,35},{33,32},{34,33},{35,34},{64,67},{6... | collective-permute-start | bytes 2457608 | tf_op jit(solution)/shard_map/cond/branch_1_fun/ppermute | solution.py:329
  146.6 40.2 %collective-permute-start.6 = (bf16[640,640]{1,0:T(8,128)(2,1)}, bf16[640,640]{1,0:T(8,128)(2,1)}, u32[]{:S(2)}, u32[]{:S(2)}) collective-permute-start(bf16[640,640]{1,0:T(8,128)(2,1)} %collective-permute-done), channel_id=1, source_target_pairs={{0,4},{4,0},{32,36},{36,32},{64,68},{68,64},{96,100},{100,96},{128... | collective-permute-start | bytes 2457608 | tf_op jit(solution)/shard_map/cond/branch_1_fun/ppermute | solution.py:319
  154.8 31.9 %collective-permute-start.7 = (bf16[640,640]{1,0:T(8,128)(2,1)}, bf16[640,640]{1,0:T(8,128)(2,1)}, u32[]{:S(2)}, u32[]{:S(2)}) collective-permute-start(bf16[640,640]{1,0:T(8,128)(2,1)} %collective-permute-done.1), channel_id=1, source_target_pairs={{0,4},{4,0},{32,36},{36,32},{64,68},{68,64},{96,100},{100,96},{128... | collective-permute-start | bytes 2457608 | tf_op jit(solution)/shard_map/cond/branch_1_fun/ppermute | solution.py:319
  186.8 6.6 collective-permute-start.8
  191.1 4.6 collective-permute-start.9
  195.7 0.6 copy-start.13
  202.1 363.8 %collective-permute-start.10 = (bf16[32,1408]{1,0:T(8,128)(2,1)}, bf16[32,1408]{1,0:T(8,128)(2,1)S(1)}, u32[]{:S(2)}, u32[]{:S(2)}) collective-permute-start(bf16[32,1408]{1,0:T(8,128)(2,1)} %param.11), channel_id=1, source_target_pairs={{480,448},{416,384},{352,320},{288,256},{224,192},{160,128},{96,64... | collective-permute-start | bytes 270344 | tf_op jit(solution)/shard_map/while/body/eval_jaxpr/cond/branch_1_fun/ppermute | solution.py:455
  586.1 30.2 %collective-permute-start.10 = (bf16[32,1408]{1,0:T(8,128)(2,1)}, bf16[32,1408]{1,0:T(8,128)(2,1)S(1)}, u32[]{:S(2)}, u32[]{:S(2)}) collective-permute-start(bf16[32,1408]{1,0:T(8,128)(2,1)} %param.11), channel_id=1, source_target_pairs={{480,448},{416,384},{352,320},{288,256},{224,192},{160,128},{96,64... | collective-permute-start | bytes 270344 | tf_op jit(solution)/shard_map/while/body/eval_jaxpr/cond/branch_1_fun/ppermute | solution.py:455
  636.4 12.8 %copy-start.9 = (bf16[64,1280]{1,0:T(8,128)(2,1)S(1)}, bf16[64,1280]{1,0:T(8,128)(2,1)}, u32[]{:S(2)}) copy-start(bf16[64,1280]{1,0:T(8,128)(2,1)} %get-tuple-element.1523) | copy-start | bytes 491524
  636.4 12.8 %copy-start.12 = (f32[8,8,16]{2,1,0:T(8,128)S(1)}, f32[8,8,16]{2,1,0:T(8,128)}, u32[]{:S(2)}) copy-start(f32[8,8,16]{2,1,0:T(8,128)} %copy-done.11) | copy-start | bytes 12292
  649.1 0.9 copy-start.7
  652.2 36.9 %copy-start.3 = (bf16[2,32,1280]{2,1,0:T(8,128)(2,1)S(1)}, bf16[2,32,1280]{2,1,0:T(8,128)(2,1)}, u32[]{:S(2)}) copy-start(bf16[2,32,1280]{2,1,0:T(8,128)(2,1)} %get-tuple-element.1899) | copy-start | bytes 491524
  652.2 36.9 %copy-start.6 = (bf16[2,32,1280]{2,1,0:T(8,128)(2,1)S(1)}, bf16[2,32,1280]{2,1,0:T(8,128)(2,1)}, u32[]{:S(2)}) copy-start(bf16[2,32,1280]{2,1,0:T(8,128)(2,1)} %get-tuple-element.1169) | copy-start | bytes 491524
  652.2 42.8 %collective-permute-start.20 = (f32[8,16,640]{2,1,0:T(8,128)}, f32[8,16,640]{2,1,0:T(8,128)}, u32[]{:S(2)}, u32[]{:S(2)}) collective-permute-start(f32[8,16,640]{2,1,0:T(8,128)} %slice_select_fusion), channel_id=1, source_target_pairs={{0,4},{4,0},{1,5},{5,1},{2,6},{6,2},{3,7},{7,3},{8,12},{12,8},{9,1... | collective-permute-start | bytes 983048 | tf_op jit(solution)/shard_map/ppermute | solution.py:43
  680.6 8.4 %all-to-all-start.4 = ((f32[4,2,32,128]{3,2,1,0:T(8,128)}), f32[4,2,32,128]{3,2,1,0:T(8,128)S(1)}, u32[]{:S(2)}, u32[]{:S(2)}) async-start(f32[4,2,32,128]{3,2,1,0:T(8,128)} %broadcast_in_dim.108), calls=%async_computation.4 | async-start | bytes 262144 | tf_op jit(solution)/shard_map/all_to_all | solution.py:48
  689.3 5.0 collective-permute-start.18
  692.3 4.7 collective-permute-start.19

commit v5 on v3

v5 whole, which is shorter than its diff:
```python
import functools

import jax
import jax.numpy as jnp
from jax import lax
from jax.experimental import pallas as pl
from jax.experimental.pallas import tpu as pltpu
from jax.sharding import Mesh, PartitionSpec as P

norm_eps = 1e-05
low_rank_scale = 2.0
CHUNKS = 2
TAIL = 128
SWAP = [(0, 1), (1, 0)]
ODD = [(s, s - 1) for s in range(15, 0, -2)]
EVEN = [(s, s - 1) for s in range(14, 0, -2)]
EVERY = [(s, s - 1) for s in range(15, 0, -1)]
f32 = jnp.float32
bf16 = jnp.bfloat16
contract_last = (((1,), (1,)), ((), ()))
contract_inner = (((1,), (0,)), ((), ()))
TOP_SWAP = [(30, 31), (31, 30)]
AHEAD = 3


def both_cores(value, axis):
    core = lax.axis_index("c")
    other = lax.ppermute(value, "c", SWAP)
    low = jnp.where(core == 0, value, other)
    high = jnp.where(core == 0, other, value)
    return jnp.concatenate([low, high], axis)


def half_sum(value, axis):
    core = lax.axis_index("c")
    width = value.shape[axis] // 2
    low = lax.slice_in_dim(value, 0, width, axis=axis)
    high = lax.slice_in_dim(value, width, 2 * width, axis=axis)
    mine = jnp.where(core == 0, low, high)
    theirs = jnp.where(core == 0, high, low)
    return mine + lax.ppermute(theirs, "c", SWAP)


def spread(value):
    sent = jnp.broadcast_to(value[None], (4,) + value.shape)
    return lax.all_to_all(sent, "y", 0, 0)


def own_group(low, group):
    rows, cols = low.shape
    row_group = lax.broadcasted_iota(jnp.int32, low.shape, 0) // (rows // group)
    col_group = lax.broadcasted_iota(jnp.int32, low.shape, 1) // (cols // group)
    return jnp.where(row_group == col_group, low, 0.0).astype(bf16)


def message(total, grad_y, gain, inv, x, width_all):
    rows, width = total.shape
    normed_grad = (total * gain).astype(bf16).astype(f32)
    sent = (grad_y.astype(f32) + inv * normed_grad).astype(bf16)
    coef = jnp.sum(normed_grad * x.astype(f32), axis=1, keepdims=True)
    coef = coef * (inv * inv * inv / width_all)
    lane = lax.broadcasted_iota(jnp.int32, (rows, TAIL), 1)
    high = lax.reduce_precision(coef, 8, 7)
    tail = jnp.where(lane == 0, high, jnp.where(lane == 1, coef - high, 0.0)).astype(bf16)
    return sent, tail


def stage_kernel(
    place_ref,
    parts_ref,
    gain_ref,
    before_any,
    up_any,
    down_any,
    inv_any,
    x_any,
    own_any,
    other_any,
    boxes_in,
    low_in,
    grad_in,
    box_ref,
    boxes_any,
    low_any,
    grad_any,
    before_ref,
    up_ref,
    down_ref,
    inv_ref,
    x_ref,
    full,
    weight,
    low_ref,
    grad_ref,
    in_sems,
    w_sems,
    out_sems,
    *,
    group,
):
    del boxes_in, low_in, grad_in
    m, ypos, core = place_ref[0], place_ref[1], place_ref[2]
    width = x_ref.shape[1]
    width_all = full.shape[1]
    half = width // 2
    pieces = w_sems.shape[0]
    depth = width_all // pieces

    def started(source, target, sem):
        copy = pltpu.make_async_copy(source, target, sem)
        copy.start()
        return copy

    before_copy = started(before_any.at[:, m], before_ref, in_sems.at[0])
    up_copy = started(up_any.at[m], up_ref, in_sems.at[1])
    copies = []
    for piece in range(pieces):
        span = pl.ds(piece * depth, depth)
        for side, (ref, base) in enumerate(((own_any, core * half), (other_any, (1 - core) * half))):
            lanes = pl.ds(pl.multiple_of(base, 128), half)
            copies.append(started(ref.at[span], weight.at[span, lanes], w_sems.at[piece, side]))
        if piece == 0:
            down_copy = started(down_any.at[m], down_ref, in_sems.at[2])
            inv_copy = started(inv_any.at[m], inv_ref, in_sems.at[3])
            x_copy = started(x_any.at[m], x_ref, in_sems.at[4])

    tail = parts_ref[:, :, width:].astype(f32)
    coef = jnp.sum(jnp.sum(tail, axis=0), axis=1, keepdims=True)
    before_copy.wait()
    for part in range(4):
        fixed = parts_ref[part, :, :width].astype(f32) - coef * before_ref[part].astype(f32)
        full[:, part * width : (part + 1) * width] = fixed.astype(bf16)
    grad_ref[...] = full[:, pl.ds(pl.multiple_of(ypos * width, 128), width)]
    grad_copy = started(grad_ref, grad_any.at[m], out_sems.at[0])
    up_copy.wait()
    low = lax.dot_general(full[...], up_ref[...], contract_last, preferred_element_type=f32)
    low = own_group(low, group)
    low_ref[...] = low
    low_copy = started(low_ref, low_any.at[m], out_sems.at[1])
    down_copy.wait()
    total = low_rank_scale * lax.dot_general(
        low, down_ref[...], contract_inner, preferred_element_type=f32
    )
    for piece in range(pieces):
        copies[2 * piece].wait()
        copies[2 * piece + 1].wait()
        span = slice(piece * depth, (piece + 1) * depth)
        total = total + lax.dot_general(
            full[:, span], weight[span], contract_inner, preferred_element_type=f32
        )
    inv_copy.wait()
    x_copy.wait()
    sent, tail = message(
        total, grad_ref[...], gain_ref[...], inv_ref[:, 0:1], x_ref[...], width_all
    )
    box_ref[:, :width] = sent
    box_ref[:, width:] = tail
    box_copy = started(box_ref, boxes_any.at[m], out_sems.at[2])
    grad_copy.wait()
    low_copy.wait()
    box_copy.wait()


def run_stage(place, parts, before, up, down, gain, inv, x, own, other, kept):
    _, rows, width = x.shape
    width_all = own.shape[0]
    cols = up.shape[1]
    pieces = 5
    vmem = pl.BlockSpec(memory_space=pltpu.VMEM)
    any_space = pl.BlockSpec(memory_space=pl.ANY)
    return pl.pallas_call(
        functools.partial(stage_kernel, group=cols // 16),
        in_specs=[pl.BlockSpec(memory_space=pltpu.SMEM), vmem, vmem] + [any_space] * 10,
        out_specs=[vmem] + [any_space] * 3,
        scratch_shapes=[
            pltpu.VMEM((4, rows, width), bf16),
            pltpu.VMEM((cols, width_all), bf16),
            pltpu.VMEM((cols, width), bf16),
            pltpu.VMEM((rows, TAIL), f32),
            pltpu.VMEM((rows, width), bf16),
            pltpu.VMEM((rows, width_all), bf16),
            pltpu.VMEM((width_all, width), bf16),
            pltpu.VMEM((rows, cols), bf16),
            pltpu.VMEM((rows, width), bf16),
            pltpu.SemaphoreType.DMA((5,)),
            pltpu.SemaphoreType.DMA((pieces, 2)),
            pltpu.SemaphoreType.DMA((3,)),
        ],
        out_shape=[jax.ShapeDtypeStruct((rows, width + TAIL), bf16)]
        + [jax.ShapeDtypeStruct(k.shape, k.dtype) for k in kept],
        input_output_aliases={10: 1, 11: 2, 12: 3},
        compiler_params=pltpu.CompilerParams(vmem_limit_bytes=32 * 1024 * 1024),
        cost_estimate=pl.CostEstimate(
            flops=2 * rows * width * width_all, bytes_accessed=2 * width * width_all, transcendentals=0
        ),
        name="stage",
    )(place, parts, gain, before, up, down, inv, x, own, other, *kept)


def local(
    section_inputs,
    out_grads,
    proj_weight,
    norm_gain,
    adapter_down,
    adapter_up,
    tenant_ids,
    slot_table,
):
    sec = lax.axis_index("s")
    ypos = lax.axis_index("y")
    core = lax.axis_index("c")
    micro = section_inputs.shape[1]
    width_all = section_inputs.shape[3]
    half = proj_weight.shape[1]
    width = 2 * half
    toks = section_inputs.shape[2] // 2
    rank = adapter_down.shape[3]
    rows_all = micro * toks
    group = micro // CHUNKS
    rows = group * toks
    multiplier = low_rank_scale / (toks * 2 * lax.axis_size("z"))

    shard = proj_weight[0].T
    w_own = lax.all_gather(shard, "z", axis=0, tiled=True)

    x_full = section_inputs[0]
    x_mine = lax.dynamic_slice_in_dim(x_full, core * toks, toks, 1).reshape(rows_all, width_all)
    x_f = x_mine.astype(f32)
    inv_rms = lax.rsqrt(jnp.mean(x_f * x_f, axis=-1, keepdims=True) + norm_eps)
    x_y = lax.dynamic_slice_in_dim(x_mine, ypos * width, width, 1)
    normed_y = x_y.astype(f32) * inv_rms
    x_before = lax.cond(
        sec == 15,
        lambda x: jnp.zeros((4,) + x.shape, x.dtype),
        spread,
        lax.ppermute(x_y, "s", EVERY),
    )
    gain_y = both_cores(norm_gain, 1)
    down_y = both_cores(adapter_down[0], 1)
    h_y = (normed_y * gain_y).astype(bf16)

    iota = jnp.arange(micro, dtype=jnp.int32)
    tenant_hot = tenant_ids[:, None] == iota[None, :]
    slot_ids = jnp.sum(jnp.where(tenant_hot, slot_table[0][None, :], 0), axis=1)
    down_sel = down_y[slot_ids]
    up_sel = adapter_up[0][slot_ids]
    low_part = jnp.einsum(
        "mtd,mdr->mtr", h_y.reshape(micro, toks, width), down_sel, preferred_element_type=f32
    )

    def extra(args):
        h_y, low_part = args
        low_in = lax.psum(low_part, "y").astype(bf16)
        return lax.all_gather(h_y, "z"), lax.all_gather(low_in, "z")

    x_before = x_before.reshape(4, CHUNKS, rows, width)
    x_chunk = x_y.reshape(CHUNKS, rows, width)
    inv_chunk = jnp.broadcast_to(inv_rms.reshape(CHUNKS, rows, 1), (CHUNKS, rows, TAIL))
    down_chunk = down_sel.transpose(0, 2, 1).reshape(CHUNKS, group * rank, width)
    up_chunk = up_sel.reshape(CHUNKS, group * rank, width_all)

    def top(args):
        out_grads, shard = args
        shard_x = lax.ppermute(shard, ("s", "c"), TOP_SWAP)
        grad = lax.dynamic_slice_in_dim(out_grads, core * toks, toks, 1)
        low = jnp.einsum("mtd,mrd->mtr", grad, up_sel, preferred_element_type=f32).astype(bf16)
        adapt = jnp.einsum("mtr,mdr->mtd", low, down_sel, preferred_element_type=f32)
        grad = grad.reshape(rows_all, width_all)
        blocks = jnp.stack([grad[:, i * width : (i + 1) * width] for i in range(4)])
        blocks = lax.all_to_all(blocks, "z", 0, 0).reshape(4 * rows_all, width)
        mine, theirs = (
            lax.dot_general(blocks, w, contract_inner, preferred_element_type=f32).astype(bf16)
            for w in (shard, shard_x)
        )
        terms = jnp.concatenate(
            [jnp.where(core == 0, mine, theirs), jnp.where(core == 0, theirs, mine)], 1
        )
        terms = lax.all_to_all(terms.reshape(4, rows_all, width), "z", 0, 0)
        total = jnp.sum(terms.astype(f32), axis=0)
        total = total + low_rank_scale * adapt.reshape(rows_all, width)
        grad_y = lax.dynamic_slice_in_dim(grad, ypos * width, width, 1)
        sent, tail = message(total, grad_y, gain_y, inv_rms, x_y, width_all)
        boxes = jnp.concatenate([sent, tail], 1).reshape(CHUNKS, rows, width + TAIL)
        member = jnp.arange(rows_all)[:, None] // toks % group == jnp.arange(group)[None, :]
        low = jnp.where(member[:, :, None], low.reshape(rows_all, 1, rank), 0)
        low = low.astype(bf16).reshape(CHUNKS, rows, group * rank)
        return boxes, low, grad_y.reshape(CHUNKS, rows, width)

    def empty(args):
        return (
            jnp.zeros((CHUNKS, rows, width + TAIL), bf16),
            jnp.zeros((CHUNKS, rows, group * rank), bf16),
            jnp.zeros((CHUNKS, rows, width), bf16),
        )

    kept = lax.cond(sec == 15, top, empty, (out_grads, shard))

    ready = (x_before, x_chunk, inv_chunk, down_chunk, up_chunk, gain_y, kept)
    w_own, ready = lax.optimization_barrier((w_own, ready))
    x_before, x_chunk, inv_chunk, down_chunk, up_chunk, gain_y, kept = ready
    w_other = lax.ppermute(w_own, "c", SWAP)

    def pick(array, m):
        return lax.dynamic_index_in_dim(array, m, 0, keepdims=False)

    def step(u, state):
        box, kept, extras = state
        t, m = u // CHUNKS, u % CHUNKS
        turn = 15 - t + m

        def stored(args):
            _, kept = args
            return pick(kept[0], m), kept

        def computed(args):
            box, kept = args
            place = jnp.stack([m, ypos, core]).astype(jnp.int32)
            box, *kept = run_stage(
                place,
                spread(box),
                x_before,
                up_chunk,
                down_chunk,
                gain_y,
                inv_chunk,
                x_chunk,
                w_own,
                w_other,
                kept,
            )
            return box, tuple(kept)

        kind = jnp.where(sec == turn, jnp.where(sec == 15, 1, 2), 0)
        box, kept = lax.switch(kind, [lambda args: args, stored, computed], (box, kept))
        part = ((sec == turn) | (sec == turn - 1)) & (turn >= 1) & (turn <= 15)
        kind = jnp.where(part, jnp.where(turn % 2 == 1, 1, 2), 0)
        box = lax.switch(
            kind,
            [
                lambda box: box,
                lambda box: lax.ppermute(box, "s", ODD),
                lambda box: lax.ppermute(box, "s", EVEN),
            ],
            box,
        )
        extras = lax.cond(
            (sec == turn - AHEAD) & (m == 0),
            lambda args: extra((h_y, low_part)),
            lambda args: args,
            extras,
        )
        return box, kept, extras

    start = (
        jnp.zeros((rows, width + TAIL), bf16),
        kept,
        (
            jnp.zeros((4, rows_all, width), bf16),
            jnp.zeros((4, micro, toks, rank), bf16),
        ),
    )
    _, kept, extras = lax.fori_loop(0, (15 + CHUNKS) * CHUNKS, step, start)
    boxes, low_all, grad_all = kept
    h_all, low_in_all = lax.cond(
        sec > 15 - AHEAD, lambda args: extra((h_y, low_part)), lambda args: args, extras
    )

    coef_sum = jnp.sum(spread(boxes[:, :, width:]).astype(f32), axis=(0, -1))[..., None]
    new_grads = boxes[:, :, :width].astype(f32) - coef_sum * x_chunk.astype(f32)
    new_grads = new_grads.astype(bf16).reshape(micro, toks, width)
    keep = jnp.where(core == 0, new_grads[:, :, :half], new_grads[:, :, half:])
    give = jnp.where(core == 0, new_grads[:, :, half:], new_grads[:, :, :half])
    got = lax.ppermute(give, "c", SWAP)
    kept = jnp.concatenate(
        [jnp.where(core == 0, keep, got), jnp.where(core == 0, got, keep)], 1
    )

    both = jnp.concatenate(
        [
            grad_all.reshape(rows_all, width),
            jnp.pad(low_all.reshape(rows_all, group * rank), ((0, 0), (0, TAIL - group * rank))),
        ],
        1,
    )
    both = lax.all_gather(both, "z").reshape(4, micro, toks, width + TAIL)
    grads_z = both[..., :width]
    low_z = both[..., width : width + group * rank].reshape(4, micro, toks, group, rank)
    low_z = jnp.sum(low_z.astype(f32), axis=3).astype(bf16)
    hidden_z = h_all.reshape(4, micro, toks, width)
    down_part = multiplier * jnp.einsum(
        "zmtd,zmtr->mdr", hidden_z, low_z, preferred_element_type=f32
    )
    up_part = multiplier * jnp.einsum(
        "zmtr,zmtd->mrd", low_in_all, grads_z, preferred_element_type=f32
    )
    down_acc = half_sum(down_part, 1)
    up_acc = half_sum(up_part, 2)
    slot_hot = slot_ids[None, :] == iota[:, None]
    down_out = jnp.sum(jnp.where(slot_hot[:, :, None, None], down_acc[None], 0.0), axis=1)
    up_out = jnp.sum(jnp.where(slot_hot[:, :, None, None], up_acc[None], 0.0), axis=1)
    return (kept[None], down_out[None], up_out[None])


def solution(mesh):
    fine = Mesh(mesh.devices.reshape(16, 4, 2, 4), ("s", "y", "c", "z"))
    mp = ("y", "c")
    placed = (
        P("s", None, "z", None),
        P(None, "z", None),
        P("s", mp, "z"),
        P("s", mp),
        P("s", None, mp, None),
        P("s", None, None, None),
        P(),
        P("s", None),
    )
    return jax.shard_map(
        local,
        mesh=fine,
        in_specs=placed,
        out_specs=(
            P("s", None, "z", mp),
            P("s", None, mp, None),
            P("s", None, None, mp),
        ),
        check_vma=False,
    )
```

time: 685 us -> 702 us (1.025)
  waiting for transfers between devices: 462 us -> 496 us
  blocking collectives: 93.2 us -> 71.7 us
    ppermute x2, waiting for transfers between devices: 395 us -> 368 us  [step(): lax.ppermute(box, 's', ODD)]
    all_gather x1, waiting for transfers between devices: 60.3 us -> 86.7 us  [local(): w_own = lax.all_gather(shard, 'z', axis=0, tiled=True)]
    ppermute x1, waiting for transfers between devices: 0.01 us -> 17.7 us  [local(): lax.ppermute(x_y, 's', EVERY)]
    all_gather x2, blocking collectives: 45.8 us -> 28.7 us  [extra(): return (lax.all_gather(h_y, 'z'), lax.all_gather(low_in, 'z'))]
    all_to_all x2 -> x3, waiting for transfers between devices: 0.01 us -> 15 us  [spread(): return lax.all_to_all(sent, 'y', 0, 0)]
    all_to_all x2 -> x1, blocking collectives: 16.9 us -> 13.1 us  [spread(): return lax.all_to_all(sent, 'y', 0, 0)]
  transfers between devices with their start and end apart: 12 -> 13, of which waited for: 4 -> 8; matrix products, arithmetic and copies ran while one was open for 3% -> 2% of each run, Pallas kernels for 0% -> 0%
where the time goes in v5:
time: 702 us; the launch traced here: 701 us
  waiting for transfers between devices  496 us (71%)
  blocking collectives  71.7 us (10%)
  starting transfers between devices  70.2 us (10%)
  local copies, waits for them, and re-layouts  16.7 us (2%)
  Pallas kernels  14.9 us (2%)
  between operations  14.4 us (2%)
  other arithmetic  8.76 us (1%)
    ppermute x2, waiting for transfers between devices, step(): lax.ppermute(box, 's', ODD)  368 us
    all_gather x1, waiting for transfers between devices, local(): w_own = lax.all_gather(shard, 'z', axis=0, tiled=True)  86.7 us
    ppermute x2, starting transfers between devices, half_sum(): return mine + lax.ppermute(theirs, 'c', SWAP)  39.9 us
    all_gather x2, blocking collectives, extra(): return (lax.all_gather(h_y, 'z'), lax.all_gather(low_in, 'z'))  28.7 us
    ppermute x1, waiting for transfers between devices, local(): lax.ppermute(x_y, 's', EVERY)  17.7 us
    all_gather x1, blocking collectives, local(): both = lax.all_gather(both, 'z').reshape(4, micro, toks, width + TAIL)  17.7 us
    all_to_all x3, waiting for transfers between devices, spread(): return lax.all_to_all(sent, 'y', 0, 0)  15 us
    pallas_call x2, Pallas kernels, run_stage(): pl.pallas_call(functools.partial(stage_kernel, group=cols // 16), in_spec...  14.9 us
  transfers between devices with their start and end apart: 13, of which 8 were waited for; matrix products, arithmetic and copies ran while one was open for 2% of the time, Pallas kernels for 0%

profile of v5, /device:TPU:1, one launch (start us, length us, event | category | flops | bytes accessed | tf_op | source)
XLA Modules:
  0.0 701.1 jit_solution(7538694532459485825)
XLA Ops:
  7.2 3.7 copy.31
  10.9 0.6 copy-done.4
  11.6 8.8 %collective-permute-start.5 = (f32[1,640]{1,0:T(1,128)S(1)}, f32[1,640]{1,0:T(1,128)S(1)}, u32[]{:S(2)}, u32[]{:S(2)}) collective-permute-start(f32[1,640]{1,0:T(1,128)S(1)} %copy-done.4), channel_id=1, source_target_pairs={{0,4},{4,0},{1,5},{5,1},{2,6},{6,2},{3,7},{7,3},{8,12},{12,8},{9,1... | collective-permute-start | bytes 7688 | tf_op jit(solution)/shard_map/ppermute | solution.py:28
  20.4 1.9 collective-permute-start.4
  22.3 0.2 multiply_reduce_fusion.1
  22.5 0.2 select_reduce_fusion.2
  22.7 0.9 dynamic-slice_bitcast_fusion.2
  23.8 0.6 gather_fusion.1
  24.5 1.7 multiply_convert_fusion
  26.2 1.3 collective-permute-start.3
  27.6 0.6 gather_fusion
  28.2 0.7 conditional.7
  28.2 0.7 broadcast.203
  28.9 17.7 %collective-permute-done.3 = bf16[64,1280]{1,0:T(8,128)(2,1)} collective-permute-done((bf16[64,1280]{1,0:T(8,128)(2,1)}, bf16[64,1280]{1,0:T(8,128)(2,1)}, u32[]{:S(2)}, u32[]{:S(2)}) %collective-permute-start.3) | collective-permute-done | bytes 163872 | tf_op jit(solution)/shard_map/ppermute | solution.py:237
  46.6 14.1 %conditional.6 = (bf16[4,2,32,1280]{3,2,1,0:T(8,128)(2,1)}) conditional(s32[]{:T(128)} %convert_element_type.82, bf16[64,1280]{1,0:T(8,128)(2,1)} %collective-permute-done.3, () %tuple.100), branch_computations={%region_0.0_spmd, %region_1.0_spmd} | conditional | bytes 2129928 | solution.py:233
  46.6 1.0 broadcast_in_dim.94
  47.6 13.1 %all_to_all.21 = bf16[4,64,1280]{2,1,0:T(8,128)(2,1)} all-to-all(bf16[4,64,1280]{2,1,0:T(8,128)(2,1)S(1)} %broadcast_in_dim.94), channel_id=1, replica_groups=mesh['s'=16,'y'=4,'c'=2,'z'=4] {'y'}, dimensions={0} | all-to-all | bytes 1310720 | tf_op jit(solution)/shard_map/cond/branch_0_fun/all_to_all | solution.py:46
  60.7 86.7 %all-gather.7.cloned.1.call-done = bf16[5120,640]{1,0:T(8,128)(2,1)} async-done(((bf16[1280,640]{1,0:T(8,128)(2,1)}), bf16[5120,640]{1,0:T(8,128)(2,1)}) %all-gather.7.cloned.1.call-update) | async-done | bytes 6553616 | tf_op jit(solution)/shard_map/all_gather | solution.py:225
  147.4 0.7 broadcast_in_dim.151
  148.1 2.5 collective-permute-start.6
  150.6 1.1 fusion.15
  151.8 9.3 %collective-permute-done.6 = bf16[5120,640]{1,0:T(8,128)(2,1)} collective-permute-done((bf16[5120,640]{1,0:T(8,128)(2,1)}, bf16[5120,640]{1,0:T(8,128)(2,1)}, u32[]{:S(2)}, u32[]{:S(2)}) %collective-permute-start.6) | collective-permute-done | bytes 6553632 | tf_op jit(solution)/shard_map/ppermute | solution.py:302
  161.0 0.9 broadcast.219
  161.9 0.6 broadcast_in_dim.150
  162.6 0.6 broadcast_in_dim.155
  163.2 454.2 %while.26 = (s32[]{:T(128)}, bf16[32,1408]{1,0:T(8,128)(2,1)}, bf16[2,32,1408]{2,1,0:T(8,128)(2,1)S(1)}, bf16[2,32,64]{2,1,0:T(8,128)(2,1)S(1)}, bf16[2,32,1280]...) while((s32[]{:T(128)}, bf16[32,1408]{1,0:T(8,128)(2,1)}, ...), condition=%wide.region_18.19_spmd, body=%wide.region_8.18_spmd.sunk | while | flops 419431456 | bytes 16016404 | solution.py:363
  167.0 40.9 %conditional.14 = ((bf16[4,64,1280]{2,1,0:T(8,128)(2,1)}, bf16[4,8,8,16]{3,2,1,0:T(8,128)(2,1)})) conditional(s32[]{:T(128)} %convert_element_type.115, (bf16[4,64,1280]{2,1,0:T(8,128)(2,1)}, bf16[4,8,8,16]{3,2,1,0:T(8,128)(2,1)}) %tuple.142, (bf16[64,1280]{1,0:T(8,128)(2,1)}, f32[8,8,16]{2,1,0:T(8,128)S(1)}) %tuple.143), branch_computations={%region_15.15_spmd, %region_16.17_spmd} | conditional | flops 1024 | bytes 835608 | solution.py:347
  167.1 17.7 %all-gather = bf16[256,1280]{1,0:T(8,128)(2,1)} all-gather(bf16[64,1280]{1,0:T(8,128)(2,1)} %get-tuple-element.695), channel_id=2, replica_groups=mesh['s'=16,'y'=4,'c'=2,'z'=4] {'z'}, dimensions={0}, use_global_device_ids=true | all-gather | bytes 819200 | tf_op jit(solution)/shard_map/while/body/eval_jaxpr/cond/branch_1_fun/all_gather | solution.py:255
  184.8 12.2 %psum.12 = bf16[8,8,16]{2,1,0:T(8,128)(2,1)S(1)} all-reduce(f32[8,8,16]{2,1,0:T(8,128)S(1)} %get-tuple-element.696), channel_id=1, replica_groups=mesh['s'=16,'y'=4,'c'=2,'z'=4] {'y'}, use_global_device_ids=true, to_apply=%region_17.16 | all-reduce | flops 1024 | bytes 6144 | tf_op jit(solution)/shard_map/while/body/eval_jaxpr/cond/branch_1_fun/psum | solution.py:254
  197.0 11.0 %all-gather.1 = bf16[32,8,16]{2,1,0:T(8,128)(2,1)} all-gather(bf16[8,8,16]{2,1,0:T(8,128)(2,1)S(1)} %psum.12), channel_id=3, replica_groups=mesh['s'=16,'y'=4,'c'=2,'z'=4] {'z'}, dimensions={0}, use_global_device_ids=true | all-gather | bytes 10240 | tf_op jit(solution)/shard_map/while/body/eval_jaxpr/cond/branch_1_fun/all_gather | solution.py:255
  208.4 355.3 %conditional.13 = (bf16[32,1408]{1,0:T(8,128)(2,1)}) conditional(s32[]{:T(128)} %clamp.27, bf16[32,1408]{1,0:T(8,128)(2,1)} %get-tuple-element.1036, bf16[32,1408]{1,0:T(8,128)(2,1)} %get-tuple-element.1036, bf16[32,1408]{1,0:T(8,128)(2,1)} %get-tuple-element.1036), branch_computations={%region_12.12_spmd, %region_13.13_spmd, %region_14.14_spmd} | conditional | bytes 540720 | solution.py:338
  208.4 1.3 collective-permute-start
  209.7 353.3 %collective-permute-done = bf16[32,1408]{1,0:T(8,128)(2,1)S(1)} collective-permute-done((bf16[32,1408]{1,0:T(8,128)(2,1)}, bf16[32,1408]{1,0:T(8,128)(2,1)S(1)}, u32[]{:S(2)}, u32[]{:S(2)}) %collective-permute-start) | collective-permute-done | bytes 90144 | tf_op jit(solution)/shard_map/while/body/eval_jaxpr/cond/branch_1_fun/ppermute | solution.py:342
  563.0 0.6 copy.49
  563.7 18.6 %conditional.12 = ((bf16[2,32,1408]{2,1,0:T(8,128)(2,1)S(1)}, bf16[2,32,64]{2,1,0:T(8,128)(2,1)S(1)}, bf16[2,32,1280]{2,1,0:T(8,128)(2,1)}, bf16[32,1408]{1,0:T(8,128)(2,1)})) conditional(s32[]{:T(128)} %clamp.28, (bf16[2,32,1408]{2,1,0:T(8,128)(2,1)S(1)}, bf16[2,32,64]{2,1,0:T(8,128)(2,1)S(1)}, bf16[2,32,1280]{2,1,0:T(8,128)(2,1)}, ...), branch_computations={%region_9.9_spmd, %region_10.10_spmd, %region_11.11_spmd} | conditional | flops 419430400 | bytes 14639200 | solution.py:335
  563.7 1.7 broadcast_in_dim.109
  565.3 3.5 all-to-all-start.1
  568.9 5.9 all-to-all-done.1.parts_ref
  574.8 7.4 %stage.1 = (bf16[32,1408]{1,0:T(8,128)(2,1)}, bf16[2,32,1408]{2,1,0:T(8,128)(2,1)S(1)}, bf16[2,32,64]{2,1,0:T(8,128)(2,1)S(1)}, bf16[2,32,1280]{2,1,0:T(8,128)(2,1)}) custom-call(s32[3]{0:T(128)S(1)} %pad_add_fusion.place_ref, bf16[4,32,1408]{2,1,0:T(8,128)(2,1)S(1)} %all-to-all-done.1.parts_ref, ...), custom_call_target="tpu_custom_call", output_to_operand_aliasing={{1}: (10, {}), {2}: (11, {}), {3}: (12, {})} | custom-call | flops 419430400 | bytes 13107200 | tf_op jit(solution)/shard_map/while/body/eval_jaxpr/cond/branch_2_fun/stage/pallas_call | solution.py:171
  582.5 16.2 %conditional.13 = (bf16[32,1408]{1,0:T(8,128)(2,1)}) conditional(s32[]{:T(128)} %clamp.27, bf16[32,1408]{1,0:T(8,128)(2,1)} %get-tuple-element.1036, bf16[32,1408]{1,0:T(8,128)(2,1)} %get-tuple-element.1036, bf16[32,1408]{1,0:T(8,128)(2,1)} %get-tuple-element.1036), branch_computations={%region_12.12_spmd, %region_13.13_spmd, %region_14.14_spmd} | conditional | bytes 540720 | solution.py:338
  582.5 1.3 collective-permute-start
  583.8 14.3 %collective-permute-done = bf16[32,1408]{1,0:T(8,128)(2,1)S(1)} collective-permute-done((bf16[32,1408]{1,0:T(8,128)(2,1)}, bf16[32,1408]{1,0:T(8,128)(2,1)S(1)}, u32[]{:S(2)}, u32[]{:S(2)}) %collective-permute-start) | collective-permute-done | bytes 90144 | tf_op jit(solution)/shard_map/while/body/eval_jaxpr/cond/branch_1_fun/ppermute | solution.py:342
  598.1 0.6 copy.49
  598.7 18.6 %conditional.12 = ((bf16[2,32,1408]{2,1,0:T(8,128)(2,1)S(1)}, bf16[2,32,64]{2,1,0:T(8,128)(2,1)S(1)}, bf16[2,32,1280]{2,1,0:T(8,128)(2,1)}, bf16[32,1408]{1,0:T(8,128)(2,1)})) conditional(s32[]{:T(128)} %clamp.28, (bf16[2,32,1408]{2,1,0:T(8,128)(2,1)S(1)}, bf16[2,32,64]{2,1,0:T(8,128)(2,1)S(1)}, bf16[2,32,1280]{2,1,0:T(8,128)(2,1)}, ...), branch_computations={%region_9.9_spmd, %region_10.10_spmd, %region_11.11_spmd} | conditional | flops 419430400 | bytes 14639200 | solution.py:335
  598.7 1.7 broadcast_in_dim.109
  600.4 3.5 all-to-all-start.1
  603.9 5.9 all-to-all-done.1.parts_ref
  609.9 7.4 %stage.1 = (bf16[32,1408]{1,0:T(8,128)(2,1)}, bf16[2,32,1408]{2,1,0:T(8,128)(2,1)S(1)}, bf16[2,32,64]{2,1,0:T(8,128)(2,1)S(1)}, bf16[2,32,1280]{2,1,0:T(8,128)(2,1)}) custom-call(s32[3]{0:T(128)S(1)} %pad_add_fusion.place_ref, bf16[4,32,1408]{2,1,0:T(8,128)(2,1)S(1)} %all-to-all-done.1.parts_ref, ...), custom_call_target="tpu_custom_call", output_to_operand_aliasing={{1}: (10, {}), {2}: (11, {}), {3}: (12, {})} | custom-call | flops 419430400 | bytes 13107200 | tf_op jit(solution)/shard_map/while/body/eval_jaxpr/cond/branch_2_fun/stage/pallas_call | solution.py:171
  617.5 0.9 fusion.14
  618.4 17.7 %all-gather.4 = bf16[256,1408]{1,0:T(8,128)(2,1)S(1)} all-gather(bf16[64,1408]{1,0:T(8,128)(2,1)S(1)} %fusion.14), channel_id=6, replica_groups=mesh['s'=16,'y'=4,'c'=2,'z'=4] {'z'}, dimensions={0}, use_global_device_ids=true | all-gather | bytes 901120 | tf_op jit(solution)/shard_map/all_gather | solution.py:386
  636.1 1.1 fusion.10
  637.3 38.0 %collective-permute-start.9 = (f32[8,16,640]{2,1,0:T(8,128)S(1)}, f32[8,16,640]{2,1,0:T(8,128)}, u32[]{:S(2)}, u32[]{:S(2)}) collective-permute-start(f32[8,16,640]{2,1,0:T(8,128)S(1)} %slice_select_fusion), channel_id=1, source_target_pairs={{0,4},{4,0},{1,5},{5,1},{2,6},{6,2},{3,7},{7,3},{8,12},{12,8},{9,1... | collective-permute-start | bytes 983048 | tf_op jit(solution)/shard_map/ppermute | solution.py:41
  675.4 0.4 reduce_sum.81
  675.8 0.6 broadcast_in_dim.156
  676.4 3.3 all-to-all-start.4
  679.7 1.4 fusion.11
  681.1 3.1 all-to-all-done.4
  684.3 1.0 subtract_convert_fusion
  685.3 3.1 collective-permute-start.7
  688.5 1.9 collective-permute-start.8
  690.4 0.7 maximum_bitcast_fusion
  691.1 1.0 select_add_fusion
  692.1 1.0 select_reduce_fusion
  693.2 1.0 select_reduce_fusion.1
  (140 shorter events, 2.3 us)
Async XLA Ops:
  7.2 16.7 %copy-start = (bf16[1,8,16,5120]{3,2,1,0:T(8,128)(2,1)S(1)}, bf16[1,8,16,5120]{3,2,1,0:T(8,128)(2,1)}, u32[]{:S(2)}) copy-start(bf16[1,8,16,5120]{3,2,1,0:T(8,128)(2,1)} %param.29) | copy-start | bytes 3932164
  7.2 140.2 %all-gather.7.cloned.1.call-start = ((), (), s32[]{:S(2)}) async-start(), calls=%async_computation.5 | async-start | bytes 8192000 | tf_op jit(solution)/shard_map/all_gather | solution.py:225
  10.9 0.7 copy-start.4
  10.9 9.5 %copy-start.3 = (bf16[1,8,640,16]{2,3,1,0:T(8,128)(2,1)S(1)}, bf16[1,8,640,16]{2,3,1,0:T(8,128)(2,1)}, u32[]{:S(2)}) copy-start(bf16[1,8,640,16]{2,3,1,0:T(8,128)(2,1)} %param.28) | copy-start | bytes 491524
  10.9 11.4 %copy-start.2 = (bf16[1,8,16,5120]{3,2,1,0:T(8,128)(2,1)S(1)}, bf16[1,8,16,5120]{3,2,1,0:T(8,128)(2,1)}, u32[]{:S(2)}) copy-start(bf16[1,8,16,5120]{3,2,1,0:T(8,128)(2,1)} %param.24) | copy-start | bytes 3932164
  10.9 11.6 %copy-start.5 = (s32[1,8]{1,0:T(1,128)S(1)}, s32[1,8]{1,0:T(1,128)}, u32[]{:S(2)}) copy-start(s32[1,8]{1,0:T(1,128)} %param.31) | copy-start | bytes 100
  10.9 11.6 %copy-start.6 = (s32[8]{0:T(128)S(1)}, s32[8]{0:T(128)}, u32[]{:S(2)}) copy-start(s32[8]{0:T(128)} %param.30) | copy-start | bytes 100
  11.6 12.9 %collective-permute-start.5 = (f32[1,640]{1,0:T(1,128)S(1)}, f32[1,640]{1,0:T(1,128)S(1)}, u32[]{:S(2)}, u32[]{:S(2)}) collective-permute-start(f32[1,640]{1,0:T(1,128)S(1)} %copy-done.4), channel_id=1, source_target_pairs={{0,4},{4,0},{1,5},{5,1},{2,6},{6,2},{3,7},{7,3},{8,12},{12,8},{9,1... | collective-permute-start | bytes 7688 | tf_op jit(solution)/shard_map/ppermute | solution.py:28
  20.4 7.2 %collective-permute-start.4 = (bf16[8,640,16]{1,2,0:T(8,128)(2,1)S(1)}, bf16[8,640,16]{1,2,0:T(8,128)(2,1)S(1)}, u32[]{:S(2)}, u32[]{:S(2)}) collective-permute-start(bf16[8,640,16]{1,2,0:T(8,128)(2,1)S(1)} %bitcast.111), channel_id=1, source_target_pairs={{0,4},{4,0},{1,5},{5,1},{2,6},{6,2},{3,7},{7,3},{8,12},{12,8},{9,1... | collective-permute-start | bytes 491528 | tf_op jit(solution)/shard_map/ppermute | solution.py:28
  26.2 20.4 %collective-permute-start.3 = (bf16[64,1280]{1,0:T(8,128)(2,1)}, bf16[64,1280]{1,0:T(8,128)(2,1)}, u32[]{:S(2)}, u32[]{:S(2)}) collective-permute-start(bf16[64,1280]{1,0:T(8,128)(2,1)} %get-tuple-element.885), channel_id=1, source_target_pairs={{480,448},{448,416},{416,384},{384,352},{352,320},{320,288},{288,2... | collective-permute-start | bytes 491528 | tf_op jit(solution)/shard_map/ppermute | solution.py:237
  148.1 13.0 %collective-permute-start.6 = (bf16[5120,640]{1,0:T(8,128)(2,1)}, bf16[5120,640]{1,0:T(8,128)(2,1)}, u32[]{:S(2)}, u32[]{:S(2)}) collective-permute-start(bf16[5120,640]{1,0:T(8,128)(2,1)} %all-gather.7.cloned.1.call-done), channel_id=1, source_target_pairs={{0,4},{4,0},{1,5},{5,1},{2,6},{6,2},{3,7},{7,3},{8,12},{12,8},{9,1... | collective-permute-start | bytes 19660808 | tf_op jit(solution)/shard_map/ppermute | solution.py:302
  208.4 354.6 %collective-permute-start = (bf16[32,1408]{1,0:T(8,128)(2,1)}, bf16[32,1408]{1,0:T(8,128)(2,1)S(1)}, u32[]{:S(2)}, u32[]{:S(2)}) collective-permute-start(bf16[32,1408]{1,0:T(8,128)(2,1)} %param.8), channel_id=1, source_target_pairs={{480,448},{416,384},{352,320},{288,256},{224,192},{160,128},{96,64... | collective-permute-start | bytes 270344 | tf_op jit(solution)/shard_map/while/body/eval_jaxpr/cond/branch_1_fun/ppermute | solution.py:342
  565.3 9.5 %all-to-all-start.1 = ((bf16[4,32,1408]{2,1,0:T(8,128)(2,1)}), bf16[4,32,1408]{2,1,0:T(8,128)(2,1)S(1)}, u32[]{:S(2)}, u32[]{:S(2)}) async-start(bf16[4,32,1408]{2,1,0:T(8,128)(2,1)} %broadcast_in_dim.109), calls=%async_computation.1 | async-start | bytes 720896 | tf_op jit(solution)/shard_map/while/body/eval_jaxpr/cond/branch_2_fun/all_to_all | solution.py:46
  582.5 15.6 %collective-permute-start = (bf16[32,1408]{1,0:T(8,128)(2,1)}, bf16[32,1408]{1,0:T(8,128)(2,1)S(1)}, u32[]{:S(2)}, u32[]{:S(2)}) collective-permute-start(bf16[32,1408]{1,0:T(8,128)(2,1)} %param.8), channel_id=1, source_target_pairs={{480,448},{416,384},{352,320},{288,256},{224,192},{160,128},{96,64... | collective-permute-start | bytes 270344 | tf_op jit(solution)/shard_map/while/body/eval_jaxpr/cond/branch_1_fun/ppermute | solution.py:342
  600.4 9.5 %all-to-all-start.1 = ((bf16[4,32,1408]{2,1,0:T(8,128)(2,1)}), bf16[4,32,1408]{2,1,0:T(8,128)(2,1)S(1)}, u32[]{:S(2)}, u32[]{:S(2)}) async-start(bf16[4,32,1408]{2,1,0:T(8,128)(2,1)} %broadcast_in_dim.109), calls=%async_computation.1 | async-start | bytes 720896 | tf_op jit(solution)/shard_map/while/body/eval_jaxpr/cond/branch_2_fun/all_to_all | solution.py:46
  637.3 53.8 %collective-permute-start.9 = (f32[8,16,640]{2,1,0:T(8,128)S(1)}, f32[8,16,640]{2,1,0:T(8,128)}, u32[]{:S(2)}, u32[]{:S(2)}) collective-permute-start(f32[8,16,640]{2,1,0:T(8,128)S(1)} %slice_select_fusion), channel_id=1, source_target_pairs={{0,4},{4,0},{1,5},{5,1},{2,6},{6,2},{3,7},{7,3},{8,12},{12,8},{9,1... | collective-permute-start | bytes 983048 | tf_op jit(solution)/shard_map/ppermute | solution.py:41
  676.4 7.7 %all-to-all-start.4 = ((bf16[4,2,32,128]{3,2,1,0:T(8,128)(2,1)}), bf16[4,2,32,128]{3,2,1,0:T(8,128)(2,1)S(1)}, u32[]{:S(2)}, u32[]{:S(2)}) async-start(bf16[4,2,32,128]{3,2,1,0:T(8,128)(2,1)} %broadcast_in_dim.156), calls=%async_computation.4 | async-start | bytes 131072 | tf_op jit(solution)/shard_map/all_to_all | solution.py:46
  685.3 5.0 collective-permute-start.7
  688.5 4.7 collective-permute-start.8
Sparse Core Ops, SparseCore 0:
  11.1 136.2 all-gather.6

commit v6 on v5

--- a/solution.py
+++ b/solution.py
@@ -296,9 +296,11 @@
 
     kept = lax.cond(sec == 15, top, empty, (out_grads, shard))
 
-    ready = (x_before, x_chunk, inv_chunk, down_chunk, up_chunk, gain_y, kept)
+    boxes_top = lax.ppermute(kept[0], "s", [(15, 14)])
+
+    ready = (x_before, x_chunk, inv_chunk, down_chunk, up_chunk, gain_y, kept, boxes_top)
     w_own, ready = lax.optimization_barrier((w_own, ready))
-    x_before, x_chunk, inv_chunk, down_chunk, up_chunk, gain_y, kept = ready
+    x_before, x_chunk, inv_chunk, down_chunk, up_chunk, gain_y, kept, boxes_top = ready
     w_other = lax.ppermute(w_own, "c", SWAP)
 
     def pick(array, m):
@@ -309,16 +311,15 @@
         t, m = u // CHUNKS, u % CHUNKS
         turn = 15 - t + m
 
-        def stored(args):
-            _, kept = args
-            return pick(kept[0], m), kept
-
         def computed(args):
             box, kept = args
             place = jnp.stack([m, ypos, core]).astype(jnp.int32)
+            parts = lax.cond(
+                sec == 15, lambda box: jnp.zeros((4,) + box.shape, box.dtype), spread, box
+            )
             box, *kept = run_stage(
                 place,
-                spread(box),
+                parts,
                 x_before,
                 up_chunk,
                 down_chunk,
@@ -331,16 +332,19 @@
             )
             return box, tuple(kept)
 
-        kind = jnp.where(sec == turn, jnp.where(sec == 15, 1, 2), 0)
-        box, kept = lax.switch(kind, [lambda args: args, stored, computed], (box, kept))
-        part = ((sec == turn) | (sec == turn - 1)) & (turn >= 1) & (turn <= 15)
+        box, kept = lax.cond(
+            (sec == turn) & (sec < 15), computed, lambda args: args, (box, kept)
+        )
+        part = ((sec == turn) | (sec == turn - 1)) & (turn >= 1) & (turn <= 14)
         kind = jnp.where(part, jnp.where(turn % 2 == 1, 1, 2), 0)
+        kind = jnp.where((turn == 15) & (sec == 14), 3, kind)
         box = lax.switch(
             kind,
             [
                 lambda box: box,
                 lambda box: lax.ppermute(box, "s", ODD),
                 lambda box: lax.ppermute(box, "s", EVEN),
+                lambda box: pick(boxes_top, m),
             ],
             box,
         )
@@ -366,7 +370,9 @@
         sec > 15 - AHEAD, lambda args: extra((h_y, low_part)), lambda args: args, extras
     )
 
-    coef_sum = jnp.sum(spread(boxes[:, :, width:]).astype(f32), axis=(0, -1))[..., None]
+    coefs = spread(boxes[:, :, width:])
+    coefs, low_all, grad_all = lax.optimization_barrier((coefs, low_all, grad_all))
+    coef_sum = jnp.sum(coefs.astype(f32), axis=(0, -1))[..., None]
     new_grads = boxes[:, :, :width].astype(f32) - coef_sum * x_chunk.astype(f32)
     new_grads = new_grads.astype(bf16).reshape(micro, toks, width)
     keep = jnp.where(core == 0, new_grads[:, :, :half], new_grads[:, :, half:])

time: 702 us -> 692 us (0.986)
  waiting for transfers between devices: 496 us -> 453 us
  blocking collectives: 71.7 us -> 111 us
    ppermute x2, waiting for transfers between devices: 368 us -> 336 us  [step(): lax.ppermute(box, 's', ODD)]
    all_gather x1, blocking collectives: 17.7 us -> 39.9 us  [local(): both = lax.all_gather(both, 'z').reshape(4, micro, toks, width + TAIL)]
    all_to_all x1 -> x3, blocking collectives: 13.1 us -> 30.1 us  [spread(): return lax.all_to_all(sent, 'y', 0, 0)]
    all_to_all x3 -> x1, waiting for transfers between devices: 15 us -> 4.1 us  [spread(): return lax.all_to_all(sent, 'y', 0, 0)]
  transfers between devices with their start and end apart: 13 -> 12, of which waited for: 8 -> 6; matrix products, arithmetic and copies ran while one was open for 2% -> 2% of each run, Pallas kernels for 0% -> 0%
where the time goes in v6:
time: 692 us; the launch traced here: 691 us
  waiting for transfers between devices  453 us (65%)
  blocking collectives  111 us (16%)
  starting transfers between devices  63.6 us (9%)
  Pallas kernels  16.3 us (2%)
  local copies, waits for them, and re-layouts  15 us (2%)
  between operations  14.3 us (2%)
  other arithmetic  9.93 us (1%)
    ppermute x2, waiting for transfers between devices, step(): lax.ppermute(box, 's', ODD)  336 us
    all_gather x1, waiting for transfers between devices, local(): w_own = lax.all_gather(shard, 'z', axis=0, tiled=True)  86.8 us
    all_gather x1, blocking collectives, local(): both = lax.all_gather(both, 'z').reshape(4, micro, toks, width + TAIL)  39.9 us
    ppermute x2, starting transfers between devices, half_sum(): return mine + lax.ppermute(theirs, 'c', SWAP)  39.6 us
    all_to_all x3, blocking collectives, spread(): return lax.all_to_all(sent, 'y', 0, 0)  30.1 us
    all_gather x2, blocking collectives, extra(): return (lax.all_gather(h_y, 'z'), lax.all_gather(low_in, 'z'))  28.6 us
    ppermute x1, waiting for transfers between devices, local(): lax.ppermute(x_y, 's', EVERY)  17.5 us
    pallas_call x2, Pallas kernels, run_stage(): pl.pallas_call(functools.partial(stage_kernel, group=cols // 16), in_spec...  16.3 us
  transfers between devices with their start and end apart: 12, of which 6 were waited for; matrix products, arithmetic and copies ran while one was open for 2% of the time, Pallas kernels for 0%

profile of v6, /device:TPU:1, one launch (start us, length us, event | category | flops | bytes accessed | tf_op | source)
XLA Modules:
  0.0 691.1 jit_solution(15329841459186449892)
XLA Ops:
  7.2 3.7 copy.31
  10.9 0.6 copy-done.5
  11.6 8.8 %collective-permute-start.5 = (f32[1,640]{1,0:T(1,128)S(1)}, f32[1,640]{1,0:T(1,128)S(1)}, u32[]{:S(2)}, u32[]{:S(2)}) collective-permute-start(f32[1,640]{1,0:T(1,128)S(1)} %copy-done.5), channel_id=1, source_target_pairs={{0,4},{4,0},{1,5},{5,1},{2,6},{6,2},{3,7},{7,3},{8,12},{12,8},{9,1... | collective-permute-start | bytes 7688 | tf_op jit(solution)/shard_map/ppermute | solution.py:28
  20.4 1.9 collective-permute-start.4
  22.8 0.9 dynamic-slice_bitcast_fusion.2
  23.8 0.6 gather_fusion.1
  24.4 0.6 fusion.20
  25.0 1.7 multiply_convert_fusion
  26.8 0.6 gather_fusion
  27.4 1.4 conditional.8
  27.4 0.7 broadcast.203
  28.1 0.7 broadcast.205
  28.8 1.3 collective-permute-start.6
  30.1 1.3 collective-permute-start.3
  31.5 17.5 %collective-permute-done.3 = bf16[64,1280]{1,0:T(8,128)(2,1)S(1)} collective-permute-done((bf16[64,1280]{1,0:T(8,128)(2,1)S(1)}, bf16[64,1280]{1,0:T(8,128)(2,1)S(1)}, u32[]{:S(2)}, u32[]{:S(2)}) %collective-permute-start.3) | collective-permute-done | bytes 163872 | tf_op jit(solution)/shard_map/ppermute | solution.py:237
  49.0 13.3 %conditional.7 = (bf16[4,2,32,1280]{3,2,1,0:T(8,128)(2,1)}) conditional(s32[]{:T(128)} %convert_element_type.96, bf16[64,1280]{1,0:T(8,128)(2,1)S(1)} %collective-permute-done.3, () %tuple.104), branch_computations={%region_0.0_spmd, %region_1.0_spmd} | conditional | bytes 2129928 | solution.py:233
  49.1 13.2 %all_to_all.21 = bf16[4,64,1280]{2,1,0:T(8,128)(2,1)} all-to-all(bf16[4,64,1280]{2,1,0:T(8,128)(2,1)S(1)} %broadcast_in_dim.94), channel_id=1, replica_groups=mesh['s'=16,'y'=4,'c'=2,'z'=4] {'y'}, dimensions={0} | all-to-all | bytes 1310720 | tf_op jit(solution)/shard_map/cond/branch_0_fun/all_to_all | solution.py:46
  62.3 86.8 %all-gather.7.cloned.1.call-done = bf16[5120,640]{1,0:T(8,128)(2,1)} async-done(((bf16[1280,640]{1,0:T(8,128)(2,1)}), bf16[5120,640]{1,0:T(8,128)(2,1)}) %all-gather.7.cloned.1.call-update) | async-done | bytes 6553616 | tf_op jit(solution)/shard_map/all_gather | solution.py:225
  149.2 2.8 collective-permute-start.7
  152.0 1.1 fusion.15
  153.2 9.3 %collective-permute-done.7 = bf16[5120,640]{1,0:T(8,128)(2,1)} collective-permute-done((bf16[5120,640]{1,0:T(8,128)(2,1)}, bf16[5120,640]{1,0:T(8,128)(2,1)}, u32[]{:S(2)}, u32[]{:S(2)}) %collective-permute-start.7) | collective-permute-done | bytes 6553632 | tf_op jit(solution)/shard_map/ppermute | solution.py:304
  162.5 0.9 broadcast.222
  163.4 0.6 broadcast_in_dim.150
  164.0 0.6 broadcast_in_dim.155
  164.6 420.5 %while.29 = (s32[]{:T(128)}, bf16[32,1408]{1,0:T(8,128)(2,1)}, bf16[2,32,1408]{2,1,0:T(8,128)(2,1)}, bf16[2,32,64]{2,1,0:T(8,128)(2,1)S(1)}, bf16[2,32,1280]{2,1...) while((s32[]{:T(128)}, bf16[32,1408]{1,0:T(8,128)(2,1)}, ...), condition=%wide.region_20.21_spmd, body=%wide.region_8.20_spmd.sunk | while | flops 419431456 | bytes 15655974 | solution.py:367
  168.9 40.6 %conditional.15 = ((bf16[4,64,1280]{2,1,0:T(8,128)(2,1)}, bf16[4,8,8,16]{3,2,1,0:T(8,128)(2,1)})) conditional(s32[]{:T(128)} %convert_element_type.131, (bf16[4,64,1280]{2,1,0:T(8,128)(2,1)}, bf16[4,8,8,16]{3,2,1,0:T(8,128)(2,1)}) %tuple.147, (bf16[64,1280]{1,0:T(8,128)(2,1)}, f32[8,8,16]{2,1,0:T(8,128)S(1)}) %tuple.148), branch_computations={%region_17.17_spmd, %region_18.19_spmd} | conditional | flops 1024 | bytes 835608 | solution.py:351
  168.9 17.6 %all-gather = bf16[256,1280]{1,0:T(8,128)(2,1)} all-gather(bf16[64,1280]{1,0:T(8,128)(2,1)} %get-tuple-element.723), channel_id=2, replica_groups=mesh['s'=16,'y'=4,'c'=2,'z'=4] {'z'}, dimensions={0}, use_global_device_ids=true | all-gather | bytes 819200 | tf_op jit(solution)/shard_map/while/body/eval_jaxpr/cond/branch_1_fun/all_gather | solution.py:255
  186.6 12.0 %psum.12 = bf16[8,8,16]{2,1,0:T(8,128)(2,1)S(1)} all-reduce(f32[8,8,16]{2,1,0:T(8,128)S(1)} %get-tuple-element.724), channel_id=1, replica_groups=mesh['s'=16,'y'=4,'c'=2,'z'=4] {'y'}, use_global_device_ids=true, to_apply=%region_19.18 | all-reduce | flops 1024 | bytes 6144 | tf_op jit(solution)/shard_map/while/body/eval_jaxpr/cond/branch_1_fun/psum | solution.py:254
  198.5 11.0 %all-gather.1 = bf16[32,8,16]{2,1,0:T(8,128)(2,1)} all-gather(bf16[8,8,16]{2,1,0:T(8,128)(2,1)S(1)} %psum.12), channel_id=3, replica_groups=mesh['s'=16,'y'=4,'c'=2,'z'=4] {'z'}, dimensions={0}, use_global_device_ids=true | all-gather | bytes 10240 | tf_op jit(solution)/shard_map/while/body/eval_jaxpr/cond/branch_1_fun/all_gather | solution.py:255
  210.0 323.5 %conditional.14 = (bf16[32,1408]{1,0:T(8,128)(2,1)}) conditional(s32[]{:T(128)} %clamp.15, bf16[32,1408]{1,0:T(8,128)(2,1)} %get-tuple-element.1096, bf16[32,1408]{1,0:T(8,128)(2,1)} %get-tuple-element.1096, bf16[32,1408]{1,0:T(8,128)(2,1)} %get-tuple-element.1096, (s32[]{:T(128)}, ...), branch_computations={%region_13.13_spmd, %region_14.14_spmd, %region_15.15_spmd, %regio... | conditional | flops 3 | bytes 540720 | solution.py:341
  210.1 1.3 collective-permute-start
  211.4 321.5 %collective-permute-done = bf16[32,1408]{1,0:T(8,128)(2,1)S(1)} collective-permute-done((bf16[32,1408]{1,0:T(8,128)(2,1)}, bf16[32,1408]{1,0:T(8,128)(2,1)S(1)}, u32[]{:S(2)}, u32[]{:S(2)}) %collective-permute-start) | collective-permute-done | bytes 90144 | tf_op jit(solution)/shard_map/while/body/eval_jaxpr/cond/branch_1_fun/ppermute | solution.py:345
  532.9 0.6 copy.47
  533.5 17.6 %conditional.13 = ((bf16[2,32,1408]{2,1,0:T(8,128)(2,1)}, bf16[2,32,64]{2,1,0:T(8,128)(2,1)S(1)}, bf16[2,32,1280]{2,1,0:T(8,128)(2,1)}, bf16[32,1408]{1,0:T(8,128)(2,1)})) conditional(s32[]{:T(128)} %convert_element_type.130, (bf16[2,32,1408]{2,1,0:T(8,128)(2,1)}, bf16[2,32,64]{2,1,0:T(8,128)(2,1)S(1)}, bf16[2,32,1280]{2,1,0:T(8,128)(2,1)}, ...), branch_computations={%region_9.9_spmd, %region_10.12_spmd} | conditional | flops 419430400 | bytes 14278742 | solution.py:335
  533.5 9.4 %conditional = (bf16[4,32,1408]{2,1,0:T(8,128)(2,1)S(1)}) conditional(s32[]{:T(128)} %convert_element_type.82, bf16[32,1408]{1,0:T(8,128)(2,1)} %get-tuple-element.705, () %tuple.84), branch_computations={%region_11.10_spmd, %region_12.11_spmd} | conditional | bytes 1171464 | solution.py:317
  533.5 0.9 broadcast_in_dim.109
  534.4 8.4 %all_to_all.22 = bf16[4,32,1408]{2,1,0:T(8,128)(2,1)S(1)} all-to-all(bf16[4,32,1408]{2,1,0:T(8,128)(2,1)S(1)} %broadcast_in_dim.109), channel_id=1, replica_groups=mesh['s'=16,'y'=4,'c'=2,'z'=4] {'y'}, dimensions={0} | all-to-all | bytes 720896 | tf_op jit(solution)/shard_map/while/body/eval_jaxpr/cond/branch_1_fun/cond/branch_0_fun/all_to_all | solution.py:46
  542.9 8.1 %stage.1 = (bf16[32,1408]{1,0:T(8,128)(2,1)}, bf16[2,32,1408]{2,1,0:T(8,128)(2,1)}, bf16[2,32,64]{2,1,0:T(8,128)(2,1)S(1)}, bf16[2,32,1280]{2,1,0:T(8,128)(2,1)}) custom-call(s32[3]{0:T(128)S(1)} %pad_add_fusion.place_ref, bf16[4,32,1408]{2,1,0:T(8,128)(2,1)S(1)} %get-tuple-element.1219.parts_ref, ...), custom_call_target="tpu_custom_call", output_to_operand_aliasing={{1}: (10, {}), {2}: (11, {}), {3}: (12, {})} | custom-call | flops 419430400 | bytes 13107200 | tf_op jit(solution)/shard_map/while/body/eval_jaxpr/cond/branch_1_fun/stage/pallas_call | solution.py:171
  551.3 16.1 %conditional.14 = (bf16[32,1408]{1,0:T(8,128)(2,1)}) conditional(s32[]{:T(128)} %clamp.15, bf16[32,1408]{1,0:T(8,128)(2,1)} %get-tuple-element.1096, bf16[32,1408]{1,0:T(8,128)(2,1)} %get-tuple-element.1096, bf16[32,1408]{1,0:T(8,128)(2,1)} %get-tuple-element.1096, (s32[]{:T(128)}, ...), branch_computations={%region_13.13_spmd, %region_14.14_spmd, %region_15.15_spmd, %regio... | conditional | flops 3 | bytes 540720 | solution.py:341
  551.4 1.3 collective-permute-start
  552.6 14.1 %collective-permute-done = bf16[32,1408]{1,0:T(8,128)(2,1)S(1)} collective-permute-done((bf16[32,1408]{1,0:T(8,128)(2,1)}, bf16[32,1408]{1,0:T(8,128)(2,1)S(1)}, u32[]{:S(2)}, u32[]{:S(2)}) %collective-permute-start) | collective-permute-done | bytes 90144 | tf_op jit(solution)/shard_map/while/body/eval_jaxpr/cond/branch_1_fun/ppermute | solution.py:345
  566.8 0.6 copy.47
  567.4 17.6 %conditional.13 = ((bf16[2,32,1408]{2,1,0:T(8,128)(2,1)}, bf16[2,32,64]{2,1,0:T(8,128)(2,1)S(1)}, bf16[2,32,1280]{2,1,0:T(8,128)(2,1)}, bf16[32,1408]{1,0:T(8,128)(2,1)})) conditional(s32[]{:T(128)} %convert_element_type.130, (bf16[2,32,1408]{2,1,0:T(8,128)(2,1)}, bf16[2,32,64]{2,1,0:T(8,128)(2,1)S(1)}, bf16[2,32,1280]{2,1,0:T(8,128)(2,1)}, ...), branch_computations={%region_9.9_spmd, %region_10.12_spmd} | conditional | flops 419430400 | bytes 14278742 | solution.py:335
  567.4 9.4 %conditional = (bf16[4,32,1408]{2,1,0:T(8,128)(2,1)S(1)}) conditional(s32[]{:T(128)} %convert_element_type.82, bf16[32,1408]{1,0:T(8,128)(2,1)} %get-tuple-element.705, () %tuple.84), branch_computations={%region_11.10_spmd, %region_12.11_spmd} | conditional | bytes 1171464 | solution.py:317
  567.4 0.9 broadcast_in_dim.109
  568.3 8.4 %all_to_all.22 = bf16[4,32,1408]{2,1,0:T(8,128)(2,1)S(1)} all-to-all(bf16[4,32,1408]{2,1,0:T(8,128)(2,1)S(1)} %broadcast_in_dim.109), channel_id=1, replica_groups=mesh['s'=16,'y'=4,'c'=2,'z'=4] {'y'}, dimensions={0} | all-to-all | bytes 720896 | tf_op jit(solution)/shard_map/while/body/eval_jaxpr/cond/branch_1_fun/cond/branch_0_fun/all_to_all | solution.py:46
  576.8 8.1 %stage.1 = (bf16[32,1408]{1,0:T(8,128)(2,1)}, bf16[2,32,1408]{2,1,0:T(8,128)(2,1)}, bf16[2,32,64]{2,1,0:T(8,128)(2,1)S(1)}, bf16[2,32,1280]{2,1,0:T(8,128)(2,1)}) custom-call(s32[3]{0:T(128)S(1)} %pad_add_fusion.place_ref, bf16[4,32,1408]{2,1,0:T(8,128)(2,1)S(1)} %get-tuple-element.1219.parts_ref, ...), custom_call_target="tpu_custom_call", output_to_operand_aliasing={{1}: (10, {}), {2}: (11, {}), {3}: (12, {})} | custom-call | flops 419430400 | bytes 13107200 | tf_op jit(solution)/shard_map/while/body/eval_jaxpr/cond/branch_1_fun/stage/pallas_call | solution.py:171
  585.1 0.7 slice.45
  585.8 0.6 broadcast_in_dim.156
  586.5 3.3 all-to-all-start.4
  589.7 0.6 iota_compare_fusion.4
  590.4 4.1 all-to-all-done.4
  594.5 0.9 fusion.14
  595.4 39.9 %all-gather.4 = bf16[256,1408]{1,0:T(8,128)(2,1)S(1)} all-gather(bf16[64,1408]{1,0:T(8,128)(2,1)S(1)} %fusion.14), channel_id=6, replica_groups=mesh['s'=16,'y'=4,'c'=2,'z'=4] {'z'}, dimensions={0}, use_global_device_ids=true | all-gather | bytes 901120 | tf_op jit(solution)/shard_map/all_gather | solution.py:392
  635.7 37.2 %collective-permute-start.10 = (f32[8,16,640]{2,1,0:T(8,128)S(1)}, f32[8,16,640]{2,1,0:T(8,128)}, u32[]{:S(2)}, u32[]{:S(2)}) collective-permute-start(f32[8,16,640]{2,1,0:T(8,128)S(1)} %slice_select_fusion), channel_id=1, source_target_pairs={{0,4},{4,0},{1,5},{5,1},{2,6},{6,2},{3,7},{7,3},{8,12},{12,8},{9,1... | collective-permute-start | bytes 983048 | tf_op jit(solution)/shard_map/ppermute | solution.py:41
  673.1 0.4 reduce_sum.81
  673.6 1.0 subtract_convert_fusion
  674.6 1.9 collective-permute-start.8
  676.6 1.4 fusion.11
  678.0 2.4 collective-permute-start.9
  680.4 0.7 maximum_bitcast_fusion
  681.1 1.0 select_add_fusion
  682.2 1.0 select_reduce_fusion
  683.2 1.0 select_reduce_fusion.1
  (146 shorter events, 3.5 us)
Async XLA Ops:
  7.2 16.6 %copy-start = (bf16[1,8,16,5120]{3,2,1,0:T(8,128)(2,1)S(1)}, bf16[1,8,16,5120]{3,2,1,0:T(8,128)(2,1)}, u32[]{:S(2)}) copy-start(bf16[1,8,16,5120]{3,2,1,0:T(8,128)(2,1)} %param.31) | copy-start | bytes 3932164
  7.2 141.9 %all-gather.7.cloned.1.call-start = ((), (), s32[]{:S(2)}) async-start(), calls=%async_computation.5 | async-start | bytes 8192000 | tf_op jit(solution)/shard_map/all_gather | solution.py:225
  10.9 0.7 copy-start.5
  10.9 9.5 %copy-start.4 = (bf16[1,8,640,16]{2,3,1,0:T(8,128)(2,1)S(1)}, bf16[1,8,640,16]{2,3,1,0:T(8,128)(2,1)}, u32[]{:S(2)}) copy-start(bf16[1,8,640,16]{2,3,1,0:T(8,128)(2,1)} %param.30) | copy-start | bytes 491524
  10.9 11.4 %copy-start.2 = (bf16[1,8,16,5120]{3,2,1,0:T(8,128)(2,1)S(1)}, bf16[1,8,16,5120]{3,2,1,0:T(8,128)(2,1)}, u32[]{:S(2)}) copy-start(bf16[1,8,16,5120]{3,2,1,0:T(8,128)(2,1)} %param.26) | copy-start | bytes 3932164
  10.9 11.6 %copy-start.6 = (s32[1,8]{1,0:T(1,128)S(1)}, s32[1,8]{1,0:T(1,128)}, u32[]{:S(2)}) copy-start(s32[1,8]{1,0:T(1,128)} %param.33) | copy-start | bytes 100
  10.9 11.6 %copy-start.7 = (s32[8]{0:T(128)S(1)}, s32[8]{0:T(128)}, u32[]{:S(2)}) copy-start(s32[8]{0:T(128)} %param.32) | copy-start | bytes 100
  11.6 12.8 %collective-permute-start.5 = (f32[1,640]{1,0:T(1,128)S(1)}, f32[1,640]{1,0:T(1,128)S(1)}, u32[]{:S(2)}, u32[]{:S(2)}) collective-permute-start(f32[1,640]{1,0:T(1,128)S(1)} %copy-done.5), channel_id=1, source_target_pairs={{0,4},{4,0},{1,5},{5,1},{2,6},{6,2},{3,7},{7,3},{8,12},{12,8},{9,1... | collective-permute-start | bytes 7688 | tf_op jit(solution)/shard_map/ppermute | solution.py:28
  20.4 6.4 collective-permute-start.4
  22.7 1.0 copy-start.8
  28.8 33.5 %collective-permute-start.6 = (bf16[2,32,1408]{2,1,0:T(8,128)(2,1)}, bf16[2,32,1408]{2,1,0:T(8,128)(2,1)}, u32[]{:S(2)}, u32[]{:S(2)}) collective-permute-start(bf16[2,32,1408]{2,1,0:T(8,128)(2,1)} %get-tuple-element.1122), channel_id=1, source_target_pairs={{480,448},{481,449},{482,450},{483,451},{484,452},{485,453},{486,4... | collective-permute-start | bytes 540680 | tf_op jit(solution)/shard_map/ppermute | solution.py:299
  30.1 18.9 %collective-permute-start.3 = (bf16[64,1280]{1,0:T(8,128)(2,1)S(1)}, bf16[64,1280]{1,0:T(8,128)(2,1)S(1)}, u32[]{:S(2)}, u32[]{:S(2)}) collective-permute-start(bf16[64,1280]{1,0:T(8,128)(2,1)S(1)} %get-tuple-element.933), channel_id=1, source_target_pairs={{480,448},{448,416},{416,384},{384,352},{352,320},{320,288},{288,2... | collective-permute-start | bytes 491528 | tf_op jit(solution)/shard_map/ppermute | solution.py:237
  149.2 13.3 %collective-permute-start.7 = (bf16[5120,640]{1,0:T(8,128)(2,1)}, bf16[5120,640]{1,0:T(8,128)(2,1)}, u32[]{:S(2)}, u32[]{:S(2)}) collective-permute-start(bf16[5120,640]{1,0:T(8,128)(2,1)} %all-gather.7.cloned.1.call-done), channel_id=1, source_target_pairs={{0,4},{4,0},{1,5},{5,1},{2,6},{6,2},{3,7},{7,3},{8,12},{12,8},{9,1... | collective-permute-start | bytes 19660808 | tf_op jit(solution)/shard_map/ppermute | solution.py:304
  210.1 322.8 %collective-permute-start = (bf16[32,1408]{1,0:T(8,128)(2,1)}, bf16[32,1408]{1,0:T(8,128)(2,1)S(1)}, u32[]{:S(2)}, u32[]{:S(2)}) collective-permute-start(bf16[32,1408]{1,0:T(8,128)(2,1)} %param.9), channel_id=1, source_target_pairs={{480,448},{416,384},{352,320},{288,256},{224,192},{160,128},{96,64... | collective-permute-start | bytes 270344 | tf_op jit(solution)/shard_map/while/body/eval_jaxpr/cond/branch_1_fun/ppermute | solution.py:345
  551.4 15.4 %collective-permute-start = (bf16[32,1408]{1,0:T(8,128)(2,1)}, bf16[32,1408]{1,0:T(8,128)(2,1)S(1)}, u32[]{:S(2)}, u32[]{:S(2)}) collective-permute-start(bf16[32,1408]{1,0:T(8,128)(2,1)} %param.9), channel_id=1, source_target_pairs={{480,448},{416,384},{352,320},{288,256},{224,192},{160,128},{96,64... | collective-permute-start | bytes 270344 | tf_op jit(solution)/shard_map/while/body/eval_jaxpr/cond/branch_1_fun/ppermute | solution.py:345
  586.5 8.0 %all-to-all-start.4 = ((bf16[4,2,32,128]{3,2,1,0:T(8,128)(2,1)}), bf16[4,2,32,128]{3,2,1,0:T(8,128)(2,1)S(1)}, u32[]{:S(2)}, u32[]{:S(2)}) async-start(bf16[4,2,32,128]{3,2,1,0:T(8,128)(2,1)} %broadcast_in_dim.156), calls=%async_computation.4 | async-start | bytes 131072 | tf_op jit(solution)/shard_map/all_to_all | solution.py:46
  590.4 45.0 %copy-start.3 = (bf16[4,8,8,16]{3,2,1,0:T(8,128)(2,1)S(1)}, bf16[4,8,8,16]{3,2,1,0:T(8,128)(2,1)}, u32[]{:S(2)}) copy-start(bf16[4,8,8,16]{3,2,1,0:T(8,128)(2,1)} %get-tuple-element.807) | copy-start | bytes 24580
  635.7 45.4 %collective-permute-start.10 = (f32[8,16,640]{2,1,0:T(8,128)S(1)}, f32[8,16,640]{2,1,0:T(8,128)}, u32[]{:S(2)}, u32[]{:S(2)}) collective-permute-start(f32[8,16,640]{2,1,0:T(8,128)S(1)} %slice_select_fusion), channel_id=1, source_target_pairs={{0,4},{4,0},{1,5},{5,1},{2,6},{6,2},{3,7},{7,3},{8,12},{12,8},{9,1... | collective-permute-start | bytes 983048 | tf_op jit(solution)/shard_map/ppermute | solution.py:41
  674.6 5.8 collective-permute-start.8
  678.0 5.2 collective-permute-start.9
Sparse Core Ops, SparseCore 0:
  11.1 138.0 all-gather.6

commit v7 on v6

--- a/solution.py
+++ b/solution.py
@@ -19,7 +19,6 @@
 bf16 = jnp.bfloat16
 contract_last = (((1,), (1,)), ((), ()))
 contract_inner = (((1,), (0,)), ((), ()))
-TOP_SWAP = [(30, 31), (31, 30)]
 AHEAD = 3
 
 
@@ -260,47 +259,19 @@
     down_chunk = down_sel.transpose(0, 2, 1).reshape(CHUNKS, group * rank, width)
     up_chunk = up_sel.reshape(CHUNKS, group * rank, width_all)
 
-    def top(args):
-        out_grads, shard = args
-        shard_x = lax.ppermute(shard, ("s", "c"), TOP_SWAP)
-        grad = lax.dynamic_slice_in_dim(out_grads, core * toks, toks, 1)
-        low = jnp.einsum("mtd,mrd->mtr", grad, up_sel, preferred_element_type=f32).astype(bf16)
-        adapt = jnp.einsum("mtr,mdr->mtd", low, down_sel, preferred_element_type=f32)
-        grad = grad.reshape(rows_all, width_all)
-        blocks = jnp.stack([grad[:, i * width : (i + 1) * width] for i in range(4)])
-        blocks = lax.all_to_all(blocks, "z", 0, 0).reshape(4 * rows_all, width)
-        mine, theirs = (
-            lax.dot_general(blocks, w, contract_inner, preferred_element_type=f32).astype(bf16)
-            for w in (shard, shard_x)
-        )
-        terms = jnp.concatenate(
-            [jnp.where(core == 0, mine, theirs), jnp.where(core == 0, theirs, mine)], 1
-        )
-        terms = lax.all_to_all(terms.reshape(4, rows_all, width), "z", 0, 0)
-        total = jnp.sum(terms.astype(f32), axis=0)
-        total = total + low_rank_scale * adapt.reshape(rows_all, width)
-        grad_y = lax.dynamic_slice_in_dim(grad, ypos * width, width, 1)
-        sent, tail = message(total, grad_y, gain_y, inv_rms, x_y, width_all)
-        boxes = jnp.concatenate([sent, tail], 1).reshape(CHUNKS, rows, width + TAIL)
-        member = jnp.arange(rows_all)[:, None] // toks % group == jnp.arange(group)[None, :]
-        low = jnp.where(member[:, :, None], low.reshape(rows_all, 1, rank), 0)
-        low = low.astype(bf16).reshape(CHUNKS, rows, group * rank)
-        return boxes, low, grad_y.reshape(CHUNKS, rows, width)
-
-    def empty(args):
-        return (
-            jnp.zeros((CHUNKS, rows, width + TAIL), bf16),
-            jnp.zeros((CHUNKS, rows, group * rank), bf16),
-            jnp.zeros((CHUNKS, rows, width), bf16),
-        )
-
-    kept = lax.cond(sec == 15, top, empty, (out_grads, shard))
-
-    boxes_top = lax.ppermute(kept[0], "s", [(15, 14)])
-
-    ready = (x_before, x_chunk, inv_chunk, down_chunk, up_chunk, gain_y, kept, boxes_top)
+    grads_top = lax.dynamic_slice_in_dim(out_grads, core * toks, toks, 1)
+    grads_top = grads_top.reshape(CHUNKS, rows, width_all)
+    grads_top = jnp.stack([grads_top[:, :, i * width : (i + 1) * width] for i in range(4)], 1)
+    grads_top = jnp.pad(grads_top, ((0, 0), (0, 0), (0, 0), (0, TAIL)))
+    kept = (
+        jnp.zeros((CHUNKS, rows, width + TAIL), bf16),
+        jnp.zeros((CHUNKS, rows, group * rank), bf16),
+        jnp.zeros((CHUNKS, rows, width), bf16),
+    )
+
+    ready = (x_before, x_chunk, inv_chunk, down_chunk, up_chunk, gain_y, kept, grads_top)
     w_own, ready = lax.optimization_barrier((w_own, ready))
-    x_before, x_chunk, inv_chunk, down_chunk, up_chunk, gain_y, kept, boxes_top = ready
+    x_before, x_chunk, inv_chunk, down_chunk, up_chunk, gain_y, kept, grads_top = ready
     w_other = lax.ppermute(w_own, "c", SWAP)
 
     def pick(array, m):
@@ -314,9 +285,7 @@
         def computed(args):
             box, kept = args
             place = jnp.stack([m, ypos, core]).astype(jnp.int32)
-            parts = lax.cond(
-                sec == 15, lambda box: jnp.zeros((4,) + box.shape, box.dtype), spread, box
-            )
+            parts = lax.cond(sec == 15, lambda box: pick(grads_top, m), spread, box)
             box, *kept = run_stage(
                 place,
                 parts,
@@ -332,19 +301,15 @@
             )
             return box, tuple(kept)
 
-        box, kept = lax.cond(
-            (sec == turn) & (sec < 15), computed, lambda args: args, (box, kept)
-        )
-        part = ((sec == turn) | (sec == turn - 1)) & (turn >= 1) & (turn <= 14)
+        box, kept = lax.cond(sec == turn, computed, lambda args: args, (box, kept))
+        part = ((sec == turn) | (sec == turn - 1)) & (turn >= 1) & (turn <= 15)
         kind = jnp.where(part, jnp.where(turn % 2 == 1, 1, 2), 0)
-        kind = jnp.where((turn == 15) & (sec == 14), 3, kind)
         box = lax.switch(
             kind,
             [
                 lambda box: box,
                 lambda box: lax.ppermute(box, "s", ODD),
                 lambda box: lax.ppermute(box, "s", EVEN),
-                lambda box: pick(boxes_top, m),
             ],
             box,
         )

time: 692 us -> 680 us (0.983)
  blocking collectives: 111 us -> 82.8 us
  waiting for transfers between devices: 453 us -> 467 us
    all_gather x1, blocking collectives: 39.9 us -> 12.9 us  [local(): both = lax.all_gather(both, 'z').reshape(4, micro, toks, width + TAIL)]
    ppermute x2, waiting for transfers between devices: 336 us -> 350 us  [step(): lax.ppermute(box, 's', ODD)]
  transfers between devices with their start and end apart: 12 -> 11, of which waited for: 6 -> 6; matrix products, arithmetic and copies ran while one was open for 2% -> 2% of each run, Pallas kernels for 0% -> 0%
where the time goes in v7:
time: 680 us; the launch traced here: 678 us
  waiting for transfers between devices  467 us (69%)
  blocking collectives  82.8 us (12%)
  starting transfers between devices  62 us (9%)
  local copies, waits for them, and re-layouts  17.6 us (3%)
  Pallas kernels  16.3 us (2%)
  between operations  14.4 us (2%)
  other arithmetic  12 us (2%)
    ppermute x2, waiting for transfers between devices, step(): lax.ppermute(box, 's', ODD)  350 us
    all_gather x1, waiting for transfers between devices, local(): w_own = lax.all_gather(shard, 'z', axis=0, tiled=True)  86.7 us
    ppermute x2, starting transfers between devices, half_sum(): return mine + lax.ppermute(theirs, 'c', SWAP)  39.8 us
    all_to_all x3, blocking collectives, spread(): return lax.all_to_all(sent, 'y', 0, 0)  30 us
    all_gather x2, blocking collectives, extra(): return (lax.all_gather(h_y, 'z'), lax.all_gather(low_in, 'z'))  27.6 us
    ppermute x1, waiting for transfers between devices, local(): lax.ppermute(x_y, 's', EVERY)  17.4 us
    pallas_call x2, Pallas kernels, run_stage(): pl.pallas_call(functools.partial(stage_kernel, group=cols // 16), in_spec...  16.3 us
  transfers between devices with their start and end apart: 11, of which 6 were waited for; matrix products, arithmetic and copies ran while one was open for 2% of the time, Pallas kernels for 0%

profile of v7, /device:TPU:1, one launch (start us, length us, event | category | flops | bytes accessed | tf_op | source)
XLA Modules:
  0.0 678.4 jit_solution(18350973930405510004)
XLA Ops:
  7.2 3.7 copy.34
  10.9 0.6 copy-done.6
  11.6 8.8 %collective-permute-start.4 = (f32[1,640]{1,0:T(1,128)S(1)}, f32[1,640]{1,0:T(1,128)S(1)}, u32[]{:S(2)}, u32[]{:S(2)}) collective-permute-start(f32[1,640]{1,0:T(1,128)S(1)} %copy-done.6), channel_id=1, source_target_pairs={{0,4},{4,0},{1,5},{5,1},{2,6},{6,2},{3,7},{7,3},{8,12},{12,8},{9,1... | collective-permute-start | bytes 7688 | tf_op jit(solution)/shard_map/ppermute | solution.py:27
  20.4 1.9 collective-permute-start.3
  22.7 1.1 constant_dynamic-slice_fusion
  23.9 0.9 fusion.8
  25.1 0.6 gather_fusion.1
  26.4 0.7 multiply_convert_fusion
  27.0 1.3 collective-permute-start.2
  28.3 1.0 broadcast_select_fusion.1
  30.0 17.4 %collective-permute-done.2 = bf16[64,1280]{1,0:T(8,128)(2,1)} collective-permute-done((bf16[64,1280]{1,0:T(8,128)(2,1)}, bf16[64,1280]{1,0:T(8,128)(2,1)}, u32[]{:S(2)}, u32[]{:S(2)}) %collective-permute-start.2) | collective-permute-done | bytes 163872 | tf_op jit(solution)/shard_map/ppermute | solution.py:236
  47.4 14.1 %conditional.6 = (bf16[4,2,32,1280]{3,2,1,0:T(8,128)(2,1)}) conditional(s32[]{:T(128)} %convert_element_type.65, bf16[64,1280]{1,0:T(8,128)(2,1)} %collective-permute-done.2, () %tuple.93), branch_computations={%region_0.0_spmd, %region_1.0_spmd} | conditional | bytes 2129928 | solution.py:232
  47.4 1.0 broadcast_in_dim.51
  48.4 13.1 %all_to_all.13 = bf16[4,64,1280]{2,1,0:T(8,128)(2,1)} all-to-all(bf16[4,64,1280]{2,1,0:T(8,128)(2,1)S(1)} %broadcast_in_dim.51), channel_id=1, replica_groups=mesh['s'=16,'y'=4,'c'=2,'z'=4] {'y'}, dimensions={0} | all-to-all | bytes 1310720 | tf_op jit(solution)/shard_map/cond/branch_0_fun/all_to_all | solution.py:45
  61.5 86.7 %all-gather.7.cloned.1.call-done = bf16[5120,640]{1,0:T(8,128)(2,1)} async-done(((bf16[1280,640]{1,0:T(8,128)(2,1)}), bf16[5120,640]{1,0:T(8,128)(2,1)}) %all-gather.7.cloned.1.call-update) | async-done | bytes 6553616 | tf_op jit(solution)/shard_map/all_gather | solution.py:224
  148.3 2.4 collective-permute-start.5
  150.9 10.3 %collective-permute-done.5 = bf16[5120,640]{1,0:T(8,128)(2,1)} collective-permute-done((bf16[5120,640]{1,0:T(8,128)(2,1)}, bf16[5120,640]{1,0:T(8,128)(2,1)}, u32[]{:S(2)}, u32[]{:S(2)}) %collective-permute-start.5) | collective-permute-done | bytes 6553632 | tf_op jit(solution)/shard_map/ppermute | solution.py:275
  161.2 0.7 broadcast_in_dim.118
  161.9 0.7 broadcast_in_dim.120
  162.5 0.9 broadcast.79
  163.4 0.6 broadcast_in_dim.113
  164.1 0.6 broadcast_in_dim.121
  164.7 432.9 %while.29 = (s32[]{:T(128)}, bf16[32,1408]{1,0:T(8,128)(2,1)}, bf16[2,32,1408]{2,1,0:T(8,128)(2,1)}, bf16[2,32,64]{2,1,0:T(8,128)(2,1)S(1)}, bf16[2,32,1280]{2,1...) while((s32[]{:T(128)}, bf16[32,1408]{1,0:T(8,128)(2,1)}, ...), condition=%wide.region_15.16_spmd, body=%wide.region_4.15_spmd.sunk | while | flops 419431456 | bytes 15655922 | solution.py:332
  168.3 39.9 %conditional.13 = ((bf16[4,64,1280]{2,1,0:T(8,128)(2,1)}, bf16[4,8,8,16]{3,2,1,0:T(8,128)(2,1)})) conditional(s32[]{:T(128)} %convert_element_type.84, (bf16[4,64,1280]{2,1,0:T(8,128)(2,1)}, bf16[4,8,8,16]{3,2,1,0:T(8,128)(2,1)}) %tuple.124, (bf16[64,1280]{1,0:T(8,128)(2,1)S(1)}, f32[8,8,16]{2,1,0:T(8,128)S(1)}) %tuple.125), branch_computations={%region_12.12_spmd, %region_13.14_spmd} | conditional | flops 1024 | bytes 835608 | solution.py:316
  168.4 16.6 %all-gather = bf16[256,1280]{1,0:T(8,128)(2,1)} all-gather(bf16[64,1280]{1,0:T(8,128)(2,1)S(1)} %get-tuple-element.677), channel_id=2, replica_groups=mesh['s'=16,'y'=4,'c'=2,'z'=4] {'z'}, dimensions={0}, use_global_device_ids=true | all-gather | bytes 819200 | tf_op jit(solution)/shard_map/while/body/eval_jaxpr/cond/branch_1_fun/all_gather | solution.py:254
  184.9 12.3 %psum.12 = bf16[8,8,16]{2,1,0:T(8,128)(2,1)S(1)} all-reduce(f32[8,8,16]{2,1,0:T(8,128)S(1)} %get-tuple-element.678), channel_id=1, replica_groups=mesh['s'=16,'y'=4,'c'=2,'z'=4] {'y'}, use_global_device_ids=true, to_apply=%region_14.13 | all-reduce | flops 1024 | bytes 6144 | tf_op jit(solution)/shard_map/while/body/eval_jaxpr/cond/branch_1_fun/psum | solution.py:253
  197.3 11.0 %all-gather.1 = bf16[32,8,16]{2,1,0:T(8,128)(2,1)} all-gather(bf16[8,8,16]{2,1,0:T(8,128)(2,1)S(1)} %psum.12), channel_id=3, replica_groups=mesh['s'=16,'y'=4,'c'=2,'z'=4] {'z'}, dimensions={0}, use_global_device_ids=true | all-gather | bytes 10240 | tf_op jit(solution)/shard_map/while/body/eval_jaxpr/cond/branch_1_fun/all_gather | solution.py:254
  208.6 338.9 %conditional.12 = (bf16[32,1408]{1,0:T(8,128)(2,1)}) conditional(s32[]{:T(128)} %clamp.15, bf16[32,1408]{1,0:T(8,128)(2,1)} %get-tuple-element.946, bf16[32,1408]{1,0:T(8,128)(2,1)} %get-tuple-element.946, bf16[32,1408]{1,0:T(8,128)(2,1)} %get-tuple-element.946), branch_computations={%region_9.9_spmd, %region_10.10_spmd, %region_11.11_spmd} | conditional | bytes 540720 | solution.py:307
  208.6 1.3 collective-permute-start
  209.9 337.0 %collective-permute-done = bf16[32,1408]{1,0:T(8,128)(2,1)S(1)} collective-permute-done((bf16[32,1408]{1,0:T(8,128)(2,1)}, bf16[32,1408]{1,0:T(8,128)(2,1)S(1)}, u32[]{:S(2)}, u32[]{:S(2)}) %collective-permute-start) | collective-permute-done | bytes 90144 | tf_op jit(solution)/shard_map/while/body/eval_jaxpr/cond/branch_1_fun/ppermute | solution.py:311
  546.9 0.6 copy.52
  547.5 17.6 %conditional.11 = ((bf16[2,32,1408]{2,1,0:T(8,128)(2,1)}, bf16[2,32,64]{2,1,0:T(8,128)(2,1)S(1)}, bf16[2,32,1280]{2,1,0:T(8,128)(2,1)}, bf16[32,1408]{1,0:T(8,128)(2,1)})) conditional(s32[]{:T(128)} %convert_element_type.83, (bf16[2,32,1408]{2,1,0:T(8,128)(2,1)}, bf16[2,32,64]{2,1,0:T(8,128)(2,1)S(1)}, bf16[2,32,1280]{2,1,0:T(8,128)(2,1)}, ...), branch_computations={%region_5.5_spmd, %region_6.8_spmd} | conditional | flops 419430400 | bytes 14278758 | solution.py:304
  547.5 9.4 %conditional = (bf16[4,32,1408]{2,1,0:T(8,128)(2,1)S(1)}) conditional(s32[]{:T(128)} %convert_element_type.51, bf16[32,1408]{1,0:T(8,128)(2,1)} %get-tuple-element.660, (s32[]{:T(128)}, bf16[2,4,32,1408]{3,2,1,0:T(8,128)(2,1)}) %tuple.76), branch_computations={%region_7.6_spmd, %region_8.7_spmd} | conditional | flops 3 | bytes 1171464 | solution.py:288
  547.5 0.9 broadcast_in_dim.52
  548.5 8.4 %all_to_all.14 = bf16[4,32,1408]{2,1,0:T(8,128)(2,1)S(1)} all-to-all(bf16[4,32,1408]{2,1,0:T(8,128)(2,1)S(1)} %broadcast_in_dim.52), channel_id=1, replica_groups=mesh['s'=16,'y'=4,'c'=2,'z'=4] {'y'}, dimensions={0} | all-to-all | bytes 720896 | tf_op jit(solution)/shard_map/while/body/eval_jaxpr/cond/branch_1_fun/cond/branch_0_fun/all_to_all | solution.py:45
  557.0 8.1 %stage.1 = (bf16[32,1408]{1,0:T(8,128)(2,1)}, bf16[2,32,1408]{2,1,0:T(8,128)(2,1)}, bf16[2,32,64]{2,1,0:T(8,128)(2,1)S(1)}, bf16[2,32,1280]{2,1,0:T(8,128)(2,1)}) custom-call(s32[3]{0:T(128)S(1)} %pad_add_fusion.place_ref, bf16[4,32,1408]{2,1,0:T(8,128)(2,1)S(1)} %get-tuple-element.1051.parts_ref, ...), custom_call_target="tpu_custom_call", output_to_operand_aliasing={{1}: (10, {}), {2}: (11, {}), {3}: (12, {})} | custom-call | flops 419430400 | bytes 13107200 | tf_op jit(solution)/shard_map/while/body/eval_jaxpr/cond/branch_1_fun/stage/pallas_call | solution.py:170
  565.3 14.6 %conditional.12 = (bf16[32,1408]{1,0:T(8,128)(2,1)}) conditional(s32[]{:T(128)} %clamp.15, bf16[32,1408]{1,0:T(8,128)(2,1)} %get-tuple-element.946, bf16[32,1408]{1,0:T(8,128)(2,1)} %get-tuple-element.946, bf16[32,1408]{1,0:T(8,128)(2,1)} %get-tuple-element.946), branch_computations={%region_9.9_spmd, %region_10.10_spmd, %region_11.11_spmd} | conditional | bytes 540720 | solution.py:307
  565.4 1.3 collective-permute-start
  566.7 12.6 %collective-permute-done = bf16[32,1408]{1,0:T(8,128)(2,1)S(1)} collective-permute-done((bf16[32,1408]{1,0:T(8,128)(2,1)}, bf16[32,1408]{1,0:T(8,128)(2,1)S(1)}, u32[]{:S(2)}, u32[]{:S(2)}) %collective-permute-start) | collective-permute-done | bytes 90144 | tf_op jit(solution)/shard_map/while/body/eval_jaxpr/cond/branch_1_fun/ppermute | solution.py:311
  579.3 0.6 copy.52
  579.9 17.6 %conditional.11 = ((bf16[2,32,1408]{2,1,0:T(8,128)(2,1)}, bf16[2,32,64]{2,1,0:T(8,128)(2,1)S(1)}, bf16[2,32,1280]{2,1,0:T(8,128)(2,1)}, bf16[32,1408]{1,0:T(8,128)(2,1)})) conditional(s32[]{:T(128)} %convert_element_type.83, (bf16[2,32,1408]{2,1,0:T(8,128)(2,1)}, bf16[2,32,64]{2,1,0:T(8,128)(2,1)S(1)}, bf16[2,32,1280]{2,1,0:T(8,128)(2,1)}, ...), branch_computations={%region_5.5_spmd, %region_6.8_spmd} | conditional | flops 419430400 | bytes 14278758 | solution.py:304
  579.9 9.4 %conditional = (bf16[4,32,1408]{2,1,0:T(8,128)(2,1)S(1)}) conditional(s32[]{:T(128)} %convert_element_type.51, bf16[32,1408]{1,0:T(8,128)(2,1)} %get-tuple-element.660, (s32[]{:T(128)}, bf16[2,4,32,1408]{3,2,1,0:T(8,128)(2,1)}) %tuple.76), branch_computations={%region_7.6_spmd, %region_8.7_spmd} | conditional | flops 3 | bytes 1171464 | solution.py:288
  579.9 0.9 broadcast_in_dim.52
  580.8 8.4 %all_to_all.14 = bf16[4,32,1408]{2,1,0:T(8,128)(2,1)S(1)} all-to-all(bf16[4,32,1408]{2,1,0:T(8,128)(2,1)S(1)} %broadcast_in_dim.52), channel_id=1, replica_groups=mesh['s'=16,'y'=4,'c'=2,'z'=4] {'y'}, dimensions={0} | all-to-all | bytes 720896 | tf_op jit(solution)/shard_map/while/body/eval_jaxpr/cond/branch_1_fun/cond/branch_0_fun/all_to_all | solution.py:45
  589.3 8.1 %stage.1 = (bf16[32,1408]{1,0:T(8,128)(2,1)}, bf16[2,32,1408]{2,1,0:T(8,128)(2,1)}, bf16[2,32,64]{2,1,0:T(8,128)(2,1)S(1)}, bf16[2,32,1280]{2,1,0:T(8,128)(2,1)}) custom-call(s32[3]{0:T(128)S(1)} %pad_add_fusion.place_ref, bf16[4,32,1408]{2,1,0:T(8,128)(2,1)S(1)} %get-tuple-element.1051.parts_ref, ...), custom_call_target="tpu_custom_call", output_to_operand_aliasing={{1}: (10, {}), {2}: (11, {}), {3}: (12, {})} | custom-call | flops 419430400 | bytes 13107200 | tf_op jit(solution)/shard_map/while/body/eval_jaxpr/cond/branch_1_fun/stage/pallas_call | solution.py:170
  597.6 0.7 slice.49
  598.3 0.6 broadcast_in_dim.122
  599.0 3.3 all-to-all-start.2
  602.3 1.2 iota_compare_fusion.2
  603.4 3.3 all-to-all-done.2
  606.7 1.0 fusion.11
  607.7 12.9 %all-gather.4 = bf16[256,1408]{1,0:T(8,128)(2,1)S(1)} all-gather(bf16[64,1408]{1,0:T(8,128)(2,1)S(1)} %fusion.11), channel_id=6, replica_groups=mesh['s'=16,'y'=4,'c'=2,'z'=4] {'z'}, dimensions={0}, use_global_device_ids=true | all-gather | bytes 901120 | tf_op jit(solution)/shard_map/all_gather | solution.py:357
  620.6 0.6 slice.68
  621.6 37.4 %collective-permute-start.8 = (f32[8,16,640]{2,1,0:T(8,128)S(1)}, f32[8,16,640]{2,1,0:T(8,128)S(1)}, u32[]{:S(2)}, u32[]{:S(2)}) collective-permute-start(f32[8,16,640]{2,1,0:T(8,128)S(1)} %slice_select_fusion), channel_id=1, source_target_pairs={{0,4},{4,0},{1,5},{5,1},{2,6},{6,2},{3,7},{7,3},{8,12},{12,8},{9,1... | collective-permute-start | bytes 983048 | tf_op jit(solution)/shard_map/ppermute | solution.py:40
  659.0 1.0 reshape.134
  660.0 1.0 reduce_sum.63
  661.0 0.9 convert_reduce_fusion
  661.9 1.1 subtract_convert_fusion
  663.1 1.9 collective-permute-start.6
  665.0 1.1 fusion.1
  666.2 2.4 collective-permute-start.7
  668.7 0.7 maximum_bitcast_fusion
  669.4 1.0 select_reduce_fusion
  670.5 1.0 select_reduce_fusion.1
  (149 shorter events, 4.1 us)
Async XLA Ops:
  7.2 17.9 %copy-start = (bf16[1,8,16,5120]{3,2,1,0:T(8,128)(2,1)S(1)}, bf16[1,8,16,5120]{3,2,1,0:T(8,128)(2,1)}, u32[]{:S(2)}) copy-start(bf16[1,8,16,5120]{3,2,1,0:T(8,128)(2,1)} %param.28) | copy-start | bytes 3932164
  7.2 141.0 %all-gather.7.cloned.1.call-start = ((), (), s32[]{:S(2)}) async-start(), calls=%async_computation.3 | async-start | bytes 8192000 | tf_op jit(solution)/shard_map/all_gather | solution.py:224
  10.9 0.7 copy-start.6
  10.9 11.4 %copy-start.2 = (bf16[1,8,16,5120]{3,2,1,0:T(8,128)(2,1)S(1)}, bf16[1,8,16,5120]{3,2,1,0:T(8,128)(2,1)}, u32[]{:S(2)}) copy-start(bf16[1,8,16,5120]{3,2,1,0:T(8,128)(2,1)} %param.23) | copy-start | bytes 3932164
  10.9 11.6 %copy-start.7 = (s32[1,8]{1,0:T(1,128)S(1)}, s32[1,8]{1,0:T(1,128)}, u32[]{:S(2)}) copy-start(s32[1,8]{1,0:T(1,128)} %param.30) | copy-start | bytes 100
  10.9 11.6 %copy-start.8 = (s32[8]{0:T(128)S(1)}, s32[8]{0:T(128)}, u32[]{:S(2)}) copy-start(s32[8]{0:T(128)} %param.29) | copy-start | bytes 100
  11.6 14.2 %collective-permute-start.4 = (f32[1,640]{1,0:T(1,128)S(1)}, f32[1,640]{1,0:T(1,128)S(1)}, u32[]{:S(2)}, u32[]{:S(2)}) collective-permute-start(f32[1,640]{1,0:T(1,128)S(1)} %copy-done.6), channel_id=1, source_target_pairs={{0,4},{4,0},{1,5},{5,1},{2,6},{6,2},{3,7},{7,3},{8,12},{12,8},{9,1... | collective-permute-start | bytes 7688 | tf_op jit(solution)/shard_map/ppermute | solution.py:27
  20.4 8.0 %collective-permute-start.3 = (bf16[8,640,16]{1,2,0:T(8,128)(2,1)}, bf16[8,640,16]{1,2,0:T(8,128)(2,1)}, u32[]{:S(2)}, u32[]{:S(2)}) collective-permute-start(bf16[8,640,16]{1,2,0:T(8,128)(2,1)} %bitcast.14), channel_id=1, source_target_pairs={{0,4},{4,0},{1,5},{5,1},{2,6},{6,2},{3,7},{7,3},{8,12},{12,8},{9,1... | collective-permute-start | bytes 491528 | tf_op jit(solution)/shard_map/ppermute | solution.py:27
  22.7 2.1 copy-start.9
  27.0 20.4 %collective-permute-start.2 = (bf16[64,1280]{1,0:T(8,128)(2,1)}, bf16[64,1280]{1,0:T(8,128)(2,1)}, u32[]{:S(2)}, u32[]{:S(2)}) collective-permute-start(bf16[64,1280]{1,0:T(8,128)(2,1)} %get-tuple-element.800), channel_id=1, source_target_pairs={{480,448},{448,416},{416,384},{384,352},{352,320},{320,288},{288,2... | collective-permute-start | bytes 491528 | tf_op jit(solution)/shard_map/ppermute | solution.py:236
  148.3 12.9 %collective-permute-start.5 = (bf16[5120,640]{1,0:T(8,128)(2,1)}, bf16[5120,640]{1,0:T(8,128)(2,1)}, u32[]{:S(2)}, u32[]{:S(2)}) collective-permute-start(bf16[5120,640]{1,0:T(8,128)(2,1)} %all-gather.7.cloned.1.call-done), channel_id=1, source_target_pairs={{0,4},{4,0},{1,5},{5,1},{2,6},{6,2},{3,7},{7,3},{8,12},{12,8},{9,1... | collective-permute-start | bytes 19660808 | tf_op jit(solution)/shard_map/ppermute | solution.py:275
  208.6 338.3 %collective-permute-start = (bf16[32,1408]{1,0:T(8,128)(2,1)}, bf16[32,1408]{1,0:T(8,128)(2,1)S(1)}, u32[]{:S(2)}, u32[]{:S(2)}) collective-permute-start(bf16[32,1408]{1,0:T(8,128)(2,1)} %param.7), channel_id=1, source_target_pairs={{480,448},{416,384},{352,320},{288,256},{224,192},{160,128},{96,64... | collective-permute-start | bytes 270344 | tf_op jit(solution)/shard_map/while/body/eval_jaxpr/cond/branch_1_fun/ppermute | solution.py:311
  565.4 13.9 %collective-permute-start = (bf16[32,1408]{1,0:T(8,128)(2,1)}, bf16[32,1408]{1,0:T(8,128)(2,1)S(1)}, u32[]{:S(2)}, u32[]{:S(2)}) collective-permute-start(bf16[32,1408]{1,0:T(8,128)(2,1)} %param.7), channel_id=1, source_target_pairs={{480,448},{416,384},{352,320},{288,256},{224,192},{160,128},{96,64... | collective-permute-start | bytes 270344 | tf_op jit(solution)/shard_map/while/body/eval_jaxpr/cond/branch_1_fun/ppermute | solution.py:311
  599.0 7.7 %all-to-all-start.2 = ((bf16[4,2,32,128]{3,2,1,0:T(8,128)(2,1)}), bf16[4,2,32,128]{3,2,1,0:T(8,128)(2,1)S(1)}, u32[]{:S(2)}, u32[]{:S(2)}) async-start(bf16[4,2,32,128]{3,2,1,0:T(8,128)(2,1)} %broadcast_in_dim.122), calls=%async_computation.2 | async-start | bytes 131072 | tf_op jit(solution)/shard_map/all_to_all | solution.py:45
  603.4 17.8 %copy-start.4 = (bf16[4,8,8,16]{3,2,1,0:T(8,128)(2,1)S(1)}, bf16[4,8,8,16]{3,2,1,0:T(8,128)(2,1)}, u32[]{:S(2)}) copy-start(bf16[4,8,8,16]{3,2,1,0:T(8,128)(2,1)} %get-tuple-element.753) | copy-start | bytes 24580
  606.7 14.5 %copy-start.3 = (bf16[4,2,32,128]{3,2,1,0:T(8,128)(2,1)}, bf16[4,2,32,128]{3,2,1,0:T(8,128)(2,1)S(1)}, u32[]{:S(2)}) copy-start(bf16[4,2,32,128]{3,2,1,0:T(8,128)(2,1)S(1)} %all-to-all-done.2) | copy-start | bytes 196612
  621.5 43.5 %copy-start.1 = (bf16[4,8,8,1280]{3,2,1,0:T(8,128)(2,1)S(1)}, bf16[4,8,8,1280]{3,2,1,0:T(8,128)(2,1)}, u32[]{:S(2)}) copy-start(bf16[4,8,8,1280]{3,2,1,0:T(8,128)(2,1)} %get-tuple-element.756) | copy-start | bytes 1966084
  621.6 47.8 %collective-permute-start.8 = (f32[8,16,640]{2,1,0:T(8,128)S(1)}, f32[8,16,640]{2,1,0:T(8,128)S(1)}, u32[]{:S(2)}, u32[]{:S(2)}) collective-permute-start(f32[8,16,640]{2,1,0:T(8,128)S(1)} %slice_select_fusion), channel_id=1, source_target_pairs={{0,4},{4,0},{1,5},{5,1},{2,6},{6,2},{3,7},{7,3},{8,12},{12,8},{9,1... | collective-permute-start | bytes 983048 | tf_op jit(solution)/shard_map/ppermute | solution.py:40
  663.1 5.5 collective-permute-start.6
  666.2 3.3 copy-start.5
  666.2 4.2 collective-permute-start.7
Sparse Core Ops, SparseCore 0:
  11.0 137.1 all-gather.6

commit v8 on v5

--- a/solution.py
+++ b/solution.py
@@ -19,8 +19,11 @@
 bf16 = jnp.bfloat16
 contract_last = (((1,), (1,)), ((), ()))
 contract_inner = (((1,), (0,)), ((), ()))
+AHEAD = 3
 TOP_SWAP = [(30, 31), (31, 30)]
-AHEAD = 3
+RIGHT = [(4 * s + z, 4 * s + (z + 1) % 4) for s in range(15) for z in range(4)]
+LEFT = [(4 * s + z, 4 * s + (z + 3) % 4) for s in range(15) for z in range(4)]
+PAIRS = [(2 * s + c, 2 * s + 1 - c) for s in range(15) for c in range(2)]
 
 
 def both_cores(value, axis):
@@ -65,46 +68,15 @@
     return sent, tail
 
 
-def stage_kernel(
-    place_ref,
-    parts_ref,
-    gain_ref,
-    before_any,
-    up_any,
-    down_any,
-    inv_any,
-    x_any,
-    own_any,
-    other_any,
-    boxes_in,
-    low_in,
-    grad_in,
-    box_ref,
-    boxes_any,
-    low_any,
-    grad_any,
-    before_ref,
-    up_ref,
-    down_ref,
-    inv_ref,
-    x_ref,
-    full,
-    weight,
-    low_ref,
-    grad_ref,
-    in_sems,
-    w_sems,
-    out_sems,
-    *,
-    group,
-):
-    del boxes_in, low_in, grad_in
-    m, ypos, core = place_ref[0], place_ref[1], place_ref[2]
+def stage_kernel(place_ref, parts_ref, gain_ref, before_any, up_any, down_any, inv_any, x_any, *refs, group):
+    weights, refs = refs[:16], refs[16 + 4 :]
+    box_ref, boxes_any, low_any, grad_any, tail_any = refs[:5]
+    before_ref, up_ref, down_ref, inv_ref, x_ref, full, weight, low_ref, grad_ref, tail_ref = refs[5:15]
+    in_sems, w_sems, out_sems = refs[15:]
+    m, ypos, core, zpos = place_ref[0], place_ref[1], place_ref[2], place_ref[3]
     width = x_ref.shape[1]
     width_all = full.shape[1]
     half = width // 2
-    pieces = w_sems.shape[0]
-    depth = width_all // pieces
 
     def started(source, target, sem):
         copy = pltpu.make_async_copy(source, target, sem)
@@ -114,11 +86,11 @@
     before_copy = started(before_any.at[:, m], before_ref, in_sems.at[0])
     up_copy = started(up_any.at[m], up_ref, in_sems.at[1])
     copies = []
-    for piece in range(pieces):
-        span = pl.ds(piece * depth, depth)
-        for side, (ref, base) in enumerate(((own_any, core * half), (other_any, (1 - core) * half))):
+    for piece in range(8):
+        for side, base in enumerate((core * half, (1 - core) * half)):
             lanes = pl.ds(pl.multiple_of(base, 128), half)
-            copies.append(started(ref.at[span], weight.at[span, lanes], w_sems.at[piece, side]))
+            target = weight.at[pl.ds(piece * half, half), lanes]
+            copies.append(started(weights[8 * side + piece], target, w_sems.at[piece, side]))
         if piece == 0:
             down_copy = started(down_any.at[m], down_ref, in_sems.at[2])
             inv_copy = started(inv_any.at[m], inv_ref, in_sems.at[3])
@@ -127,13 +99,28 @@
     tail = parts_ref[:, :, width:].astype(f32)
     coef = jnp.sum(jnp.sum(tail, axis=0), axis=1, keepdims=True)
     before_copy.wait()
+    up_copy.wait()
+    low = None
     for part in range(4):
         fixed = parts_ref[part, :, :width].astype(f32) - coef * before_ref[part].astype(f32)
-        full[:, part * width : (part + 1) * width] = fixed.astype(bf16)
-    grad_ref[...] = full[:, pl.ds(pl.multiple_of(ypos * width, 128), width)]
+        fixed = fixed.astype(bf16)
+        first = 2 * lax.rem(zpos - part + 4, 4) * half
+        second = (2 * lax.rem(part - zpos + 4, 4) + 1) * half
+        full[:, pl.ds(pl.multiple_of(first, 128), half)] = fixed[:, :half]
+        full[:, pl.ds(pl.multiple_of(second, 128), half)] = fixed[:, half:]
+
+        @pl.when(part == ypos)
+        def _(fixed=fixed):
+            grad_ref[...] = fixed
+
+        term = lax.dot_general(
+            fixed,
+            up_ref[:, part * width : (part + 1) * width],
+            contract_last,
+            preferred_element_type=f32,
+        )
+        low = term if low is None else low + term
     grad_copy = started(grad_ref, grad_any.at[m], out_sems.at[0])
-    up_copy.wait()
-    low = lax.dot_general(full[...], up_ref[...], contract_last, preferred_element_type=f32)
     low = own_group(low, group)
     low_ref[...] = low
     low_copy = started(low_ref, low_any.at[m], out_sems.at[1])
@@ -141,10 +128,10 @@
     total = low_rank_scale * lax.dot_general(
         low, down_ref[...], contract_inner, preferred_element_type=f32
     )
-    for piece in range(pieces):
-        copies[2 * piece].wait()
-        copies[2 * piece + 1].wait()
-        span = slice(piece * depth, (piece + 1) * depth)
+    for part in range(4):
+        for copy in copies[4 * part : 4 * part + 4]:
+            copy.wait()
+        span = slice(part * width, (part + 1) * width)
         total = total + lax.dot_general(
             full[:, span], weight[span], contract_inner, preferred_element_type=f32
         )
@@ -155,23 +142,27 @@
     )
     box_ref[:, :width] = sent
     box_ref[:, width:] = tail
+    tail_ref[...] = tail
     box_copy = started(box_ref, boxes_any.at[m], out_sems.at[2])
+    tail_copy = started(tail_ref, tail_any.at[m], out_sems.at[3])
     grad_copy.wait()
     low_copy.wait()
     box_copy.wait()
-
-
-def run_stage(place, parts, before, up, down, gain, inv, x, own, other, kept):
+    tail_copy.wait()
+
+
+def run_stage(place, parts, before, up, down, gain, inv, x, weights, kept):
     _, rows, width = x.shape
-    width_all = own.shape[0]
+    width_all = 4 * width
     cols = up.shape[1]
-    pieces = 5
     vmem = pl.BlockSpec(memory_space=pltpu.VMEM)
     any_space = pl.BlockSpec(memory_space=pl.ANY)
+    inputs = [place, parts, gain, before, up, down, inv, x, *weights]
     return pl.pallas_call(
         functools.partial(stage_kernel, group=cols // 16),
-        in_specs=[pl.BlockSpec(memory_space=pltpu.SMEM), vmem, vmem] + [any_space] * 10,
-        out_specs=[vmem] + [any_space] * 3,
+        in_specs=[pl.BlockSpec(memory_space=pltpu.SMEM), vmem, vmem]
+        + [any_space] * (len(inputs) + len(kept) - 3),
+        out_specs=[vmem] + [any_space] * len(kept),
         scratch_shapes=[
             pltpu.VMEM((4, rows, width), bf16),
             pltpu.VMEM((cols, width_all), bf16),
@@ -182,19 +173,20 @@
             pltpu.VMEM((width_all, width), bf16),
             pltpu.VMEM((rows, cols), bf16),
             pltpu.VMEM((rows, width), bf16),
+            pltpu.VMEM((rows, TAIL), bf16),
             pltpu.SemaphoreType.DMA((5,)),
-            pltpu.SemaphoreType.DMA((pieces, 2)),
-            pltpu.SemaphoreType.DMA((3,)),
+            pltpu.SemaphoreType.DMA((8, 2)),
+            pltpu.SemaphoreType.DMA((4,)),
         ],
         out_shape=[jax.ShapeDtypeStruct((rows, width + TAIL), bf16)]
         + [jax.ShapeDtypeStruct(k.shape, k.dtype) for k in kept],
-        input_output_aliases={10: 1, 11: 2, 12: 3},
+        input_output_aliases={len(inputs) + i: 1 + i for i in range(len(kept))},
         compiler_params=pltpu.CompilerParams(vmem_limit_bytes=32 * 1024 * 1024),
         cost_estimate=pl.CostEstimate(
             flops=2 * rows * width * width_all, bytes_accessed=2 * width * width_all, transcendentals=0
         ),
         name="stage",
-    )(place, parts, gain, before, up, down, inv, x, own, other, *kept)
+    )(*inputs, *kept)
 
 
 def local(
@@ -221,8 +213,11 @@
     rows = group * toks
     multiplier = low_rank_scale / (toks * 2 * lax.axis_size("z"))
 
-    shard = proj_weight[0].T
-    w_own = lax.all_gather(shard, "z", axis=0, tiled=True)
+    zpos = lax.axis_index("z")
+    first = proj_weight[0][:, :half].T
+    second = proj_weight[0][:, half:].T
+    right_1 = lax.ppermute(first, ("s", "z"), RIGHT)
+    left_1 = lax.ppermute(second, ("s", "z"), LEFT)
 
     x_full = section_inputs[0]
     x_mine = lax.dynamic_slice_in_dim(x_full, core * toks, toks, 1).reshape(rows_all, width_all)
@@ -260,8 +255,13 @@
     down_chunk = down_sel.transpose(0, 2, 1).reshape(CHUNKS, group * rank, width)
     up_chunk = up_sel.reshape(CHUNKS, group * rank, width_all)
 
+    ready = (x_before, x_chunk, inv_chunk, down_chunk, up_chunk, gain_y)
+    right_1, left_1, ready = lax.optimization_barrier((right_1, left_1, ready))
+    x_before, x_chunk, inv_chunk, down_chunk, up_chunk, gain_y = ready
+
     def top(args):
-        out_grads, shard = args
+        out_grads, first, second = args[:3]
+        shard = jnp.concatenate([first, second], 0)
         shard_x = lax.ppermute(shard, ("s", "c"), TOP_SWAP)
         grad = lax.dynamic_slice_in_dim(out_grads, core * toks, toks, 1)
         low = jnp.einsum("mtd,mrd->mtr", grad, up_sel, preferred_element_type=f32).astype(bf16)
@@ -285,21 +285,36 @@
         member = jnp.arange(rows_all)[:, None] // toks % group == jnp.arange(group)[None, :]
         low = jnp.where(member[:, :, None], low.reshape(rows_all, 1, rank), 0)
         low = low.astype(bf16).reshape(CHUNKS, rows, group * rank)
-        return boxes, low, grad_y.reshape(CHUNKS, rows, width)
-
-    def empty(args):
-        return (
+        tail = tail.reshape(CHUNKS, rows, TAIL)
+        moved = tuple(jnp.zeros(first.shape, first.dtype) for _ in range(12))
+        return moved, (boxes, low, grad_y.reshape(CHUNKS, rows, width), tail)
+
+    def around(args):
+        _, first, second, right_1, left_1 = args
+
+        def swapped(value):
+            return lax.ppermute(value, ("s", "c"), PAIRS)
+
+        right_2 = lax.ppermute(right_1, ("s", "z"), RIGHT)
+        left_2 = lax.ppermute(left_1, ("s", "z"), LEFT)
+        others = [swapped(w) for w in (first, second, right_1, left_1)]
+        right_2, left_2, others = lax.optimization_barrier((right_2, left_2, others))
+        right_3 = lax.ppermute(right_2, ("s", "z"), RIGHT)
+        left_3 = lax.ppermute(left_2, ("s", "z"), LEFT)
+        more = [swapped(w) for w in (right_2, left_2)]
+        right_3, left_3, more = lax.optimization_barrier((right_3, left_3, more))
+        more = more + [swapped(w) for w in (right_3, left_3)]
+        kept = (
             jnp.zeros((CHUNKS, rows, width + TAIL), bf16),
             jnp.zeros((CHUNKS, rows, group * rank), bf16),
             jnp.zeros((CHUNKS, rows, width), bf16),
-        )
-
-    kept = lax.cond(sec == 15, top, empty, (out_grads, shard))
-
-    ready = (x_before, x_chunk, inv_chunk, down_chunk, up_chunk, gain_y, kept)
-    w_own, ready = lax.optimization_barrier((w_own, ready))
-    x_before, x_chunk, inv_chunk, down_chunk, up_chunk, gain_y, kept = ready
-    w_other = lax.ppermute(w_own, "c", SWAP)
+            jnp.zeros((CHUNKS, rows, TAIL), bf16),
+        )
+        return (right_2, left_2, right_3, left_3, *others, *more), kept
+
+    args = (out_grads, first, second, right_1, left_1)
+    moved, kept = lax.cond(sec == 15, top, around, args)
+    weights = [first, second, right_1, left_1, *moved]
 
     def pick(array, m):
         return lax.dynamic_index_in_dim(array, m, 0, keepdims=False)
@@ -315,18 +330,20 @@
 
         def computed(args):
             box, kept = args
-            place = jnp.stack([m, ypos, core]).astype(jnp.int32)
+            place = jnp.stack([m, ypos, core, zpos]).astype(jnp.int32)
+            parts = lax.cond(
+                sec == 15, lambda box: jnp.zeros((4,) + box.shape, box.dtype), spread, box
+            )
             box, *kept = run_stage(
                 place,
-                spread(box),
+                parts,
                 x_before,
                 up_chunk,
                 down_chunk,
                 gain_y,
                 inv_chunk,
                 x_chunk,
-                w_own,
-                w_other,
+                weights,
                 kept,
             )
             return box, tuple(kept)
@@ -361,12 +378,13 @@
         ),
     )
     _, kept, extras = lax.fori_loop(0, (15 + CHUNKS) * CHUNKS, step, start)
-    boxes, low_all, grad_all = kept
+    boxes, low_all, grad_all, tail_all = kept
     h_all, low_in_all = lax.cond(
         sec > 15 - AHEAD, lambda args: extra((h_y, low_part)), lambda args: args, extras
     )
 
-    coef_sum = jnp.sum(spread(boxes[:, :, width:]).astype(f32), axis=(0, -1))[..., None]
+    coefs = spread(tail_all)
+    coef_sum = jnp.sum(coefs.astype(f32), axis=(0, -1))[..., None]
     new_grads = boxes[:, :, :width].astype(f32) - coef_sum * x_chunk.astype(f32)
     new_grads = new_grads.astype(bf16).reshape(micro, toks, width)
     keep = jnp.where(core == 0, new_grads[:, :, :half], new_grads[:, :, half:])

time: 702 us -> 675 us (0.962)
  waiting for transfers between devices: 496 us -> 433 us
  starting transfers between devices: 70.2 us -> 104 us
  between operations: 14.4 us -> 0.97 us
  blocking collectives: 71.7 us -> 81.3 us
    all_gather x1 -> x0, waiting for transfers between devices: 86.7 us -> none  [local(): w_own = lax.all_gather(shard, 'z', axis=0, tiled=True)]
    ppermute x1 -> x14, starting transfers between devices: 2.47 us -> 74.6 us  [the longest x1 29.9 us: around(): right_2 = lax.ppermute(right_1, ('s', 'z'), RIGHT)]
    ppermute x1 -> x14, waiting for transfers between devices: 9.26 us -> 56.3 us  [the longest x1 19.2 us: around(): left_3 = lax.ppermute(left_2, ('s', 'z'), LEFT)]
    ppermute x2, starting transfers between devices: 39.9 us -> 8.44 us  [half_sum(): return mine + lax.ppermute(theirs, 'c', SWAP)]
    all_to_all x1 -> x3, blocking collectives: 13.1 us -> 28.5 us  [spread(): return lax.all_to_all(sent, 'y', 0, 0)]
    all_to_all x3 -> x1, waiting for transfers between devices: 15 us -> 3.07 us  [spread(): return lax.all_to_all(sent, 'y', 0, 0)]
    ppermute x1, waiting for transfers between devices: 17.7 us -> 6.76 us  [local(): lax.ppermute(x_y, 's', EVERY)]
  transfers between devices with their start and end apart: 13 -> 23, of which waited for: 8 -> 11; matrix products, arithmetic and copies ran while one was open for 2% -> 3% of each run, Pallas kernels for 0% -> 0%
where the time goes in v8:
time: 675 us; the launch traced here: 673 us
  waiting for transfers between devices  433 us (64%)
  starting transfers between devices  104 us (15%)
  blocking collectives  81.3 us (12%)
  local copies, waits for them, and re-layouts  18.3 us (3%)
  Pallas kernels  16.4 us (2%)
  other arithmetic  9.94 us (1%)
    ppermute x2, waiting for transfers between devices, step(): lax.ppermute(box, 's', ODD)  367 us
    ppermute x1, starting transfers between devices, around(): right_2 = lax.ppermute(right_1, ('s', 'z'), RIGHT)  29.9 us
    all_to_all x3, blocking collectives, spread(): return lax.all_to_all(sent, 'y', 0, 0)  28.5 us
    ppermute x8, starting transfers between devices, swapped(): return lax.ppermute(value, ('s', 'c'), PAIRS)  27.8 us
    all_gather x2, blocking collectives, extra(): return (lax.all_gather(h_y, 'z'), lax.all_gather(low_in, 'z'))  26.3 us
    ppermute x1, waiting for transfers between devices, around(): left_3 = lax.ppermute(left_2, ('s', 'z'), LEFT)  19.2 us
    pallas_call x2, Pallas kernels, run_stage(): pl.pallas_call(functools.partial(stage_kernel, group=cols // 16), in_spec...  16.4 us
    all_gather x1, blocking collectives, local(): both = lax.all_gather(both, 'z').reshape(4, micro, toks, width + TAIL)  14.7 us
  transfers between devices with their start and end apart: 23, of which 11 were waited for; matrix products, arithmetic and copies ran while one was open for 3% of the time, Pallas kernels for 0%

profile of v8, /device:TPU:1, one launch (start us, length us, event | category | flops | bytes accessed | tf_op | source)
XLA Modules:
  0.0 673.1 jit_solution(6721444650083918236)
XLA Ops:
  0.6 8.9 %collective-permute-start.19 = (f32[1,640]{1,0:T(1,128)}, f32[1,640]{1,0:T(1,128)S(1)}, u32[]{:S(2)}, u32[]{:S(2)}) collective-permute-start(f32[1,640]{1,0:T(1,128)} %param.29), channel_id=1, source_target_pairs={{0,4},{4,0},{1,5},{5,1},{2,6},{6,2},{3,7},{7,3},{8,12},{12,8},{9,1... | collective-permute-start | bytes 7688 | tf_op jit(solution)/shard_map/ppermute | solution.py:31
  9.6 1.9 collective-permute-start.18
  11.5 3.5 copy.32
  15.0 2.8 slice_bitcast_fusion.4
  17.8 2.0 collective-permute-start.15
  19.9 5.2 collective-permute-start.16
  28.4 1.3 collective-permute-start.17
  29.7 1.0 broadcast_select_fusion.4
  31.3 1.1 fusion.18
  32.4 6.8 %collective-permute-done.17 = bf16[64,1280]{1,0:T(8,128)(2,1)} collective-permute-done((bf16[64,1280]{1,0:T(8,128)(2,1)}, bf16[64,1280]{1,0:T(8,128)(2,1)}, u32[]{:S(2)}, u32[]{:S(2)}) %collective-permute-start.17) | collective-permute-done | bytes 163872 | tf_op jit(solution)/shard_map/ppermute | solution.py:232
  39.2 12.6 %conditional.7 = (bf16[4,2,32,1280]{3,2,1,0:T(8,128)(2,1)}) conditional(s32[]{:T(128)} %convert_element_type.88, bf16[64,1280]{1,0:T(8,128)(2,1)} %collective-permute-done.17, () %tuple.108), branch_computations={%region_0.0_spmd, %region_1.0_spmd} | conditional | bytes 2129928 | solution.py:228
  39.2 1.0 broadcast_in_dim.97
  40.1 11.6 %all_to_all.21 = bf16[4,64,1280]{2,1,0:T(8,128)(2,1)} all-to-all(bf16[4,64,1280]{2,1,0:T(8,128)(2,1)S(1)} %broadcast_in_dim.97), channel_id=1, replica_groups=mesh['s'=16,'y'=4,'c'=2,'z'=4] {'y'}, dimensions={0} | all-to-all | bytes 1310720 | tf_op jit(solution)/shard_map/cond/branch_0_fun/all_to_all | solution.py:49
  51.8 11.5 %collective-permute-done.16 = bf16[640,640]{1,0:T(8,128)(2,1)} collective-permute-done((bf16[640,640]{1,0:T(8,128)(2,1)}, bf16[640,640]{1,0:T(8,128)(2,1)}, u32[]{:S(2)}, u32[]{:S(2)}) %collective-permute-start.16) | collective-permute-done | bytes 819232 | tf_op jit(solution)/shard_map/ppermute | solution.py:220
  63.4 114.2 %conditional.8 = (bf16[640,640]{1,0:T(8,128)(2,1)}, bf16[640,640]{1,0:T(8,128)(2,1)}, bf16[640,640]{1,0:T(8,128)(2,1)}, bf16[640,640]{1,0:T(8,128)(2,1)}, bf16[6...) conditional(s32[]{:T(128)} %convert_element_type.88, ...), branch_computations={%region_4.5_spmd, %region_5.8_spmd} | conditional | flops 856874752 | bytes 42082448 | solution.py:316
  63.4 29.9 %collective-permute-start = (bf16[640,640]{1,0:T(8,128)(2,1)}, bf16[640,640]{1,0:T(8,128)(2,1)}, u32[]{:S(2)}, u32[]{:S(2)}) collective-permute-start(bf16[640,640]{1,0:T(8,128)(2,1)} %get-tuple-element.1091), channel_id=1, source_target_pairs={{0,1},{1,2},{2,3},{3,0},{32,33},{33,34},{34,35},{35,32},{64,65},{6... | collective-permute-start | bytes 2457608 | tf_op jit(solution)/shard_map/cond/branch_0_fun/ppermute | solution.py:298
  93.3 4.1 collective-permute-start.4
  97.4 1.9 collective-permute-start.1
  99.4 1.9 collective-permute-start.5
  101.3 2.4 collective-permute-start.2
  103.7 5.5 collective-permute-done
  109.2 7.2 %collective-permute-start.3 = (bf16[640,640]{1,0:T(8,128)(2,1)}, bf16[640,640]{1,0:T(8,128)(2,1)}, u32[]{:S(2)}, u32[]{:S(2)}) collective-permute-start(bf16[640,640]{1,0:T(8,128)(2,1)} %get-tuple-element.1094), channel_id=1, source_target_pairs={{0,4},{4,0},{32,36},{36,32},{64,68},{68,64},{96,100},{100,96},{128... | collective-permute-start | bytes 2457608 | tf_op jit(solution)/shard_map/cond/branch_0_fun/ppermute | solution.py:296
  116.4 10.4 %collective-permute-done.1 = bf16[640,640]{1,0:T(8,128)(2,1)} collective-permute-done((bf16[640,640]{1,0:T(8,128)(2,1)}, bf16[640,640]{1,0:T(8,128)(2,1)}, u32[]{:S(2)}, u32[]{:S(2)}) %collective-permute-start.1) | collective-permute-done | bytes 819232 | tf_op jit(solution)/shard_map/cond/branch_0_fun/ppermute | solution.py:299
  126.8 1.9 collective-permute-start.6
  128.7 5.9 collective-permute-start.7
  134.7 5.1 collective-permute-start.8
  139.8 1.9 collective-permute-start.9
  141.7 7.0 %collective-permute-done.6 = bf16[640,640]{1,0:T(8,128)(2,1)} collective-permute-done((bf16[640,640]{1,0:T(8,128)(2,1)}, bf16[640,640]{1,0:T(8,128)(2,1)}, u32[]{:S(2)}, u32[]{:S(2)}) %collective-permute-start.6) | collective-permute-done | bytes 819232 | tf_op jit(solution)/shard_map/cond/branch_0_fun/ppermute | solution.py:302
  148.8 19.2 %collective-permute-done.7 = bf16[640,640]{1,0:T(8,128)(2,1)} collective-permute-done((bf16[640,640]{1,0:T(8,128)(2,1)}, bf16[640,640]{1,0:T(8,128)(2,1)}, u32[]{:S(2)}, u32[]{:S(2)}) %collective-permute-start.7) | collective-permute-done | bytes 819232 | tf_op jit(solution)/shard_map/cond/branch_0_fun/ppermute | solution.py:303
  168.0 3.1 collective-permute-start.10
  171.1 1.9 collective-permute-start.11
  173.4 2.3 collective-permute-done.11
  179.7 449.1 %while.31 = (s32[]{:T(128)}, bf16[32,1408]{1,0:T(8,128)(2,1)}, bf16[2,32,1408]{2,1,0:T(8,128)(2,1)S(1)}, bf16[2,32,64]{2,1,0:T(8,128)(2,1)}, bf16[2,32,1280]{2,1...) while((s32[]{:T(128)}, bf16[32,1408]{1,0:T(8,128)(2,1)}, ...), condition=%wide.region_20.21_spmd, body=%wide.region_8.20_spmd.sunk | while | flops 419431456 | bytes 15656242 | solution.py:380
  183.6 38.1 %conditional.15 = ((bf16[4,64,1280]{2,1,0:T(8,128)(2,1)}, bf16[4,8,8,16]{3,2,1,0:T(8,128)(2,1)})) conditional(s32[]{:T(128)} %convert_element_type.122, (bf16[4,64,1280]{2,1,0:T(8,128)(2,1)}, bf16[4,8,8,16]{3,2,1,0:T(8,128)(2,1)}) %tuple.154, (bf16[64,1280]{1,0:T(8,128)(2,1)}, f32[8,8,16]{2,1,0:T(8,128)S(1)}) %tuple.155), branch_computations={%region_17.17_spmd, %region_18.19_spmd} | conditional | flops 1024 | bytes 835608 | solution.py:364
  183.6 15.4 %all-gather = bf16[256,1280]{1,0:T(8,128)(2,1)} all-gather(bf16[64,1280]{1,0:T(8,128)(2,1)} %get-tuple-element.1157), channel_id=2, replica_groups=mesh['s'=16,'y'=4,'c'=2,'z'=4] {'z'}, dimensions={0}, use_global_device_ids=true | all-gather | bytes 819200 | tf_op jit(solution)/shard_map/while/body/eval_jaxpr/cond/branch_1_fun/all_gather | solution.py:250
  199.0 11.7 %psum.12 = bf16[8,8,16]{2,1,0:T(8,128)(2,1)S(1)} all-reduce(f32[8,8,16]{2,1,0:T(8,128)S(1)} %get-tuple-element.1158), channel_id=1, replica_groups=mesh['s'=16,'y'=4,'c'=2,'z'=4] {'y'}, use_global_device_ids=true, to_apply=%region_19.18 | all-reduce | flops 1024 | bytes 6144 | tf_op jit(solution)/shard_map/while/body/eval_jaxpr/cond/branch_1_fun/psum | solution.py:249
  210.7 10.9 %all-gather.1 = bf16[32,8,16]{2,1,0:T(8,128)(2,1)} all-gather(bf16[8,8,16]{2,1,0:T(8,128)(2,1)S(1)} %psum.12), channel_id=3, replica_groups=mesh['s'=16,'y'=4,'c'=2,'z'=4] {'z'}, dimensions={0}, use_global_device_ids=true | all-gather | bytes 10240 | tf_op jit(solution)/shard_map/while/body/eval_jaxpr/cond/branch_1_fun/all_gather | solution.py:250
  222.1 353.3 %conditional.14 = (bf16[32,1408]{1,0:T(8,128)(2,1)}) conditional(s32[]{:T(128)} %clamp.27, bf16[32,1408]{1,0:T(8,128)(2,1)} %get-tuple-element.1721, bf16[32,1408]{1,0:T(8,128)(2,1)} %get-tuple-element.1721, bf16[32,1408]{1,0:T(8,128)(2,1)} %get-tuple-element.1721), branch_computations={%region_14.14_spmd, %region_15.15_spmd, %region_16.16_spmd} | conditional | bytes 540720 | solution.py:355
  222.1 1.3 collective-permute-start.12
  223.4 351.3 %collective-permute-done.12 = bf16[32,1408]{1,0:T(8,128)(2,1)S(1)} collective-permute-done((bf16[32,1408]{1,0:T(8,128)(2,1)}, bf16[32,1408]{1,0:T(8,128)(2,1)S(1)}, u32[]{:S(2)}, u32[]{:S(2)}) %collective-permute-start.12) | collective-permute-done | bytes 90144 | tf_op jit(solution)/shard_map/while/body/eval_jaxpr/cond/branch_1_fun/ppermute | solution.py:359
  575.4 17.7 %conditional.13 = ((bf16[2,32,1408]{2,1,0:T(8,128)(2,1)S(1)}, bf16[2,32,64]{2,1,0:T(8,128)(2,1)}, bf16[2,32,1280]{2,1,0:T(8,128)(2,1)}, bf16[2,32,128]{2,1,0:T(8,128)(2,1)}, bf16[32,1408]{1,0:T(8,128)(2,1)})) conditional(s32[]{:T(128)} %clamp.28, (bf16[2,32,1408]{2,1,0:T(8,128)(2,1)S(1)}, bf16[2,32,64]{2,1,0:T(8,128)(2,1)}, ...), branch_computations={%region_9.9_spmd, %region_10.10_spmd, %region_11.13_spmd} | conditional | flops 419430400 | bytes 14278758 | solution.py:352
  575.4 9.4 %conditional = (bf16[4,32,1408]{2,1,0:T(8,128)(2,1)S(1)}) conditional(s32[]{:T(128)} %convert_element_type.75, bf16[32,1408]{1,0:T(8,128)(2,1)} %get-tuple-element.1125, () %tuple.89), branch_computations={%region_12.11_spmd, %region_13.12_spmd} | conditional | bytes 1171464 | solution.py:334
  576.3 8.4 %all_to_all.22 = bf16[4,32,1408]{2,1,0:T(8,128)(2,1)S(1)} all-to-all(bf16[4,32,1408]{2,1,0:T(8,128)(2,1)S(1)} %broadcast_in_dim.139), channel_id=1, replica_groups=mesh['s'=16,'y'=4,'c'=2,'z'=4] {'y'}, dimensions={0} | all-to-all | bytes 720896 | tf_op jit(solution)/shard_map/while/body/eval_jaxpr/cond/branch_2_fun/cond/branch_0_fun/all_to_all | solution.py:49
  584.8 8.2 %stage.1 = (bf16[32,1408]{1,0:T(8,128)(2,1)}, bf16[2,32,1408]{2,1,0:T(8,128)(2,1)S(1)}, bf16[2,32,64]{2,1,0:T(8,128)(2,1)}, bf16[2,32,1280]{2,1,0:T(8,128)(2,1)}, bf16[2,32,128]{2,1,0:T(8,128)(2,1)}) custom-call(s32[4]{0:T(128)S(1)} %pad_add_fusion.place_ref, ...), custom_call_target="tpu_custom_call", output_to_operand_aliasing={{1}: (24, {}), {2}: (25, {}), {3}: (26, {}), {4}: (27, {})} | custom-call | flops 419430400 | bytes 13107200 | tf_op jit(solution)/shard_map/while/body/eval_jaxpr/cond/branch_2_fun/stage/pallas_call | solution.py:161
  593.3 17.7 %conditional.14 = (bf16[32,1408]{1,0:T(8,128)(2,1)}) conditional(s32[]{:T(128)} %clamp.27, bf16[32,1408]{1,0:T(8,128)(2,1)} %get-tuple-element.1721, bf16[32,1408]{1,0:T(8,128)(2,1)} %get-tuple-element.1721, bf16[32,1408]{1,0:T(8,128)(2,1)} %get-tuple-element.1721), branch_computations={%region_14.14_spmd, %region_15.15_spmd, %region_16.16_spmd} | conditional | bytes 540720 | solution.py:355
  593.3 1.3 collective-permute-start.12
  594.6 15.8 %collective-permute-done.12 = bf16[32,1408]{1,0:T(8,128)(2,1)S(1)} collective-permute-done((bf16[32,1408]{1,0:T(8,128)(2,1)}, bf16[32,1408]{1,0:T(8,128)(2,1)S(1)}, u32[]{:S(2)}, u32[]{:S(2)}) %collective-permute-start.12) | collective-permute-done | bytes 90144 | tf_op jit(solution)/shard_map/while/body/eval_jaxpr/cond/branch_1_fun/ppermute | solution.py:359
  611.0 17.7 %conditional.13 = ((bf16[2,32,1408]{2,1,0:T(8,128)(2,1)S(1)}, bf16[2,32,64]{2,1,0:T(8,128)(2,1)}, bf16[2,32,1280]{2,1,0:T(8,128)(2,1)}, bf16[2,32,128]{2,1,0:T(8,128)(2,1)}, bf16[32,1408]{1,0:T(8,128)(2,1)})) conditional(s32[]{:T(128)} %clamp.28, (bf16[2,32,1408]{2,1,0:T(8,128)(2,1)S(1)}, bf16[2,32,64]{2,1,0:T(8,128)(2,1)}, ...), branch_computations={%region_9.9_spmd, %region_10.10_spmd, %region_11.13_spmd} | conditional | flops 419430400 | bytes 14278758 | solution.py:352
  611.0 9.4 %conditional = (bf16[4,32,1408]{2,1,0:T(8,128)(2,1)S(1)}) conditional(s32[]{:T(128)} %convert_element_type.75, bf16[32,1408]{1,0:T(8,128)(2,1)} %get-tuple-element.1125, () %tuple.89), branch_computations={%region_12.11_spmd, %region_13.12_spmd} | conditional | bytes 1171464 | solution.py:334
  611.9 8.4 %all_to_all.22 = bf16[4,32,1408]{2,1,0:T(8,128)(2,1)S(1)} all-to-all(bf16[4,32,1408]{2,1,0:T(8,128)(2,1)S(1)} %broadcast_in_dim.139), channel_id=1, replica_groups=mesh['s'=16,'y'=4,'c'=2,'z'=4] {'y'}, dimensions={0} | all-to-all | bytes 720896 | tf_op jit(solution)/shard_map/while/body/eval_jaxpr/cond/branch_2_fun/cond/branch_0_fun/all_to_all | solution.py:49
  620.4 8.2 %stage.1 = (bf16[32,1408]{1,0:T(8,128)(2,1)}, bf16[2,32,1408]{2,1,0:T(8,128)(2,1)S(1)}, bf16[2,32,64]{2,1,0:T(8,128)(2,1)}, bf16[2,32,1280]{2,1,0:T(8,128)(2,1)}, bf16[2,32,128]{2,1,0:T(8,128)(2,1)}) custom-call(s32[4]{0:T(128)S(1)} %pad_add_fusion.place_ref, ...), custom_call_target="tpu_custom_call", output_to_operand_aliasing={{1}: (24, {}), {2}: (25, {}), {3}: (26, {}), {4}: (27, {})} | custom-call | flops 419430400 | bytes 13107200 | tf_op jit(solution)/shard_map/while/body/eval_jaxpr/cond/branch_2_fun/stage/pallas_call | solution.py:161
  629.7 14.7 %all-gather.4 = bf16[256,1408]{1,0:T(8,128)(2,1)S(1)} all-gather(bf16[64,1408]{1,0:T(8,128)(2,1)S(1)} %fusion.17), channel_id=6, replica_groups=mesh['s'=16,'y'=4,'c'=2,'z'=4] {'z'}, dimensions={0}, use_global_device_ids=true | all-gather | bytes 901120 | tf_op jit(solution)/shard_map/all_gather | solution.py:404
  645.3 1.4 fusion.13
  646.8 6.5 collective-permute-start.22
  653.9 1.4 broadcast_in_dim.162
  655.2 3.3 all-to-all-start.4
  658.5 1.4 fusion.14
  659.9 3.1 all-to-all-done.4
  663.1 1.0 subtract_convert_fusion
  664.1 3.1 collective-permute-start.20
  667.2 1.9 collective-permute-start.21
  669.9 1.0 select_add_fusion
  670.9 1.0 select_reduce_fusion
  672.0 1.0 select_reduce_fusion.1
  (167 shorter events, 16.1 us)
Async XLA Ops:
  0.6 25.7 %copy-start = (bf16[1,8,16,5120]{3,2,1,0:T(8,128)(2,1)S(1)}, bf16[1,8,16,5120]{3,2,1,0:T(8,128)(2,1)}, u32[]{:S(2)}) copy-start(bf16[1,8,16,5120]{3,2,1,0:T(8,128)(2,1)} %param.31) | copy-start | bytes 3932164
  0.6 26.4 %collective-permute-start.19 = (f32[1,640]{1,0:T(1,128)}, f32[1,640]{1,0:T(1,128)S(1)}, u32[]{:S(2)}, u32[]{:S(2)}) collective-permute-start(f32[1,640]{1,0:T(1,128)} %param.29), channel_id=1, source_target_pairs={{0,4},{4,0},{1,5},{5,1},{2,6},{6,2},{3,7},{7,3},{8,12},{12,8},{9,1... | collective-permute-start | bytes 7688 | tf_op jit(solution)/shard_map/ppermute | solution.py:31
  9.6 20.1 %collective-permute-start.18 = (bf16[8,640,16]{1,2,0:T(8,128)(2,1)}, bf16[8,640,16]{1,2,0:T(8,128)(2,1)}, u32[]{:S(2)}, u32[]{:S(2)}) collective-permute-start(bf16[8,640,16]{1,2,0:T(8,128)(2,1)} %bitcast.112), channel_id=1, source_target_pairs={{0,4},{4,0},{1,5},{5,1},{2,6},{6,2},{3,7},{7,3},{8,12},{12,8},{9,1... | collective-permute-start | bytes 491528 | tf_op jit(solution)/shard_map/ppermute | solution.py:31
  15.0 10.0 %copy-start.3 = (bf16[1,8,16,5120]{3,2,1,0:T(8,128)(2,1)S(1)}, bf16[1,8,16,5120]{3,2,1,0:T(8,128)(2,1)}, u32[]{:S(2)}) copy-start(bf16[1,8,16,5120]{3,2,1,0:T(8,128)(2,1)} %param.26) | copy-start | bytes 3932164
  17.8 7.5 %copy-start.7 = (s32[1,8]{1,0:T(1,128)S(1)}, s32[1,8]{1,0:T(1,128)}, u32[]{:S(2)}) copy-start(s32[1,8]{1,0:T(1,128)} %param.33) | copy-start | bytes 100
  17.8 7.6 %copy-start.8 = (s32[8]{0:T(128)S(1)}, s32[8]{0:T(128)}, u32[]{:S(2)}) copy-start(s32[8]{0:T(128)} %param.32) | copy-start | bytes 100
  17.8 33.9 %collective-permute-start.15 = (bf16[640,640]{1,0:T(8,128)(2,1)}, bf16[640,640]{1,0:T(8,128)(2,1)}, u32[]{:S(2)}, u32[]{:S(2)}) collective-permute-start(bf16[640,640]{1,0:T(8,128)(2,1)} %get-tuple-element.1798), channel_id=1, source_target_pairs={{0,1},{1,2},{2,3},{3,0},{32,33},{33,34},{34,35},{35,32},{64,65},{6... | collective-permute-start | bytes 2457608 | tf_op jit(solution)/shard_map/ppermute | solution.py:219
  19.9 43.4 %collective-permute-start.16 = (bf16[640,640]{1,0:T(8,128)(2,1)}, bf16[640,640]{1,0:T(8,128)(2,1)}, u32[]{:S(2)}, u32[]{:S(2)}) collective-permute-start(bf16[640,640]{1,0:T(8,128)(2,1)} %get-tuple-element.1799), channel_id=1, source_target_pairs={{0,3},{1,0},{2,1},{3,2},{32,35},{33,32},{34,33},{35,34},{64,67},{6... | collective-permute-start | bytes 2457608 | tf_op jit(solution)/shard_map/ppermute | solution.py:220
  25.4 1.7 copy-start.6
  25.4 4.4 copy-start.4
  28.4 10.7 %collective-permute-start.17 = (bf16[64,1280]{1,0:T(8,128)(2,1)}, bf16[64,1280]{1,0:T(8,128)(2,1)}, u32[]{:S(2)}, u32[]{:S(2)}) collective-permute-start(bf16[64,1280]{1,0:T(8,128)(2,1)} %get-tuple-element.1469), channel_id=1, source_target_pairs={{480,448},{448,416},{416,384},{384,352},{352,320},{320,288},{288,2... | collective-permute-start | bytes 491528 | tf_op jit(solution)/shard_map/ppermute | solution.py:232
  63.4 45.8 %collective-permute-start = (bf16[640,640]{1,0:T(8,128)(2,1)}, bf16[640,640]{1,0:T(8,128)(2,1)}, u32[]{:S(2)}, u32[]{:S(2)}) collective-permute-start(bf16[640,640]{1,0:T(8,128)(2,1)} %get-tuple-element.1091), channel_id=1, source_target_pairs={{0,1},{1,2},{2,3},{3,0},{32,33},{33,34},{34,35},{35,32},{64,65},{6... | collective-permute-start | bytes 2457608 | tf_op jit(solution)/shard_map/cond/branch_0_fun/ppermute | solution.py:298
  93.3 33.5 %collective-permute-start.4 = (bf16[640,640]{1,0:T(8,128)(2,1)}, bf16[640,640]{1,0:T(8,128)(2,1)}, u32[]{:S(2)}, u32[]{:S(2)}) collective-permute-start(bf16[640,640]{1,0:T(8,128)(2,1)} %get-tuple-element.1091), channel_id=1, source_target_pairs={{0,4},{4,0},{32,36},{36,32},{64,68},{68,64},{96,100},{100,96},{128... | collective-permute-start | bytes 2457608 | tf_op jit(solution)/shard_map/cond/branch_0_fun/ppermute | solution.py:296
  97.4 29.3 %collective-permute-start.1 = (bf16[640,640]{1,0:T(8,128)(2,1)}, bf16[640,640]{1,0:T(8,128)(2,1)}, u32[]{:S(2)}, u32[]{:S(2)}) collective-permute-start(bf16[640,640]{1,0:T(8,128)(2,1)} %get-tuple-element.1092), channel_id=1, source_target_pairs={{0,3},{1,0},{2,1},{3,2},{32,35},{33,32},{34,33},{35,34},{64,67},{6... | collective-permute-start | bytes 2457608 | tf_op jit(solution)/shard_map/cond/branch_0_fun/ppermute | solution.py:299
  99.4 27.4 %collective-permute-start.5 = (bf16[640,640]{1,0:T(8,128)(2,1)}, bf16[640,640]{1,0:T(8,128)(2,1)}, u32[]{:S(2)}, u32[]{:S(2)}) collective-permute-start(bf16[640,640]{1,0:T(8,128)(2,1)} %get-tuple-element.1092), channel_id=1, source_target_pairs={{0,4},{4,0},{32,36},{36,32},{64,68},{68,64},{96,100},{100,96},{128... | collective-permute-start | bytes 2457608 | tf_op jit(solution)/shard_map/cond/branch_0_fun/ppermute | solution.py:296
  101.3 25.5 %collective-permute-start.2 = (bf16[640,640]{1,0:T(8,128)(2,1)}, bf16[640,640]{1,0:T(8,128)(2,1)}, u32[]{:S(2)}, u32[]{:S(2)}) collective-permute-start(bf16[640,640]{1,0:T(8,128)(2,1)} %get-tuple-element.1093), channel_id=1, source_target_pairs={{0,4},{4,0},{32,36},{36,32},{64,68},{68,64},{96,100},{100,96},{128... | collective-permute-start | bytes 2457608 | tf_op jit(solution)/shard_map/cond/branch_0_fun/ppermute | solution.py:296
  109.2 17.6 %collective-permute-start.3 = (bf16[640,640]{1,0:T(8,128)(2,1)}, bf16[640,640]{1,0:T(8,128)(2,1)}, u32[]{:S(2)}, u32[]{:S(2)}) collective-permute-start(bf16[640,640]{1,0:T(8,128)(2,1)} %get-tuple-element.1094), channel_id=1, source_target_pairs={{0,4},{4,0},{32,36},{36,32},{64,68},{68,64},{96,100},{100,96},{128... | collective-permute-start | bytes 2457608 | tf_op jit(solution)/shard_map/cond/branch_0_fun/ppermute | solution.py:296
  126.8 21.9 %collective-permute-start.6 = (bf16[640,640]{1,0:T(8,128)(2,1)}, bf16[640,640]{1,0:T(8,128)(2,1)}, u32[]{:S(2)}, u32[]{:S(2)}) collective-permute-start(bf16[640,640]{1,0:T(8,128)(2,1)} %collective-permute-done), channel_id=1, source_target_pairs={{0,1},{1,2},{2,3},{3,0},{32,33},{33,34},{34,35},{35,32},{64,65},{6... | collective-permute-start | bytes 2457608 | tf_op jit(solution)/shard_map/cond/branch_0_fun/ppermute | solution.py:302
  128.7 39.2 %collective-permute-start.7 = (bf16[640,640]{1,0:T(8,128)(2,1)}, bf16[640,640]{1,0:T(8,128)(2,1)}, u32[]{:S(2)}, u32[]{:S(2)}) collective-permute-start(bf16[640,640]{1,0:T(8,128)(2,1)} %collective-permute-done.1), channel_id=1, source_target_pairs={{0,3},{1,0},{2,1},{3,2},{32,35},{33,32},{34,33},{35,34},{64,67},{6... | collective-permute-start | bytes 2457608 | tf_op jit(solution)/shard_map/cond/branch_0_fun/ppermute | solution.py:303
  134.7 33.3 %collective-permute-start.8 = (bf16[640,640]{1,0:T(8,128)(2,1)}, bf16[640,640]{1,0:T(8,128)(2,1)}, u32[]{:S(2)}, u32[]{:S(2)}) collective-permute-start(bf16[640,640]{1,0:T(8,128)(2,1)} %collective-permute-done), channel_id=1, source_target_pairs={{0,4},{4,0},{32,36},{36,32},{64,68},{68,64},{96,100},{100,96},{128... | collective-permute-start | bytes 2457608 | tf_op jit(solution)/shard_map/cond/branch_0_fun/ppermute | solution.py:296
  139.8 28.2 %collective-permute-start.9 = (bf16[640,640]{1,0:T(8,128)(2,1)}, bf16[640,640]{1,0:T(8,128)(2,1)}, u32[]{:S(2)}, u32[]{:S(2)}) collective-permute-start(bf16[640,640]{1,0:T(8,128)(2,1)} %collective-permute-done.1), channel_id=1, source_target_pairs={{0,4},{4,0},{32,36},{36,32},{64,68},{68,64},{96,100},{100,96},{128... | collective-permute-start | bytes 2457608 | tf_op jit(solution)/shard_map/cond/branch_0_fun/ppermute | solution.py:296
  168.0 5.4 collective-permute-start.10
  171.1 4.6 collective-permute-start.11
  222.1 352.6 %collective-permute-start.12 = (bf16[32,1408]{1,0:T(8,128)(2,1)}, bf16[32,1408]{1,0:T(8,128)(2,1)S(1)}, u32[]{:S(2)}, u32[]{:S(2)}) collective-permute-start(bf16[32,1408]{1,0:T(8,128)(2,1)} %param.10), channel_id=1, source_target_pairs={{480,448},{416,384},{352,320},{288,256},{224,192},{160,128},{96,64... | collective-permute-start | bytes 270344 | tf_op jit(solution)/shard_map/while/body/eval_jaxpr/cond/branch_1_fun/ppermute | solution.py:359
  593.3 17.1 %collective-permute-start.12 = (bf16[32,1408]{1,0:T(8,128)(2,1)}, bf16[32,1408]{1,0:T(8,128)(2,1)S(1)}, u32[]{:S(2)}, u32[]{:S(2)}) collective-permute-start(bf16[32,1408]{1,0:T(8,128)(2,1)} %param.10), channel_id=1, source_target_pairs={{480,448},{416,384},{352,320},{288,256},{224,192},{160,128},{96,64... | collective-permute-start | bytes 270344 | tf_op jit(solution)/shard_map/while/body/eval_jaxpr/cond/branch_1_fun/ppermute | solution.py:359
  644.5 0.9 copy-start.2
  646.8 23.1 %collective-permute-start.22 = (f32[8,16,640]{2,1,0:T(8,128)S(1)}, f32[8,16,640]{2,1,0:T(8,128)}, u32[]{:S(2)}, u32[]{:S(2)}) collective-permute-start(f32[8,16,640]{2,1,0:T(8,128)S(1)} %slice_select_fusion), channel_id=1, source_target_pairs={{0,4},{4,0},{1,5},{5,1},{2,6},{6,2},{3,7},{7,3},{8,12},{12,8},{9,1... | collective-permute-start | bytes 983048 | tf_op jit(solution)/shard_map/ppermute | solution.py:44
  655.2 7.7 %all-to-all-start.4 = ((bf16[4,2,32,128]{3,2,1,0:T(8,128)(2,1)}), bf16[4,2,32,128]{3,2,1,0:T(8,128)(2,1)S(1)}, u32[]{:S(2)}, u32[]{:S(2)}) async-start(bf16[4,2,32,128]{3,2,1,0:T(8,128)(2,1)} %broadcast_in_dim.162), calls=%async_computation.4 | async-start | bytes 131072 | tf_op jit(solution)/shard_map/all_to_all | solution.py:49
  664.1 6.8 %copy-start.5 = (pred[8,8]{1,0:T(8,128)(4,1)S(1)}, pred[8,8]{1,0:T(8,128)(4,1)}, u32[]{:S(2)}) copy-start(pred[8,8]{1,0:T(8,128)(4,1)} %iota_compare_fusion.4) | copy-start | bytes 196
  664.1 5.0 collective-permute-start.20
  667.2 4.7 collective-permute-start.21

commit v9 on v8

--- a/solution.py
+++ b/solution.py
@@ -216,20 +216,21 @@
     zpos = lax.axis_index("z")
     first = proj_weight[0][:, :half].T
     second = proj_weight[0][:, half:].T
+
+    x_tokens = lax.dynamic_slice_in_dim(section_inputs[0], core * toks, toks, 1)
+    x_y = lax.dynamic_slice_in_dim(x_tokens, ypos * width, width, 2).reshape(rows_all, width)
+    x_moved = lax.ppermute(x_y, "s", EVERY)
+    x_moved, first, second, norm_gain, adapter_down, x_tokens = lax.optimization_barrier(
+        (x_moved, first, second, norm_gain, adapter_down, x_tokens)
+    )
     right_1 = lax.ppermute(first, ("s", "z"), RIGHT)
     left_1 = lax.ppermute(second, ("s", "z"), LEFT)
 
-    x_full = section_inputs[0]
-    x_mine = lax.dynamic_slice_in_dim(x_full, core * toks, toks, 1).reshape(rows_all, width_all)
-    x_f = x_mine.astype(f32)
+    x_f = x_tokens.reshape(rows_all, width_all).astype(f32)
     inv_rms = lax.rsqrt(jnp.mean(x_f * x_f, axis=-1, keepdims=True) + norm_eps)
-    x_y = lax.dynamic_slice_in_dim(x_mine, ypos * width, width, 1)
     normed_y = x_y.astype(f32) * inv_rms
     x_before = lax.cond(
-        sec == 15,
-        lambda x: jnp.zeros((4,) + x.shape, x.dtype),
-        spread,
-        lax.ppermute(x_y, "s", EVERY),
+        sec == 15, lambda x: jnp.zeros((4,) + x.shape, x.dtype), spread, x_moved
     )
     gain_y = both_cores(norm_gain, 1)
     down_y = both_cores(adapter_down[0], 1)

time: 675 us -> 665 us (0.985)
  starting transfers between devices: 104 us -> 94.8 us
  waiting for transfers between devices: 433 us -> 426 us
    ppermute x1, starting transfers between devices: 29.9 us -> 1.91 us  [around(): right_2 = lax.ppermute(right_1, ('s', 'z'), RIGHT)]
    ppermute x2, starting transfers between devices: 8.44 us -> 34.3 us  [half_sum(): return mine + lax.ppermute(theirs, 'c', SWAP)]
    ppermute x2, waiting for transfers between devices: 367 us -> 342 us  [step(): lax.ppermute(box, 's', ODD)]
    ppermute x8, starting transfers between devices: 27.8 us -> 20.1 us  [swapped(): return lax.ppermute(value, ('s', 'c'), PAIRS)]
where the time goes in v9:
time: 665 us; the launch traced here: 663 us
  waiting for transfers between devices  426 us (64%)
  starting transfers between devices  94.8 us (14%)
  blocking collectives  84.9 us (13%)
  local copies, waits for them, and re-layouts  21.8 us (3%)
  Pallas kernels  16.4 us (2%)
  other arithmetic  10.8 us (2%)
    ppermute x2, waiting for transfers between devices, step(): lax.ppermute(box, 's', ODD)  342 us
    ppermute x2, starting transfers between devices, half_sum(): return mine + lax.ppermute(theirs, 'c', SWAP)  34.3 us
    all_to_all x3, blocking collectives, spread(): return lax.all_to_all(sent, 'y', 0, 0)  30.4 us
    all_gather x2, blocking collectives, extra(): return (lax.all_gather(h_y, 'z'), lax.all_gather(low_in, 'z'))  26.2 us
    ppermute x8, starting transfers between devices, swapped(): return lax.ppermute(value, ('s', 'c'), PAIRS)  20.1 us
    ppermute x1, waiting for transfers between devices, around(): left_3 = lax.ppermute(left_2, ('s', 'z'), LEFT)  18.3 us
    pallas_call x2, Pallas kernels, run_stage(): pl.pallas_call(functools.partial(stage_kernel, group=cols // 16), in_spec...  16.4 us
    ppermute x1, waiting for transfers between devices, local(): left_1 = lax.ppermute(second, ('s', 'z'), LEFT)  15.6 us
  transfers between devices with their start and end apart: 23, of which 11 were waited for; matrix products, arithmetic and copies ran while one was open for 3% of the time, Pallas kernels for 0%

profile of v9, /device:TPU:1, one launch (start us, length us, event | category | flops | bytes accessed | tf_op | source)
XLA Modules:
  0.0 663.1 jit_solution(8417206812354498488)
XLA Ops:
  0.7 1.2 fusion.40
  1.8 1.3 collective-permute-start.15
  3.1 1.1 dynamic-slice_bitcast_fusion.2
  4.3 1.7 constant_dynamic-slice_fusion.1
  6.0 3.5 copy.32
  9.6 2.7 slice_bitcast_fusion.4
  13.8 8.7 %collective-permute-done.15 = bf16[64,1280]{1,0:T(8,128)(2,1)} collective-permute-done((bf16[64,1280]{1,0:T(8,128)(2,1)S(1)}, bf16[64,1280]{1,0:T(8,128)(2,1)}, u32[]{:S(2)}, u32[]{:S(2)}) %collective-permute-start.15) | collective-permute-done | bytes 163872 | tf_op jit(solution)/shard_map/ppermute | solution.py:222
  22.5 6.7 %collective-permute-start.19 = (f32[1,640]{1,0:T(1,128)S(1)}, f32[1,640]{1,0:T(1,128)S(1)}, u32[]{:S(2)}, u32[]{:S(2)}) collective-permute-start(f32[1,640]{1,0:T(1,128)S(1)} %copy-done.9), channel_id=1, source_target_pairs={{0,4},{4,0},{1,5},{5,1},{2,6},{6,2},{3,7},{7,3},{8,12},{12,8},{9,1... | collective-permute-start | bytes 7688 | tf_op jit(solution)/shard_map/ppermute | solution.py:31
  29.6 1.9 collective-permute-start.18
  31.5 1.9 collective-permute-start.16
  33.4 5.2 collective-permute-start.17
  38.6 14.5 %conditional.7 = (bf16[4,2,32,1280]{3,2,1,0:T(8,128)(2,1)S(1)}) conditional(s32[]{:T(128)} %convert_element_type.97, bf16[64,1280]{1,0:T(8,128)(2,1)} %collective-permute-done.15, () %tuple.110), branch_computations={%region_0.0_spmd, %region_1.0_spmd} | conditional | bytes 2129928 | solution.py:232
  39.6 13.5 %all_to_all.21 = bf16[4,64,1280]{2,1,0:T(8,128)(2,1)S(1)} all-to-all(bf16[4,64,1280]{2,1,0:T(8,128)(2,1)S(1)} %broadcast_in_dim.97), channel_id=1, replica_groups=mesh['s'=16,'y'=4,'c'=2,'z'=4] {'y'}, dimensions={0} | all-to-all | bytes 1310720 | tf_op jit(solution)/shard_map/cond/branch_0_fun/all_to_all | solution.py:49
  53.8 1.7 multiply_convert_fusion
  57.7 15.6 %collective-permute-done.17 = bf16[640,640]{1,0:T(8,128)(2,1)} collective-permute-done((bf16[640,640]{1,0:T(8,128)(2,1)}, bf16[640,640]{1,0:T(8,128)(2,1)}, u32[]{:S(2)}, u32[]{:S(2)}) %collective-permute-start.17) | collective-permute-done | bytes 819232 | tf_op jit(solution)/shard_map/ppermute | solution.py:227
  73.4 92.4 %conditional.8 = (bf16[640,640]{1,0:T(8,128)(2,1)}, bf16[640,640]{1,0:T(8,128)(2,1)}, bf16[640,640]{1,0:T(8,128)(2,1)}, bf16[640,640]{1,0:T(8,128)(2,1)}, bf16[6...) conditional(s32[]{:T(128)} %convert_element_type.97, ...), branch_computations={%region_4.5_spmd, %region_5.8_spmd} | conditional | flops 856874752 | bytes 42737836 | solution.py:317
  73.4 1.9 collective-permute-start
  75.3 2.4 collective-permute-start.4
  77.7 5.4 collective-permute-start.1
  83.2 2.2 collective-permute-start.5
  85.4 2.1 collective-permute-start.2
  87.5 9.2 %collective-permute-done = bf16[640,640]{1,0:T(8,128)(2,1)} collective-permute-done((bf16[640,640]{1,0:T(8,128)(2,1)}, bf16[640,640]{1,0:T(8,128)(2,1)}, u32[]{:S(2)}, u32[]{:S(2)}) %collective-permute-start) | collective-permute-done | bytes 819232 | tf_op jit(solution)/shard_map/cond/branch_0_fun/ppermute | solution.py:299
  96.8 4.2 collective-permute-start.3
  101.0 14.2 %collective-permute-done.1 = bf16[640,640]{1,0:T(8,128)(2,1)} collective-permute-done((bf16[640,640]{1,0:T(8,128)(2,1)}, bf16[640,640]{1,0:T(8,128)(2,1)}, u32[]{:S(2)}, u32[]{:S(2)}) %collective-permute-start.1) | collective-permute-done | bytes 819232 | tf_op jit(solution)/shard_map/cond/branch_0_fun/ppermute | solution.py:300
  115.2 2.2 collective-permute-start.6
  117.4 4.9 collective-permute-start.7
  122.3 2.9 collective-permute-start.8
  125.2 1.9 collective-permute-start.9
  127.2 11.5 %collective-permute-done.6 = bf16[640,640]{1,0:T(8,128)(2,1)} collective-permute-done((bf16[640,640]{1,0:T(8,128)(2,1)}, bf16[640,640]{1,0:T(8,128)(2,1)}, u32[]{:S(2)}, u32[]{:S(2)}) %collective-permute-start.6) | collective-permute-done | bytes 819232 | tf_op jit(solution)/shard_map/cond/branch_0_fun/ppermute | solution.py:303
  138.6 18.3 %collective-permute-done.7 = bf16[640,640]{1,0:T(8,128)(2,1)} collective-permute-done((bf16[640,640]{1,0:T(8,128)(2,1)}, bf16[640,640]{1,0:T(8,128)(2,1)}, u32[]{:S(2)}, u32[]{:S(2)}) %collective-permute-start.7) | collective-permute-done | bytes 819232 | tf_op jit(solution)/shard_map/cond/branch_0_fun/ppermute | solution.py:304
  156.9 2.4 collective-permute-start.10
  159.4 1.9 collective-permute-start.11
  161.7 2.3 collective-permute-done.11
  168.0 426.5 %while.31 = (s32[]{:T(128)}, bf16[32,1408]{1,0:T(8,128)(2,1)}, bf16[2,32,1408]{2,1,0:T(8,128)(2,1)S(1)}, bf16[2,32,64]{2,1,0:T(8,128)(2,1)}, bf16[2,32,1280]{2,1...) while((s32[]{:T(128)}, bf16[32,1408]{1,0:T(8,128)(2,1)}, ...), condition=%wide.region_20.21_spmd, body=%wide.region_8.20_spmd.sunk | while | flops 419431456 | bytes 15656242 | solution.py:381
  171.9 40.1 %conditional.15 = ((bf16[4,64,1280]{2,1,0:T(8,128)(2,1)}, bf16[4,8,8,16]{3,2,1,0:T(8,128)(2,1)})) conditional(s32[]{:T(128)} %convert_element_type.137, (bf16[4,64,1280]{2,1,0:T(8,128)(2,1)}, bf16[4,8,8,16]{3,2,1,0:T(8,128)(2,1)}) %tuple.155, (bf16[64,1280]{1,0:T(8,128)(2,1)}, f32[8,8,16]{2,1,0:T(8,128)S(1)}) %tuple.156), branch_computations={%region_17.17_spmd, %region_18.19_spmd} | conditional | flops 1024 | bytes 835608 | solution.py:365
  171.9 15.3 %all-gather = bf16[256,1280]{1,0:T(8,128)(2,1)} all-gather(bf16[64,1280]{1,0:T(8,128)(2,1)} %get-tuple-element.1157), channel_id=2, replica_groups=mesh['s'=16,'y'=4,'c'=2,'z'=4] {'z'}, dimensions={0}, use_global_device_ids=true | all-gather | bytes 819200 | tf_op jit(solution)/shard_map/while/body/eval_jaxpr/cond/branch_1_fun/all_gather | solution.py:251
  187.2 13.8 %psum.12 = bf16[8,8,16]{2,1,0:T(8,128)(2,1)S(1)} all-reduce(f32[8,8,16]{2,1,0:T(8,128)S(1)} %get-tuple-element.1158), channel_id=1, replica_groups=mesh['s'=16,'y'=4,'c'=2,'z'=4] {'y'}, use_global_device_ids=true, to_apply=%region_19.18 | all-reduce | flops 1024 | bytes 6144 | tf_op jit(solution)/shard_map/while/body/eval_jaxpr/cond/branch_1_fun/psum | solution.py:250
  201.0 11.0 %all-gather.1 = bf16[32,8,16]{2,1,0:T(8,128)(2,1)} all-gather(bf16[8,8,16]{2,1,0:T(8,128)(2,1)S(1)} %psum.12), channel_id=3, replica_groups=mesh['s'=16,'y'=4,'c'=2,'z'=4] {'z'}, dimensions={0}, use_global_device_ids=true | all-gather | bytes 10240 | tf_op jit(solution)/shard_map/while/body/eval_jaxpr/cond/branch_1_fun/all_gather | solution.py:251
  212.5 331.6 %conditional.14 = (bf16[32,1408]{1,0:T(8,128)(2,1)}) conditional(s32[]{:T(128)} %clamp.35, bf16[32,1408]{1,0:T(8,128)(2,1)} %get-tuple-element.1731, bf16[32,1408]{1,0:T(8,128)(2,1)} %get-tuple-element.1731, bf16[32,1408]{1,0:T(8,128)(2,1)} %get-tuple-element.1731), branch_computations={%region_14.14_spmd, %region_15.15_spmd, %region_16.16_spmd} | conditional | bytes 540720 | solution.py:356
  212.5 1.3 collective-permute-start.12
  213.8 329.6 %collective-permute-done.12 = bf16[32,1408]{1,0:T(8,128)(2,1)S(1)} collective-permute-done((bf16[32,1408]{1,0:T(8,128)(2,1)}, bf16[32,1408]{1,0:T(8,128)(2,1)S(1)}, u32[]{:S(2)}, u32[]{:S(2)}) %collective-permute-start.12) | collective-permute-done | bytes 90144 | tf_op jit(solution)/shard_map/while/body/eval_jaxpr/cond/branch_1_fun/ppermute | solution.py:360
  544.1 17.7 %conditional.13 = ((bf16[2,32,1408]{2,1,0:T(8,128)(2,1)S(1)}, bf16[2,32,64]{2,1,0:T(8,128)(2,1)}, bf16[2,32,1280]{2,1,0:T(8,128)(2,1)}, bf16[2,32,128]{2,1,0:T(8,128)(2,1)}, bf16[32,1408]{1,0:T(8,128)(2,1)})) conditional(s32[]{:T(128)} %clamp.36, (bf16[2,32,1408]{2,1,0:T(8,128)(2,1)S(1)}, bf16[2,32,64]{2,1,0:T(8,128)(2,1)}, ...), branch_computations={%region_9.9_spmd, %region_10.10_spmd, %region_11.13_spmd} | conditional | flops 419430400 | bytes 14278758 | solution.py:353
  544.1 9.4 %conditional = (bf16[4,32,1408]{2,1,0:T(8,128)(2,1)S(1)}) conditional(s32[]{:T(128)} %convert_element_type.81, bf16[32,1408]{1,0:T(8,128)(2,1)} %get-tuple-element.1125, () %tuple.89), branch_computations={%region_12.11_spmd, %region_13.12_spmd} | conditional | bytes 1171464 | solution.py:335
  545.0 8.4 %all_to_all.22 = bf16[4,32,1408]{2,1,0:T(8,128)(2,1)S(1)} all-to-all(bf16[4,32,1408]{2,1,0:T(8,128)(2,1)S(1)} %broadcast_in_dim.139), channel_id=1, replica_groups=mesh['s'=16,'y'=4,'c'=2,'z'=4] {'y'}, dimensions={0} | all-to-all | bytes 720896 | tf_op jit(solution)/shard_map/while/body/eval_jaxpr/cond/branch_2_fun/cond/branch_0_fun/all_to_all | solution.py:49
  553.5 8.2 %stage.1 = (bf16[32,1408]{1,0:T(8,128)(2,1)}, bf16[2,32,1408]{2,1,0:T(8,128)(2,1)S(1)}, bf16[2,32,64]{2,1,0:T(8,128)(2,1)}, bf16[2,32,1280]{2,1,0:T(8,128)(2,1)}, bf16[2,32,128]{2,1,0:T(8,128)(2,1)}) custom-call(s32[4]{0:T(128)S(1)} %pad_add_fusion.place_ref, ...), custom_call_target="tpu_custom_call", output_to_operand_aliasing={{1}: (24, {}), {2}: (25, {}), {3}: (26, {}), {4}: (27, {})} | custom-call | flops 419430400 | bytes 13107200 | tf_op jit(solution)/shard_map/while/body/eval_jaxpr/cond/branch_2_fun/stage/pallas_call | solution.py:161
  562.0 14.8 %conditional.14 = (bf16[32,1408]{1,0:T(8,128)(2,1)}) conditional(s32[]{:T(128)} %clamp.35, bf16[32,1408]{1,0:T(8,128)(2,1)} %get-tuple-element.1731, bf16[32,1408]{1,0:T(8,128)(2,1)} %get-tuple-element.1731, bf16[32,1408]{1,0:T(8,128)(2,1)} %get-tuple-element.1731), branch_computations={%region_14.14_spmd, %region_15.15_spmd, %region_16.16_spmd} | conditional | bytes 540720 | solution.py:356
  562.0 1.3 collective-permute-start.12
  563.3 12.8 %collective-permute-done.12 = bf16[32,1408]{1,0:T(8,128)(2,1)S(1)} collective-permute-done((bf16[32,1408]{1,0:T(8,128)(2,1)}, bf16[32,1408]{1,0:T(8,128)(2,1)S(1)}, u32[]{:S(2)}, u32[]{:S(2)}) %collective-permute-start.12) | collective-permute-done | bytes 90144 | tf_op jit(solution)/shard_map/while/body/eval_jaxpr/cond/branch_1_fun/ppermute | solution.py:360
  576.8 17.7 %conditional.13 = ((bf16[2,32,1408]{2,1,0:T(8,128)(2,1)S(1)}, bf16[2,32,64]{2,1,0:T(8,128)(2,1)}, bf16[2,32,1280]{2,1,0:T(8,128)(2,1)}, bf16[2,32,128]{2,1,0:T(8,128)(2,1)}, bf16[32,1408]{1,0:T(8,128)(2,1)})) conditional(s32[]{:T(128)} %clamp.36, (bf16[2,32,1408]{2,1,0:T(8,128)(2,1)S(1)}, bf16[2,32,64]{2,1,0:T(8,128)(2,1)}, ...), branch_computations={%region_9.9_spmd, %region_10.10_spmd, %region_11.13_spmd} | conditional | flops 419430400 | bytes 14278758 | solution.py:353
  576.8 9.4 %conditional = (bf16[4,32,1408]{2,1,0:T(8,128)(2,1)S(1)}) conditional(s32[]{:T(128)} %convert_element_type.81, bf16[32,1408]{1,0:T(8,128)(2,1)} %get-tuple-element.1125, () %tuple.89), branch_computations={%region_12.11_spmd, %region_13.12_spmd} | conditional | bytes 1171464 | solution.py:335
  577.7 8.4 %all_to_all.22 = bf16[4,32,1408]{2,1,0:T(8,128)(2,1)S(1)} all-to-all(bf16[4,32,1408]{2,1,0:T(8,128)(2,1)S(1)} %broadcast_in_dim.139), channel_id=1, replica_groups=mesh['s'=16,'y'=4,'c'=2,'z'=4] {'y'}, dimensions={0} | all-to-all | bytes 720896 | tf_op jit(solution)/shard_map/while/body/eval_jaxpr/cond/branch_2_fun/cond/branch_0_fun/all_to_all | solution.py:49
  586.2 8.2 %stage.1 = (bf16[32,1408]{1,0:T(8,128)(2,1)}, bf16[2,32,1408]{2,1,0:T(8,128)(2,1)S(1)}, bf16[2,32,64]{2,1,0:T(8,128)(2,1)}, bf16[2,32,1280]{2,1,0:T(8,128)(2,1)}, bf16[2,32,128]{2,1,0:T(8,128)(2,1)}) custom-call(s32[4]{0:T(128)S(1)} %pad_add_fusion.place_ref, ...), custom_call_target="tpu_custom_call", output_to_operand_aliasing={{1}: (24, {}), {2}: (25, {}), {3}: (26, {}), {4}: (27, {})} | custom-call | flops 419430400 | bytes 13107200 | tf_op jit(solution)/shard_map/while/body/eval_jaxpr/cond/branch_2_fun/stage/pallas_call | solution.py:161
  595.5 14.4 %all-gather.4 = bf16[256,1408]{1,0:T(8,128)(2,1)S(1)} all-gather(bf16[64,1408]{1,0:T(8,128)(2,1)S(1)} %fusion.19), channel_id=6, replica_groups=mesh['s'=16,'y'=4,'c'=2,'z'=4] {'z'}, dimensions={0}, use_global_device_ids=true | all-gather | bytes 901120 | tf_op jit(solution)/shard_map/all_gather | solution.py:405
  609.9 1.1 fusion.13
  611.9 32.4 %collective-permute-start.22 = (f32[8,16,640]{2,1,0:T(8,128)}, f32[8,16,640]{2,1,0:T(8,128)}, u32[]{:S(2)}, u32[]{:S(2)}) collective-permute-start(f32[8,16,640]{2,1,0:T(8,128)} %slice_select_fusion), channel_id=1, source_target_pairs={{0,4},{4,0},{1,5},{5,1},{2,6},{6,2},{3,7},{7,3},{8,12},{12,8},{9,1... | collective-permute-start | bytes 983048 | tf_op jit(solution)/shard_map/ppermute | solution.py:44
  644.8 1.4 broadcast_in_dim.162
  646.2 3.3 all-to-all-start.4
  649.5 1.4 fusion.14
  650.8 3.1 all-to-all-done.4
  654.2 3.1 collective-permute-start.20
  657.3 1.9 collective-permute-start.21
  659.9 1.0 select_add_fusion
  661.0 1.0 select_reduce_fusion
  662.1 1.0 select_reduce_fusion.1
  (173 shorter events, 18.0 us)
Async XLA Ops:
  0.6 11.9 %copy-start = (bf16[1,8,16,5120]{3,2,1,0:T(8,128)(2,1)S(1)}, bf16[1,8,16,5120]{3,2,1,0:T(8,128)(2,1)}, u32[]{:S(2)}) copy-start(bf16[1,8,16,5120]{3,2,1,0:T(8,128)(2,1)} %param.31) | copy-start | bytes 3932164
  1.8 7.7 %copy-start.5 = (bf16[64,1280]{1,0:T(8,128)(2,1)}, bf16[64,1280]{1,0:T(8,128)(2,1)S(1)}, u32[]{:S(2)}) copy-start(bf16[64,1280]{1,0:T(8,128)(2,1)S(1)} %fusion.40) | copy-start | bytes 491524
  1.8 20.6 %collective-permute-start.15 = (bf16[64,1280]{1,0:T(8,128)(2,1)S(1)}, bf16[64,1280]{1,0:T(8,128)(2,1)}, u32[]{:S(2)}, u32[]{:S(2)}) collective-permute-start(bf16[64,1280]{1,0:T(8,128)(2,1)S(1)} %fusion.40), channel_id=1, source_target_pairs={{480,448},{448,416},{416,384},{384,352},{352,320},{320,288},{288,2... | collective-permute-start | bytes 491528 | tf_op jit(solution)/shard_map/ppermute | solution.py:222
  9.6 2.8 copy-start.10
  9.6 2.8 copy-start.11
  12.3 10.2 %copy-start.9 = (f32[1,640]{1,0:T(1,128)S(1)}, f32[1,640]{1,0:T(1,128)}, u32[]{:S(2)}) copy-start(f32[1,640]{1,0:T(1,128)} %param.29) | copy-start | bytes 7684
  22.5 30.6 %collective-permute-start.19 = (f32[1,640]{1,0:T(1,128)S(1)}, f32[1,640]{1,0:T(1,128)S(1)}, u32[]{:S(2)}, u32[]{:S(2)}) collective-permute-start(f32[1,640]{1,0:T(1,128)S(1)} %copy-done.9), channel_id=1, source_target_pairs={{0,4},{4,0},{1,5},{5,1},{2,6},{6,2},{3,7},{7,3},{8,12},{12,8},{9,1... | collective-permute-start | bytes 7688 | tf_op jit(solution)/shard_map/ppermute | solution.py:31
  29.4 26.1 %copy-start.7 = (bf16[1,8,640,16]{2,3,1,0:T(8,128)(2,1)S(1)}, bf16[1,8,640,16]{2,3,1,0:T(8,128)(2,1)}, u32[]{:S(2)}) copy-start(bf16[1,8,640,16]{2,3,1,0:T(8,128)(2,1)} %param.30) | copy-start | bytes 491524
  29.6 25.9 %collective-permute-start.18 = (bf16[8,640,16]{1,2,0:T(8,128)(2,1)}, bf16[8,640,16]{1,2,0:T(8,128)(2,1)}, u32[]{:S(2)}, u32[]{:S(2)}) collective-permute-start(bf16[8,640,16]{1,2,0:T(8,128)(2,1)} %bitcast.119), channel_id=1, source_target_pairs={{0,4},{4,0},{1,5},{5,1},{2,6},{6,2},{3,7},{7,3},{8,12},{12,8},{9,1... | collective-permute-start | bytes 491528 | tf_op jit(solution)/shard_map/ppermute | solution.py:31
  31.5 26.2 %collective-permute-start.16 = (bf16[640,640]{1,0:T(8,128)(2,1)}, bf16[640,640]{1,0:T(8,128)(2,1)}, u32[]{:S(2)}, u32[]{:S(2)}) collective-permute-start(bf16[640,640]{1,0:T(8,128)(2,1)} %get-tuple-element.1808), channel_id=1, source_target_pairs={{0,1},{1,2},{2,3},{3,0},{32,33},{33,34},{34,35},{35,32},{64,65},{6... | collective-permute-start | bytes 2457608 | tf_op jit(solution)/shard_map/ppermute | solution.py:226
  33.4 39.9 %collective-permute-start.17 = (bf16[640,640]{1,0:T(8,128)(2,1)}, bf16[640,640]{1,0:T(8,128)(2,1)}, u32[]{:S(2)}, u32[]{:S(2)}) collective-permute-start(bf16[640,640]{1,0:T(8,128)(2,1)} %get-tuple-element.1809), channel_id=1, source_target_pairs={{0,3},{1,0},{2,1},{3,2},{32,35},{33,32},{34,33},{35,34},{64,67},{6... | collective-permute-start | bytes 2457608 | tf_op jit(solution)/shard_map/ppermute | solution.py:227
  53.1 3.4 copy-start.1
  56.5 0.9 copy-start.2
  73.4 23.4 %collective-permute-start = (bf16[640,640]{1,0:T(8,128)(2,1)}, bf16[640,640]{1,0:T(8,128)(2,1)}, u32[]{:S(2)}, u32[]{:S(2)}) collective-permute-start(bf16[640,640]{1,0:T(8,128)(2,1)} %get-tuple-element.1091), channel_id=1, source_target_pairs={{0,1},{1,2},{2,3},{3,0},{32,33},{33,34},{34,35},{35,32},{64,65},{6... | collective-permute-start | bytes 2457608 | tf_op jit(solution)/shard_map/cond/branch_0_fun/ppermute | solution.py:299
  75.3 39.9 %collective-permute-start.4 = (bf16[640,640]{1,0:T(8,128)(2,1)}, bf16[640,640]{1,0:T(8,128)(2,1)}, u32[]{:S(2)}, u32[]{:S(2)}) collective-permute-start(bf16[640,640]{1,0:T(8,128)(2,1)} %get-tuple-element.1091), channel_id=1, source_target_pairs={{0,4},{4,0},{32,36},{36,32},{64,68},{68,64},{96,100},{100,96},{128... | collective-permute-start | bytes 2457608 | tf_op jit(solution)/shard_map/cond/branch_0_fun/ppermute | solution.py:297
  77.7 37.4 %collective-permute-start.1 = (bf16[640,640]{1,0:T(8,128)(2,1)}, bf16[640,640]{1,0:T(8,128)(2,1)}, u32[]{:S(2)}, u32[]{:S(2)}) collective-permute-start(bf16[640,640]{1,0:T(8,128)(2,1)} %get-tuple-element.1092), channel_id=1, source_target_pairs={{0,3},{1,0},{2,1},{3,2},{32,35},{33,32},{34,33},{35,34},{64,67},{6... | collective-permute-start | bytes 2457608 | tf_op jit(solution)/shard_map/cond/branch_0_fun/ppermute | solution.py:300
  83.2 32.0 %collective-permute-start.5 = (bf16[640,640]{1,0:T(8,128)(2,1)}, bf16[640,640]{1,0:T(8,128)(2,1)}, u32[]{:S(2)}, u32[]{:S(2)}) collective-permute-start(bf16[640,640]{1,0:T(8,128)(2,1)} %get-tuple-element.1092), channel_id=1, source_target_pairs={{0,4},{4,0},{32,36},{36,32},{64,68},{68,64},{96,100},{100,96},{128... | collective-permute-start | bytes 2457608 | tf_op jit(solution)/shard_map/cond/branch_0_fun/ppermute | solution.py:297
  85.4 29.8 %collective-permute-start.2 = (bf16[640,640]{1,0:T(8,128)(2,1)}, bf16[640,640]{1,0:T(8,128)(2,1)}, u32[]{:S(2)}, u32[]{:S(2)}) collective-permute-start(bf16[640,640]{1,0:T(8,128)(2,1)} %get-tuple-element.1093), channel_id=1, source_target_pairs={{0,4},{4,0},{32,36},{36,32},{64,68},{68,64},{96,100},{100,96},{128... | collective-permute-start | bytes 2457608 | tf_op jit(solution)/shard_map/cond/branch_0_fun/ppermute | solution.py:297
  96.8 18.4 %collective-permute-start.3 = (bf16[640,640]{1,0:T(8,128)(2,1)}, bf16[640,640]{1,0:T(8,128)(2,1)}, u32[]{:S(2)}, u32[]{:S(2)}) collective-permute-start(bf16[640,640]{1,0:T(8,128)(2,1)} %get-tuple-element.1094), channel_id=1, source_target_pairs={{0,4},{4,0},{32,36},{36,32},{64,68},{68,64},{96,100},{100,96},{128... | collective-permute-start | bytes 2457608 | tf_op jit(solution)/shard_map/cond/branch_0_fun/ppermute | solution.py:297
  115.2 23.4 %collective-permute-start.6 = (bf16[640,640]{1,0:T(8,128)(2,1)}, bf16[640,640]{1,0:T(8,128)(2,1)}, u32[]{:S(2)}, u32[]{:S(2)}) collective-permute-start(bf16[640,640]{1,0:T(8,128)(2,1)} %collective-permute-done), channel_id=1, source_target_pairs={{0,1},{1,2},{2,3},{3,0},{32,33},{33,34},{34,35},{35,32},{64,65},{6... | collective-permute-start | bytes 2457608 | tf_op jit(solution)/shard_map/cond/branch_0_fun/ppermute | solution.py:303
  117.4 39.5 %collective-permute-start.7 = (bf16[640,640]{1,0:T(8,128)(2,1)}, bf16[640,640]{1,0:T(8,128)(2,1)}, u32[]{:S(2)}, u32[]{:S(2)}) collective-permute-start(bf16[640,640]{1,0:T(8,128)(2,1)} %collective-permute-done.1), channel_id=1, source_target_pairs={{0,3},{1,0},{2,1},{3,2},{32,35},{33,32},{34,33},{35,34},{64,67},{6... | collective-permute-start | bytes 2457608 | tf_op jit(solution)/shard_map/cond/branch_0_fun/ppermute | solution.py:304
  122.3 34.6 %collective-permute-start.8 = (bf16[640,640]{1,0:T(8,128)(2,1)}, bf16[640,640]{1,0:T(8,128)(2,1)}, u32[]{:S(2)}, u32[]{:S(2)}) collective-permute-start(bf16[640,640]{1,0:T(8,128)(2,1)} %collective-permute-done), channel_id=1, source_target_pairs={{0,4},{4,0},{32,36},{36,32},{64,68},{68,64},{96,100},{100,96},{128... | collective-permute-start | bytes 2457608 | tf_op jit(solution)/shard_map/cond/branch_0_fun/ppermute | solution.py:297
  125.2 31.7 %collective-permute-start.9 = (bf16[640,640]{1,0:T(8,128)(2,1)}, bf16[640,640]{1,0:T(8,128)(2,1)}, u32[]{:S(2)}, u32[]{:S(2)}) collective-permute-start(bf16[640,640]{1,0:T(8,128)(2,1)} %collective-permute-done.1), channel_id=1, source_target_pairs={{0,4},{4,0},{32,36},{36,32},{64,68},{68,64},{96,100},{100,96},{128... | collective-permute-start | bytes 2457608 | tf_op jit(solution)/shard_map/cond/branch_0_fun/ppermute | solution.py:297
  156.9 4.7 collective-permute-start.10
  159.4 4.6 collective-permute-start.11
  212.5 330.9 %collective-permute-start.12 = (bf16[32,1408]{1,0:T(8,128)(2,1)}, bf16[32,1408]{1,0:T(8,128)(2,1)S(1)}, u32[]{:S(2)}, u32[]{:S(2)}) collective-permute-start(bf16[32,1408]{1,0:T(8,128)(2,1)} %param.10), channel_id=1, source_target_pairs={{480,448},{416,384},{352,320},{288,256},{224,192},{160,128},{96,64... | collective-permute-start | bytes 270344 | tf_op jit(solution)/shard_map/while/body/eval_jaxpr/cond/branch_1_fun/ppermute | solution.py:360
  562.0 14.1 %collective-permute-start.12 = (bf16[32,1408]{1,0:T(8,128)(2,1)}, bf16[32,1408]{1,0:T(8,128)(2,1)S(1)}, u32[]{:S(2)}, u32[]{:S(2)}) collective-permute-start(bf16[32,1408]{1,0:T(8,128)(2,1)} %param.10), channel_id=1, source_target_pairs={{480,448},{416,384},{352,320},{288,256},{224,192},{160,128},{96,64... | collective-permute-start | bytes 270344 | tf_op jit(solution)/shard_map/while/body/eval_jaxpr/cond/branch_1_fun/ppermute | solution.py:360
  611.1 42.9 %copy-start.3 = (bf16[2,32,1280]{2,1,0:T(8,128)(2,1)S(1)}, bf16[2,32,1280]{2,1,0:T(8,128)(2,1)}, u32[]{:S(2)}) copy-start(bf16[2,32,1280]{2,1,0:T(8,128)(2,1)} %get-tuple-element.1930) | copy-start | bytes 491524
  611.9 48.1 %collective-permute-start.22 = (f32[8,16,640]{2,1,0:T(8,128)}, f32[8,16,640]{2,1,0:T(8,128)}, u32[]{:S(2)}, u32[]{:S(2)}) collective-permute-start(f32[8,16,640]{2,1,0:T(8,128)} %slice_select_fusion), channel_id=1, source_target_pairs={{0,4},{4,0},{1,5},{5,1},{2,6},{6,2},{3,7},{7,3},{8,12},{12,8},{9,1... | collective-permute-start | bytes 983048 | tf_op jit(solution)/shard_map/ppermute | solution.py:44
  646.2 7.7 %all-to-all-start.4 = ((bf16[4,2,32,128]{3,2,1,0:T(8,128)(2,1)}), bf16[4,2,32,128]{3,2,1,0:T(8,128)(2,1)S(1)}, u32[]{:S(2)}, u32[]{:S(2)}) async-start(bf16[4,2,32,128]{3,2,1,0:T(8,128)(2,1)} %broadcast_in_dim.162), calls=%async_computation.4 | async-start | bytes 131072 | tf_op jit(solution)/shard_map/all_to_all | solution.py:49
  654.1 6.8 %copy-start.8 = (pred[8,8]{1,0:T(8,128)(4,1)S(1)}, pred[8,8]{1,0:T(8,128)(4,1)}, u32[]{:S(2)}) copy-start(pred[8,8]{1,0:T(8,128)(4,1)} %iota_compare_fusion.4) | copy-start | bytes 196
  654.2 5.0 collective-permute-start.20
  657.3 4.7 collective-permute-start.21

commit v10 on v9

--- a/solution.py
+++ b/solution.py
@@ -220,8 +220,24 @@
     x_tokens = lax.dynamic_slice_in_dim(section_inputs[0], core * toks, toks, 1)
     x_y = lax.dynamic_slice_in_dim(x_tokens, ypos * width, width, 2).reshape(rows_all, width)
     x_moved = lax.ppermute(x_y, "s", EVERY)
-    x_moved, first, second, norm_gain, adapter_down, x_tokens = lax.optimization_barrier(
-        (x_moved, first, second, norm_gain, adapter_down, x_tokens)
+    first, second, norm_gain, adapter_down = lax.optimization_barrier(
+        (first, second, norm_gain, adapter_down)
+    )
+    gain_y = both_cores(norm_gain, 1)
+    down_y = both_cores(adapter_down[0], 1)
+    empty = (
+        jnp.zeros((CHUNKS, rows, width + TAIL), bf16),
+        jnp.zeros((CHUNKS, rows, group * rank), bf16),
+        jnp.zeros((CHUNKS, rows, width), bf16),
+        jnp.zeros((CHUNKS, rows, TAIL), bf16),
+    )
+    idle = (
+        jnp.zeros((rows, width + TAIL), bf16),
+        jnp.zeros((4, rows_all, width), bf16),
+        jnp.zeros((4, micro, toks, rank), bf16),
+    )
+    x_moved, first, second, gain_y, down_y, x_tokens, empty, idle = lax.optimization_barrier(
+        (x_moved, first, second, gain_y, down_y, x_tokens, empty, idle)
     )
     right_1 = lax.ppermute(first, ("s", "z"), RIGHT)
     left_1 = lax.ppermute(second, ("s", "z"), LEFT)
@@ -232,8 +248,6 @@
     x_before = lax.cond(
         sec == 15, lambda x: jnp.zeros((4,) + x.shape, x.dtype), spread, x_moved
     )
-    gain_y = both_cores(norm_gain, 1)
-    down_y = both_cores(adapter_down[0], 1)
     h_y = (normed_y * gain_y).astype(bf16)
 
     iota = jnp.arange(micro, dtype=jnp.int32)
@@ -256,12 +270,8 @@
     down_chunk = down_sel.transpose(0, 2, 1).reshape(CHUNKS, group * rank, width)
     up_chunk = up_sel.reshape(CHUNKS, group * rank, width_all)
 
-    ready = (x_before, x_chunk, inv_chunk, down_chunk, up_chunk, gain_y)
-    right_1, left_1, ready = lax.optimization_barrier((right_1, left_1, ready))
-    x_before, x_chunk, inv_chunk, down_chunk, up_chunk, gain_y = ready
-
     def top(args):
-        out_grads, first, second = args[:3]
+        out_grads, first, second, _ = args
         shard = jnp.concatenate([first, second], 0)
         shard_x = lax.ppermute(shard, ("s", "c"), TOP_SWAP)
         grad = lax.dynamic_slice_in_dim(out_grads, core * toks, toks, 1)
@@ -287,35 +297,28 @@
         low = jnp.where(member[:, :, None], low.reshape(rows_all, 1, rank), 0)
         low = low.astype(bf16).reshape(CHUNKS, rows, group * rank)
         tail = tail.reshape(CHUNKS, rows, TAIL)
-        moved = tuple(jnp.zeros(first.shape, first.dtype) for _ in range(12))
-        return moved, (boxes, low, grad_y.reshape(CHUNKS, rows, width), tail)
-
-    def around(args):
-        _, first, second, right_1, left_1 = args
-
-        def swapped(value):
-            return lax.ppermute(value, ("s", "c"), PAIRS)
-
-        right_2 = lax.ppermute(right_1, ("s", "z"), RIGHT)
-        left_2 = lax.ppermute(left_1, ("s", "z"), LEFT)
-        others = [swapped(w) for w in (first, second, right_1, left_1)]
-        right_2, left_2, others = lax.optimization_barrier((right_2, left_2, others))
-        right_3 = lax.ppermute(right_2, ("s", "z"), RIGHT)
-        left_3 = lax.ppermute(left_2, ("s", "z"), LEFT)
-        more = [swapped(w) for w in (right_2, left_2)]
-        right_3, left_3, more = lax.optimization_barrier((right_3, left_3, more))
-        more = more + [swapped(w) for w in (right_3, left_3)]
-        kept = (
-            jnp.zeros((CHUNKS, rows, width + TAIL), bf16),
-            jnp.zeros((CHUNKS, rows, group * rank), bf16),
-            jnp.zeros((CHUNKS, rows, width), bf16),
-            jnp.zeros((CHUNKS, rows, TAIL), bf16),
-        )
-        return (right_2, left_2, right_3, left_3, *others, *more), kept
-
-    args = (out_grads, first, second, right_1, left_1)
-    moved, kept = lax.cond(sec == 15, top, around, args)
-    weights = [first, second, right_1, left_1, *moved]
+        return boxes, low, grad_y.reshape(CHUNKS, rows, width), tail
+
+    def swapped(value):
+        return lax.ppermute(value, ("s", "c"), PAIRS)
+
+    ready = (x_before, x_chunk, inv_chunk, down_chunk, up_chunk, gain_y)
+    right_1, left_1, ready = lax.optimization_barrier((right_1, left_1, ready))
+    kept = lax.cond(sec == 15, top, lambda args: args[3], (out_grads, first, second, empty))
+    boxes_top = lax.ppermute(kept[0], "s", [(15, 14)])
+    right_2 = lax.ppermute(right_1, ("s", "z"), RIGHT)
+    left_2 = lax.ppermute(left_1, ("s", "z"), LEFT)
+    others = [swapped(w) for w in (first, second, right_1, left_1)]
+    right_2, left_2, others = lax.optimization_barrier((right_2, left_2, others))
+    right_3 = lax.ppermute(right_2, ("s", "z"), RIGHT)
+    left_3 = lax.ppermute(left_2, ("s", "z"), LEFT)
+    more = [swapped(w) for w in (right_2, left_2)]
+    right_3, left_3, more, kept, boxes_top, ready = lax.optimization_barrier(
+        (right_3, left_3, more, kept, boxes_top, ready)
+    )
+    x_before, x_chunk, inv_chunk, down_chunk, up_chunk, gain_y = ready
+    more = more + [swapped(w) for w in (right_3, left_3)]
+    weights = [first, second, right_1, left_1, right_2, left_2, right_3, left_3, *others, *more]
 
     def pick(array, m):
         return lax.dynamic_index_in_dim(array, m, 0, keepdims=False)
@@ -324,10 +327,6 @@
         box, kept, extras = state
         t, m = u // CHUNKS, u % CHUNKS
         turn = 15 - t + m
-
-        def stored(args):
-            _, kept = args
-            return pick(kept[0], m), kept
 
         def computed(args):
             box, kept = args
@@ -349,16 +348,19 @@
             )
             return box, tuple(kept)
 
-        kind = jnp.where(sec == turn, jnp.where(sec == 15, 1, 2), 0)
-        box, kept = lax.switch(kind, [lambda args: args, stored, computed], (box, kept))
-        part = ((sec == turn) | (sec == turn - 1)) & (turn >= 1) & (turn <= 15)
+        box, kept = lax.cond(
+            (sec == turn) & (sec < 15), computed, lambda args: args, (box, kept)
+        )
+        part = ((sec == turn) | (sec == turn - 1)) & (turn >= 1) & (turn <= 14)
         kind = jnp.where(part, jnp.where(turn % 2 == 1, 1, 2), 0)
+        kind = jnp.where((turn == 15) & (sec == 14), 3, kind)
         box = lax.switch(
             kind,
             [
                 lambda box: box,
                 lambda box: lax.ppermute(box, "s", ODD),
                 lambda box: lax.ppermute(box, "s", EVEN),
+                lambda box: pick(boxes_top, m),
             ],
             box,
         )
@@ -370,14 +372,7 @@
         )
         return box, kept, extras
 
-    start = (
-        jnp.zeros((rows, width + TAIL), bf16),
-        kept,
-        (
-            jnp.zeros((4, rows_all, width), bf16),
-            jnp.zeros((4, micro, toks, rank), bf16),
-        ),
-    )
+    start = (idle[0], kept, idle[1:])
     _, kept, extras = lax.fori_loop(0, (15 + CHUNKS) * CHUNKS, step, start)
     boxes, low_all, grad_all, tail_all = kept
     h_all, low_in_all = lax.cond(

time: 665 us -> 698 us (1.050)
  local copies, waits for them, and re-layouts: 21.8 us -> 50 us
  starting transfers between devices: 94.8 us -> 106 us
    while x0 -> x69, local copies, waits for them, and re-layouts: none -> 29.3 us
    ppermute x2, waiting for transfers between devices: 342 us -> 332 us  [step(): lax.ppermute(box, 's', ODD)]
    ppermute x2, starting transfers between devices: 34.3 us -> 42.9 us  [half_sum(): return mine + lax.ppermute(theirs, 'c', SWAP)]
    ppermute x1, waiting for transfers between devices: 8.68 us -> 15.8 us  [local(): x_moved = lax.ppermute(x_y, 's', EVERY)]
    ppermute x4 -> x5, waiting for transfers between devices: 53.3 us -> 59.3 us  [the longest x1 18.3 us: local(): left_3 = lax.ppermute(left_2, ('s', 'z'), LEFT)]
    ppermute x4 -> x5, starting transfers between devices: 14.4 us -> 15.6 us  [the longest x1 4.99 us: local(): left_2 = lax.ppermute(left_1, ('s', 'z'), LEFT)]
  transfers between devices with their start and end apart: 23 -> 24, of which waited for: 11 -> 9; matrix products, arithmetic and copies ran while one was open for 3% -> 3% of each run, Pallas kernels for 0% -> 0%
where the time goes in v10:
time: 698 us; the launch traced here: 696 us
  waiting for transfers between devices  422 us (60%)
  starting transfers between devices  106 us (15%)
  blocking collectives  83.9 us (12%)
  local copies, waits for them, and re-layouts  50 us (7%)
  Pallas kernels  16.4 us (2%)
  other arithmetic  12.2 us (2%)
    ppermute x2, waiting for transfers between devices, step(): lax.ppermute(box, 's', ODD)  332 us
    ppermute x2, starting transfers between devices, half_sum(): return mine + lax.ppermute(theirs, 'c', SWAP)  42.9 us
    all_to_all x3, blocking collectives, spread(): return lax.all_to_all(sent, 'y', 0, 0)  31.8 us
    while x68, local copies, waits for them, and re-layouts  27.8 us
    all_gather x2, blocking collectives, extra(): return (lax.all_gather(h_y, 'z'), lax.all_gather(low_in, 'z'))  25.8 us
    ppermute x8, starting transfers between devices, swapped(): return lax.ppermute(value, ('s', 'c'), PAIRS)  18.6 us
    ppermute x1, waiting for transfers between devices, local(): left_3 = lax.ppermute(left_2, ('s', 'z'), LEFT)  18.3 us
    ppermute x1, waiting for transfers between devices, local(): left_2 = lax.ppermute(left_1, ('s', 'z'), LEFT)  17.9 us
  transfers between devices with their start and end apart: 24, of which 9 were waited for; matrix products, arithmetic and copies ran while one was open for 3% of the time, Pallas kernels for 0%

profile of v10, /device:TPU:1, one launch (start us, length us, event | category | flops | bytes accessed | tf_op | source)
XLA Modules:
  0.0 695.6 jit_solution(10154769457647257931)
XLA Ops:
  0.6 3.0 copy.32
  3.6 1.3 slice_bitcast_fusion.4
  5.0 8.9 %collective-permute-start.5 = (bf16[8,640,16]{1,2,0:T(8,128)(2,1)S(1)}, bf16[8,640,16]{1,2,0:T(8,128)(2,1)S(1)}, u32[]{:S(2)}, u32[]{:S(2)}) collective-permute-start(bf16[8,640,16]{1,2,0:T(8,128)(2,1)S(1)} %bitcast.120), channel_id=1, source_target_pairs={{0,4},{4,0},{1,5},{5,1},{2,6},{6,2},{3,7},{7,3},{8,12},{12,8},{9,1... | collective-permute-start | bytes 491528 | tf_op jit(solution)/shard_map/ppermute | solution.py:31
  13.9 1.9 collective-permute-start.4
  15.8 1.1 fusion.39
  16.9 1.3 collective-permute-start.3
  18.2 2.0 dynamic-slice_bitcast_fusion.2
  21.1 15.8 %collective-permute-done.3 = bf16[64,1280]{1,0:T(8,128)(2,1)S(1)} collective-permute-done((bf16[64,1280]{1,0:T(8,128)(2,1)S(1)}, bf16[64,1280]{1,0:T(8,128)(2,1)S(1)}, u32[]{:S(2)}, u32[]{:S(2)}) %collective-permute-start.3) | collective-permute-done | bytes 163872 | tf_op jit(solution)/shard_map/ppermute | solution.py:222
  36.9 1.9 collective-permute-start.6
  38.8 2.4 collective-permute-start.10
  41.2 5.4 collective-permute-start.7
  47.4 1.7 constant_dynamic-slice_fusion.1
  49.1 2.4 collective-permute-start.11
  52.1 1.3 multiply_reduce_fusion.1
  53.5 13.7 %conditional.7 = (bf16[4,2,32,1280]{3,2,1,0:T(8,128)(2,1)}) conditional(s32[]{:T(128)} %convert_element_type.108, bf16[64,1280]{1,0:T(8,128)(2,1)S(1)} %copy-done.8, () %tuple.108), branch_computations={%region_0.1_spmd, %region_1.2_spmd} | conditional | bytes 2129928 | solution.py:248
  53.6 13.7 %all_to_all.21 = bf16[4,64,1280]{2,1,0:T(8,128)(2,1)} all-to-all(bf16[4,64,1280]{2,1,0:T(8,128)(2,1)S(1)} %broadcast_in_dim.101), channel_id=1, replica_groups=mesh['s'=16,'y'=4,'c'=2,'z'=4] {'y'}, dimensions={0} | all-to-all | bytes 1310720 | tf_op jit(solution)/shard_map/cond/branch_0_fun/all_to_all | solution.py:49
  67.3 11.5 %collective-permute-done.7 = bf16[640,640]{1,0:T(8,128)(2,1)} collective-permute-done((bf16[640,640]{1,0:T(8,128)(2,1)}, bf16[640,640]{1,0:T(8,128)(2,1)}, u32[]{:S(2)}, u32[]{:S(2)}) %collective-permute-start.7) | collective-permute-done | bytes 819232 | tf_op jit(solution)/shard_map/ppermute | solution.py:243
  78.9 2.3 collective-permute-start.12
  81.2 2.1 collective-permute-start.8
  83.3 2.3 collective-permute-start.13
  85.6 5.0 collective-permute-start.9
  90.6 14.4 %collective-permute-done.8 = bf16[640,640]{1,0:T(8,128)(2,1)} collective-permute-done((bf16[640,640]{1,0:T(8,128)(2,1)}, bf16[640,640]{1,0:T(8,128)(2,1)}, u32[]{:S(2)}, u32[]{:S(2)}) %collective-permute-start.8) | collective-permute-done | bytes 819232 | tf_op jit(solution)/shard_map/ppermute | solution.py:309
  105.1 17.9 %collective-permute-done.9 = bf16[640,640]{1,0:T(8,128)(2,1)} collective-permute-done((bf16[640,640]{1,0:T(8,128)(2,1)}, bf16[640,640]{1,0:T(8,128)(2,1)}, u32[]{:S(2)}, u32[]{:S(2)}) %collective-permute-start.9) | collective-permute-done | bytes 819232 | tf_op jit(solution)/shard_map/ppermute | solution.py:310
  123.0 2.2 collective-permute-start.14
  125.2 4.9 collective-permute-start.15
  130.1 2.9 collective-permute-start.16
  133.0 1.9 collective-permute-start.17
  136.3 1.5 collective-permute-start.18
  137.7 8.6 %collective-permute-done.14 = bf16[640,640]{1,0:T(8,128)(2,1)} collective-permute-done((bf16[640,640]{1,0:T(8,128)(2,1)}, bf16[640,640]{1,0:T(8,128)(2,1)}, u32[]{:S(2)}, u32[]{:S(2)}) %collective-permute-start.14) | collective-permute-done | bytes 819232 | tf_op jit(solution)/shard_map/ppermute | solution.py:313
  146.4 18.3 %collective-permute-done.15 = bf16[640,640]{1,0:T(8,128)(2,1)} collective-permute-done((bf16[640,640]{1,0:T(8,128)(2,1)}, bf16[640,640]{1,0:T(8,128)(2,1)}, u32[]{:S(2)}, u32[]{:S(2)}) %collective-permute-start.15) | collective-permute-done | bytes 819232 | tf_op jit(solution)/shard_map/ppermute | solution.py:314
  164.7 2.4 collective-permute-start.19
  167.1 1.9 collective-permute-start.20
  169.0 1.2 iota_compare_fusion.4
  172.7 1.7 multiply_convert_fusion
  174.5 1.4 copy.33
  178.1 440.1 %while.31 = (s32[]{:T(128)}, bf16[32,1408]{1,0:T(8,128)(2,1)}, bf16[2,32,1408]{2,1,0:T(8,128)(2,1)S(1)}, bf16[2,32,64]{2,1,0:T(8,128)(2,1)}, bf16[2,32,1280]{2,1...) while((s32[]{:T(128)}, bf16[32,1408]{1,0:T(8,128)(2,1)}, ...), condition=%wide.region_20.21_spmd, body=%wide.region_8.20_spmd.sunk | while | flops 419431456 | bytes 16967036 | solution.py:376
  200.1 37.4 %conditional.15 = ((bf16[4,64,1280]{2,1,0:T(8,128)(2,1)}, bf16[4,8,8,16]{3,2,1,0:T(8,128)(2,1)})) conditional(s32[]{:T(128)} %convert_element_type.150, (bf16[4,64,1280]{2,1,0:T(8,128)(2,1)}, bf16[4,8,8,16]{3,2,1,0:T(8,128)(2,1)}) %tuple.152, (bf16[64,1280]{1,0:T(8,128)(2,1)}, f32[8,8,16]{2,1,0:T(8,128)S(1)}) %tuple.153), branch_computations={%region_17.17_spmd, %region_18.19_spmd} | conditional | flops 1024 | bytes 835608 | solution.py:367
  200.1 14.9 %all-gather = bf16[256,1280]{1,0:T(8,128)(2,1)} all-gather(bf16[64,1280]{1,0:T(8,128)(2,1)} %get-tuple-element.1161), channel_id=2, replica_groups=mesh['s'=16,'y'=4,'c'=2,'z'=4] {'z'}, dimensions={0}, use_global_device_ids=true | all-gather | bytes 819200 | tf_op jit(solution)/shard_map/while/body/eval_jaxpr/cond/branch_1_fun/all_gather | solution.py:265
  215.0 11.6 %psum.12 = bf16[8,8,16]{2,1,0:T(8,128)(2,1)S(1)} all-reduce(f32[8,8,16]{2,1,0:T(8,128)S(1)} %get-tuple-element.1162), channel_id=1, replica_groups=mesh['s'=16,'y'=4,'c'=2,'z'=4] {'y'}, use_global_device_ids=true, to_apply=%region_19.18 | all-reduce | flops 1024 | bytes 6144 | tf_op jit(solution)/shard_map/while/body/eval_jaxpr/cond/branch_1_fun/psum | solution.py:264
  226.6 11.0 %all-gather.1 = bf16[32,8,16]{2,1,0:T(8,128)(2,1)} all-gather(bf16[8,8,16]{2,1,0:T(8,128)(2,1)S(1)} %psum.12), channel_id=3, replica_groups=mesh['s'=16,'y'=4,'c'=2,'z'=4] {'z'}, dimensions={0}, use_global_device_ids=true | all-gather | bytes 10240 | tf_op jit(solution)/shard_map/while/body/eval_jaxpr/cond/branch_1_fun/all_gather | solution.py:265
  240.3 317.2 %conditional.14 = (bf16[32,1408]{1,0:T(8,128)(2,1)}) conditional(s32[]{:T(128)} %clamp.23, bf16[32,1408]{1,0:T(8,128)(2,1)} %get-tuple-element.1796, bf16[32,1408]{1,0:T(8,128)(2,1)} %get-tuple-element.1796, bf16[32,1408]{1,0:T(8,128)(2,1)} %get-tuple-element.1796, (s32[]{:T(128)}, ...), branch_computations={%region_13.13_spmd, %region_14.14_spmd, %region_15.15_spmd, %regio... | conditional | flops 3 | bytes 540720 | solution.py:357
  240.3 1.4 collective-permute-start
  241.7 315.2 %collective-permute-done = bf16[32,1408]{1,0:T(8,128)(2,1)S(1)} collective-permute-done((bf16[32,1408]{1,0:T(8,128)(2,1)}, bf16[32,1408]{1,0:T(8,128)(2,1)S(1)}, u32[]{:S(2)}, u32[]{:S(2)}) %collective-permute-start) | collective-permute-done | bytes 90144 | tf_op jit(solution)/shard_map/while/body/eval_jaxpr/cond/branch_1_fun/ppermute | solution.py:361
  558.5 18.3 %conditional.13 = ((bf16[2,32,1408]{2,1,0:T(8,128)(2,1)S(1)}, bf16[2,32,64]{2,1,0:T(8,128)(2,1)}, bf16[2,32,1280]{2,1,0:T(8,128)(2,1)}, bf16[2,32,128]{2,1,0:T(8,128)(2,1)}, bf16[32,1408]{1,0:T(8,128)(2,1)})) conditional(s32[]{:T(128)} %convert_element_type.149, (bf16[2,32,1408]{2,1,0:T(8,128)(2,1)S(1)}, bf16[2,32,64]{2,1,0:T(8,128)(2,1)}, ...), branch_computations={%region_9.9_spmd, %region_10.12_spmd} | conditional | flops 419430400 | bytes 14934146 | solution.py:351
  559.1 9.4 %conditional = (bf16[4,32,1408]{2,1,0:T(8,128)(2,1)S(1)}) conditional(s32[]{:T(128)} %convert_element_type.91, bf16[32,1408]{1,0:T(8,128)(2,1)} %get-tuple-element.1127, () %tuple.83), branch_computations={%region_11.10_spmd, %region_12.11_spmd} | conditional | bytes 1171464 | solution.py:334
  560.0 8.4 %all_to_all.22 = bf16[4,32,1408]{2,1,0:T(8,128)(2,1)S(1)} all-to-all(bf16[4,32,1408]{2,1,0:T(8,128)(2,1)S(1)} %broadcast_in_dim.147), channel_id=1, replica_groups=mesh['s'=16,'y'=4,'c'=2,'z'=4] {'y'}, dimensions={0} | all-to-all | bytes 720896 | tf_op jit(solution)/shard_map/while/body/eval_jaxpr/cond/branch_1_fun/cond/branch_0_fun/all_to_all | solution.py:49
  568.6 8.2 %stage.1 = (bf16[32,1408]{1,0:T(8,128)(2,1)}, bf16[2,32,1408]{2,1,0:T(8,128)(2,1)S(1)}, bf16[2,32,64]{2,1,0:T(8,128)(2,1)}, bf16[2,32,1280]{2,1,0:T(8,128)(2,1)}, bf16[2,32,128]{2,1,0:T(8,128)(2,1)}) custom-call(s32[4]{0:T(128)S(1)} %pad_add_fusion.place_ref, ...), custom_call_target="tpu_custom_call", output_to_operand_aliasing={{1}: (24, {}), {2}: (25, {}), {3}: (26, {}), {4}: (27, {})} | custom-call | flops 419430400 | bytes 13107200 | tf_op jit(solution)/shard_map/while/body/eval_jaxpr/cond/branch_1_fun/stage/pallas_call | solution.py:161
  577.7 19.0 %conditional.14 = (bf16[32,1408]{1,0:T(8,128)(2,1)}) conditional(s32[]{:T(128)} %clamp.23, bf16[32,1408]{1,0:T(8,128)(2,1)} %get-tuple-element.1796, bf16[32,1408]{1,0:T(8,128)(2,1)} %get-tuple-element.1796, bf16[32,1408]{1,0:T(8,128)(2,1)} %get-tuple-element.1796, (s32[]{:T(128)}, ...), branch_computations={%region_13.13_spmd, %region_14.14_spmd, %region_15.15_spmd, %regio... | conditional | flops 3 | bytes 540720 | solution.py:357
  577.7 1.4 collective-permute-start
  579.1 17.0 %collective-permute-done = bf16[32,1408]{1,0:T(8,128)(2,1)S(1)} collective-permute-done((bf16[32,1408]{1,0:T(8,128)(2,1)}, bf16[32,1408]{1,0:T(8,128)(2,1)S(1)}, u32[]{:S(2)}, u32[]{:S(2)}) %collective-permute-start) | collective-permute-done | bytes 90144 | tf_op jit(solution)/shard_map/while/body/eval_jaxpr/cond/branch_1_fun/ppermute | solution.py:361
  597.7 19.6 %conditional.13 = ((bf16[2,32,1408]{2,1,0:T(8,128)(2,1)S(1)}, bf16[2,32,64]{2,1,0:T(8,128)(2,1)}, bf16[2,32,1280]{2,1,0:T(8,128)(2,1)}, bf16[2,32,128]{2,1,0:T(8,128)(2,1)}, bf16[32,1408]{1,0:T(8,128)(2,1)})) conditional(s32[]{:T(128)} %convert_element_type.149, (bf16[2,32,1408]{2,1,0:T(8,128)(2,1)S(1)}, bf16[2,32,64]{2,1,0:T(8,128)(2,1)}, ...), branch_computations={%region_9.9_spmd, %region_10.12_spmd} | conditional | flops 419430400 | bytes 14934146 | solution.py:351
  598.3 10.6 %conditional = (bf16[4,32,1408]{2,1,0:T(8,128)(2,1)S(1)}) conditional(s32[]{:T(128)} %convert_element_type.91, bf16[32,1408]{1,0:T(8,128)(2,1)} %get-tuple-element.1127, () %tuple.83), branch_computations={%region_11.10_spmd, %region_12.11_spmd} | conditional | bytes 1171464 | solution.py:334
  599.2 9.7 %all_to_all.22 = bf16[4,32,1408]{2,1,0:T(8,128)(2,1)S(1)} all-to-all(bf16[4,32,1408]{2,1,0:T(8,128)(2,1)S(1)} %broadcast_in_dim.147), channel_id=1, replica_groups=mesh['s'=16,'y'=4,'c'=2,'z'=4] {'y'}, dimensions={0} | all-to-all | bytes 720896 | tf_op jit(solution)/shard_map/while/body/eval_jaxpr/cond/branch_1_fun/cond/branch_0_fun/all_to_all | solution.py:49
  609.0 8.2 %stage.1 = (bf16[32,1408]{1,0:T(8,128)(2,1)}, bf16[2,32,1408]{2,1,0:T(8,128)(2,1)S(1)}, bf16[2,32,64]{2,1,0:T(8,128)(2,1)}, bf16[2,32,1280]{2,1,0:T(8,128)(2,1)}, bf16[2,32,128]{2,1,0:T(8,128)(2,1)}) custom-call(s32[4]{0:T(128)S(1)} %pad_add_fusion.place_ref, ...), custom_call_target="tpu_custom_call", output_to_operand_aliasing={{1}: (24, {}), {2}: (25, {}), {3}: (26, {}), {4}: (27, {})} | custom-call | flops 419430400 | bytes 13107200 | tf_op jit(solution)/shard_map/while/body/eval_jaxpr/cond/branch_1_fun/stage/pallas_call | solution.py:161
  619.1 14.7 %all-gather.4 = bf16[256,1408]{1,0:T(8,128)(2,1)S(1)} all-gather(bf16[64,1408]{1,0:T(8,128)(2,1)S(1)} %fusion.19), channel_id=6, replica_groups=mesh['s'=16,'y'=4,'c'=2,'z'=4] {'z'}, dimensions={0}, use_global_device_ids=true | all-gather | bytes 901120 | tf_op jit(solution)/shard_map/all_gather | solution.py:400
  633.8 1.1 fusion.13
  635.7 41.0 %collective-permute-start.23 = (f32[8,16,640]{2,1,0:T(8,128)}, f32[8,16,640]{2,1,0:T(8,128)}, u32[]{:S(2)}, u32[]{:S(2)}) collective-permute-start(f32[8,16,640]{2,1,0:T(8,128)} %slice_select_fusion), channel_id=1, source_target_pairs={{0,4},{4,0},{1,5},{5,1},{2,6},{6,2},{3,7},{7,3},{8,12},{12,8},{9,1... | collective-permute-start | bytes 983048 | tf_op jit(solution)/shard_map/ppermute | solution.py:44
  677.3 1.4 broadcast_in_dim.178
  678.6 3.3 all-to-all-start.4
  681.9 1.4 fusion.14
  683.3 3.1 all-to-all-done.4
  686.6 3.1 collective-permute-start.21
  689.7 1.9 collective-permute-start.22
  693.4 1.0 select_reduce_fusion
  (255 shorter events, 46.2 us)
Async XLA Ops:
  0.6 46.1 %copy-start = (bf16[1,8,16,5120]{3,2,1,0:T(8,128)(2,1)S(1)}, bf16[1,8,16,5120]{3,2,1,0:T(8,128)(2,1)}, u32[]{:S(2)}) copy-start(bf16[1,8,16,5120]{3,2,1,0:T(8,128)(2,1)} %param.31) | copy-start | bytes 3932164
  3.6 1.4 copy-start.6
  3.6 10.3 %copy-start.12 = (f32[1,640]{1,0:T(1,128)S(1)}, f32[1,640]{1,0:T(1,128)}, u32[]{:S(2)}) copy-start(f32[1,640]{1,0:T(1,128)} %param.29) | copy-start | bytes 7684
  5.0 15.3 %copy-start.13 = (s32[1,8]{1,0:T(1,128)S(1)}, s32[1,8]{1,0:T(1,128)}, u32[]{:S(2)}) copy-start(s32[1,8]{1,0:T(1,128)} %param.33) | copy-start | bytes 100
  5.0 15.3 %copy-start.14 = (s32[8]{0:T(128)S(1)}, s32[8]{0:T(128)}, u32[]{:S(2)}) copy-start(s32[8]{0:T(128)} %param.32) | copy-start | bytes 100
  5.0 16.1 %collective-permute-start.5 = (bf16[8,640,16]{1,2,0:T(8,128)(2,1)S(1)}, bf16[8,640,16]{1,2,0:T(8,128)(2,1)S(1)}, u32[]{:S(2)}, u32[]{:S(2)}) collective-permute-start(bf16[8,640,16]{1,2,0:T(8,128)(2,1)S(1)} %bitcast.120), channel_id=1, source_target_pairs={{0,4},{4,0},{1,5},{5,1},{2,6},{6,2},{3,7},{7,3},{8,12},{12,8},{9,1... | collective-permute-start | bytes 491528 | tf_op jit(solution)/shard_map/ppermute | solution.py:31
  13.9 6.5 collective-permute-start.4
  16.9 29.8 %copy-start.4 = (bf16[64,1280]{1,0:T(8,128)(2,1)}, bf16[64,1280]{1,0:T(8,128)(2,1)S(1)}, u32[]{:S(2)}) copy-start(bf16[64,1280]{1,0:T(8,128)(2,1)S(1)} %fusion.39) | copy-start | bytes 491524
  16.9 20.0 %collective-permute-start.3 = (bf16[64,1280]{1,0:T(8,128)(2,1)S(1)}, bf16[64,1280]{1,0:T(8,128)(2,1)S(1)}, u32[]{:S(2)}, u32[]{:S(2)}) collective-permute-start(bf16[64,1280]{1,0:T(8,128)(2,1)S(1)} %fusion.39), channel_id=1, source_target_pairs={{480,448},{448,416},{416,384},{384,352},{352,320},{320,288},{288,2... | collective-permute-start | bytes 491528 | tf_op jit(solution)/shard_map/ppermute | solution.py:222
  20.4 26.3 %copy-start.15 = (s32[8]{0:T(128)}, s32[8]{0:T(128)S(1)}, u32[]{:S(2)}) copy-start(s32[8]{0:T(128)S(1)} %select_reduce_fusion.2) | copy-start | bytes 100
  36.9 9.8 %copy-start.7 = (bf16[64,1280]{1,0:T(8,128)(2,1)}, bf16[64,1280]{1,0:T(8,128)(2,1)S(1)}, u32[]{:S(2)}) copy-start(bf16[64,1280]{1,0:T(8,128)(2,1)S(1)} %collective-permute-done.3) | copy-start | bytes 491524
  36.9 30.3 %collective-permute-start.6 = (bf16[640,640]{1,0:T(8,128)(2,1)}, bf16[640,640]{1,0:T(8,128)(2,1)}, u32[]{:S(2)}, u32[]{:S(2)}) collective-permute-start(bf16[640,640]{1,0:T(8,128)(2,1)} %get-tuple-element.1845), channel_id=1, source_target_pairs={{0,1},{1,2},{2,3},{3,0},{32,33},{33,34},{34,35},{35,32},{64,65},{6... | collective-permute-start | bytes 2457608 | tf_op jit(solution)/shard_map/ppermute | solution.py:242
  38.8 46.7 %collective-permute-start.10 = (bf16[640,640]{1,0:T(8,128)(2,1)}, bf16[640,640]{1,0:T(8,128)(2,1)}, u32[]{:S(2)}, u32[]{:S(2)}) collective-permute-start(bf16[640,640]{1,0:T(8,128)(2,1)} %get-tuple-element.1845), channel_id=1, source_target_pairs={{0,4},{4,0},{32,36},{36,32},{64,68},{68,64},{96,100},{100,96},{128... | collective-permute-start | bytes 2457608 | tf_op jit(solution)/shard_map/ppermute | solution.py:303
  41.2 37.5 %collective-permute-start.7 = (bf16[640,640]{1,0:T(8,128)(2,1)}, bf16[640,640]{1,0:T(8,128)(2,1)}, u32[]{:S(2)}, u32[]{:S(2)}) collective-permute-start(bf16[640,640]{1,0:T(8,128)(2,1)} %get-tuple-element.1846), channel_id=1, source_target_pairs={{0,3},{1,0},{2,1},{3,2},{32,35},{33,32},{34,33},{35,34},{64,67},{6... | collective-permute-start | bytes 2457608 | tf_op jit(solution)/shard_map/ppermute | solution.py:243
  49.1 4.3 copy-start.8
  49.1 41.4 %collective-permute-start.11 = (bf16[640,640]{1,0:T(8,128)(2,1)}, bf16[640,640]{1,0:T(8,128)(2,1)}, u32[]{:S(2)}, u32[]{:S(2)}) collective-permute-start(bf16[640,640]{1,0:T(8,128)(2,1)} %get-tuple-element.1846), channel_id=1, source_target_pairs={{0,4},{4,0},{32,36},{36,32},{64,68},{68,64},{96,100},{100,96},{128... | collective-permute-start | bytes 2457608 | tf_op jit(solution)/shard_map/ppermute | solution.py:303
  53.4 81.5 %copy-start.10 = (f32[8,8]{1,0:T(8,128)}, f32[8,8]{1,0:T(8,128)S(1)}, u32[]{:S(2)}) copy-start(f32[8,8]{1,0:T(8,128)S(1)} %add_rsqrt_fusion.1) | copy-start | bytes 772
  78.9 11.7 %collective-permute-start.12 = (bf16[640,640]{1,0:T(8,128)(2,1)}, bf16[640,640]{1,0:T(8,128)(2,1)}, u32[]{:S(2)}, u32[]{:S(2)}) collective-permute-start(bf16[640,640]{1,0:T(8,128)(2,1)} %collective-permute-done.6), channel_id=1, source_target_pairs={{0,4},{4,0},{32,36},{36,32},{64,68},{68,64},{96,100},{100,96},{128... | collective-permute-start | bytes 2457608 | tf_op jit(solution)/shard_map/ppermute | solution.py:303
  81.2 23.8 %collective-permute-start.8 = (bf16[640,640]{1,0:T(8,128)(2,1)}, bf16[640,640]{1,0:T(8,128)(2,1)}, u32[]{:S(2)}, u32[]{:S(2)}) collective-permute-start(bf16[640,640]{1,0:T(8,128)(2,1)} %collective-permute-done.6), channel_id=1, source_target_pairs={{0,1},{1,2},{2,3},{3,0},{32,33},{33,34},{34,35},{35,32},{64,65},{6... | collective-permute-start | bytes 2457608 | tf_op jit(solution)/shard_map/ppermute | solution.py:309
  83.3 7.3 %collective-permute-start.13 = (bf16[640,640]{1,0:T(8,128)(2,1)}, bf16[640,640]{1,0:T(8,128)(2,1)}, u32[]{:S(2)}, u32[]{:S(2)}) collective-permute-start(bf16[640,640]{1,0:T(8,128)(2,1)} %collective-permute-done.7), channel_id=1, source_target_pairs={{0,4},{4,0},{32,36},{36,32},{64,68},{68,64},{96,100},{100,96},{128... | collective-permute-start | bytes 2457608 | tf_op jit(solution)/shard_map/ppermute | solution.py:303
  85.6 37.4 %collective-permute-start.9 = (bf16[640,640]{1,0:T(8,128)(2,1)}, bf16[640,640]{1,0:T(8,128)(2,1)}, u32[]{:S(2)}, u32[]{:S(2)}) collective-permute-start(bf16[640,640]{1,0:T(8,128)(2,1)} %collective-permute-done.7), channel_id=1, source_target_pairs={{0,3},{1,0},{2,1},{3,2},{32,35},{33,32},{34,33},{35,34},{64,67},{6... | collective-permute-start | bytes 2457608 | tf_op jit(solution)/shard_map/ppermute | solution.py:310
  123.0 23.4 %collective-permute-start.14 = (bf16[640,640]{1,0:T(8,128)(2,1)}, bf16[640,640]{1,0:T(8,128)(2,1)}, u32[]{:S(2)}, u32[]{:S(2)}) collective-permute-start(bf16[640,640]{1,0:T(8,128)(2,1)} %collective-permute-done.8), channel_id=1, source_target_pairs={{0,1},{1,2},{2,3},{3,0},{32,33},{33,34},{34,35},{35,32},{64,65},{6... | collective-permute-start | bytes 2457608 | tf_op jit(solution)/shard_map/ppermute | solution.py:313
  125.2 39.5 %collective-permute-start.15 = (bf16[640,640]{1,0:T(8,128)(2,1)}, bf16[640,640]{1,0:T(8,128)(2,1)}, u32[]{:S(2)}, u32[]{:S(2)}) collective-permute-start(bf16[640,640]{1,0:T(8,128)(2,1)} %collective-permute-done.9), channel_id=1, source_target_pairs={{0,3},{1,0},{2,1},{3,2},{32,35},{33,32},{34,33},{35,34},{64,67},{6... | collective-permute-start | bytes 2457608 | tf_op jit(solution)/shard_map/ppermute | solution.py:314
  130.1 34.6 %collective-permute-start.16 = (bf16[640,640]{1,0:T(8,128)(2,1)}, bf16[640,640]{1,0:T(8,128)(2,1)}, u32[]{:S(2)}, u32[]{:S(2)}) collective-permute-start(bf16[640,640]{1,0:T(8,128)(2,1)} %collective-permute-done.8), channel_id=1, source_target_pairs={{0,4},{4,0},{32,36},{36,32},{64,68},{68,64},{96,100},{100,96},{128... | collective-permute-start | bytes 2457608 | tf_op jit(solution)/shard_map/ppermute | solution.py:303
  133.0 31.7 %collective-permute-start.17 = (bf16[640,640]{1,0:T(8,128)(2,1)}, bf16[640,640]{1,0:T(8,128)(2,1)}, u32[]{:S(2)}, u32[]{:S(2)}) collective-permute-start(bf16[640,640]{1,0:T(8,128)(2,1)} %collective-permute-done.9), channel_id=1, source_target_pairs={{0,4},{4,0},{32,36},{36,32},{64,68},{68,64},{96,100},{100,96},{128... | collective-permute-start | bytes 2457608 | tf_op jit(solution)/shard_map/ppermute | solution.py:303
  136.3 35.5 %copy-start.1 = (bf16[1,8,8,1280]{3,2,1,0:T(8,128)(2,1)S(1)}, bf16[1,8,8,1280]{3,2,1,0:T(8,128)(2,1)}, u32[]{:S(2)}) copy-start(bf16[1,8,8,1280]{3,2,1,0:T(8,128)(2,1)} %constant_dynamic-slice_fusion.1) | copy-start | bytes 491524
  136.3 34.8 %copy-start.9 = (bf16[2,32,64]{1,0,2:T(2,128)(2,1)}, bf16[2,32,64]{1,0,2:T(2,128)(2,1)S(1)}, u32[]{:S(2)}) copy-start(bf16[2,32,64]{1,0,2:T(2,128)(2,1)S(1)} %get-tuple-element.1417) | copy-start | bytes 24580
  136.3 1.5 collective-permute-start.18
  164.7 11.2 %collective-permute-start.19 = (bf16[640,640]{1,0:T(8,128)(2,1)}, bf16[640,640]{1,0:T(8,128)(2,1)}, u32[]{:S(2)}, u32[]{:S(2)}) collective-permute-start(bf16[640,640]{1,0:T(8,128)(2,1)} %collective-permute-done.14), channel_id=1, source_target_pairs={{0,4},{4,0},{32,36},{36,32},{64,68},{68,64},{96,100},{100,96},{128... | collective-permute-start | bytes 2457608 | tf_op jit(solution)/shard_map/ppermute | solution.py:303
  167.1 8.8 %collective-permute-start.20 = (bf16[640,640]{1,0:T(8,128)(2,1)}, bf16[640,640]{1,0:T(8,128)(2,1)}, u32[]{:S(2)}, u32[]{:S(2)}) collective-permute-start(bf16[640,640]{1,0:T(8,128)(2,1)} %collective-permute-done.15), channel_id=1, source_target_pairs={{0,4},{4,0},{32,36},{36,32},{64,68},{68,64},{96,100},{100,96},{128... | collective-permute-start | bytes 2457608 | tf_op jit(solution)/shard_map/ppermute | solution.py:303
  178.1 0.9 copy-start.2
  179.0 0.9 copy-start.2
  179.9 0.9 copy-start.2
  180.9 0.9 copy-start.2
  181.8 0.9 copy-start.2
  182.7 0.9 copy-start.2
  183.6 0.9 copy-start.2
  184.5 0.9 copy-start.2
  185.4 0.9 copy-start.2
  186.4 0.9 copy-start.2
  187.3 0.9 copy-start.2
  188.2 0.9 copy-start.2
  190.0 0.9 copy-start.2
  191.9 0.9 copy-start.2
  192.8 0.9 copy-start.2
  194.6 0.9 copy-start.2
  196.4 0.9 copy-start.2
  199.2 0.9 copy-start.2
  200.1 37.4 %copy-start.2 = (bf16[1,8,8,1280]{3,2,1,0:T(8,128)(2,1)S(1)}, bf16[1,8,8,1280]{3,2,1,0:T(8,128)(2,1)}, u32[]{:S(2)}) copy-start(bf16[1,8,8,1280]{3,2,1,0:T(8,128)(2,1)} %get-tuple-element.2028) | copy-start | bytes 491524 | tf_op jit(solution)/shard_map/while
  237.6 0.9 copy-start.2
  239.4 0.9 copy-start.2
  240.3 317.2 %copy-start.2 = (bf16[1,8,8,1280]{3,2,1,0:T(8,128)(2,1)S(1)}, bf16[1,8,8,1280]{3,2,1,0:T(8,128)(2,1)}, u32[]{:S(2)}) copy-start(bf16[1,8,8,1280]{3,2,1,0:T(8,128)(2,1)} %get-tuple-element.2028) | copy-start | bytes 491524 | tf_op jit(solution)/shard_map/while
  240.3 316.6 %collective-permute-start = (bf16[32,1408]{1,0:T(8,128)(2,1)}, bf16[32,1408]{1,0:T(8,128)(2,1)S(1)}, u32[]{:S(2)}, u32[]{:S(2)}) collective-permute-start(bf16[32,1408]{1,0:T(8,128)(2,1)} %param.9), channel_id=1, source_target_pairs={{480,448},{416,384},{352,320},{288,256},{224,192},{160,128},{96,64... | collective-permute-start | bytes 270344 | tf_op jit(solution)/shard_map/while/body/eval_jaxpr/cond/branch_1_fun/ppermute | solution.py:361
  557.5 0.9 copy-start.2
  576.8 0.9 copy-start.2
  577.7 19.0 %copy-start.2 = (bf16[1,8,8,1280]{3,2,1,0:T(8,128)(2,1)S(1)}, bf16[1,8,8,1280]{3,2,1,0:T(8,128)(2,1)}, u32[]{:S(2)}) copy-start(bf16[1,8,8,1280]{3,2,1,0:T(8,128)(2,1)} %get-tuple-element.2028) | copy-start | bytes 491524 | tf_op jit(solution)/shard_map/while
  577.7 18.4 %collective-permute-start = (bf16[32,1408]{1,0:T(8,128)(2,1)}, bf16[32,1408]{1,0:T(8,128)(2,1)S(1)}, u32[]{:S(2)}, u32[]{:S(2)}) collective-permute-start(bf16[32,1408]{1,0:T(8,128)(2,1)} %param.9), channel_id=1, source_target_pairs={{480,448},{416,384},{352,320},{288,256},{224,192},{160,128},{96,64... | collective-permute-start | bytes 270344 | tf_op jit(solution)/shard_map/while/body/eval_jaxpr/cond/branch_1_fun/ppermute | solution.py:361
  596.7 0.9 copy-start.2
  617.2 0.9 copy-start.2
  635.7 56.7 %collective-permute-start.23 = (f32[8,16,640]{2,1,0:T(8,128)}, f32[8,16,640]{2,1,0:T(8,128)}, u32[]{:S(2)}, u32[]{:S(2)}) collective-permute-start(f32[8,16,640]{2,1,0:T(8,128)} %slice_select_fusion), channel_id=1, source_target_pairs={{0,4},{4,0},{1,5},{5,1},{2,6},{6,2},{3,7},{7,3},{8,12},{12,8},{9,1... | collective-permute-start | bytes 983048 | tf_op jit(solution)/shard_map/ppermute | solution.py:44
  678.6 7.7 %all-to-all-start.4 = ((bf16[4,2,32,128]{3,2,1,0:T(8,128)(2,1)}), bf16[4,2,32,128]{3,2,1,0:T(8,128)(2,1)S(1)}, u32[]{:S(2)}, u32[]{:S(2)}) async-start(bf16[4,2,32,128]{3,2,1,0:T(8,128)(2,1)} %broadcast_in_dim.178), calls=%async_computation.4 | async-start | bytes 131072 | tf_op jit(solution)/shard_map/all_to_all | solution.py:49
  686.6 6.8 copy-start.11
  686.6 5.0 collective-permute-start.21
  689.7 4.7 collective-permute-start.22
  (9 other events, 7.7 us)

commit v11 on v10

--- a/solution.py
+++ b/solution.py
@@ -214,30 +214,19 @@
     multiplier = low_rank_scale / (toks * 2 * lax.axis_size("z"))
 
     zpos = lax.axis_index("z")
-    first = proj_weight[0][:, :half].T
-    second = proj_weight[0][:, half:].T
-
     x_tokens = lax.dynamic_slice_in_dim(section_inputs[0], core * toks, toks, 1)
     x_y = lax.dynamic_slice_in_dim(x_tokens, ypos * width, width, 2).reshape(rows_all, width)
     x_moved = lax.ppermute(x_y, "s", EVERY)
-    first, second, norm_gain, adapter_down = lax.optimization_barrier(
-        (first, second, norm_gain, adapter_down)
-    )
-    gain_y = both_cores(norm_gain, 1)
-    down_y = both_cores(adapter_down[0], 1)
+    first = proj_weight[0][:, :half].T
+    second = proj_weight[0][:, half:].T
     empty = (
         jnp.zeros((CHUNKS, rows, width + TAIL), bf16),
         jnp.zeros((CHUNKS, rows, group * rank), bf16),
         jnp.zeros((CHUNKS, rows, width), bf16),
         jnp.zeros((CHUNKS, rows, TAIL), bf16),
     )
-    idle = (
-        jnp.zeros((rows, width + TAIL), bf16),
-        jnp.zeros((4, rows_all, width), bf16),
-        jnp.zeros((4, micro, toks, rank), bf16),
-    )
-    x_moved, first, second, gain_y, down_y, x_tokens, empty, idle = lax.optimization_barrier(
-        (x_moved, first, second, gain_y, down_y, x_tokens, empty, idle)
+    x_moved, first, second, x_tokens, x_y, empty = lax.optimization_barrier(
+        (x_moved, first, second, x_tokens, x_y, empty)
     )
     right_1 = lax.ppermute(first, ("s", "z"), RIGHT)
     left_1 = lax.ppermute(second, ("s", "z"), LEFT)
@@ -248,6 +237,11 @@
     x_before = lax.cond(
         sec == 15, lambda x: jnp.zeros((4,) + x.shape, x.dtype), spread, x_moved
     )
+    x_before, norm_gain, adapter_down = lax.optimization_barrier(
+        (x_before, norm_gain, adapter_down)
+    )
+    gain_y = both_cores(norm_gain, 1)
+    down_y = both_cores(adapter_down[0], 1)
     h_y = (normed_y * gain_y).astype(bf16)
 
     iota = jnp.arange(micro, dtype=jnp.int32)
@@ -302,29 +296,41 @@
     def swapped(value):
         return lax.ppermute(value, ("s", "c"), PAIRS)
 
-    ready = (x_before, x_chunk, inv_chunk, down_chunk, up_chunk, gain_y)
+    ready = (x_before, x_chunk, inv_chunk, down_chunk, up_chunk, gain_y, h_y, low_part)
     right_1, left_1, ready = lax.optimization_barrier((right_1, left_1, ready))
     kept = lax.cond(sec == 15, top, lambda args: args[3], (out_grads, first, second, empty))
     boxes_top = lax.ppermute(kept[0], "s", [(15, 14)])
     right_2 = lax.ppermute(right_1, ("s", "z"), RIGHT)
     left_2 = lax.ppermute(left_1, ("s", "z"), LEFT)
-    others = [swapped(w) for w in (first, second, right_1, left_1)]
-    right_2, left_2, others = lax.optimization_barrier((right_2, left_2, others))
+    others = [swapped(w) for w in (right_1, left_1)]
+    right_2, left_2, others, first, second = lax.optimization_barrier(
+        (right_2, left_2, others, first, second)
+    )
     right_3 = lax.ppermute(right_2, ("s", "z"), RIGHT)
     left_3 = lax.ppermute(left_2, ("s", "z"), LEFT)
-    more = [swapped(w) for w in (right_2, left_2)]
+    more = [swapped(w) for w in (first, second, right_2, left_2)]
     right_3, left_3, more, kept, boxes_top, ready = lax.optimization_barrier(
         (right_3, left_3, more, kept, boxes_top, ready)
     )
-    x_before, x_chunk, inv_chunk, down_chunk, up_chunk, gain_y = ready
-    more = more + [swapped(w) for w in (right_3, left_3)]
-    weights = [first, second, right_1, left_1, right_2, left_2, right_3, left_3, *others, *more]
+    x_before, x_chunk, inv_chunk, down_chunk, up_chunk, gain_y, h_y, low_part = ready
+    last = [swapped(w) for w in (right_3, left_3)]
+    weights = [first, second, right_1, left_1, right_2, left_2, right_3, left_3]
+    weights = weights + more[:2] + others + more[2:] + last
+    extras = lax.cond(
+        sec <= 15 - AHEAD,
+        extra,
+        lambda args: (
+            jnp.zeros((4, rows_all, width), bf16),
+            jnp.zeros((4, micro, toks, rank), bf16),
+        ),
+        (h_y, low_part),
+    )
 
     def pick(array, m):
         return lax.dynamic_index_in_dim(array, m, 0, keepdims=False)
 
     def step(u, state):
-        box, kept, extras = state
+        box, kept = state
         t, m = u // CHUNKS, u % CHUNKS
         turn = 15 - t + m
 
@@ -364,17 +370,12 @@
             ],
             box,
         )
-        extras = lax.cond(
-            (sec == turn - AHEAD) & (m == 0),
-            lambda args: extra((h_y, low_part)),
-            lambda args: args,
-            extras,
-        )
-        return box, kept, extras
-
-    start = (idle[0], kept, idle[1:])
-    _, kept, extras = lax.fori_loop(0, (15 + CHUNKS) * CHUNKS, step, start)
+        return box, kept
+
+    start = (pick(boxes_top, 0), kept)
+    _, kept = lax.fori_loop(0, (15 + CHUNKS) * CHUNKS, step, start)
     boxes, low_all, grad_all, tail_all = kept
+    low_all, h_y, low_part = lax.optimization_barrier((low_all, h_y, low_part))
     h_all, low_in_all = lax.cond(
         sec > 15 - AHEAD, lambda args: extra((h_y, low_part)), lambda args: args, extras
     )

time: 698 us -> 674 us (0.966)
  local copies, waits for them, and re-layouts: 50 us -> 17.9 us
  waiting for transfers between devices: 422 us -> 435 us
    while x69 -> x1, local copies, waits for them, and re-layouts: 29.3 us -> 0.84 us  [local(): _, kept = lax.fori_loop(0, (15 + CHUNKS) * CHUNKS, step, start)]
    ppermute x1, waiting for transfers between devices: 0.01 us -> 13.7 us  [local(): right_1 = lax.ppermute(first, ('s', 'z'), RIGHT)]
  transfers between devices with their start and end apart: 24 -> 24, of which waited for: 9 -> 10; matrix products, arithmetic and copies ran while one was open for 3% -> 3% of each run, Pallas kernels for 0% -> 0%
where the time goes in v11:
time: 674 us; the launch traced here: 673 us
  waiting for transfers between devices  435 us (65%)
  starting transfers between devices  100 us (15%)
  blocking collectives  84.2 us (12%)
  local copies, waits for them, and re-layouts  17.9 us (3%)
  Pallas kernels  16 us (2%)
  other arithmetic  9.58 us (1%)
    ppermute x2, waiting for transfers between devices, step(): lax.ppermute(box, 's', ODD)  334 us
    ppermute x2, starting transfers between devices, half_sum(): return mine + lax.ppermute(theirs, 'c', SWAP)  41.4 us
    all_to_all x3, blocking collectives, spread(): return lax.all_to_all(sent, 'y', 0, 0)  33.9 us
    all_gather x2, blocking collectives, extra(): return (lax.all_gather(h_y, 'z'), lax.all_gather(low_in, 'z'))  24.4 us
    ppermute x8, starting transfers between devices, swapped(): return lax.ppermute(value, ('s', 'c'), PAIRS)  19.8 us
    ppermute x1, waiting for transfers between devices, local(): left_1 = lax.ppermute(second, ('s', 'z'), LEFT)  18.4 us
    ppermute x1, waiting for transfers between devices, local(): left_2 = lax.ppermute(left_1, ('s', 'z'), LEFT)  18.4 us
    ppermute x1, waiting for transfers between devices, local(): right_2 = lax.ppermute(right_1, ('s', 'z'), RIGHT)  16.3 us
  transfers between devices with their start and end apart: 24, of which 10 were waited for; matrix products, arithmetic and copies ran while one was open for 3% of the time, Pallas kernels for 0%

profile of v11, /device:TPU:1, one launch (start us, length us, event | category | flops | bytes accessed | tf_op | source)
XLA Modules:
  0.0 672.6 jit_solution(8875183769077123085)
XLA Ops:
  0.7 1.2 dynamic-slice_bitcast_fusion.3
  1.9 1.3 collective-permute-start.3
  3.2 2.0 dynamic-slice_bitcast_fusion.2
  5.2 2.2 copy.32
  8.2 2.7 slice_bitcast_fusion.4
  11.0 11.4 %collective-permute-done.3 = bf16[64,1280]{1,0:T(8,128)(2,1)S(1)} collective-permute-done((bf16[64,1280]{1,0:T(8,128)(2,1)S(1)}, bf16[64,1280]{1,0:T(8,128)(2,1)S(1)}, u32[]{:S(2)}, u32[]{:S(2)}) %collective-permute-start.3) | collective-permute-done | bytes 163872 | tf_op jit(solution)/shard_map/ppermute | solution.py:219
  22.4 17.1 %conditional.7 = (bf16[4,64,1280]{2,1,0:T(8,128)(2,1)}) conditional(s32[]{:T(128)} %convert_element_type.91, bf16[64,1280]{1,0:T(8,128)(2,1)S(1)} %collective-permute-done.3, () %tuple.107), branch_computations={%region_0.0_spmd, %region_1.0_spmd} | conditional | bytes 2129928 | solution.py:237
  22.5 17.1 %all_to_all.21 = bf16[4,64,1280]{2,1,0:T(8,128)(2,1)} all-to-all(bf16[4,64,1280]{2,1,0:T(8,128)(2,1)S(1)} %broadcast_in_dim.99), channel_id=1, replica_groups=mesh['s'=16,'y'=4,'c'=2,'z'=4] {'y'}, dimensions={0} | all-to-all | bytes 1310720 | tf_op jit(solution)/shard_map/cond/branch_0_fun/all_to_all | solution.py:49
  39.5 4.4 collective-permute-start.7
  43.9 1.3 multiply_reduce_fusion.1
  45.4 1.9 collective-permute-start.6
  47.3 1.9 collective-permute-start.4
  49.3 5.2 collective-permute-start.5
  55.9 1.1 fusion.18
  57.0 13.7 %collective-permute-done.4 = bf16[640,640]{1,0:T(8,128)(2,1)} collective-permute-done((bf16[640,640]{1,0:T(8,128)(2,1)}, bf16[640,640]{1,0:T(8,128)(2,1)}, u32[]{:S(2)}, u32[]{:S(2)}) %collective-permute-start.4) | collective-permute-done | bytes 819232 | tf_op jit(solution)/shard_map/ppermute | solution.py:231
  70.7 18.4 %collective-permute-done.5 = bf16[640,640]{1,0:T(8,128)(2,1)} collective-permute-done((bf16[640,640]{1,0:T(8,128)(2,1)}, bf16[640,640]{1,0:T(8,128)(2,1)}, u32[]{:S(2)}, u32[]{:S(2)}) %collective-permute-start.5) | collective-permute-done | bytes 819232 | tf_op jit(solution)/shard_map/ppermute | solution.py:232
  89.2 2.4 collective-permute-start.10
  91.6 1.9 collective-permute-start.11
  93.6 1.9 collective-permute-start.8
  95.5 5.2 collective-permute-start.9
  100.7 16.3 %collective-permute-done.8 = bf16[640,640]{1,0:T(8,128)(2,1)} collective-permute-done((bf16[640,640]{1,0:T(8,128)(2,1)}, bf16[640,640]{1,0:T(8,128)(2,1)}, u32[]{:S(2)}, u32[]{:S(2)}) %collective-permute-start.8) | collective-permute-done | bytes 819232 | tf_op jit(solution)/shard_map/ppermute | solution.py:303
  117.0 18.4 %collective-permute-done.9 = bf16[640,640]{1,0:T(8,128)(2,1)} collective-permute-done((bf16[640,640]{1,0:T(8,128)(2,1)}, bf16[640,640]{1,0:T(8,128)(2,1)}, u32[]{:S(2)}, u32[]{:S(2)}) %collective-permute-start.9) | collective-permute-done | bytes 819232 | tf_op jit(solution)/shard_map/ppermute | solution.py:304
  135.3 2.2 collective-permute-start.12
  139.5 1.5 collective-permute-start.18
  141.0 2.7 collective-permute-start.16
  143.7 4.9 collective-permute-start.13
  148.6 2.2 collective-permute-start.14
  150.8 2.1 collective-permute-start.15
  152.9 5.8 collective-permute-done.12
  158.7 4.2 collective-permute-start.17
  162.9 14.2 %collective-permute-done.13 = bf16[640,640]{1,0:T(8,128)(2,1)} collective-permute-done((bf16[640,640]{1,0:T(8,128)(2,1)}, bf16[640,640]{1,0:T(8,128)(2,1)}, u32[]{:S(2)}, u32[]{:S(2)}) %collective-permute-start.13) | collective-permute-done | bytes 819232 | tf_op jit(solution)/shard_map/ppermute | solution.py:310
  177.1 2.3 collective-permute-start.19
  179.5 2.0 collective-permute-start.20
  183.0 36.2 %conditional.9 = (bf16[4,64,1280]{2,1,0:T(8,128)(2,1)}, bf16[4,8,8,16]{3,2,1,0:T(8,128)(2,1)S(1)}) conditional(s32[]{:T(128)} %convert_element_type.100, () %tuple.115, (bf16[64,1280]{1,0:T(8,128)(2,1)S(1)}, f32[8,8,16]{2,1,0:T(8,128)S(1)}) %tuple.182), branch_computations={%region_19.20_spmd, %region_20.22_spmd} | conditional | flops 1024 | bytes 835600 | solution.py:319
  183.0 14.2 %all-gather = bf16[256,1280]{1,0:T(8,128)(2,1)} all-gather(bf16[64,1280]{1,0:T(8,128)(2,1)S(1)} %get-tuple-element.1090), channel_id=2, replica_groups=mesh['s'=16,'y'=4,'c'=2,'z'=4] {'z'}, dimensions={0}, use_global_device_ids=true | all-gather | bytes 819200 | tf_op jit(solution)/shard_map/cond/branch_1_fun/all_gather | solution.py:259
  197.2 11.7 %psum.12 = bf16[8,8,16]{2,1,0:T(8,128)(2,1)S(1)} all-reduce(f32[8,8,16]{2,1,0:T(8,128)S(1)} %get-tuple-element.1091), channel_id=1, replica_groups=mesh['s'=16,'y'=4,'c'=2,'z'=4] {'y'}, use_global_device_ids=true, to_apply=%region_21.21 | all-reduce | flops 1024 | bytes 6144 | tf_op jit(solution)/shard_map/cond/branch_1_fun/psum | solution.py:258
  209.0 10.2 %all-gather.1 = bf16[32,8,16]{2,1,0:T(8,128)(2,1)S(1)} all-gather(bf16[8,8,16]{2,1,0:T(8,128)(2,1)S(1)} %psum.12), channel_id=3, replica_groups=mesh['s'=16,'y'=4,'c'=2,'z'=4] {'z'}, dimensions={0}, use_global_device_ids=true | all-gather | bytes 10240 | tf_op jit(solution)/shard_map/cond/branch_1_fun/all_gather | solution.py:259
  219.2 1.5 slice_bitcast_fusion.6
  220.8 377.1 %while.27 = (s32[]{:T(128)}, bf16[32,1408]{1,0:T(8,128)(2,1)}, bf16[2,32,1408]{2,1,0:T(8,128)(2,1)}, bf16[2,32,64]{2,1,0:T(8,128)(2,1)S(1)}, bf16[2,32,1280]{2,1...) while((s32[]{:T(128)}, bf16[32,1408]{1,0:T(8,128)(2,1)}, ...), condition=%wide.region_17.18_spmd, body=%wide.region_8.17_spmd.sunk | while | flops 419430432 | bytes 14820536 | solution.py:376
  225.1 315.6 %conditional.14 = (bf16[32,1408]{1,0:T(8,128)(2,1)}) conditional(s32[]{:T(128)} %clamp.23, bf16[32,1408]{1,0:T(8,128)(2,1)} %get-tuple-element.1642, bf16[32,1408]{1,0:T(8,128)(2,1)} %get-tuple-element.1642, bf16[32,1408]{1,0:T(8,128)(2,1)} %get-tuple-element.1642, (s32[]{:T(128)}, ...), branch_computations={%region_13.13_spmd, %region_14.14_spmd, %region_15.15_spmd, %regio... | conditional | flops 3 | bytes 540720 | solution.py:363
  225.1 1.3 collective-permute-start
  226.4 313.7 %collective-permute-done = bf16[32,1408]{1,0:T(8,128)(2,1)S(1)} collective-permute-done((bf16[32,1408]{1,0:T(8,128)(2,1)}, bf16[32,1408]{1,0:T(8,128)(2,1)S(1)}, u32[]{:S(2)}, u32[]{:S(2)}) %collective-permute-start) | collective-permute-done | bytes 90144 | tf_op jit(solution)/shard_map/while/body/eval_jaxpr/cond/branch_1_fun/ppermute | solution.py:367
  540.7 17.4 %conditional.13 = ((bf16[2,32,1408]{2,1,0:T(8,128)(2,1)}, bf16[2,32,64]{2,1,0:T(8,128)(2,1)S(1)}, bf16[2,32,1280]{2,1,0:T(8,128)(2,1)}, bf16[2,32,128]{2,1,0:T(8,128)(2,1)S(1)}, bf16[32,1408]{1,0:T(8,128)(2,1)})) conditional(s32[]{:T(128)} %convert_element_type.126, (bf16[2,32,1408]{2,1,0:T(8,128)(2,1)}, bf16[2,32,64]{2,1,0:T(8,128)(2,1)S(1)}, ...), branch_computations={%region_9.9_spmd, %region_10.12_spmd} | conditional | flops 419430400 | bytes 14278758 | solution.py:357
  540.7 9.4 %conditional = (bf16[4,32,1408]{2,1,0:T(8,128)(2,1)S(1)}) conditional(s32[]{:T(128)} %convert_element_type.77, bf16[32,1408]{1,0:T(8,128)(2,1)} %get-tuple-element.1015, () %tuple.81), branch_computations={%region_11.10_spmd, %region_12.11_spmd} | conditional | bytes 1171464 | solution.py:340
  541.7 8.4 %all_to_all.22 = bf16[4,32,1408]{2,1,0:T(8,128)(2,1)S(1)} all-to-all(bf16[4,32,1408]{2,1,0:T(8,128)(2,1)S(1)} %broadcast_in_dim.143), channel_id=1, replica_groups=mesh['s'=16,'y'=4,'c'=2,'z'=4] {'y'}, dimensions={0} | all-to-all | bytes 720896 | tf_op jit(solution)/shard_map/while/body/eval_jaxpr/cond/branch_1_fun/cond/branch_0_fun/all_to_all | solution.py:49
  550.2 8.0 %stage.1 = (bf16[32,1408]{1,0:T(8,128)(2,1)}, bf16[2,32,1408]{2,1,0:T(8,128)(2,1)}, bf16[2,32,64]{2,1,0:T(8,128)(2,1)S(1)}, bf16[2,32,1280]{2,1,0:T(8,128)(2,1)}, bf16[2,32,128]{2,1,0:T(8,128)(2,1)S(1)}) custom-call(s32[4]{0:T(128)S(1)} %pad_add_fusion.place_ref, ...), custom_call_target="tpu_custom_call", output_to_operand_aliasing={{1}: (24, {}), {2}: (25, {}), {3}: (26, {}), {4}: (27, {})} | custom-call | flops 419430400 | bytes 13107200 | tf_op jit(solution)/shard_map/while/body/eval_jaxpr/cond/branch_1_fun/stage/pallas_call | solution.py:161
  558.4 22.0 %conditional.14 = (bf16[32,1408]{1,0:T(8,128)(2,1)}) conditional(s32[]{:T(128)} %clamp.23, bf16[32,1408]{1,0:T(8,128)(2,1)} %get-tuple-element.1642, bf16[32,1408]{1,0:T(8,128)(2,1)} %get-tuple-element.1642, bf16[32,1408]{1,0:T(8,128)(2,1)} %get-tuple-element.1642, (s32[]{:T(128)}, ...), branch_computations={%region_13.13_spmd, %region_14.14_spmd, %region_15.15_spmd, %regio... | conditional | flops 3 | bytes 540720 | solution.py:363
  558.4 1.3 collective-permute-start
  559.7 20.0 %collective-permute-done = bf16[32,1408]{1,0:T(8,128)(2,1)S(1)} collective-permute-done((bf16[32,1408]{1,0:T(8,128)(2,1)}, bf16[32,1408]{1,0:T(8,128)(2,1)S(1)}, u32[]{:S(2)}, u32[]{:S(2)}) %collective-permute-start) | collective-permute-done | bytes 90144 | tf_op jit(solution)/shard_map/while/body/eval_jaxpr/cond/branch_1_fun/ppermute | solution.py:367
  580.3 17.4 %conditional.13 = ((bf16[2,32,1408]{2,1,0:T(8,128)(2,1)}, bf16[2,32,64]{2,1,0:T(8,128)(2,1)S(1)}, bf16[2,32,1280]{2,1,0:T(8,128)(2,1)}, bf16[2,32,128]{2,1,0:T(8,128)(2,1)S(1)}, bf16[32,1408]{1,0:T(8,128)(2,1)})) conditional(s32[]{:T(128)} %convert_element_type.126, (bf16[2,32,1408]{2,1,0:T(8,128)(2,1)}, bf16[2,32,64]{2,1,0:T(8,128)(2,1)S(1)}, ...), branch_computations={%region_9.9_spmd, %region_10.12_spmd} | conditional | flops 419430400 | bytes 14278758 | solution.py:357
  580.3 9.4 %conditional = (bf16[4,32,1408]{2,1,0:T(8,128)(2,1)S(1)}) conditional(s32[]{:T(128)} %convert_element_type.77, bf16[32,1408]{1,0:T(8,128)(2,1)} %get-tuple-element.1015, () %tuple.81), branch_computations={%region_11.10_spmd, %region_12.11_spmd} | conditional | bytes 1171464 | solution.py:340
  581.3 8.4 %all_to_all.22 = bf16[4,32,1408]{2,1,0:T(8,128)(2,1)S(1)} all-to-all(bf16[4,32,1408]{2,1,0:T(8,128)(2,1)S(1)} %broadcast_in_dim.143), channel_id=1, replica_groups=mesh['s'=16,'y'=4,'c'=2,'z'=4] {'y'}, dimensions={0} | all-to-all | bytes 720896 | tf_op jit(solution)/shard_map/while/body/eval_jaxpr/cond/branch_1_fun/cond/branch_0_fun/all_to_all | solution.py:49
  589.8 8.0 %stage.1 = (bf16[32,1408]{1,0:T(8,128)(2,1)}, bf16[2,32,1408]{2,1,0:T(8,128)(2,1)}, bf16[2,32,64]{2,1,0:T(8,128)(2,1)S(1)}, bf16[2,32,1280]{2,1,0:T(8,128)(2,1)}, bf16[2,32,128]{2,1,0:T(8,128)(2,1)S(1)}) custom-call(s32[4]{0:T(128)S(1)} %pad_add_fusion.place_ref, ...), custom_call_target="tpu_custom_call", output_to_operand_aliasing={{1}: (24, {}), {2}: (25, {}), {3}: (26, {}), {4}: (27, {})} | custom-call | flops 419430400 | bytes 13107200 | tf_op jit(solution)/shard_map/while/body/eval_jaxpr/cond/branch_1_fun/stage/pallas_call | solution.py:161
  598.8 14.1 %all-gather.4 = bf16[256,1408]{1,0:T(8,128)(2,1)S(1)} all-gather(bf16[64,1408]{1,0:T(8,128)(2,1)S(1)} %fusion.17), channel_id=6, replica_groups=mesh['s'=16,'y'=4,'c'=2,'z'=4] {'z'}, dimensions={0}, use_global_device_ids=true | all-gather | bytes 901120 | tf_op jit(solution)/shard_map/all_gather | solution.py:401
  612.9 1.1 fusion.13
  614.1 39.5 %collective-permute-start.23 = (f32[8,16,640]{2,1,0:T(8,128)S(1)}, f32[8,16,640]{2,1,0:T(8,128)}, u32[]{:S(2)}, u32[]{:S(2)}) collective-permute-start(f32[8,16,640]{2,1,0:T(8,128)S(1)} %slice_select_fusion), channel_id=1, source_target_pairs={{0,4},{4,0},{1,5},{5,1},{2,6},{6,2},{3,7},{7,3},{8,12},{12,8},{9,1... | collective-permute-start | bytes 983048 | tf_op jit(solution)/shard_map/ppermute | solution.py:44
  654.8 3.3 all-to-all-start.4
  658.1 1.4 fusion.14
  659.4 3.1 all-to-all-done.4
  662.6 1.0 subtract_convert_fusion
  663.7 3.1 collective-permute-start.21
  666.8 1.9 collective-permute-start.22
  670.5 1.0 select_reduce_fusion
  671.6 1.0 select_reduce_fusion.1
  (140 shorter events, 14.8 us)
Async XLA Ops:
  0.6 7.0 %copy-start = (bf16[1,8,16,5120]{3,2,1,0:T(8,128)(2,1)S(1)}, bf16[1,8,16,5120]{3,2,1,0:T(8,128)(2,1)}, u32[]{:S(2)}) copy-start(bf16[1,8,16,5120]{3,2,1,0:T(8,128)(2,1)} %param.31) | copy-start | bytes 3932164
  0.6 4.5 copy-start.4
  1.9 20.5 %collective-permute-start.3 = (bf16[64,1280]{1,0:T(8,128)(2,1)S(1)}, bf16[64,1280]{1,0:T(8,128)(2,1)S(1)}, u32[]{:S(2)}, u32[]{:S(2)}) collective-permute-start(bf16[64,1280]{1,0:T(8,128)(2,1)S(1)} %dynamic-slice_bitcast_fusion.3), channel_id=1, source_target_pairs={{480,448},{448,416},{416,384},{384,352},{352,320},{320,288},{288,2... | collective-permute-start | bytes 491528 | tf_op jit(solution)/shard_map/ppermute | solution.py:219
  5.2 2.2 copy-start.10
  5.2 2.2 copy-start.11
  7.6 3.4 copy-start.12
  11.0 28.6 %copy-start.8 = (f32[1,640]{1,0:T(1,128)S(1)}, f32[1,640]{1,0:T(1,128)}, u32[]{:S(2)}) copy-start(f32[1,640]{1,0:T(1,128)} %param.29) | copy-start | bytes 7684
  22.4 23.0 %copy-start.7 = (bf16[1,8,640,16]{2,3,1,0:T(8,128)(2,1)S(1)}, bf16[1,8,640,16]{2,3,1,0:T(8,128)(2,1)}, u32[]{:S(2)}) copy-start(bf16[1,8,640,16]{2,3,1,0:T(8,128)(2,1)} %param.30) | copy-start | bytes 491524
  39.5 14.9 %collective-permute-start.7 = (f32[1,640]{1,0:T(1,128)S(1)}, f32[1,640]{1,0:T(1,128)S(1)}, u32[]{:S(2)}, u32[]{:S(2)}) collective-permute-start(f32[1,640]{1,0:T(1,128)S(1)} %copy-done.8), channel_id=1, source_target_pairs={{0,4},{4,0},{1,5},{5,1},{2,6},{6,2},{3,7},{7,3},{8,12},{12,8},{9,1... | collective-permute-start | bytes 7688 | tf_op jit(solution)/shard_map/ppermute | solution.py:31
  45.4 9.9 %collective-permute-start.6 = (bf16[8,640,16]{1,2,0:T(8,128)(2,1)S(1)}, bf16[8,640,16]{1,2,0:T(8,128)(2,1)S(1)}, u32[]{:S(2)}, u32[]{:S(2)}) collective-permute-start(bf16[8,640,16]{1,2,0:T(8,128)(2,1)S(1)} %bitcast.114), channel_id=1, source_target_pairs={{0,4},{4,0},{1,5},{5,1},{2,6},{6,2},{3,7},{7,3},{8,12},{12,8},{9,1... | collective-permute-start | bytes 491528 | tf_op jit(solution)/shard_map/ppermute | solution.py:31
  47.3 23.4 %collective-permute-start.4 = (bf16[640,640]{1,0:T(8,128)(2,1)}, bf16[640,640]{1,0:T(8,128)(2,1)}, u32[]{:S(2)}, u32[]{:S(2)}) collective-permute-start(bf16[640,640]{1,0:T(8,128)(2,1)} %get-tuple-element.1683), channel_id=1, source_target_pairs={{0,1},{1,2},{2,3},{3,0},{32,33},{33,34},{34,35},{35,32},{64,65},{6... | collective-permute-start | bytes 2457608 | tf_op jit(solution)/shard_map/ppermute | solution.py:231
  49.3 39.9 %collective-permute-start.5 = (bf16[640,640]{1,0:T(8,128)(2,1)}, bf16[640,640]{1,0:T(8,128)(2,1)}, u32[]{:S(2)}, u32[]{:S(2)}) collective-permute-start(bf16[640,640]{1,0:T(8,128)(2,1)} %get-tuple-element.1684), channel_id=1, source_target_pairs={{0,3},{1,0},{2,1},{3,2},{32,35},{33,32},{34,33},{35,34},{64,67},{6... | collective-permute-start | bytes 2457608 | tf_op jit(solution)/shard_map/ppermute | solution.py:232
  57.0 126.0 %copy-start.5 = (f32[8,8,16]{2,1,0:T(8,128)}, f32[8,8,16]{2,1,0:T(8,128)S(1)}, u32[]{:S(2)}) copy-start(f32[8,8,16]{2,1,0:T(8,128)S(1)} %fusion.18) | copy-start | bytes 12292
  89.2 11.4 %collective-permute-start.10 = (bf16[640,640]{1,0:T(8,128)(2,1)}, bf16[640,640]{1,0:T(8,128)(2,1)}, u32[]{:S(2)}, u32[]{:S(2)}) collective-permute-start(bf16[640,640]{1,0:T(8,128)(2,1)} %collective-permute-done.4), channel_id=1, source_target_pairs={{0,4},{4,0},{32,36},{36,32},{64,68},{68,64},{96,100},{100,96},{128... | collective-permute-start | bytes 2457608 | tf_op jit(solution)/shard_map/ppermute | solution.py:297
  91.6 9.1 %collective-permute-start.11 = (bf16[640,640]{1,0:T(8,128)(2,1)}, bf16[640,640]{1,0:T(8,128)(2,1)}, u32[]{:S(2)}, u32[]{:S(2)}) collective-permute-start(bf16[640,640]{1,0:T(8,128)(2,1)} %collective-permute-done.5), channel_id=1, source_target_pairs={{0,4},{4,0},{32,36},{36,32},{64,68},{68,64},{96,100},{100,96},{128... | collective-permute-start | bytes 2457608 | tf_op jit(solution)/shard_map/ppermute | solution.py:297
  93.6 23.4 %collective-permute-start.8 = (bf16[640,640]{1,0:T(8,128)(2,1)}, bf16[640,640]{1,0:T(8,128)(2,1)}, u32[]{:S(2)}, u32[]{:S(2)}) collective-permute-start(bf16[640,640]{1,0:T(8,128)(2,1)} %collective-permute-done.4), channel_id=1, source_target_pairs={{0,1},{1,2},{2,3},{3,0},{32,33},{33,34},{34,35},{35,32},{64,65},{6... | collective-permute-start | bytes 2457608 | tf_op jit(solution)/shard_map/ppermute | solution.py:303
  95.5 39.8 %collective-permute-start.9 = (bf16[640,640]{1,0:T(8,128)(2,1)}, bf16[640,640]{1,0:T(8,128)(2,1)}, u32[]{:S(2)}, u32[]{:S(2)}) collective-permute-start(bf16[640,640]{1,0:T(8,128)(2,1)} %collective-permute-done.5), channel_id=1, source_target_pairs={{0,3},{1,0},{2,1},{3,2},{32,35},{33,32},{34,33},{35,34},{64,67},{6... | collective-permute-start | bytes 2457608 | tf_op jit(solution)/shard_map/ppermute | solution.py:304
  135.3 23.4 %collective-permute-start.12 = (bf16[640,640]{1,0:T(8,128)(2,1)}, bf16[640,640]{1,0:T(8,128)(2,1)}, u32[]{:S(2)}, u32[]{:S(2)}) collective-permute-start(bf16[640,640]{1,0:T(8,128)(2,1)} %collective-permute-done.8), channel_id=1, source_target_pairs={{0,1},{1,2},{2,3},{3,0},{32,33},{33,34},{34,35},{35,32},{64,65},{6... | collective-permute-start | bytes 2457608 | tf_op jit(solution)/shard_map/ppermute | solution.py:309
  139.5 43.5 %copy-start.3 = (bf16[64,1280]{1,0:T(8,128)(2,1)S(1)}, bf16[64,1280]{1,0:T(8,128)(2,1)}, u32[]{:S(2)}) copy-start(bf16[64,1280]{1,0:T(8,128)(2,1)} %multiply_convert_fusion) | copy-start | bytes 491524
  139.5 11.3 %collective-permute-start.18 = (bf16[2,32,1408]{2,1,0:T(8,128)(2,1)}, bf16[2,32,1408]{2,1,0:T(8,128)(2,1)}, u32[]{:S(2)}, u32[]{:S(2)}) collective-permute-start(bf16[2,32,1408]{2,1,0:T(8,128)(2,1)} %get-tuple-element.1667), channel_id=1, source_target_pairs={{480,448},{481,449},{482,450},{483,451},{484,452},{485,453},{486,4... | collective-permute-start | bytes 540680 | tf_op jit(solution)/shard_map/ppermute | solution.py:302
  141.0 36.1 %collective-permute-start.16 = (bf16[640,640]{1,0:T(8,128)(2,1)}, bf16[640,640]{1,0:T(8,128)(2,1)}, u32[]{:S(2)}, u32[]{:S(2)}) collective-permute-start(bf16[640,640]{1,0:T(8,128)(2,1)} %collective-permute-done.8), channel_id=1, source_target_pairs={{0,4},{4,0},{32,36},{36,32},{64,68},{68,64},{96,100},{100,96},{128... | collective-permute-start | bytes 2457608 | tf_op jit(solution)/shard_map/ppermute | solution.py:297
  143.7 33.4 %collective-permute-start.13 = (bf16[640,640]{1,0:T(8,128)(2,1)}, bf16[640,640]{1,0:T(8,128)(2,1)}, u32[]{:S(2)}, u32[]{:S(2)}) collective-permute-start(bf16[640,640]{1,0:T(8,128)(2,1)} %collective-permute-done.9), channel_id=1, source_target_pairs={{0,3},{1,0},{2,1},{3,2},{32,35},{33,32},{34,33},{35,34},{64,67},{6... | collective-permute-start | bytes 2457608 | tf_op jit(solution)/shard_map/ppermute | solution.py:310
  148.6 28.5 %collective-permute-start.14 = (bf16[640,640]{1,0:T(8,128)(2,1)}, bf16[640,640]{1,0:T(8,128)(2,1)}, u32[]{:S(2)}, u32[]{:S(2)}) collective-permute-start(bf16[640,640]{1,0:T(8,128)(2,1)} %get-tuple-element.1683), channel_id=1, source_target_pairs={{0,4},{4,0},{32,36},{36,32},{64,68},{68,64},{96,100},{100,96},{128... | collective-permute-start | bytes 2457608 | tf_op jit(solution)/shard_map/ppermute | solution.py:297
  150.8 26.3 %collective-permute-start.15 = (bf16[640,640]{1,0:T(8,128)(2,1)}, bf16[640,640]{1,0:T(8,128)(2,1)}, u32[]{:S(2)}, u32[]{:S(2)}) collective-permute-start(bf16[640,640]{1,0:T(8,128)(2,1)} %get-tuple-element.1684), channel_id=1, source_target_pairs={{0,4},{4,0},{32,36},{36,32},{64,68},{68,64},{96,100},{100,96},{128... | collective-permute-start | bytes 2457608 | tf_op jit(solution)/shard_map/ppermute | solution.py:297
  158.7 18.4 %collective-permute-start.17 = (bf16[640,640]{1,0:T(8,128)(2,1)}, bf16[640,640]{1,0:T(8,128)(2,1)}, u32[]{:S(2)}, u32[]{:S(2)}) collective-permute-start(bf16[640,640]{1,0:T(8,128)(2,1)} %collective-permute-done.9), channel_id=1, source_target_pairs={{0,4},{4,0},{32,36},{36,32},{64,68},{68,64},{96,100},{100,96},{128... | collective-permute-start | bytes 2457608 | tf_op jit(solution)/shard_map/ppermute | solution.py:297
  177.1 43.6 %collective-permute-start.19 = (bf16[640,640]{1,0:T(8,128)(2,1)}, bf16[640,640]{1,0:T(8,128)(2,1)}, u32[]{:S(2)}, u32[]{:S(2)}) collective-permute-start(bf16[640,640]{1,0:T(8,128)(2,1)} %collective-permute-done.12), channel_id=1, source_target_pairs={{0,4},{4,0},{32,36},{36,32},{64,68},{68,64},{96,100},{100,96},{128... | collective-permute-start | bytes 2457608 | tf_op jit(solution)/shard_map/ppermute | solution.py:297
  179.5 41.3 %collective-permute-start.20 = (bf16[640,640]{1,0:T(8,128)(2,1)}, bf16[640,640]{1,0:T(8,128)(2,1)}, u32[]{:S(2)}, u32[]{:S(2)}) collective-permute-start(bf16[640,640]{1,0:T(8,128)(2,1)} %collective-permute-done.13), channel_id=1, source_target_pairs={{0,4},{4,0},{32,36},{36,32},{64,68},{68,64},{96,100},{100,96},{128... | collective-permute-start | bytes 2457608 | tf_op jit(solution)/shard_map/ppermute | solution.py:297
  219.2 1.6 copy-start.6
  225.1 315.0 %collective-permute-start = (bf16[32,1408]{1,0:T(8,128)(2,1)}, bf16[32,1408]{1,0:T(8,128)(2,1)S(1)}, u32[]{:S(2)}, u32[]{:S(2)}) collective-permute-start(bf16[32,1408]{1,0:T(8,128)(2,1)} %param.9), channel_id=1, source_target_pairs={{480,448},{416,384},{352,320},{288,256},{224,192},{160,128},{96,64... | collective-permute-start | bytes 270344 | tf_op jit(solution)/shard_map/while/body/eval_jaxpr/cond/branch_1_fun/ppermute | solution.py:367
  558.4 21.3 %collective-permute-start = (bf16[32,1408]{1,0:T(8,128)(2,1)}, bf16[32,1408]{1,0:T(8,128)(2,1)S(1)}, u32[]{:S(2)}, u32[]{:S(2)}) collective-permute-start(bf16[32,1408]{1,0:T(8,128)(2,1)} %param.9), channel_id=1, source_target_pairs={{480,448},{416,384},{352,320},{288,256},{224,192},{160,128},{96,64... | collective-permute-start | bytes 270344 | tf_op jit(solution)/shard_map/while/body/eval_jaxpr/cond/branch_1_fun/ppermute | solution.py:367
  614.1 55.3 %collective-permute-start.23 = (f32[8,16,640]{2,1,0:T(8,128)S(1)}, f32[8,16,640]{2,1,0:T(8,128)}, u32[]{:S(2)}, u32[]{:S(2)}) collective-permute-start(f32[8,16,640]{2,1,0:T(8,128)S(1)} %slice_select_fusion), channel_id=1, source_target_pairs={{0,4},{4,0},{1,5},{5,1},{2,6},{6,2},{3,7},{7,3},{8,12},{12,8},{9,1... | collective-permute-start | bytes 983048 | tf_op jit(solution)/shard_map/ppermute | solution.py:44
  654.8 7.7 %all-to-all-start.4 = ((bf16[4,2,32,128]{3,2,1,0:T(8,128)(2,1)}), bf16[4,2,32,128]{3,2,1,0:T(8,128)(2,1)S(1)}, u32[]{:S(2)}, u32[]{:S(2)}) async-start(bf16[4,2,32,128]{3,2,1,0:T(8,128)(2,1)} %broadcast_in_dim.170), calls=%async_computation.4 | async-start | bytes 131072 | tf_op jit(solution)/shard_map/all_to_all | solution.py:49
  663.7 5.0 collective-permute-start.21
  666.8 4.7 collective-permute-start.22

commit v12 on v11

--- a/solution.py
+++ b/solution.py
@@ -225,8 +225,8 @@
         jnp.zeros((CHUNKS, rows, width), bf16),
         jnp.zeros((CHUNKS, rows, TAIL), bf16),
     )
-    x_moved, first, second, x_tokens, x_y, empty = lax.optimization_barrier(
-        (x_moved, first, second, x_tokens, x_y, empty)
+    x_moved, first, second, norm_gain, adapter_down, x_tokens, x_y, empty = lax.optimization_barrier(
+        (x_moved, first, second, norm_gain, adapter_down, x_tokens, x_y, empty)
     )
     right_1 = lax.ppermute(first, ("s", "z"), RIGHT)
     left_1 = lax.ppermute(second, ("s", "z"), LEFT)
@@ -236,9 +236,6 @@
     normed_y = x_y.astype(f32) * inv_rms
     x_before = lax.cond(
         sec == 15, lambda x: jnp.zeros((4,) + x.shape, x.dtype), spread, x_moved
-    )
-    x_before, norm_gain, adapter_down = lax.optimization_barrier(
-        (x_before, norm_gain, adapter_down)
     )
     gain_y = both_cores(norm_gain, 1)
     down_y = both_cores(adapter_down[0], 1)

time: 674 us -> 661 us (0.981)
  waiting for transfers between devices: 435 us -> 421 us
    ppermute x1, waiting for transfers between devices: 13.7 us -> 0.01 us  [local(): right_1 = lax.ppermute(first, ('s', 'z'), RIGHT)]
  transfers between devices with their start and end apart: 24 -> 24, of which waited for: 10 -> 9; matrix products, arithmetic and copies ran while one was open for 3% -> 4% of each run, Pallas kernels for 0% -> 0%
where the time goes in v12:
time: 661 us; the launch traced here: 659 us
  waiting for transfers between devices  421 us (64%)
  starting transfers between devices  103 us (16%)
  blocking collectives  82.8 us (13%)
  local copies, waits for them, and re-layouts  18 us (3%)
  Pallas kernels  16 us (2%)
  other arithmetic  9.36 us (1%)
    ppermute x2, waiting for transfers between devices, step(): lax.ppermute(box, 's', ODD)  334 us
    ppermute x2, starting transfers between devices, half_sum(): return mine + lax.ppermute(theirs, 'c', SWAP)  41.7 us
    all_to_all x3, blocking collectives, spread(): return lax.all_to_all(sent, 'y', 0, 0)  30.4 us
    all_gather x2, blocking collectives, extra(): return (lax.all_gather(h_y, 'z'), lax.all_gather(low_in, 'z'))  24.4 us
    ppermute x8, starting transfers between devices, swapped(): return lax.ppermute(value, ('s', 'c'), PAIRS)  19.8 us
    ppermute x1, waiting for transfers between devices, local(): left_2 = lax.ppermute(left_1, ('s', 'z'), LEFT)  18.4 us
    ppermute x1, waiting for transfers between devices, local(): left_1 = lax.ppermute(second, ('s', 'z'), LEFT)  17.7 us
    ppermute x1, waiting for transfers between devices, local(): right_2 = lax.ppermute(right_1, ('s', 'z'), RIGHT)  16.3 us
  transfers between devices with their start and end apart: 24, of which 9 were waited for; matrix products, arithmetic and copies ran while one was open for 4% of the time, Pallas kernels for 0%

profile of v12, /device:TPU:1, one launch (start us, length us, event | category | flops | bytes accessed | tf_op | source)
XLA Modules:
  0.0 659.4 jit_solution(9551518598887955788)
XLA Ops:
  0.7 1.2 dynamic-slice_bitcast_fusion.3
  1.9 1.3 collective-permute-start.3
  3.2 2.0 dynamic-slice_bitcast_fusion.2
  5.2 2.2 copy.32
  8.3 2.8 slice_bitcast_fusion.4
  11.1 11.3 %collective-permute-done.3 = bf16[64,1280]{1,0:T(8,128)(2,1)S(1)} collective-permute-done((bf16[64,1280]{1,0:T(8,128)(2,1)S(1)}, bf16[64,1280]{1,0:T(8,128)(2,1)S(1)}, u32[]{:S(2)}, u32[]{:S(2)}) %collective-permute-start.3) | collective-permute-done | bytes 163872 | tf_op jit(solution)/shard_map/ppermute | solution.py:219
  22.4 6.7 %collective-permute-start.7 = (f32[1,640]{1,0:T(1,128)S(1)}, f32[1,640]{1,0:T(1,128)S(1)}, u32[]{:S(2)}, u32[]{:S(2)}) collective-permute-start(f32[1,640]{1,0:T(1,128)S(1)} %copy-done.9), channel_id=1, source_target_pairs={{0,4},{4,0},{1,5},{5,1},{2,6},{6,2},{3,7},{7,3},{8,12},{12,8},{9,1... | collective-permute-start | bytes 7688 | tf_op jit(solution)/shard_map/ppermute | solution.py:31
  29.5 1.9 collective-permute-start.6
  31.5 1.9 collective-permute-start.4
  33.4 5.2 collective-permute-start.5
  38.6 13.6 %conditional.7 = (bf16[4,2,32,1280]{3,2,1,0:T(8,128)(2,1)}) conditional(s32[]{:T(128)} %convert_element_type.91, bf16[64,1280]{1,0:T(8,128)(2,1)S(1)} %collective-permute-done.3, () %tuple.108), branch_computations={%region_0.0_spmd, %region_1.0_spmd} | conditional | bytes 2129928 | solution.py:237
  38.6 13.5 %all_to_all.21 = bf16[4,64,1280]{2,1,0:T(8,128)(2,1)} all-to-all(bf16[4,64,1280]{2,1,0:T(8,128)(2,1)S(1)} %broadcast_in_dim.99), channel_id=1, replica_groups=mesh['s'=16,'y'=4,'c'=2,'z'=4] {'y'}, dimensions={0} | all-to-all | bytes 1310720 | tf_op jit(solution)/shard_map/cond/branch_0_fun/all_to_all | solution.py:49
  53.0 1.0 broadcast_select_fusion.4
  54.5 1.1 fusion.18
  55.6 17.7 %collective-permute-done.5 = bf16[640,640]{1,0:T(8,128)(2,1)} collective-permute-done((bf16[640,640]{1,0:T(8,128)(2,1)}, bf16[640,640]{1,0:T(8,128)(2,1)}, u32[]{:S(2)}, u32[]{:S(2)}) %collective-permute-start.5) | collective-permute-done | bytes 819232 | tf_op jit(solution)/shard_map/ppermute | solution.py:232
  73.4 2.4 collective-permute-start.10
  75.8 1.9 collective-permute-start.11
  77.7 1.9 collective-permute-start.8
  79.6 5.2 collective-permute-start.9
  84.8 16.3 %collective-permute-done.8 = bf16[640,640]{1,0:T(8,128)(2,1)} collective-permute-done((bf16[640,640]{1,0:T(8,128)(2,1)}, bf16[640,640]{1,0:T(8,128)(2,1)}, u32[]{:S(2)}, u32[]{:S(2)}) %collective-permute-start.8) | collective-permute-done | bytes 819232 | tf_op jit(solution)/shard_map/ppermute | solution.py:300
  101.1 18.4 %collective-permute-done.9 = bf16[640,640]{1,0:T(8,128)(2,1)} collective-permute-done((bf16[640,640]{1,0:T(8,128)(2,1)}, bf16[640,640]{1,0:T(8,128)(2,1)}, u32[]{:S(2)}, u32[]{:S(2)}) %collective-permute-start.9) | collective-permute-done | bytes 819232 | tf_op jit(solution)/shard_map/ppermute | solution.py:301
  119.4 2.2 collective-permute-start.12
  123.6 1.5 collective-permute-start.18
  125.1 2.7 collective-permute-start.16
  127.8 4.9 collective-permute-start.13
  132.7 2.2 collective-permute-start.14
  134.9 2.1 collective-permute-start.15
  137.0 5.8 collective-permute-done.12
  142.8 4.2 collective-permute-start.17
  147.0 14.2 %collective-permute-done.13 = bf16[640,640]{1,0:T(8,128)(2,1)} collective-permute-done((bf16[640,640]{1,0:T(8,128)(2,1)}, bf16[640,640]{1,0:T(8,128)(2,1)}, u32[]{:S(2)}, u32[]{:S(2)}) %collective-permute-start.13) | collective-permute-done | bytes 819232 | tf_op jit(solution)/shard_map/ppermute | solution.py:307
  161.2 2.3 collective-permute-start.19
  163.6 2.0 collective-permute-start.20
  167.1 38.0 %conditional.9 = (bf16[4,64,1280]{2,1,0:T(8,128)(2,1)}, bf16[4,8,8,16]{3,2,1,0:T(8,128)(2,1)S(1)}) conditional(s32[]{:T(128)} %convert_element_type.100, () %tuple.115, (bf16[64,1280]{1,0:T(8,128)(2,1)S(1)}, f32[8,8,16]{2,1,0:T(8,128)S(1)}) %tuple.181), branch_computations={%region_19.20_spmd, %region_20.22_spmd} | conditional | flops 1024 | bytes 835600 | solution.py:316
  167.1 14.2 %all-gather = bf16[256,1280]{1,0:T(8,128)(2,1)} all-gather(bf16[64,1280]{1,0:T(8,128)(2,1)S(1)} %get-tuple-element.1091), channel_id=2, replica_groups=mesh['s'=16,'y'=4,'c'=2,'z'=4] {'z'}, dimensions={0}, use_global_device_ids=true | all-gather | bytes 819200 | tf_op jit(solution)/shard_map/cond/branch_1_fun/all_gather | solution.py:256
  181.3 13.6 %psum.12 = bf16[8,8,16]{2,1,0:T(8,128)(2,1)S(1)} all-reduce(f32[8,8,16]{2,1,0:T(8,128)S(1)} %get-tuple-element.1092), channel_id=1, replica_groups=mesh['s'=16,'y'=4,'c'=2,'z'=4] {'y'}, use_global_device_ids=true, to_apply=%region_21.21 | all-reduce | flops 1024 | bytes 6144 | tf_op jit(solution)/shard_map/cond/branch_1_fun/psum | solution.py:255
  194.9 10.2 %all-gather.1 = bf16[32,8,16]{2,1,0:T(8,128)(2,1)S(1)} all-gather(bf16[8,8,16]{2,1,0:T(8,128)(2,1)S(1)} %psum.12), channel_id=3, replica_groups=mesh['s'=16,'y'=4,'c'=2,'z'=4] {'z'}, dimensions={0}, use_global_device_ids=true | all-gather | bytes 10240 | tf_op jit(solution)/shard_map/cond/branch_1_fun/all_gather | solution.py:256
  205.1 1.6 slice_bitcast_fusion.6
  206.7 377.3 %while.27 = (s32[]{:T(128)}, bf16[32,1408]{1,0:T(8,128)(2,1)}, bf16[2,32,1408]{2,1,0:T(8,128)(2,1)}, bf16[2,32,64]{2,1,0:T(8,128)(2,1)S(1)}, bf16[2,32,1280]{2,1...) while((s32[]{:T(128)}, bf16[32,1408]{1,0:T(8,128)(2,1)}, ...), condition=%wide.region_17.18_spmd, body=%wide.region_8.17_spmd.sunk | while | flops 419430432 | bytes 14820536 | solution.py:373
  211.0 316.8 %conditional.14 = (bf16[32,1408]{1,0:T(8,128)(2,1)}) conditional(s32[]{:T(128)} %clamp.23, bf16[32,1408]{1,0:T(8,128)(2,1)} %get-tuple-element.1641, bf16[32,1408]{1,0:T(8,128)(2,1)} %get-tuple-element.1641, bf16[32,1408]{1,0:T(8,128)(2,1)} %get-tuple-element.1641, (s32[]{:T(128)}, ...), branch_computations={%region_13.13_spmd, %region_14.14_spmd, %region_15.15_spmd, %regio... | conditional | flops 3 | bytes 540720 | solution.py:360
  211.1 1.3 collective-permute-start
  212.4 314.8 %collective-permute-done = bf16[32,1408]{1,0:T(8,128)(2,1)S(1)} collective-permute-done((bf16[32,1408]{1,0:T(8,128)(2,1)}, bf16[32,1408]{1,0:T(8,128)(2,1)S(1)}, u32[]{:S(2)}, u32[]{:S(2)}) %collective-permute-start) | collective-permute-done | bytes 90144 | tf_op jit(solution)/shard_map/while/body/eval_jaxpr/cond/branch_1_fun/ppermute | solution.py:364
  527.8 17.4 %conditional.13 = ((bf16[2,32,1408]{2,1,0:T(8,128)(2,1)}, bf16[2,32,64]{2,1,0:T(8,128)(2,1)S(1)}, bf16[2,32,1280]{2,1,0:T(8,128)(2,1)}, bf16[2,32,128]{2,1,0:T(8,128)(2,1)S(1)}, bf16[32,1408]{1,0:T(8,128)(2,1)})) conditional(s32[]{:T(128)} %convert_element_type.126, (bf16[2,32,1408]{2,1,0:T(8,128)(2,1)}, bf16[2,32,64]{2,1,0:T(8,128)(2,1)S(1)}, ...), branch_computations={%region_9.9_spmd, %region_10.12_spmd} | conditional | flops 419430400 | bytes 14278758 | solution.py:354
  527.8 9.4 %conditional = (bf16[4,32,1408]{2,1,0:T(8,128)(2,1)S(1)}) conditional(s32[]{:T(128)} %convert_element_type.77, bf16[32,1408]{1,0:T(8,128)(2,1)} %get-tuple-element.1016, () %tuple.83), branch_computations={%region_11.10_spmd, %region_12.11_spmd} | conditional | bytes 1171464 | solution.py:337
  528.8 8.4 %all_to_all.22 = bf16[4,32,1408]{2,1,0:T(8,128)(2,1)S(1)} all-to-all(bf16[4,32,1408]{2,1,0:T(8,128)(2,1)S(1)} %broadcast_in_dim.143), channel_id=1, replica_groups=mesh['s'=16,'y'=4,'c'=2,'z'=4] {'y'}, dimensions={0} | all-to-all | bytes 720896 | tf_op jit(solution)/shard_map/while/body/eval_jaxpr/cond/branch_1_fun/cond/branch_0_fun/all_to_all | solution.py:49
  537.3 8.0 %stage.1 = (bf16[32,1408]{1,0:T(8,128)(2,1)}, bf16[2,32,1408]{2,1,0:T(8,128)(2,1)}, bf16[2,32,64]{2,1,0:T(8,128)(2,1)S(1)}, bf16[2,32,1280]{2,1,0:T(8,128)(2,1)}, bf16[2,32,128]{2,1,0:T(8,128)(2,1)S(1)}) custom-call(s32[4]{0:T(128)S(1)} %pad_add_fusion.place_ref, ...), custom_call_target="tpu_custom_call", output_to_operand_aliasing={{1}: (24, {}), {2}: (25, {}), {3}: (26, {}), {4}: (27, {})} | custom-call | flops 419430400 | bytes 13107200 | tf_op jit(solution)/shard_map/while/body/eval_jaxpr/cond/branch_1_fun/stage/pallas_call | solution.py:161
  545.5 21.0 %conditional.14 = (bf16[32,1408]{1,0:T(8,128)(2,1)}) conditional(s32[]{:T(128)} %clamp.23, bf16[32,1408]{1,0:T(8,128)(2,1)} %get-tuple-element.1641, bf16[32,1408]{1,0:T(8,128)(2,1)} %get-tuple-element.1641, bf16[32,1408]{1,0:T(8,128)(2,1)} %get-tuple-element.1641, (s32[]{:T(128)}, ...), branch_computations={%region_13.13_spmd, %region_14.14_spmd, %region_15.15_spmd, %regio... | conditional | flops 3 | bytes 540720 | solution.py:360
  545.5 1.3 collective-permute-start
  546.8 19.0 %collective-permute-done = bf16[32,1408]{1,0:T(8,128)(2,1)S(1)} collective-permute-done((bf16[32,1408]{1,0:T(8,128)(2,1)}, bf16[32,1408]{1,0:T(8,128)(2,1)S(1)}, u32[]{:S(2)}, u32[]{:S(2)}) %collective-permute-start) | collective-permute-done | bytes 90144 | tf_op jit(solution)/shard_map/while/body/eval_jaxpr/cond/branch_1_fun/ppermute | solution.py:364
  566.5 17.4 %conditional.13 = ((bf16[2,32,1408]{2,1,0:T(8,128)(2,1)}, bf16[2,32,64]{2,1,0:T(8,128)(2,1)S(1)}, bf16[2,32,1280]{2,1,0:T(8,128)(2,1)}, bf16[2,32,128]{2,1,0:T(8,128)(2,1)S(1)}, bf16[32,1408]{1,0:T(8,128)(2,1)})) conditional(s32[]{:T(128)} %convert_element_type.126, (bf16[2,32,1408]{2,1,0:T(8,128)(2,1)}, bf16[2,32,64]{2,1,0:T(8,128)(2,1)S(1)}, ...), branch_computations={%region_9.9_spmd, %region_10.12_spmd} | conditional | flops 419430400 | bytes 14278758 | solution.py:354
  566.5 9.4 %conditional = (bf16[4,32,1408]{2,1,0:T(8,128)(2,1)S(1)}) conditional(s32[]{:T(128)} %convert_element_type.77, bf16[32,1408]{1,0:T(8,128)(2,1)} %get-tuple-element.1016, () %tuple.83), branch_computations={%region_11.10_spmd, %region_12.11_spmd} | conditional | bytes 1171464 | solution.py:337
  567.4 8.4 %all_to_all.22 = bf16[4,32,1408]{2,1,0:T(8,128)(2,1)S(1)} all-to-all(bf16[4,32,1408]{2,1,0:T(8,128)(2,1)S(1)} %broadcast_in_dim.143), channel_id=1, replica_groups=mesh['s'=16,'y'=4,'c'=2,'z'=4] {'y'}, dimensions={0} | all-to-all | bytes 720896 | tf_op jit(solution)/shard_map/while/body/eval_jaxpr/cond/branch_1_fun/cond/branch_0_fun/all_to_all | solution.py:49
  575.9 8.0 %stage.1 = (bf16[32,1408]{1,0:T(8,128)(2,1)}, bf16[2,32,1408]{2,1,0:T(8,128)(2,1)}, bf16[2,32,64]{2,1,0:T(8,128)(2,1)S(1)}, bf16[2,32,1280]{2,1,0:T(8,128)(2,1)}, bf16[2,32,128]{2,1,0:T(8,128)(2,1)S(1)}) custom-call(s32[4]{0:T(128)S(1)} %pad_add_fusion.place_ref, ...), custom_call_target="tpu_custom_call", output_to_operand_aliasing={{1}: (24, {}), {2}: (25, {}), {3}: (26, {}), {4}: (27, {})} | custom-call | flops 419430400 | bytes 13107200 | tf_op jit(solution)/shard_map/while/body/eval_jaxpr/cond/branch_1_fun/stage/pallas_call | solution.py:161
  585.0 14.4 %all-gather.4 = bf16[256,1408]{1,0:T(8,128)(2,1)S(1)} all-gather(bf16[64,1408]{1,0:T(8,128)(2,1)S(1)} %fusion.17), channel_id=6, replica_groups=mesh['s'=16,'y'=4,'c'=2,'z'=4] {'z'}, dimensions={0}, use_global_device_ids=true | all-gather | bytes 901120 | tf_op jit(solution)/shard_map/all_gather | solution.py:398
  599.4 1.1 fusion.13
  600.6 39.8 %collective-permute-start.23 = (f32[8,16,640]{2,1,0:T(8,128)S(1)}, f32[8,16,640]{2,1,0:T(8,128)}, u32[]{:S(2)}, u32[]{:S(2)}) collective-permute-start(f32[8,16,640]{2,1,0:T(8,128)S(1)} %slice_select_fusion), channel_id=1, source_target_pairs={{0,4},{4,0},{1,5},{5,1},{2,6},{6,2},{3,7},{7,3},{8,12},{12,8},{9,1... | collective-permute-start | bytes 983048 | tf_op jit(solution)/shard_map/ppermute | solution.py:44
  641.6 3.3 all-to-all-start.4
  644.9 1.4 fusion.14
  646.3 3.1 all-to-all-done.4
  649.5 1.0 subtract_convert_fusion
  650.5 3.1 collective-permute-start.21
  653.6 1.9 collective-permute-start.22
  656.3 1.0 select_add_fusion
  657.3 1.0 select_reduce_fusion
  658.4 1.0 select_reduce_fusion.1
  (142 shorter events, 13.9 us)
Async XLA Ops:
  0.6 7.0 %copy-start = (bf16[1,8,16,5120]{3,2,1,0:T(8,128)(2,1)S(1)}, bf16[1,8,16,5120]{3,2,1,0:T(8,128)(2,1)}, u32[]{:S(2)}) copy-start(bf16[1,8,16,5120]{3,2,1,0:T(8,128)(2,1)} %param.31) | copy-start | bytes 3932164
  0.6 4.6 copy-start.5
  1.9 20.5 %collective-permute-start.3 = (bf16[64,1280]{1,0:T(8,128)(2,1)S(1)}, bf16[64,1280]{1,0:T(8,128)(2,1)S(1)}, u32[]{:S(2)}, u32[]{:S(2)}) collective-permute-start(bf16[64,1280]{1,0:T(8,128)(2,1)S(1)} %dynamic-slice_bitcast_fusion.3), channel_id=1, source_target_pairs={{480,448},{448,416},{416,384},{384,352},{352,320},{320,288},{288,2... | collective-permute-start | bytes 491528 | tf_op jit(solution)/shard_map/ppermute | solution.py:219
  5.2 2.2 copy-start.11
  5.2 2.2 copy-start.12
  7.6 0.7 copy-start.13
  8.3 14.1 %copy-start.9 = (f32[1,640]{1,0:T(1,128)S(1)}, f32[1,640]{1,0:T(1,128)}, u32[]{:S(2)}) copy-start(f32[1,640]{1,0:T(1,128)} %param.29) | copy-start | bytes 7684
  8.3 20.8 %copy-start.3 = (bf16[8,8,5120]{2,1,0:T(8,128)(2,1)S(1)}, bf16[8,8,5120]{2,1,0:T(8,128)(2,1)}, u32[]{:S(2)}) copy-start(bf16[8,8,5120]{2,1,0:T(8,128)(2,1)} %dynamic-slice_bitcast_fusion.2) | copy-start | bytes 1966084
  8.3 21.2 %copy-start.8 = (bf16[1,8,640,16]{2,3,1,0:T(8,128)(2,1)S(1)}, bf16[1,8,640,16]{2,3,1,0:T(8,128)(2,1)}, u32[]{:S(2)}) copy-start(bf16[1,8,640,16]{2,3,1,0:T(8,128)(2,1)} %param.30) | copy-start | bytes 491524
  22.4 29.7 %collective-permute-start.7 = (f32[1,640]{1,0:T(1,128)S(1)}, f32[1,640]{1,0:T(1,128)S(1)}, u32[]{:S(2)}, u32[]{:S(2)}) collective-permute-start(f32[1,640]{1,0:T(1,128)S(1)} %copy-done.9), channel_id=1, source_target_pairs={{0,4},{4,0},{1,5},{5,1},{2,6},{6,2},{3,7},{7,3},{8,12},{12,8},{9,1... | collective-permute-start | bytes 7688 | tf_op jit(solution)/shard_map/ppermute | solution.py:31
  29.5 23.4 %collective-permute-start.6 = (bf16[8,640,16]{1,2,0:T(8,128)(2,1)S(1)}, bf16[8,640,16]{1,2,0:T(8,128)(2,1)}, u32[]{:S(2)}, u32[]{:S(2)}) collective-permute-start(bf16[8,640,16]{1,2,0:T(8,128)(2,1)S(1)} %bitcast.114), channel_id=1, source_target_pairs={{0,4},{4,0},{1,5},{5,1},{2,6},{6,2},{3,7},{7,3},{8,12},{12,8},{9,1... | collective-permute-start | bytes 491528 | tf_op jit(solution)/shard_map/ppermute | solution.py:31
  31.5 24.2 %collective-permute-start.4 = (bf16[640,640]{1,0:T(8,128)(2,1)}, bf16[640,640]{1,0:T(8,128)(2,1)}, u32[]{:S(2)}, u32[]{:S(2)}) collective-permute-start(bf16[640,640]{1,0:T(8,128)(2,1)} %get-tuple-element.1682), channel_id=1, source_target_pairs={{0,1},{1,2},{2,3},{3,0},{32,33},{33,34},{34,35},{35,32},{64,65},{6... | collective-permute-start | bytes 2457608 | tf_op jit(solution)/shard_map/ppermute | solution.py:231
  33.4 39.9 %collective-permute-start.5 = (bf16[640,640]{1,0:T(8,128)(2,1)}, bf16[640,640]{1,0:T(8,128)(2,1)}, u32[]{:S(2)}, u32[]{:S(2)}) collective-permute-start(bf16[640,640]{1,0:T(8,128)(2,1)} %get-tuple-element.1683), channel_id=1, source_target_pairs={{0,3},{1,0},{2,1},{3,2},{32,35},{33,32},{34,33},{35,34},{64,67},{6... | collective-permute-start | bytes 2457608 | tf_op jit(solution)/shard_map/ppermute | solution.py:232
  55.6 111.5 %copy-start.6 = (f32[8,8,16]{2,1,0:T(8,128)}, f32[8,8,16]{2,1,0:T(8,128)S(1)}, u32[]{:S(2)}) copy-start(f32[8,8,16]{2,1,0:T(8,128)S(1)} %fusion.18) | copy-start | bytes 12292
  73.4 11.4 %collective-permute-start.10 = (bf16[640,640]{1,0:T(8,128)(2,1)}, bf16[640,640]{1,0:T(8,128)(2,1)}, u32[]{:S(2)}, u32[]{:S(2)}) collective-permute-start(bf16[640,640]{1,0:T(8,128)(2,1)} %collective-permute-done.4), channel_id=1, source_target_pairs={{0,4},{4,0},{32,36},{36,32},{64,68},{68,64},{96,100},{100,96},{128... | collective-permute-start | bytes 2457608 | tf_op jit(solution)/shard_map/ppermute | solution.py:294
  75.8 9.1 %collective-permute-start.11 = (bf16[640,640]{1,0:T(8,128)(2,1)}, bf16[640,640]{1,0:T(8,128)(2,1)}, u32[]{:S(2)}, u32[]{:S(2)}) collective-permute-start(bf16[640,640]{1,0:T(8,128)(2,1)} %collective-permute-done.5), channel_id=1, source_target_pairs={{0,4},{4,0},{32,36},{36,32},{64,68},{68,64},{96,100},{100,96},{128... | collective-permute-start | bytes 2457608 | tf_op jit(solution)/shard_map/ppermute | solution.py:294
  77.7 23.4 %collective-permute-start.8 = (bf16[640,640]{1,0:T(8,128)(2,1)}, bf16[640,640]{1,0:T(8,128)(2,1)}, u32[]{:S(2)}, u32[]{:S(2)}) collective-permute-start(bf16[640,640]{1,0:T(8,128)(2,1)} %collective-permute-done.4), channel_id=1, source_target_pairs={{0,1},{1,2},{2,3},{3,0},{32,33},{33,34},{34,35},{35,32},{64,65},{6... | collective-permute-start | bytes 2457608 | tf_op jit(solution)/shard_map/ppermute | solution.py:300
  79.6 39.8 %collective-permute-start.9 = (bf16[640,640]{1,0:T(8,128)(2,1)}, bf16[640,640]{1,0:T(8,128)(2,1)}, u32[]{:S(2)}, u32[]{:S(2)}) collective-permute-start(bf16[640,640]{1,0:T(8,128)(2,1)} %collective-permute-done.5), channel_id=1, source_target_pairs={{0,3},{1,0},{2,1},{3,2},{32,35},{33,32},{34,33},{35,34},{64,67},{6... | collective-permute-start | bytes 2457608 | tf_op jit(solution)/shard_map/ppermute | solution.py:301
  119.4 23.4 %collective-permute-start.12 = (bf16[640,640]{1,0:T(8,128)(2,1)}, bf16[640,640]{1,0:T(8,128)(2,1)}, u32[]{:S(2)}, u32[]{:S(2)}) collective-permute-start(bf16[640,640]{1,0:T(8,128)(2,1)} %collective-permute-done.8), channel_id=1, source_target_pairs={{0,1},{1,2},{2,3},{3,0},{32,33},{33,34},{34,35},{35,32},{64,65},{6... | collective-permute-start | bytes 2457608 | tf_op jit(solution)/shard_map/ppermute | solution.py:306
  123.6 43.5 %copy-start.4 = (bf16[64,1280]{1,0:T(8,128)(2,1)S(1)}, bf16[64,1280]{1,0:T(8,128)(2,1)}, u32[]{:S(2)}) copy-start(bf16[64,1280]{1,0:T(8,128)(2,1)} %multiply_convert_fusion) | copy-start | bytes 491524
  123.6 11.3 %collective-permute-start.18 = (bf16[2,32,1408]{2,1,0:T(8,128)(2,1)}, bf16[2,32,1408]{2,1,0:T(8,128)(2,1)}, u32[]{:S(2)}, u32[]{:S(2)}) collective-permute-start(bf16[2,32,1408]{2,1,0:T(8,128)(2,1)} %get-tuple-element.1666), channel_id=1, source_target_pairs={{480,448},{481,449},{482,450},{483,451},{484,452},{485,453},{486,4... | collective-permute-start | bytes 540680 | tf_op jit(solution)/shard_map/ppermute | solution.py:299
  125.1 36.1 %collective-permute-start.16 = (bf16[640,640]{1,0:T(8,128)(2,1)}, bf16[640,640]{1,0:T(8,128)(2,1)}, u32[]{:S(2)}, u32[]{:S(2)}) collective-permute-start(bf16[640,640]{1,0:T(8,128)(2,1)} %collective-permute-done.8), channel_id=1, source_target_pairs={{0,4},{4,0},{32,36},{36,32},{64,68},{68,64},{96,100},{100,96},{128... | collective-permute-start | bytes 2457608 | tf_op jit(solution)/shard_map/ppermute | solution.py:294
  127.8 33.4 %collective-permute-start.13 = (bf16[640,640]{1,0:T(8,128)(2,1)}, bf16[640,640]{1,0:T(8,128)(2,1)}, u32[]{:S(2)}, u32[]{:S(2)}) collective-permute-start(bf16[640,640]{1,0:T(8,128)(2,1)} %collective-permute-done.9), channel_id=1, source_target_pairs={{0,3},{1,0},{2,1},{3,2},{32,35},{33,32},{34,33},{35,34},{64,67},{6... | collective-permute-start | bytes 2457608 | tf_op jit(solution)/shard_map/ppermute | solution.py:307
  132.7 28.5 %collective-permute-start.14 = (bf16[640,640]{1,0:T(8,128)(2,1)}, bf16[640,640]{1,0:T(8,128)(2,1)}, u32[]{:S(2)}, u32[]{:S(2)}) collective-permute-start(bf16[640,640]{1,0:T(8,128)(2,1)} %get-tuple-element.1682), channel_id=1, source_target_pairs={{0,4},{4,0},{32,36},{36,32},{64,68},{68,64},{96,100},{100,96},{128... | collective-permute-start | bytes 2457608 | tf_op jit(solution)/shard_map/ppermute | solution.py:294
  134.9 26.3 %collective-permute-start.15 = (bf16[640,640]{1,0:T(8,128)(2,1)}, bf16[640,640]{1,0:T(8,128)(2,1)}, u32[]{:S(2)}, u32[]{:S(2)}) collective-permute-start(bf16[640,640]{1,0:T(8,128)(2,1)} %get-tuple-element.1683), channel_id=1, source_target_pairs={{0,4},{4,0},{32,36},{36,32},{64,68},{68,64},{96,100},{100,96},{128... | collective-permute-start | bytes 2457608 | tf_op jit(solution)/shard_map/ppermute | solution.py:294
  142.8 18.4 %collective-permute-start.17 = (bf16[640,640]{1,0:T(8,128)(2,1)}, bf16[640,640]{1,0:T(8,128)(2,1)}, u32[]{:S(2)}, u32[]{:S(2)}) collective-permute-start(bf16[640,640]{1,0:T(8,128)(2,1)} %collective-permute-done.9), channel_id=1, source_target_pairs={{0,4},{4,0},{32,36},{36,32},{64,68},{68,64},{96,100},{100,96},{128... | collective-permute-start | bytes 2457608 | tf_op jit(solution)/shard_map/ppermute | solution.py:294
  161.2 45.4 %collective-permute-start.19 = (bf16[640,640]{1,0:T(8,128)(2,1)}, bf16[640,640]{1,0:T(8,128)(2,1)}, u32[]{:S(2)}, u32[]{:S(2)}) collective-permute-start(bf16[640,640]{1,0:T(8,128)(2,1)} %collective-permute-done.12), channel_id=1, source_target_pairs={{0,4},{4,0},{32,36},{36,32},{64,68},{68,64},{96,100},{100,96},{128... | collective-permute-start | bytes 2457608 | tf_op jit(solution)/shard_map/ppermute | solution.py:294
  163.6 43.1 %collective-permute-start.20 = (bf16[640,640]{1,0:T(8,128)(2,1)}, bf16[640,640]{1,0:T(8,128)(2,1)}, u32[]{:S(2)}, u32[]{:S(2)}) collective-permute-start(bf16[640,640]{1,0:T(8,128)(2,1)} %collective-permute-done.13), channel_id=1, source_target_pairs={{0,4},{4,0},{32,36},{36,32},{64,68},{68,64},{96,100},{100,96},{128... | collective-permute-start | bytes 2457608 | tf_op jit(solution)/shard_map/ppermute | solution.py:294
  205.1 1.6 copy-start.7
  211.1 316.1 %collective-permute-start = (bf16[32,1408]{1,0:T(8,128)(2,1)}, bf16[32,1408]{1,0:T(8,128)(2,1)S(1)}, u32[]{:S(2)}, u32[]{:S(2)}) collective-permute-start(bf16[32,1408]{1,0:T(8,128)(2,1)} %param.9), channel_id=1, source_target_pairs={{480,448},{416,384},{352,320},{288,256},{224,192},{160,128},{96,64... | collective-permute-start | bytes 270344 | tf_op jit(solution)/shard_map/while/body/eval_jaxpr/cond/branch_1_fun/ppermute | solution.py:364
  545.5 20.3 %collective-permute-start = (bf16[32,1408]{1,0:T(8,128)(2,1)}, bf16[32,1408]{1,0:T(8,128)(2,1)S(1)}, u32[]{:S(2)}, u32[]{:S(2)}) collective-permute-start(bf16[32,1408]{1,0:T(8,128)(2,1)} %param.9), channel_id=1, source_target_pairs={{480,448},{416,384},{352,320},{288,256},{224,192},{160,128},{96,64... | collective-permute-start | bytes 270344 | tf_op jit(solution)/shard_map/while/body/eval_jaxpr/cond/branch_1_fun/ppermute | solution.py:364
  600.6 55.7 %collective-permute-start.23 = (f32[8,16,640]{2,1,0:T(8,128)S(1)}, f32[8,16,640]{2,1,0:T(8,128)}, u32[]{:S(2)}, u32[]{:S(2)}) collective-permute-start(f32[8,16,640]{2,1,0:T(8,128)S(1)} %slice_select_fusion), channel_id=1, source_target_pairs={{0,4},{4,0},{1,5},{5,1},{2,6},{6,2},{3,7},{7,3},{8,12},{12,8},{9,1... | collective-permute-start | bytes 983048 | tf_op jit(solution)/shard_map/ppermute | solution.py:44
  641.6 7.7 %all-to-all-start.4 = ((bf16[4,2,32,128]{3,2,1,0:T(8,128)(2,1)}), bf16[4,2,32,128]{3,2,1,0:T(8,128)(2,1)S(1)}, u32[]{:S(2)}, u32[]{:S(2)}) async-start(bf16[4,2,32,128]{3,2,1,0:T(8,128)(2,1)} %broadcast_in_dim.170), calls=%async_computation.4 | async-start | bytes 131072 | tf_op jit(solution)/shard_map/all_to_all | solution.py:49
  650.5 5.0 collective-permute-start.21
  653.6 4.7 collective-permute-start.22

commit v13 on v12

--- a/solution.py
+++ b/solution.py
@@ -128,10 +128,10 @@
     total = low_rank_scale * lax.dot_general(
         low, down_ref[...], contract_inner, preferred_element_type=f32
     )
-    for part in range(4):
-        for copy in copies[4 * part : 4 * part + 4]:
+    for begin, end in ((0, 2), (2, 4), (4, 6), (6, 7), (7, 8)):
+        for copy in copies[2 * begin : 2 * end]:
             copy.wait()
-        span = slice(part * width, (part + 1) * width)
+        span = slice(begin * half, end * half)
         total = total + lax.dot_general(
             full[:, span], weight[span], contract_inner, preferred_element_type=f32
         )
@@ -356,7 +356,7 @@
         )
         part = ((sec == turn) | (sec == turn - 1)) & (turn >= 1) & (turn <= 14)
         kind = jnp.where(part, jnp.where(turn % 2 == 1, 1, 2), 0)
-        kind = jnp.where((turn == 15) & (sec == 14), 3, kind)
+        kind = jnp.where((turn == 15) & (sec == 14) & (m > 0), 3, kind)
         box = lax.switch(
             kind,
             [

time: 661 us -> 657 us (level)
  waiting for transfers between devices: 421 us -> 414 us
where the time goes in v13:
time: 657 us; the launch traced here: 655 us
  waiting for transfers between devices  414 us (63%)
  starting transfers between devices  101 us (15%)
  blocking collectives  87.5 us (13%)
  local copies, waits for them, and re-layouts  18 us (3%)
  Pallas kernels  15.4 us (2%)
  other arithmetic  9.36 us (1%)
    ppermute x2, waiting for transfers between devices, step(): lax.ppermute(box, 's', ODD)  328 us
    ppermute x2, starting transfers between devices, half_sum(): return mine + lax.ppermute(theirs, 'c', SWAP)  39.3 us
    all_to_all x3, blocking collectives, spread(): return lax.all_to_all(sent, 'y', 0, 0)  30.4 us
    all_gather x2, blocking collectives, extra(): return (lax.all_gather(h_y, 'z'), lax.all_gather(low_in, 'z'))  24.4 us
    ppermute x8, starting transfers between devices, swapped(): return lax.ppermute(value, ('s', 'c'), PAIRS)  19.8 us
    all_gather x1, blocking collectives, local(): both = lax.all_gather(both, 'z').reshape(4, micro, toks, width + TAIL)  19.1 us
    ppermute x1, waiting for transfers between devices, local(): left_2 = lax.ppermute(left_1, ('s', 'z'), LEFT)  18.4 us
    ppermute x1, waiting for transfers between devices, local(): left_1 = lax.ppermute(second, ('s', 'z'), LEFT)  17.7 us
  transfers between devices with their start and end apart: 24, of which 9 were waited for; matrix products, arithmetic and copies ran while one was open for 4% of the time, Pallas kernels for 0%

profile of v13, /device:TPU:1, one launch (start us, length us, event | category | flops | bytes accessed | tf_op | source)
XLA Modules:
  0.0 655.0 jit_solution(17924657598834223996)
XLA Ops:
  0.7 1.2 dynamic-slice_bitcast_fusion.3
  1.9 1.3 collective-permute-start.3
  3.2 2.0 dynamic-slice_bitcast_fusion.2
  5.2 2.2 copy.32
  8.3 2.8 slice_bitcast_fusion.4
  11.1 11.3 %collective-permute-done.3 = bf16[64,1280]{1,0:T(8,128)(2,1)S(1)} collective-permute-done((bf16[64,1280]{1,0:T(8,128)(2,1)S(1)}, bf16[64,1280]{1,0:T(8,128)(2,1)S(1)}, u32[]{:S(2)}, u32[]{:S(2)}) %collective-permute-start.3) | collective-permute-done | bytes 163872 | tf_op jit(solution)/shard_map/ppermute | solution.py:219
  22.4 6.7 %collective-permute-start.7 = (f32[1,640]{1,0:T(1,128)S(1)}, f32[1,640]{1,0:T(1,128)S(1)}, u32[]{:S(2)}, u32[]{:S(2)}) collective-permute-start(f32[1,640]{1,0:T(1,128)S(1)} %copy-done.9), channel_id=1, source_target_pairs={{0,4},{4,0},{1,5},{5,1},{2,6},{6,2},{3,7},{7,3},{8,12},{12,8},{9,1... | collective-permute-start | bytes 7688 | tf_op jit(solution)/shard_map/ppermute | solution.py:31
  29.5 1.9 collective-permute-start.6
  31.5 1.9 collective-permute-start.4
  33.4 5.2 collective-permute-start.5
  38.6 13.6 %conditional.7 = (bf16[4,2,32,1280]{3,2,1,0:T(8,128)(2,1)}) conditional(s32[]{:T(128)} %convert_element_type.91, bf16[64,1280]{1,0:T(8,128)(2,1)S(1)} %collective-permute-done.3, () %tuple.108), branch_computations={%region_0.0_spmd, %region_1.0_spmd} | conditional | bytes 2129928 | solution.py:237
  38.6 13.5 %all_to_all.21 = bf16[4,64,1280]{2,1,0:T(8,128)(2,1)} all-to-all(bf16[4,64,1280]{2,1,0:T(8,128)(2,1)S(1)} %broadcast_in_dim.99), channel_id=1, replica_groups=mesh['s'=16,'y'=4,'c'=2,'z'=4] {'y'}, dimensions={0} | all-to-all | bytes 1310720 | tf_op jit(solution)/shard_map/cond/branch_0_fun/all_to_all | solution.py:49
  53.0 1.0 broadcast_select_fusion.4
  54.5 1.1 fusion.18
  55.6 17.7 %collective-permute-done.5 = bf16[640,640]{1,0:T(8,128)(2,1)} collective-permute-done((bf16[640,640]{1,0:T(8,128)(2,1)}, bf16[640,640]{1,0:T(8,128)(2,1)}, u32[]{:S(2)}, u32[]{:S(2)}) %collective-permute-start.5) | collective-permute-done | bytes 819232 | tf_op jit(solution)/shard_map/ppermute | solution.py:232
  73.4 2.4 collective-permute-start.10
  75.8 1.9 collective-permute-start.11
  77.7 1.9 collective-permute-start.8
  79.6 5.2 collective-permute-start.9
  84.8 16.3 %collective-permute-done.8 = bf16[640,640]{1,0:T(8,128)(2,1)} collective-permute-done((bf16[640,640]{1,0:T(8,128)(2,1)}, bf16[640,640]{1,0:T(8,128)(2,1)}, u32[]{:S(2)}, u32[]{:S(2)}) %collective-permute-start.8) | collective-permute-done | bytes 819232 | tf_op jit(solution)/shard_map/ppermute | solution.py:300
  101.1 18.4 %collective-permute-done.9 = bf16[640,640]{1,0:T(8,128)(2,1)} collective-permute-done((bf16[640,640]{1,0:T(8,128)(2,1)}, bf16[640,640]{1,0:T(8,128)(2,1)}, u32[]{:S(2)}, u32[]{:S(2)}) %collective-permute-start.9) | collective-permute-done | bytes 819232 | tf_op jit(solution)/shard_map/ppermute | solution.py:301
  119.4 2.2 collective-permute-start.12
  123.6 1.5 collective-permute-start.18
  125.1 2.7 collective-permute-start.16
  127.8 4.9 collective-permute-start.13
  132.7 2.2 collective-permute-start.14
  134.9 2.1 collective-permute-start.15
  137.0 5.8 collective-permute-done.12
  142.8 4.2 collective-permute-start.17
  147.0 14.2 %collective-permute-done.13 = bf16[640,640]{1,0:T(8,128)(2,1)} collective-permute-done((bf16[640,640]{1,0:T(8,128)(2,1)}, bf16[640,640]{1,0:T(8,128)(2,1)}, u32[]{:S(2)}, u32[]{:S(2)}) %collective-permute-start.13) | collective-permute-done | bytes 819232 | tf_op jit(solution)/shard_map/ppermute | solution.py:307
  161.2 2.3 collective-permute-start.19
  163.6 2.0 collective-permute-start.20
  167.1 38.0 %conditional.9 = (bf16[4,64,1280]{2,1,0:T(8,128)(2,1)}, bf16[4,8,8,16]{3,2,1,0:T(8,128)(2,1)S(1)}) conditional(s32[]{:T(128)} %convert_element_type.100, () %tuple.115, (bf16[64,1280]{1,0:T(8,128)(2,1)S(1)}, f32[8,8,16]{2,1,0:T(8,128)S(1)}) %tuple.181), branch_computations={%region_19.20_spmd, %region_20.22_spmd} | conditional | flops 1024 | bytes 835600 | solution.py:316
  167.1 14.2 %all-gather = bf16[256,1280]{1,0:T(8,128)(2,1)} all-gather(bf16[64,1280]{1,0:T(8,128)(2,1)S(1)} %get-tuple-element.1091), channel_id=2, replica_groups=mesh['s'=16,'y'=4,'c'=2,'z'=4] {'z'}, dimensions={0}, use_global_device_ids=true | all-gather | bytes 819200 | tf_op jit(solution)/shard_map/cond/branch_1_fun/all_gather | solution.py:256
  181.3 13.6 %psum.12 = bf16[8,8,16]{2,1,0:T(8,128)(2,1)S(1)} all-reduce(f32[8,8,16]{2,1,0:T(8,128)S(1)} %get-tuple-element.1092), channel_id=1, replica_groups=mesh['s'=16,'y'=4,'c'=2,'z'=4] {'y'}, use_global_device_ids=true, to_apply=%region_21.21 | all-reduce | flops 1024 | bytes 6144 | tf_op jit(solution)/shard_map/cond/branch_1_fun/psum | solution.py:255
  194.9 10.2 %all-gather.1 = bf16[32,8,16]{2,1,0:T(8,128)(2,1)S(1)} all-gather(bf16[8,8,16]{2,1,0:T(8,128)(2,1)S(1)} %psum.12), channel_id=3, replica_groups=mesh['s'=16,'y'=4,'c'=2,'z'=4] {'z'}, dimensions={0}, use_global_device_ids=true | all-gather | bytes 10240 | tf_op jit(solution)/shard_map/cond/branch_1_fun/all_gather | solution.py:256
  205.1 1.6 slice_bitcast_fusion.6
  206.7 370.7 %while.27 = (s32[]{:T(128)}, bf16[32,1408]{1,0:T(8,128)(2,1)}, bf16[2,32,1408]{2,1,0:T(8,128)(2,1)}, bf16[2,32,64]{2,1,0:T(8,128)(2,1)S(1)}, bf16[2,32,1280]{2,1...) while((s32[]{:T(128)}, bf16[32,1408]{1,0:T(8,128)(2,1)}, ...), condition=%wide.region_17.18_spmd, body=%wide.region_8.17_spmd.sunk | while | flops 419430432 | bytes 14820548 | solution.py:373
  211.2 311.3 %conditional.14 = (bf16[32,1408]{1,0:T(8,128)(2,1)}) conditional(s32[]{:T(128)} %clamp.23, bf16[32,1408]{1,0:T(8,128)(2,1)} %get-tuple-element.1641, bf16[32,1408]{1,0:T(8,128)(2,1)} %get-tuple-element.1641, bf16[32,1408]{1,0:T(8,128)(2,1)} %get-tuple-element.1641, (s32[]{:T(128)}, ...), branch_computations={%region_13.13_spmd, %region_14.14_spmd, %region_15.15_spmd, %regio... | conditional | flops 3 | bytes 540720 | solution.py:360
  211.3 1.3 collective-permute-start
  212.6 309.4 %collective-permute-done = bf16[32,1408]{1,0:T(8,128)(2,1)S(1)} collective-permute-done((bf16[32,1408]{1,0:T(8,128)(2,1)}, bf16[32,1408]{1,0:T(8,128)(2,1)S(1)}, u32[]{:S(2)}, u32[]{:S(2)}) %collective-permute-start) | collective-permute-done | bytes 90144 | tf_op jit(solution)/shard_map/while/body/eval_jaxpr/cond/branch_1_fun/ppermute | solution.py:364
  522.6 17.1 %conditional.13 = ((bf16[2,32,1408]{2,1,0:T(8,128)(2,1)}, bf16[2,32,64]{2,1,0:T(8,128)(2,1)S(1)}, bf16[2,32,1280]{2,1,0:T(8,128)(2,1)}, bf16[2,32,128]{2,1,0:T(8,128)(2,1)S(1)}, bf16[32,1408]{1,0:T(8,128)(2,1)})) conditional(s32[]{:T(128)} %convert_element_type.126, (bf16[2,32,1408]{2,1,0:T(8,128)(2,1)}, bf16[2,32,64]{2,1,0:T(8,128)(2,1)S(1)}, ...), branch_computations={%region_9.9_spmd, %region_10.12_spmd} | conditional | flops 419430400 | bytes 14278758 | solution.py:354
  522.6 9.4 %conditional = (bf16[4,32,1408]{2,1,0:T(8,128)(2,1)S(1)}) conditional(s32[]{:T(128)} %convert_element_type.77, bf16[32,1408]{1,0:T(8,128)(2,1)} %get-tuple-element.1016, () %tuple.83), branch_computations={%region_11.10_spmd, %region_12.11_spmd} | conditional | bytes 1171464 | solution.py:337
  523.5 8.4 %all_to_all.22 = bf16[4,32,1408]{2,1,0:T(8,128)(2,1)S(1)} all-to-all(bf16[4,32,1408]{2,1,0:T(8,128)(2,1)S(1)} %broadcast_in_dim.143), channel_id=1, replica_groups=mesh['s'=16,'y'=4,'c'=2,'z'=4] {'y'}, dimensions={0} | all-to-all | bytes 720896 | tf_op jit(solution)/shard_map/while/body/eval_jaxpr/cond/branch_1_fun/cond/branch_0_fun/all_to_all | solution.py:49
  532.0 7.7 %stage.1 = (bf16[32,1408]{1,0:T(8,128)(2,1)}, bf16[2,32,1408]{2,1,0:T(8,128)(2,1)}, bf16[2,32,64]{2,1,0:T(8,128)(2,1)S(1)}, bf16[2,32,1280]{2,1,0:T(8,128)(2,1)}, bf16[2,32,128]{2,1,0:T(8,128)(2,1)S(1)}) custom-call(s32[4]{0:T(128)S(1)} %pad_add_fusion.place_ref, ...), custom_call_target="tpu_custom_call", output_to_operand_aliasing={{1}: (24, {}), {2}: (25, {}), {3}: (26, {}), {4}: (27, {})} | custom-call | flops 419430400 | bytes 13107200 | tf_op jit(solution)/shard_map/while/body/eval_jaxpr/cond/branch_1_fun/stage/pallas_call | solution.py:161
  540.0 20.2 %conditional.14 = (bf16[32,1408]{1,0:T(8,128)(2,1)}) conditional(s32[]{:T(128)} %clamp.23, bf16[32,1408]{1,0:T(8,128)(2,1)} %get-tuple-element.1641, bf16[32,1408]{1,0:T(8,128)(2,1)} %get-tuple-element.1641, bf16[32,1408]{1,0:T(8,128)(2,1)} %get-tuple-element.1641, (s32[]{:T(128)}, ...), branch_computations={%region_13.13_spmd, %region_14.14_spmd, %region_15.15_spmd, %regio... | conditional | flops 3 | bytes 540720 | solution.py:360
  540.0 1.3 collective-permute-start
  541.3 18.3 %collective-permute-done = bf16[32,1408]{1,0:T(8,128)(2,1)S(1)} collective-permute-done((bf16[32,1408]{1,0:T(8,128)(2,1)}, bf16[32,1408]{1,0:T(8,128)(2,1)S(1)}, u32[]{:S(2)}, u32[]{:S(2)}) %collective-permute-start) | collective-permute-done | bytes 90144 | tf_op jit(solution)/shard_map/while/body/eval_jaxpr/cond/branch_1_fun/ppermute | solution.py:364
  560.2 17.1 %conditional.13 = ((bf16[2,32,1408]{2,1,0:T(8,128)(2,1)}, bf16[2,32,64]{2,1,0:T(8,128)(2,1)S(1)}, bf16[2,32,1280]{2,1,0:T(8,128)(2,1)}, bf16[2,32,128]{2,1,0:T(8,128)(2,1)S(1)}, bf16[32,1408]{1,0:T(8,128)(2,1)})) conditional(s32[]{:T(128)} %convert_element_type.126, (bf16[2,32,1408]{2,1,0:T(8,128)(2,1)}, bf16[2,32,64]{2,1,0:T(8,128)(2,1)S(1)}, ...), branch_computations={%region_9.9_spmd, %region_10.12_spmd} | conditional | flops 419430400 | bytes 14278758 | solution.py:354
  560.2 9.4 %conditional = (bf16[4,32,1408]{2,1,0:T(8,128)(2,1)S(1)}) conditional(s32[]{:T(128)} %convert_element_type.77, bf16[32,1408]{1,0:T(8,128)(2,1)} %get-tuple-element.1016, () %tuple.83), branch_computations={%region_11.10_spmd, %region_12.11_spmd} | conditional | bytes 1171464 | solution.py:337
  561.1 8.4 %all_to_all.22 = bf16[4,32,1408]{2,1,0:T(8,128)(2,1)S(1)} all-to-all(bf16[4,32,1408]{2,1,0:T(8,128)(2,1)S(1)} %broadcast_in_dim.143), channel_id=1, replica_groups=mesh['s'=16,'y'=4,'c'=2,'z'=4] {'y'}, dimensions={0} | all-to-all | bytes 720896 | tf_op jit(solution)/shard_map/while/body/eval_jaxpr/cond/branch_1_fun/cond/branch_0_fun/all_to_all | solution.py:49
  569.6 7.7 %stage.1 = (bf16[32,1408]{1,0:T(8,128)(2,1)}, bf16[2,32,1408]{2,1,0:T(8,128)(2,1)}, bf16[2,32,64]{2,1,0:T(8,128)(2,1)S(1)}, bf16[2,32,1280]{2,1,0:T(8,128)(2,1)}, bf16[2,32,128]{2,1,0:T(8,128)(2,1)S(1)}) custom-call(s32[4]{0:T(128)S(1)} %pad_add_fusion.place_ref, ...), custom_call_target="tpu_custom_call", output_to_operand_aliasing={{1}: (24, {}), {2}: (25, {}), {3}: (26, {}), {4}: (27, {})} | custom-call | flops 419430400 | bytes 13107200 | tf_op jit(solution)/shard_map/while/body/eval_jaxpr/cond/branch_1_fun/stage/pallas_call | solution.py:161
  578.4 19.1 %all-gather.4 = bf16[256,1408]{1,0:T(8,128)(2,1)S(1)} all-gather(bf16[64,1408]{1,0:T(8,128)(2,1)S(1)} %fusion.17), channel_id=6, replica_groups=mesh['s'=16,'y'=4,'c'=2,'z'=4] {'z'}, dimensions={0}, use_global_device_ids=true | all-gather | bytes 901120 | tf_op jit(solution)/shard_map/all_gather | solution.py:398
  597.5 1.1 fusion.13
  598.7 37.4 %collective-permute-start.23 = (f32[8,16,640]{2,1,0:T(8,128)S(1)}, f32[8,16,640]{2,1,0:T(8,128)}, u32[]{:S(2)}, u32[]{:S(2)}) collective-permute-start(f32[8,16,640]{2,1,0:T(8,128)S(1)} %slice_select_fusion), channel_id=1, source_target_pairs={{0,4},{4,0},{1,5},{5,1},{2,6},{6,2},{3,7},{7,3},{8,12},{12,8},{9,1... | collective-permute-start | bytes 983048 | tf_op jit(solution)/shard_map/ppermute | solution.py:44
  637.2 3.3 all-to-all-start.4
  640.5 1.4 fusion.14
  641.9 3.1 all-to-all-done.4
  645.1 1.0 subtract_convert_fusion
  646.1 3.1 collective-permute-start.21
  649.2 1.9 collective-permute-start.22
  651.9 1.0 select_add_fusion
  652.9 1.0 select_reduce_fusion
  654.0 1.0 select_reduce_fusion.1
  (142 shorter events, 13.9 us)
Async XLA Ops:
  0.6 7.0 %copy-start = (bf16[1,8,16,5120]{3,2,1,0:T(8,128)(2,1)S(1)}, bf16[1,8,16,5120]{3,2,1,0:T(8,128)(2,1)}, u32[]{:S(2)}) copy-start(bf16[1,8,16,5120]{3,2,1,0:T(8,128)(2,1)} %param.31) | copy-start | bytes 3932164
  0.6 4.6 copy-start.5
  1.9 20.5 %collective-permute-start.3 = (bf16[64,1280]{1,0:T(8,128)(2,1)S(1)}, bf16[64,1280]{1,0:T(8,128)(2,1)S(1)}, u32[]{:S(2)}, u32[]{:S(2)}) collective-permute-start(bf16[64,1280]{1,0:T(8,128)(2,1)S(1)} %dynamic-slice_bitcast_fusion.3), channel_id=1, source_target_pairs={{480,448},{448,416},{416,384},{384,352},{352,320},{320,288},{288,2... | collective-permute-start | bytes 491528 | tf_op jit(solution)/shard_map/ppermute | solution.py:219
  5.2 2.2 copy-start.11
  5.2 2.2 copy-start.12
  7.6 0.7 copy-start.13
  8.3 14.1 %copy-start.9 = (f32[1,640]{1,0:T(1,128)S(1)}, f32[1,640]{1,0:T(1,128)}, u32[]{:S(2)}) copy-start(f32[1,640]{1,0:T(1,128)} %param.29) | copy-start | bytes 7684
  8.3 20.8 %copy-start.3 = (bf16[8,8,5120]{2,1,0:T(8,128)(2,1)S(1)}, bf16[8,8,5120]{2,1,0:T(8,128)(2,1)}, u32[]{:S(2)}) copy-start(bf16[8,8,5120]{2,1,0:T(8,128)(2,1)} %dynamic-slice_bitcast_fusion.2) | copy-start | bytes 1966084
  8.3 21.2 %copy-start.8 = (bf16[1,8,640,16]{2,3,1,0:T(8,128)(2,1)S(1)}, bf16[1,8,640,16]{2,3,1,0:T(8,128)(2,1)}, u32[]{:S(2)}) copy-start(bf16[1,8,640,16]{2,3,1,0:T(8,128)(2,1)} %param.30) | copy-start | bytes 491524
  22.4 29.7 %collective-permute-start.7 = (f32[1,640]{1,0:T(1,128)S(1)}, f32[1,640]{1,0:T(1,128)S(1)}, u32[]{:S(2)}, u32[]{:S(2)}) collective-permute-start(f32[1,640]{1,0:T(1,128)S(1)} %copy-done.9), channel_id=1, source_target_pairs={{0,4},{4,0},{1,5},{5,1},{2,6},{6,2},{3,7},{7,3},{8,12},{12,8},{9,1... | collective-permute-start | bytes 7688 | tf_op jit(solution)/shard_map/ppermute | solution.py:31
  29.5 23.4 %collective-permute-start.6 = (bf16[8,640,16]{1,2,0:T(8,128)(2,1)S(1)}, bf16[8,640,16]{1,2,0:T(8,128)(2,1)}, u32[]{:S(2)}, u32[]{:S(2)}) collective-permute-start(bf16[8,640,16]{1,2,0:T(8,128)(2,1)S(1)} %bitcast.114), channel_id=1, source_target_pairs={{0,4},{4,0},{1,5},{5,1},{2,6},{6,2},{3,7},{7,3},{8,12},{12,8},{9,1... | collective-permute-start | bytes 491528 | tf_op jit(solution)/shard_map/ppermute | solution.py:31
  31.5 24.2 %collective-permute-start.4 = (bf16[640,640]{1,0:T(8,128)(2,1)}, bf16[640,640]{1,0:T(8,128)(2,1)}, u32[]{:S(2)}, u32[]{:S(2)}) collective-permute-start(bf16[640,640]{1,0:T(8,128)(2,1)} %get-tuple-element.1682), channel_id=1, source_target_pairs={{0,1},{1,2},{2,3},{3,0},{32,33},{33,34},{34,35},{35,32},{64,65},{6... | collective-permute-start | bytes 2457608 | tf_op jit(solution)/shard_map/ppermute | solution.py:231
  33.4 39.9 %collective-permute-start.5 = (bf16[640,640]{1,0:T(8,128)(2,1)}, bf16[640,640]{1,0:T(8,128)(2,1)}, u32[]{:S(2)}, u32[]{:S(2)}) collective-permute-start(bf16[640,640]{1,0:T(8,128)(2,1)} %get-tuple-element.1683), channel_id=1, source_target_pairs={{0,3},{1,0},{2,1},{3,2},{32,35},{33,32},{34,33},{35,34},{64,67},{6... | collective-permute-start | bytes 2457608 | tf_op jit(solution)/shard_map/ppermute | solution.py:232
  55.6 111.5 %copy-start.6 = (f32[8,8,16]{2,1,0:T(8,128)}, f32[8,8,16]{2,1,0:T(8,128)S(1)}, u32[]{:S(2)}) copy-start(f32[8,8,16]{2,1,0:T(8,128)S(1)} %fusion.18) | copy-start | bytes 12292
  73.4 11.4 %collective-permute-start.10 = (bf16[640,640]{1,0:T(8,128)(2,1)}, bf16[640,640]{1,0:T(8,128)(2,1)}, u32[]{:S(2)}, u32[]{:S(2)}) collective-permute-start(bf16[640,640]{1,0:T(8,128)(2,1)} %collective-permute-done.4), channel_id=1, source_target_pairs={{0,4},{4,0},{32,36},{36,32},{64,68},{68,64},{96,100},{100,96},{128... | collective-permute-start | bytes 2457608 | tf_op jit(solution)/shard_map/ppermute | solution.py:294
  75.8 9.1 %collective-permute-start.11 = (bf16[640,640]{1,0:T(8,128)(2,1)}, bf16[640,640]{1,0:T(8,128)(2,1)}, u32[]{:S(2)}, u32[]{:S(2)}) collective-permute-start(bf16[640,640]{1,0:T(8,128)(2,1)} %collective-permute-done.5), channel_id=1, source_target_pairs={{0,4},{4,0},{32,36},{36,32},{64,68},{68,64},{96,100},{100,96},{128... | collective-permute-start | bytes 2457608 | tf_op jit(solution)/shard_map/ppermute | solution.py:294
  77.7 23.4 %collective-permute-start.8 = (bf16[640,640]{1,0:T(8,128)(2,1)}, bf16[640,640]{1,0:T(8,128)(2,1)}, u32[]{:S(2)}, u32[]{:S(2)}) collective-permute-start(bf16[640,640]{1,0:T(8,128)(2,1)} %collective-permute-done.4), channel_id=1, source_target_pairs={{0,1},{1,2},{2,3},{3,0},{32,33},{33,34},{34,35},{35,32},{64,65},{6... | collective-permute-start | bytes 2457608 | tf_op jit(solution)/shard_map/ppermute | solution.py:300
  79.6 39.8 %collective-permute-start.9 = (bf16[640,640]{1,0:T(8,128)(2,1)}, bf16[640,640]{1,0:T(8,128)(2,1)}, u32[]{:S(2)}, u32[]{:S(2)}) collective-permute-start(bf16[640,640]{1,0:T(8,128)(2,1)} %collective-permute-done.5), channel_id=1, source_target_pairs={{0,3},{1,0},{2,1},{3,2},{32,35},{33,32},{34,33},{35,34},{64,67},{6... | collective-permute-start | bytes 2457608 | tf_op jit(solution)/shard_map/ppermute | solution.py:301
  119.4 23.4 %collective-permute-start.12 = (bf16[640,640]{1,0:T(8,128)(2,1)}, bf16[640,640]{1,0:T(8,128)(2,1)}, u32[]{:S(2)}, u32[]{:S(2)}) collective-permute-start(bf16[640,640]{1,0:T(8,128)(2,1)} %collective-permute-done.8), channel_id=1, source_target_pairs={{0,1},{1,2},{2,3},{3,0},{32,33},{33,34},{34,35},{35,32},{64,65},{6... | collective-permute-start | bytes 2457608 | tf_op jit(solution)/shard_map/ppermute | solution.py:306
  123.6 43.5 %copy-start.4 = (bf16[64,1280]{1,0:T(8,128)(2,1)S(1)}, bf16[64,1280]{1,0:T(8,128)(2,1)}, u32[]{:S(2)}) copy-start(bf16[64,1280]{1,0:T(8,128)(2,1)} %multiply_convert_fusion) | copy-start | bytes 491524
  123.6 11.3 %collective-permute-start.18 = (bf16[2,32,1408]{2,1,0:T(8,128)(2,1)}, bf16[2,32,1408]{2,1,0:T(8,128)(2,1)}, u32[]{:S(2)}, u32[]{:S(2)}) collective-permute-start(bf16[2,32,1408]{2,1,0:T(8,128)(2,1)} %get-tuple-element.1666), channel_id=1, source_target_pairs={{480,448},{481,449},{482,450},{483,451},{484,452},{485,453},{486,4... | collective-permute-start | bytes 540680 | tf_op jit(solution)/shard_map/ppermute | solution.py:299
  125.1 36.1 %collective-permute-start.16 = (bf16[640,640]{1,0:T(8,128)(2,1)}, bf16[640,640]{1,0:T(8,128)(2,1)}, u32[]{:S(2)}, u32[]{:S(2)}) collective-permute-start(bf16[640,640]{1,0:T(8,128)(2,1)} %collective-permute-done.8), channel_id=1, source_target_pairs={{0,4},{4,0},{32,36},{36,32},{64,68},{68,64},{96,100},{100,96},{128... | collective-permute-start | bytes 2457608 | tf_op jit(solution)/shard_map/ppermute | solution.py:294
  127.8 33.4 %collective-permute-start.13 = (bf16[640,640]{1,0:T(8,128)(2,1)}, bf16[640,640]{1,0:T(8,128)(2,1)}, u32[]{:S(2)}, u32[]{:S(2)}) collective-permute-start(bf16[640,640]{1,0:T(8,128)(2,1)} %collective-permute-done.9), channel_id=1, source_target_pairs={{0,3},{1,0},{2,1},{3,2},{32,35},{33,32},{34,33},{35,34},{64,67},{6... | collective-permute-start | bytes 2457608 | tf_op jit(solution)/shard_map/ppermute | solution.py:307
  132.7 28.5 %collective-permute-start.14 = (bf16[640,640]{1,0:T(8,128)(2,1)}, bf16[640,640]{1,0:T(8,128)(2,1)}, u32[]{:S(2)}, u32[]{:S(2)}) collective-permute-start(bf16[640,640]{1,0:T(8,128)(2,1)} %get-tuple-element.1682), channel_id=1, source_target_pairs={{0,4},{4,0},{32,36},{36,32},{64,68},{68,64},{96,100},{100,96},{128... | collective-permute-start | bytes 2457608 | tf_op jit(solution)/shard_map/ppermute | solution.py:294
  134.9 26.3 %collective-permute-start.15 = (bf16[640,640]{1,0:T(8,128)(2,1)}, bf16[640,640]{1,0:T(8,128)(2,1)}, u32[]{:S(2)}, u32[]{:S(2)}) collective-permute-start(bf16[640,640]{1,0:T(8,128)(2,1)} %get-tuple-element.1683), channel_id=1, source_target_pairs={{0,4},{4,0},{32,36},{36,32},{64,68},{68,64},{96,100},{100,96},{128... | collective-permute-start | bytes 2457608 | tf_op jit(solution)/shard_map/ppermute | solution.py:294
  142.8 18.4 %collective-permute-start.17 = (bf16[640,640]{1,0:T(8,128)(2,1)}, bf16[640,640]{1,0:T(8,128)(2,1)}, u32[]{:S(2)}, u32[]{:S(2)}) collective-permute-start(bf16[640,640]{1,0:T(8,128)(2,1)} %collective-permute-done.9), channel_id=1, source_target_pairs={{0,4},{4,0},{32,36},{36,32},{64,68},{68,64},{96,100},{100,96},{128... | collective-permute-start | bytes 2457608 | tf_op jit(solution)/shard_map/ppermute | solution.py:294
  161.2 45.4 %collective-permute-start.19 = (bf16[640,640]{1,0:T(8,128)(2,1)}, bf16[640,640]{1,0:T(8,128)(2,1)}, u32[]{:S(2)}, u32[]{:S(2)}) collective-permute-start(bf16[640,640]{1,0:T(8,128)(2,1)} %collective-permute-done.12), channel_id=1, source_target_pairs={{0,4},{4,0},{32,36},{36,32},{64,68},{68,64},{96,100},{100,96},{128... | collective-permute-start | bytes 2457608 | tf_op jit(solution)/shard_map/ppermute | solution.py:294
  163.6 43.1 %collective-permute-start.20 = (bf16[640,640]{1,0:T(8,128)(2,1)}, bf16[640,640]{1,0:T(8,128)(2,1)}, u32[]{:S(2)}, u32[]{:S(2)}) collective-permute-start(bf16[640,640]{1,0:T(8,128)(2,1)} %collective-permute-done.13), channel_id=1, source_target_pairs={{0,4},{4,0},{32,36},{36,32},{64,68},{68,64},{96,100},{100,96},{128... | collective-permute-start | bytes 2457608 | tf_op jit(solution)/shard_map/ppermute | solution.py:294
  205.1 1.6 copy-start.7
  211.3 310.7 %collective-permute-start = (bf16[32,1408]{1,0:T(8,128)(2,1)}, bf16[32,1408]{1,0:T(8,128)(2,1)S(1)}, u32[]{:S(2)}, u32[]{:S(2)}) collective-permute-start(bf16[32,1408]{1,0:T(8,128)(2,1)} %param.9), channel_id=1, source_target_pairs={{480,448},{416,384},{352,320},{288,256},{224,192},{160,128},{96,64... | collective-permute-start | bytes 270344 | tf_op jit(solution)/shard_map/while/body/eval_jaxpr/cond/branch_1_fun/ppermute | solution.py:364
  540.0 19.6 %collective-permute-start = (bf16[32,1408]{1,0:T(8,128)(2,1)}, bf16[32,1408]{1,0:T(8,128)(2,1)S(1)}, u32[]{:S(2)}, u32[]{:S(2)}) collective-permute-start(bf16[32,1408]{1,0:T(8,128)(2,1)} %param.9), channel_id=1, source_target_pairs={{480,448},{416,384},{352,320},{288,256},{224,192},{160,128},{96,64... | collective-permute-start | bytes 270344 | tf_op jit(solution)/shard_map/while/body/eval_jaxpr/cond/branch_1_fun/ppermute | solution.py:364
  598.7 53.2 %collective-permute-start.23 = (f32[8,16,640]{2,1,0:T(8,128)S(1)}, f32[8,16,640]{2,1,0:T(8,128)}, u32[]{:S(2)}, u32[]{:S(2)}) collective-permute-start(f32[8,16,640]{2,1,0:T(8,128)S(1)} %slice_select_fusion), channel_id=1, source_target_pairs={{0,4},{4,0},{1,5},{5,1},{2,6},{6,2},{3,7},{7,3},{8,12},{12,8},{9,1... | collective-permute-start | bytes 983048 | tf_op jit(solution)/shard_map/ppermute | solution.py:44
  637.2 7.7 %all-to-all-start.4 = ((bf16[4,2,32,128]{3,2,1,0:T(8,128)(2,1)}), bf16[4,2,32,128]{3,2,1,0:T(8,128)(2,1)S(1)}, u32[]{:S(2)}, u32[]{:S(2)}) async-start(bf16[4,2,32,128]{3,2,1,0:T(8,128)(2,1)} %broadcast_in_dim.170), calls=%async_computation.4 | async-start | bytes 131072 | tf_op jit(solution)/shard_map/all_to_all | solution.py:49
  646.1 5.0 collective-permute-start.21
  649.2 4.7 collective-permute-start.22

commit v14 on v13

--- a/solution.py
+++ b/solution.py
@@ -70,9 +70,9 @@
 
 def stage_kernel(place_ref, parts_ref, gain_ref, before_any, up_any, down_any, inv_any, x_any, *refs, group):
     weights, refs = refs[:16], refs[16 + 4 :]
-    box_ref, boxes_any, low_any, grad_any, tail_any = refs[:5]
+    box_any, boxes_any, low_any, grad_any, tail_any = refs[:5]
     before_ref, up_ref, down_ref, inv_ref, x_ref, full, weight, low_ref, grad_ref, tail_ref = refs[5:15]
-    in_sems, w_sems, out_sems = refs[15:]
+    box_ref, in_sems, w_sems, out_sems = refs[15:]
     m, ypos, core, zpos = place_ref[0], place_ref[1], place_ref[2], place_ref[3]
     width = x_ref.shape[1]
     width_all = full.shape[1]
@@ -143,12 +143,14 @@
     box_ref[:, :width] = sent
     box_ref[:, width:] = tail
     tail_ref[...] = tail
+    out_copy = started(box_ref, box_any, out_sems.at[4])
     box_copy = started(box_ref, boxes_any.at[m], out_sems.at[2])
     tail_copy = started(tail_ref, tail_any.at[m], out_sems.at[3])
     grad_copy.wait()
     low_copy.wait()
     box_copy.wait()
     tail_copy.wait()
+    out_copy.wait()
 
 
 def run_stage(place, parts, before, up, down, gain, inv, x, weights, kept):
@@ -162,7 +164,7 @@
         functools.partial(stage_kernel, group=cols // 16),
         in_specs=[pl.BlockSpec(memory_space=pltpu.SMEM), vmem, vmem]
         + [any_space] * (len(inputs) + len(kept) - 3),
-        out_specs=[vmem] + [any_space] * len(kept),
+        out_specs=[any_space] * (1 + len(kept)),
         scratch_shapes=[
             pltpu.VMEM((4, rows, width), bf16),
             pltpu.VMEM((cols, width_all), bf16),
@@ -174,9 +176,10 @@
             pltpu.VMEM((rows, cols), bf16),
             pltpu.VMEM((rows, width), bf16),
             pltpu.VMEM((rows, TAIL), bf16),
+            pltpu.VMEM((rows, width + TAIL), bf16),
             pltpu.SemaphoreType.DMA((5,)),
             pltpu.SemaphoreType.DMA((8, 2)),
-            pltpu.SemaphoreType.DMA((4,)),
+            pltpu.SemaphoreType.DMA((5,)),
         ],
         out_shape=[jax.ShapeDtypeStruct((rows, width + TAIL), bf16)]
         + [jax.ShapeDtypeStruct(k.shape, k.dtype) for k in kept],

time: 657 us -> 646 us (0.983)
  waiting for transfers between devices: 414 us -> 406 us
    ppermute x2, waiting for transfers between devices: 328 us -> 319 us  [step(): lax.ppermute(box, 's', ODD)]
where the time goes in v14:
time: 646 us; the launch traced here: 645 us
  waiting for transfers between devices  406 us (63%)
  starting transfers between devices  102 us (16%)
  blocking collectives  84.9 us (13%)
  local copies, waits for them, and re-layouts  18 us (3%)
  Pallas kernels  14.2 us (2%)
  other arithmetic  9.36 us (1%)
    ppermute x2, waiting for transfers between devices, step(): lax.ppermute(box, 's', ODD)  319 us
    ppermute x2, starting transfers between devices, half_sum(): return mine + lax.ppermute(theirs, 'c', SWAP)  41.1 us
    all_to_all x3, blocking collectives, spread(): return lax.all_to_all(sent, 'y', 0, 0)  30.4 us
    all_gather x2, blocking collectives, extra(): return (lax.all_gather(h_y, 'z'), lax.all_gather(low_in, 'z'))  24.4 us
    ppermute x8, starting transfers between devices, swapped(): return lax.ppermute(value, ('s', 'c'), PAIRS)  19.8 us
    ppermute x1, waiting for transfers between devices, local(): left_2 = lax.ppermute(left_1, ('s', 'z'), LEFT)  18.4 us
    ppermute x1, waiting for transfers between devices, local(): left_1 = lax.ppermute(second, ('s', 'z'), LEFT)  17.7 us
    all_gather x1, blocking collectives, local(): both = lax.all_gather(both, 'z').reshape(4, micro, toks, width + TAIL)  16.5 us
  transfers between devices with their start and end apart: 24, of which 9 were waited for; matrix products, arithmetic and copies ran while one was open for 4% of the time, Pallas kernels for 0%

profile of v14, /device:TPU:1, one launch (start us, length us, event | category | flops | bytes accessed | tf_op | source)
XLA Modules:
  0.0 644.8 jit_solution(14494035799451538512)
XLA Ops:
  0.7 1.2 dynamic-slice_bitcast_fusion.3
  1.9 1.3 collective-permute-start.3
  3.2 2.0 dynamic-slice_bitcast_fusion.2
  5.2 2.2 copy.32
  8.3 2.8 slice_bitcast_fusion.4
  11.1 11.3 %collective-permute-done.3 = bf16[64,1280]{1,0:T(8,128)(2,1)S(1)} collective-permute-done((bf16[64,1280]{1,0:T(8,128)(2,1)S(1)}, bf16[64,1280]{1,0:T(8,128)(2,1)S(1)}, u32[]{:S(2)}, u32[]{:S(2)}) %collective-permute-start.3) | collective-permute-done | bytes 163872 | tf_op jit(solution)/shard_map/ppermute | solution.py:222
  22.4 6.7 %collective-permute-start.7 = (f32[1,640]{1,0:T(1,128)S(1)}, f32[1,640]{1,0:T(1,128)S(1)}, u32[]{:S(2)}, u32[]{:S(2)}) collective-permute-start(f32[1,640]{1,0:T(1,128)S(1)} %copy-done.9), channel_id=1, source_target_pairs={{0,4},{4,0},{1,5},{5,1},{2,6},{6,2},{3,7},{7,3},{8,12},{12,8},{9,1... | collective-permute-start | bytes 7688 | tf_op jit(solution)/shard_map/ppermute | solution.py:31
  29.5 1.9 collective-permute-start.6
  31.5 1.9 collective-permute-start.4
  33.4 5.2 collective-permute-start.5
  38.6 13.6 %conditional.7 = (bf16[4,2,32,1280]{3,2,1,0:T(8,128)(2,1)}) conditional(s32[]{:T(128)} %convert_element_type.91, bf16[64,1280]{1,0:T(8,128)(2,1)S(1)} %collective-permute-done.3, () %tuple.108), branch_computations={%region_0.0_spmd, %region_1.0_spmd} | conditional | bytes 2129928 | solution.py:240
  38.6 13.5 %all_to_all.21 = bf16[4,64,1280]{2,1,0:T(8,128)(2,1)} all-to-all(bf16[4,64,1280]{2,1,0:T(8,128)(2,1)S(1)} %broadcast_in_dim.99), channel_id=1, replica_groups=mesh['s'=16,'y'=4,'c'=2,'z'=4] {'y'}, dimensions={0} | all-to-all | bytes 1310720 | tf_op jit(solution)/shard_map/cond/branch_0_fun/all_to_all | solution.py:49
  53.0 1.0 broadcast_select_fusion.4
  54.5 1.1 fusion.18
  55.6 17.7 %collective-permute-done.5 = bf16[640,640]{1,0:T(8,128)(2,1)} collective-permute-done((bf16[640,640]{1,0:T(8,128)(2,1)}, bf16[640,640]{1,0:T(8,128)(2,1)}, u32[]{:S(2)}, u32[]{:S(2)}) %collective-permute-start.5) | collective-permute-done | bytes 819232 | tf_op jit(solution)/shard_map/ppermute | solution.py:235
  73.4 2.4 collective-permute-start.10
  75.8 1.9 collective-permute-start.11
  77.7 1.9 collective-permute-start.8
  79.6 5.2 collective-permute-start.9
  84.8 16.3 %collective-permute-done.8 = bf16[640,640]{1,0:T(8,128)(2,1)} collective-permute-done((bf16[640,640]{1,0:T(8,128)(2,1)}, bf16[640,640]{1,0:T(8,128)(2,1)}, u32[]{:S(2)}, u32[]{:S(2)}) %collective-permute-start.8) | collective-permute-done | bytes 819232 | tf_op jit(solution)/shard_map/ppermute | solution.py:303
  101.1 18.4 %collective-permute-done.9 = bf16[640,640]{1,0:T(8,128)(2,1)} collective-permute-done((bf16[640,640]{1,0:T(8,128)(2,1)}, bf16[640,640]{1,0:T(8,128)(2,1)}, u32[]{:S(2)}, u32[]{:S(2)}) %collective-permute-start.9) | collective-permute-done | bytes 819232 | tf_op jit(solution)/shard_map/ppermute | solution.py:304
  119.4 2.2 collective-permute-start.12
  123.6 1.5 collective-permute-start.18
  125.1 2.7 collective-permute-start.16
  127.8 4.9 collective-permute-start.13
  132.7 2.2 collective-permute-start.14
  134.9 2.1 collective-permute-start.15
  137.0 5.8 collective-permute-done.12
  142.8 4.2 collective-permute-start.17
  147.0 14.2 %collective-permute-done.13 = bf16[640,640]{1,0:T(8,128)(2,1)} collective-permute-done((bf16[640,640]{1,0:T(8,128)(2,1)}, bf16[640,640]{1,0:T(8,128)(2,1)}, u32[]{:S(2)}, u32[]{:S(2)}) %collective-permute-start.13) | collective-permute-done | bytes 819232 | tf_op jit(solution)/shard_map/ppermute | solution.py:310
  161.2 2.3 collective-permute-start.19
  163.6 2.0 collective-permute-start.20
  167.1 38.0 %conditional.9 = (bf16[4,64,1280]{2,1,0:T(8,128)(2,1)}, bf16[4,8,8,16]{3,2,1,0:T(8,128)(2,1)S(1)}) conditional(s32[]{:T(128)} %convert_element_type.100, () %tuple.115, (bf16[64,1280]{1,0:T(8,128)(2,1)S(1)}, f32[8,8,16]{2,1,0:T(8,128)S(1)}) %tuple.181), branch_computations={%region_19.20_spmd, %region_20.22_spmd} | conditional | flops 1024 | bytes 835600 | solution.py:319
  167.1 14.2 %all-gather = bf16[256,1280]{1,0:T(8,128)(2,1)} all-gather(bf16[64,1280]{1,0:T(8,128)(2,1)S(1)} %get-tuple-element.1091), channel_id=2, replica_groups=mesh['s'=16,'y'=4,'c'=2,'z'=4] {'z'}, dimensions={0}, use_global_device_ids=true | all-gather | bytes 819200 | tf_op jit(solution)/shard_map/cond/branch_1_fun/all_gather | solution.py:259
  181.3 13.6 %psum.12 = bf16[8,8,16]{2,1,0:T(8,128)(2,1)S(1)} all-reduce(f32[8,8,16]{2,1,0:T(8,128)S(1)} %get-tuple-element.1092), channel_id=1, replica_groups=mesh['s'=16,'y'=4,'c'=2,'z'=4] {'y'}, use_global_device_ids=true, to_apply=%region_21.21 | all-reduce | flops 1024 | bytes 6144 | tf_op jit(solution)/shard_map/cond/branch_1_fun/psum | solution.py:258
  194.9 10.2 %all-gather.1 = bf16[32,8,16]{2,1,0:T(8,128)(2,1)S(1)} all-gather(bf16[8,8,16]{2,1,0:T(8,128)(2,1)S(1)} %psum.12), channel_id=3, replica_groups=mesh['s'=16,'y'=4,'c'=2,'z'=4] {'z'}, dimensions={0}, use_global_device_ids=true | all-gather | bytes 10240 | tf_op jit(solution)/shard_map/cond/branch_1_fun/all_gather | solution.py:259
  205.1 1.6 slice_bitcast_fusion.6
  206.7 361.4 %while.27 = (s32[]{:T(128)}, bf16[32,1408]{1,0:T(8,128)(2,1)}, bf16[2,32,1408]{2,1,0:T(8,128)(2,1)}, bf16[2,32,64]{2,1,0:T(8,128)(2,1)S(1)}, bf16[2,32,1280]{2,1...) while((s32[]{:T(128)}, bf16[32,1408]{1,0:T(8,128)(2,1)}, ...), condition=%wide.region_17.18_spmd, body=%wide.region_8.17_spmd.sunk | while | flops 419430432 | bytes 14820548 | solution.py:376
  211.2 303.1 %conditional.14 = (bf16[32,1408]{1,0:T(8,128)(2,1)}) conditional(s32[]{:T(128)} %clamp.23, bf16[32,1408]{1,0:T(8,128)(2,1)} %get-tuple-element.1641, bf16[32,1408]{1,0:T(8,128)(2,1)} %get-tuple-element.1641, bf16[32,1408]{1,0:T(8,128)(2,1)} %get-tuple-element.1641, (s32[]{:T(128)}, ...), branch_computations={%region_13.13_spmd, %region_14.14_spmd, %region_15.15_spmd, %regio... | conditional | flops 3 | bytes 540720 | solution.py:363
  211.3 1.3 collective-permute-start
  212.6 301.1 %collective-permute-done = bf16[32,1408]{1,0:T(8,128)(2,1)S(1)} collective-permute-done((bf16[32,1408]{1,0:T(8,128)(2,1)}, bf16[32,1408]{1,0:T(8,128)(2,1)S(1)}, u32[]{:S(2)}, u32[]{:S(2)}) %collective-permute-start) | collective-permute-done | bytes 90144 | tf_op jit(solution)/shard_map/while/body/eval_jaxpr/cond/branch_1_fun/ppermute | solution.py:367
  514.3 16.6 %conditional.13 = ((bf16[2,32,1408]{2,1,0:T(8,128)(2,1)}, bf16[2,32,64]{2,1,0:T(8,128)(2,1)S(1)}, bf16[2,32,1280]{2,1,0:T(8,128)(2,1)}, bf16[2,32,128]{2,1,0:T(8,128)(2,1)S(1)}, bf16[32,1408]{1,0:T(8,128)(2,1)})) conditional(s32[]{:T(128)} %convert_element_type.126, (bf16[2,32,1408]{2,1,0:T(8,128)(2,1)}, bf16[2,32,64]{2,1,0:T(8,128)(2,1)S(1)}, ...), branch_computations={%region_9.9_spmd, %region_10.12_spmd} | conditional | flops 419430400 | bytes 14278758 | solution.py:357
  514.3 9.4 %conditional = (bf16[4,32,1408]{2,1,0:T(8,128)(2,1)S(1)}) conditional(s32[]{:T(128)} %convert_element_type.77, bf16[32,1408]{1,0:T(8,128)(2,1)} %get-tuple-element.1016, () %tuple.83), branch_computations={%region_11.10_spmd, %region_12.11_spmd} | conditional | bytes 1171464 | solution.py:340
  515.2 8.4 %all_to_all.22 = bf16[4,32,1408]{2,1,0:T(8,128)(2,1)S(1)} all-to-all(bf16[4,32,1408]{2,1,0:T(8,128)(2,1)S(1)} %broadcast_in_dim.143), channel_id=1, replica_groups=mesh['s'=16,'y'=4,'c'=2,'z'=4] {'y'}, dimensions={0} | all-to-all | bytes 720896 | tf_op jit(solution)/shard_map/while/body/eval_jaxpr/cond/branch_1_fun/cond/branch_0_fun/all_to_all | solution.py:49
  523.8 7.1 %stage.1 = (bf16[32,1408]{1,0:T(8,128)(2,1)}, bf16[2,32,1408]{2,1,0:T(8,128)(2,1)}, bf16[2,32,64]{2,1,0:T(8,128)(2,1)S(1)}, bf16[2,32,1280]{2,1,0:T(8,128)(2,1)}, bf16[2,32,128]{2,1,0:T(8,128)(2,1)S(1)}) custom-call(s32[4]{0:T(128)S(1)} %pad_add_fusion.place_ref, ...), custom_call_target="tpu_custom_call", output_to_operand_aliasing={{1}: (24, {}), {2}: (25, {}), {3}: (26, {}), {4}: (27, {})} | custom-call | flops 419430400 | bytes 13107200 | tf_op jit(solution)/shard_map/while/body/eval_jaxpr/cond/branch_1_fun/stage/pallas_call | solution.py:163
  531.1 20.3 %conditional.14 = (bf16[32,1408]{1,0:T(8,128)(2,1)}) conditional(s32[]{:T(128)} %clamp.23, bf16[32,1408]{1,0:T(8,128)(2,1)} %get-tuple-element.1641, bf16[32,1408]{1,0:T(8,128)(2,1)} %get-tuple-element.1641, bf16[32,1408]{1,0:T(8,128)(2,1)} %get-tuple-element.1641, (s32[]{:T(128)}, ...), branch_computations={%region_13.13_spmd, %region_14.14_spmd, %region_15.15_spmd, %regio... | conditional | flops 3 | bytes 540720 | solution.py:363
  531.1 1.3 collective-permute-start
  532.4 18.3 %collective-permute-done = bf16[32,1408]{1,0:T(8,128)(2,1)S(1)} collective-permute-done((bf16[32,1408]{1,0:T(8,128)(2,1)}, bf16[32,1408]{1,0:T(8,128)(2,1)S(1)}, u32[]{:S(2)}, u32[]{:S(2)}) %collective-permute-start) | collective-permute-done | bytes 90144 | tf_op jit(solution)/shard_map/while/body/eval_jaxpr/cond/branch_1_fun/ppermute | solution.py:367
  551.4 16.6 %conditional.13 = ((bf16[2,32,1408]{2,1,0:T(8,128)(2,1)}, bf16[2,32,64]{2,1,0:T(8,128)(2,1)S(1)}, bf16[2,32,1280]{2,1,0:T(8,128)(2,1)}, bf16[2,32,128]{2,1,0:T(8,128)(2,1)S(1)}, bf16[32,1408]{1,0:T(8,128)(2,1)})) conditional(s32[]{:T(128)} %convert_element_type.126, (bf16[2,32,1408]{2,1,0:T(8,128)(2,1)}, bf16[2,32,64]{2,1,0:T(8,128)(2,1)S(1)}, ...), branch_computations={%region_9.9_spmd, %region_10.12_spmd} | conditional | flops 419430400 | bytes 14278758 | solution.py:357
  551.4 9.4 %conditional = (bf16[4,32,1408]{2,1,0:T(8,128)(2,1)S(1)}) conditional(s32[]{:T(128)} %convert_element_type.77, bf16[32,1408]{1,0:T(8,128)(2,1)} %get-tuple-element.1016, () %tuple.83), branch_computations={%region_11.10_spmd, %region_12.11_spmd} | conditional | bytes 1171464 | solution.py:340
  552.3 8.4 %all_to_all.22 = bf16[4,32,1408]{2,1,0:T(8,128)(2,1)S(1)} all-to-all(bf16[4,32,1408]{2,1,0:T(8,128)(2,1)S(1)} %broadcast_in_dim.143), channel_id=1, replica_groups=mesh['s'=16,'y'=4,'c'=2,'z'=4] {'y'}, dimensions={0} | all-to-all | bytes 720896 | tf_op jit(solution)/shard_map/while/body/eval_jaxpr/cond/branch_1_fun/cond/branch_0_fun/all_to_all | solution.py:49
  560.8 7.1 %stage.1 = (bf16[32,1408]{1,0:T(8,128)(2,1)}, bf16[2,32,1408]{2,1,0:T(8,128)(2,1)}, bf16[2,32,64]{2,1,0:T(8,128)(2,1)S(1)}, bf16[2,32,1280]{2,1,0:T(8,128)(2,1)}, bf16[2,32,128]{2,1,0:T(8,128)(2,1)S(1)}) custom-call(s32[4]{0:T(128)S(1)} %pad_add_fusion.place_ref, ...), custom_call_target="tpu_custom_call", output_to_operand_aliasing={{1}: (24, {}), {2}: (25, {}), {3}: (26, {}), {4}: (27, {})} | custom-call | flops 419430400 | bytes 13107200 | tf_op jit(solution)/shard_map/while/body/eval_jaxpr/cond/branch_1_fun/stage/pallas_call | solution.py:163
  569.0 16.5 %all-gather.4 = bf16[256,1408]{1,0:T(8,128)(2,1)S(1)} all-gather(bf16[64,1408]{1,0:T(8,128)(2,1)S(1)} %fusion.17), channel_id=6, replica_groups=mesh['s'=16,'y'=4,'c'=2,'z'=4] {'z'}, dimensions={0}, use_global_device_ids=true | all-gather | bytes 901120 | tf_op jit(solution)/shard_map/all_gather | solution.py:401
  585.5 1.1 fusion.13
  586.7 39.2 %collective-permute-start.23 = (f32[8,16,640]{2,1,0:T(8,128)S(1)}, f32[8,16,640]{2,1,0:T(8,128)}, u32[]{:S(2)}, u32[]{:S(2)}) collective-permute-start(f32[8,16,640]{2,1,0:T(8,128)S(1)} %slice_select_fusion), channel_id=1, source_target_pairs={{0,4},{4,0},{1,5},{5,1},{2,6},{6,2},{3,7},{7,3},{8,12},{12,8},{9,1... | collective-permute-start | bytes 983048 | tf_op jit(solution)/shard_map/ppermute | solution.py:44
  627.0 3.3 all-to-all-start.4
  630.3 1.4 fusion.14
  631.7 3.1 all-to-all-done.4
  634.9 1.0 subtract_convert_fusion
  635.9 3.1 collective-permute-start.21
  639.0 1.9 collective-permute-start.22
  641.7 1.0 select_add_fusion
  642.7 1.0 select_reduce_fusion
  643.8 1.0 select_reduce_fusion.1
  (142 shorter events, 13.9 us)
Async XLA Ops:
  0.6 7.0 %copy-start = (bf16[1,8,16,5120]{3,2,1,0:T(8,128)(2,1)S(1)}, bf16[1,8,16,5120]{3,2,1,0:T(8,128)(2,1)}, u32[]{:S(2)}) copy-start(bf16[1,8,16,5120]{3,2,1,0:T(8,128)(2,1)} %param.31) | copy-start | bytes 3932164
  0.6 4.6 copy-start.5
  1.9 20.5 %collective-permute-start.3 = (bf16[64,1280]{1,0:T(8,128)(2,1)S(1)}, bf16[64,1280]{1,0:T(8,128)(2,1)S(1)}, u32[]{:S(2)}, u32[]{:S(2)}) collective-permute-start(bf16[64,1280]{1,0:T(8,128)(2,1)S(1)} %dynamic-slice_bitcast_fusion.3), channel_id=1, source_target_pairs={{480,448},{448,416},{416,384},{384,352},{352,320},{320,288},{288,2... | collective-permute-start | bytes 491528 | tf_op jit(solution)/shard_map/ppermute | solution.py:222
  5.2 2.2 copy-start.11
  5.2 2.2 copy-start.12
  7.6 0.7 copy-start.13
  8.3 14.1 %copy-start.9 = (f32[1,640]{1,0:T(1,128)S(1)}, f32[1,640]{1,0:T(1,128)}, u32[]{:S(2)}) copy-start(f32[1,640]{1,0:T(1,128)} %param.29) | copy-start | bytes 7684
  8.3 20.8 %copy-start.3 = (bf16[8,8,5120]{2,1,0:T(8,128)(2,1)S(1)}, bf16[8,8,5120]{2,1,0:T(8,128)(2,1)}, u32[]{:S(2)}) copy-start(bf16[8,8,5120]{2,1,0:T(8,128)(2,1)} %dynamic-slice_bitcast_fusion.2) | copy-start | bytes 1966084
  8.3 21.2 %copy-start.8 = (bf16[1,8,640,16]{2,3,1,0:T(8,128)(2,1)S(1)}, bf16[1,8,640,16]{2,3,1,0:T(8,128)(2,1)}, u32[]{:S(2)}) copy-start(bf16[1,8,640,16]{2,3,1,0:T(8,128)(2,1)} %param.30) | copy-start | bytes 491524
  22.4 29.7 %collective-permute-start.7 = (f32[1,640]{1,0:T(1,128)S(1)}, f32[1,640]{1,0:T(1,128)S(1)}, u32[]{:S(2)}, u32[]{:S(2)}) collective-permute-start(f32[1,640]{1,0:T(1,128)S(1)} %copy-done.9), channel_id=1, source_target_pairs={{0,4},{4,0},{1,5},{5,1},{2,6},{6,2},{3,7},{7,3},{8,12},{12,8},{9,1... | collective-permute-start | bytes 7688 | tf_op jit(solution)/shard_map/ppermute | solution.py:31
  29.5 23.4 %collective-permute-start.6 = (bf16[8,640,16]{1,2,0:T(8,128)(2,1)S(1)}, bf16[8,640,16]{1,2,0:T(8,128)(2,1)}, u32[]{:S(2)}, u32[]{:S(2)}) collective-permute-start(bf16[8,640,16]{1,2,0:T(8,128)(2,1)S(1)} %bitcast.114), channel_id=1, source_target_pairs={{0,4},{4,0},{1,5},{5,1},{2,6},{6,2},{3,7},{7,3},{8,12},{12,8},{9,1... | collective-permute-start | bytes 491528 | tf_op jit(solution)/shard_map/ppermute | solution.py:31
  31.5 24.2 %collective-permute-start.4 = (bf16[640,640]{1,0:T(8,128)(2,1)}, bf16[640,640]{1,0:T(8,128)(2,1)}, u32[]{:S(2)}, u32[]{:S(2)}) collective-permute-start(bf16[640,640]{1,0:T(8,128)(2,1)} %get-tuple-element.1682), channel_id=1, source_target_pairs={{0,1},{1,2},{2,3},{3,0},{32,33},{33,34},{34,35},{35,32},{64,65},{6... | collective-permute-start | bytes 2457608 | tf_op jit(solution)/shard_map/ppermute | solution.py:234
  33.4 39.9 %collective-permute-start.5 = (bf16[640,640]{1,0:T(8,128)(2,1)}, bf16[640,640]{1,0:T(8,128)(2,1)}, u32[]{:S(2)}, u32[]{:S(2)}) collective-permute-start(bf16[640,640]{1,0:T(8,128)(2,1)} %get-tuple-element.1683), channel_id=1, source_target_pairs={{0,3},{1,0},{2,1},{3,2},{32,35},{33,32},{34,33},{35,34},{64,67},{6... | collective-permute-start | bytes 2457608 | tf_op jit(solution)/shard_map/ppermute | solution.py:235
  55.6 111.5 %copy-start.6 = (f32[8,8,16]{2,1,0:T(8,128)}, f32[8,8,16]{2,1,0:T(8,128)S(1)}, u32[]{:S(2)}) copy-start(f32[8,8,16]{2,1,0:T(8,128)S(1)} %fusion.18) | copy-start | bytes 12292
  73.4 11.4 %collective-permute-start.10 = (bf16[640,640]{1,0:T(8,128)(2,1)}, bf16[640,640]{1,0:T(8,128)(2,1)}, u32[]{:S(2)}, u32[]{:S(2)}) collective-permute-start(bf16[640,640]{1,0:T(8,128)(2,1)} %collective-permute-done.4), channel_id=1, source_target_pairs={{0,4},{4,0},{32,36},{36,32},{64,68},{68,64},{96,100},{100,96},{128... | collective-permute-start | bytes 2457608 | tf_op jit(solution)/shard_map/ppermute | solution.py:297
  75.8 9.1 %collective-permute-start.11 = (bf16[640,640]{1,0:T(8,128)(2,1)}, bf16[640,640]{1,0:T(8,128)(2,1)}, u32[]{:S(2)}, u32[]{:S(2)}) collective-permute-start(bf16[640,640]{1,0:T(8,128)(2,1)} %collective-permute-done.5), channel_id=1, source_target_pairs={{0,4},{4,0},{32,36},{36,32},{64,68},{68,64},{96,100},{100,96},{128... | collective-permute-start | bytes 2457608 | tf_op jit(solution)/shard_map/ppermute | solution.py:297
  77.7 23.4 %collective-permute-start.8 = (bf16[640,640]{1,0:T(8,128)(2,1)}, bf16[640,640]{1,0:T(8,128)(2,1)}, u32[]{:S(2)}, u32[]{:S(2)}) collective-permute-start(bf16[640,640]{1,0:T(8,128)(2,1)} %collective-permute-done.4), channel_id=1, source_target_pairs={{0,1},{1,2},{2,3},{3,0},{32,33},{33,34},{34,35},{35,32},{64,65},{6... | collective-permute-start | bytes 2457608 | tf_op jit(solution)/shard_map/ppermute | solution.py:303
  79.6 39.8 %collective-permute-start.9 = (bf16[640,640]{1,0:T(8,128)(2,1)}, bf16[640,640]{1,0:T(8,128)(2,1)}, u32[]{:S(2)}, u32[]{:S(2)}) collective-permute-start(bf16[640,640]{1,0:T(8,128)(2,1)} %collective-permute-done.5), channel_id=1, source_target_pairs={{0,3},{1,0},{2,1},{3,2},{32,35},{33,32},{34,33},{35,34},{64,67},{6... | collective-permute-start | bytes 2457608 | tf_op jit(solution)/shard_map/ppermute | solution.py:304
  119.4 23.4 %collective-permute-start.12 = (bf16[640,640]{1,0:T(8,128)(2,1)}, bf16[640,640]{1,0:T(8,128)(2,1)}, u32[]{:S(2)}, u32[]{:S(2)}) collective-permute-start(bf16[640,640]{1,0:T(8,128)(2,1)} %collective-permute-done.8), channel_id=1, source_target_pairs={{0,1},{1,2},{2,3},{3,0},{32,33},{33,34},{34,35},{35,32},{64,65},{6... | collective-permute-start | bytes 2457608 | tf_op jit(solution)/shard_map/ppermute | solution.py:309
  123.6 43.5 %copy-start.4 = (bf16[64,1280]{1,0:T(8,128)(2,1)S(1)}, bf16[64,1280]{1,0:T(8,128)(2,1)}, u32[]{:S(2)}) copy-start(bf16[64,1280]{1,0:T(8,128)(2,1)} %multiply_convert_fusion) | copy-start | bytes 491524
  123.6 11.3 %collective-permute-start.18 = (bf16[2,32,1408]{2,1,0:T(8,128)(2,1)}, bf16[2,32,1408]{2,1,0:T(8,128)(2,1)}, u32[]{:S(2)}, u32[]{:S(2)}) collective-permute-start(bf16[2,32,1408]{2,1,0:T(8,128)(2,1)} %get-tuple-element.1666), channel_id=1, source_target_pairs={{480,448},{481,449},{482,450},{483,451},{484,452},{485,453},{486,4... | collective-permute-start | bytes 540680 | tf_op jit(solution)/shard_map/ppermute | solution.py:302
  125.1 36.1 %collective-permute-start.16 = (bf16[640,640]{1,0:T(8,128)(2,1)}, bf16[640,640]{1,0:T(8,128)(2,1)}, u32[]{:S(2)}, u32[]{:S(2)}) collective-permute-start(bf16[640,640]{1,0:T(8,128)(2,1)} %collective-permute-done.8), channel_id=1, source_target_pairs={{0,4},{4,0},{32,36},{36,32},{64,68},{68,64},{96,100},{100,96},{128... | collective-permute-start | bytes 2457608 | tf_op jit(solution)/shard_map/ppermute | solution.py:297
  127.8 33.4 %collective-permute-start.13 = (bf16[640,640]{1,0:T(8,128)(2,1)}, bf16[640,640]{1,0:T(8,128)(2,1)}, u32[]{:S(2)}, u32[]{:S(2)}) collective-permute-start(bf16[640,640]{1,0:T(8,128)(2,1)} %collective-permute-done.9), channel_id=1, source_target_pairs={{0,3},{1,0},{2,1},{3,2},{32,35},{33,32},{34,33},{35,34},{64,67},{6... | collective-permute-start | bytes 2457608 | tf_op jit(solution)/shard_map/ppermute | solution.py:310
  132.7 28.5 %collective-permute-start.14 = (bf16[640,640]{1,0:T(8,128)(2,1)}, bf16[640,640]{1,0:T(8,128)(2,1)}, u32[]{:S(2)}, u32[]{:S(2)}) collective-permute-start(bf16[640,640]{1,0:T(8,128)(2,1)} %get-tuple-element.1682), channel_id=1, source_target_pairs={{0,4},{4,0},{32,36},{36,32},{64,68},{68,64},{96,100},{100,96},{128... | collective-permute-start | bytes 2457608 | tf_op jit(solution)/shard_map/ppermute | solution.py:297
  134.9 26.3 %collective-permute-start.15 = (bf16[640,640]{1,0:T(8,128)(2,1)}, bf16[640,640]{1,0:T(8,128)(2,1)}, u32[]{:S(2)}, u32[]{:S(2)}) collective-permute-start(bf16[640,640]{1,0:T(8,128)(2,1)} %get-tuple-element.1683), channel_id=1, source_target_pairs={{0,4},{4,0},{32,36},{36,32},{64,68},{68,64},{96,100},{100,96},{128... | collective-permute-start | bytes 2457608 | tf_op jit(solution)/shard_map/ppermute | solution.py:297
  142.8 18.4 %collective-permute-start.17 = (bf16[640,640]{1,0:T(8,128)(2,1)}, bf16[640,640]{1,0:T(8,128)(2,1)}, u32[]{:S(2)}, u32[]{:S(2)}) collective-permute-start(bf16[640,640]{1,0:T(8,128)(2,1)} %collective-permute-done.9), channel_id=1, source_target_pairs={{0,4},{4,0},{32,36},{36,32},{64,68},{68,64},{96,100},{100,96},{128... | collective-permute-start | bytes 2457608 | tf_op jit(solution)/shard_map/ppermute | solution.py:297
  161.2 45.4 %collective-permute-start.19 = (bf16[640,640]{1,0:T(8,128)(2,1)}, bf16[640,640]{1,0:T(8,128)(2,1)}, u32[]{:S(2)}, u32[]{:S(2)}) collective-permute-start(bf16[640,640]{1,0:T(8,128)(2,1)} %collective-permute-done.12), channel_id=1, source_target_pairs={{0,4},{4,0},{32,36},{36,32},{64,68},{68,64},{96,100},{100,96},{128... | collective-permute-start | bytes 2457608 | tf_op jit(solution)/shard_map/ppermute | solution.py:297
  163.6 43.1 %collective-permute-start.20 = (bf16[640,640]{1,0:T(8,128)(2,1)}, bf16[640,640]{1,0:T(8,128)(2,1)}, u32[]{:S(2)}, u32[]{:S(2)}) collective-permute-start(bf16[640,640]{1,0:T(8,128)(2,1)} %collective-permute-done.13), channel_id=1, source_target_pairs={{0,4},{4,0},{32,36},{36,32},{64,68},{68,64},{96,100},{100,96},{128... | collective-permute-start | bytes 2457608 | tf_op jit(solution)/shard_map/ppermute | solution.py:297
  205.1 1.6 copy-start.7
  211.3 302.4 %collective-permute-start = (bf16[32,1408]{1,0:T(8,128)(2,1)}, bf16[32,1408]{1,0:T(8,128)(2,1)S(1)}, u32[]{:S(2)}, u32[]{:S(2)}) collective-permute-start(bf16[32,1408]{1,0:T(8,128)(2,1)} %param.9), channel_id=1, source_target_pairs={{480,448},{416,384},{352,320},{288,256},{224,192},{160,128},{96,64... | collective-permute-start | bytes 270344 | tf_op jit(solution)/shard_map/while/body/eval_jaxpr/cond/branch_1_fun/ppermute | solution.py:367
  531.1 19.6 %collective-permute-start = (bf16[32,1408]{1,0:T(8,128)(2,1)}, bf16[32,1408]{1,0:T(8,128)(2,1)S(1)}, u32[]{:S(2)}, u32[]{:S(2)}) collective-permute-start(bf16[32,1408]{1,0:T(8,128)(2,1)} %param.9), channel_id=1, source_target_pairs={{480,448},{416,384},{352,320},{288,256},{224,192},{160,128},{96,64... | collective-permute-start | bytes 270344 | tf_op jit(solution)/shard_map/while/body/eval_jaxpr/cond/branch_1_fun/ppermute | solution.py:367
  586.7 55.0 %collective-permute-start.23 = (f32[8,16,640]{2,1,0:T(8,128)S(1)}, f32[8,16,640]{2,1,0:T(8,128)}, u32[]{:S(2)}, u32[]{:S(2)}) collective-permute-start(f32[8,16,640]{2,1,0:T(8,128)S(1)} %slice_select_fusion), channel_id=1, source_target_pairs={{0,4},{4,0},{1,5},{5,1},{2,6},{6,2},{3,7},{7,3},{8,12},{12,8},{9,1... | collective-permute-start | bytes 983048 | tf_op jit(solution)/shard_map/ppermute | solution.py:44
  627.0 7.7 %all-to-all-start.4 = ((bf16[4,2,32,128]{3,2,1,0:T(8,128)(2,1)}), bf16[4,2,32,128]{3,2,1,0:T(8,128)(2,1)S(1)}, u32[]{:S(2)}, u32[]{:S(2)}) async-start(bf16[4,2,32,128]{3,2,1,0:T(8,128)(2,1)} %broadcast_in_dim.170), calls=%async_computation.4 | async-start | bytes 131072 | tf_op jit(solution)/shard_map/all_to_all | solution.py:49
  635.9 5.0 collective-permute-start.21
  639.0 4.7 collective-permute-start.22
